TPU v7x, 128 devices: a whole 4x4x4 slice. The times are simulated.
128 devices in a mesh: slab: 8 (over y, z_lo), shot: 16 (over x, z_hi, core).
Axes of the slice: x: 4, y: 4, z: 4 (z_hi: 2, z_lo: 2; z = z_hi * 2 + z_lo), core: 2. Of those that a mesh axis runs over, the one named last changes fastest.
Arguments:
- forward_state: float32 [16, 9, 5, 5, 5, 2048], P('shot', None, None, None, None, 'slab'), may hold values from -6 to 6
- adjoint_state: float32 [16, 9, 5, 5, 5, 2048], P('shot', None, None, None, None, 'slab'), may hold values from -6 to 6
- materials: float32 [3, 5, 5, 5, 2048], P(None, None, None, None, 'slab'), may hold values from 0.5 to 2
- plane_neighbours: int32 [256, 4], replicated, may hold values from 0 to 255, as said below
- source_element: int32 [16], P('shot'), may hold values from 0 to 2047
- source_pulse: float32 [16, 2, 3], P('shot'), may hold values from -6 to 6
- receiver_elements: int32 [256], replicated, may hold values from 0 to 2047
- receiver_residuals: float32 [16, 2, 3, 256], P('shot'), may hold values from -6 to 6
Outputs:
- gradient: float32 [3, 5, 5, 5, 2048], P(None, None, None, None, ('slab', 'shot'))
- adjoint_end: float32 [16, 9, 5, 5, 5, 2048], P('shot', None, None, None, None, 'slab')
Inputs may be any that keep to these rules, and one draw needn't show every extreme that they name: `plane_neighbours`: the plane positions are the cells of a periodic 16 x 16 grid in some numbering; columns 0 and 1 give a position's lower and upper neighbours along y, columns 2 and 3 along z, and the two of a pair are inverse to each other.
All inputs are finite; a program needn't handle non-finite values.
Results may differ from a plain program's by a relative error of at most 0.0003.
Values sent between devices are 32-bit elements; how exact they have to be, the bound alone decides.
No kernel may reach another device: no remote copies, remote signals or barrier semaphores. Data moves between devices by JAX's collectives and lax.ppermute only.
A program may use at most 128 MiB of HBM per device.

v0:
```python
import math

import jax
import jax.numpy as jnp
import numpy as np
from jax import lax
from jax.sharding import PartitionSpec as P

STEPS = 2


time_step = 0.01
lift_gain = 10.0
stress_columns = ((3, 8, 7), (8, 4, 6), (7, 6, 5))


def passed_along(value, axis, steps):
    count = lax.axis_size(axis)
    pairs = [(source, (source + steps) % count) for source in range(count)]
    return lax.ppermute(value, axis, pairs)


def gll_tables():
    root = math.sqrt(3.0 / 7.0)
    points = np.array([-1.0, -root, 0.0, root, 1.0])
    legendre = (35.0 * points**4 - 30.0 * points**2 + 3.0) / 8.0
    matrix = np.zeros((5, 5))
    for row_index in range(5):
        for col_index in range(5):
            if row_index != col_index:
                matrix[row_index, col_index] = legendre[row_index] / (
                    legendre[col_index] * (points[row_index] - points[col_index])
                )
    matrix[0, 0] = -5.0
    matrix[4, 4] = 5.0
    quadrature = np.array([0.1, 49.0 / 90.0, 32.0 / 45.0, 49.0 / 90.0, 0.1])
    volume = quadrature[:, None, None] * quadrature[None, :, None] * quadrature[None, None, :]
    return (jnp.asarray(matrix, jnp.float32), jnp.asarray(volume, jnp.float32))


def node_derivative(wavefield, direction, derivative_table):
    einsum_forms = ("ia,zkabcuv->zkibcuv", "ib,zkabcuv->zkaicuv", "ic,zkabcuv->zkabiuv")
    return jnp.einsum(
        einsum_forms[direction], derivative_table, wavefield, precision=lax.Precision.HIGHEST
    )


def face_of(wavefield, direction, position):
    return lax.index_in_dim(wavefield, position, 2 + direction, keepdims=False)


def add_on_face(target, direction, position, addend):
    location = (slice(None),) * (2 + direction) + (position,)
    return target.at[location].add(addend)


def jump_derivative(wavefield, direction, minus_side, plus_side, derivative_table):
    grown = node_derivative(wavefield, direction, derivative_table)
    grown = add_on_face(
        grown, direction, 0, -0.5 * lift_gain * (minus_side - face_of(wavefield, direction, 0))
    )
    grown = add_on_face(
        grown, direction, 4, 0.5 * lift_gain * (plus_side - face_of(wavefield, direction, 4))
    )
    return grown


def neighbours_along(wavefield, direction, plane_neighbours, x_sides):
    if direction == 0:
        return x_sides(face_of(wavefield, 0, 4), face_of(wavefield, 0, 0))
    lower_column = 2 * direction - 2
    minus_side = jnp.take(
        face_of(wavefield, direction, 4), plane_neighbours[:, lower_column], axis=-1
    )
    plus_side = jnp.take(
        face_of(wavefield, direction, 0), plane_neighbours[:, lower_column + 1], axis=-1
    )
    return (minus_side, plus_side)


def leap_step(wavefield, shaped, plane_neighbours, inject, derivative_table, x_sides):
    lame_first = shaped[0]
    shear = shaped[1]
    density = shaped[2]
    summed = None
    for direction in range(3):
        subset = wavefield[:, list(stress_columns[direction])]
        minus_side, plus_side = neighbours_along(subset, direction, plane_neighbours, x_sides)
        contribution = jump_derivative(subset, direction, minus_side, plus_side, derivative_table)
        summed = contribution if summed is None else summed + contribution
    acceleration = summed / density
    velocity = wavefield[:, 0:3] + time_step * acceleration
    velocity = velocity.at[:, :, 2, 2, 2].add(inject)
    gradients = []
    for direction in range(3):
        minus_side, plus_side = neighbours_along(velocity, direction, plane_neighbours, x_sides)
        gradients.append(
            jump_derivative(velocity, direction, minus_side, plus_side, derivative_table)
        )
    divergence = gradients[0][:, 0] + gradients[1][:, 1] + gradients[2][:, 2]
    stress_rates = jnp.stack(
        [
            lame_first * divergence + 2.0 * shear * gradients[0][:, 0],
            lame_first * divergence + 2.0 * shear * gradients[1][:, 1],
            lame_first * divergence + 2.0 * shear * gradients[2][:, 2],
            shear * (gradients[2][:, 1] + gradients[1][:, 2]),
            shear * (gradients[2][:, 0] + gradients[0][:, 2]),
            shear * (gradients[1][:, 0] + gradients[0][:, 1]),
        ],
        axis=1,
    )
    stress = wavefield[:, 3:] + time_step * stress_rates
    return (jnp.concatenate([velocity, stress], axis=1), acceleration)


def image_terms(forward, adjoint, acceleration, derivative_table, volume_weights):
    forward_grad = [
        node_derivative(forward[:, 0:3], direction, derivative_table) for direction in range(3)
    ]
    adjoint_grad = [
        node_derivative(adjoint[:, 0:3], direction, derivative_table) for direction in range(3)
    ]
    forward_trace = forward_grad[0][:, 0] + forward_grad[1][:, 1] + forward_grad[2][:, 2]
    adjoint_trace = adjoint_grad[0][:, 0] + adjoint_grad[1][:, 1] + adjoint_grad[2][:, 2]
    strain_product = forward_grad[0][:, 0] * adjoint_grad[0][:, 0]
    strain_product = strain_product + forward_grad[1][:, 1] * adjoint_grad[1][:, 1]
    strain_product = strain_product + forward_grad[2][:, 2] * adjoint_grad[2][:, 2]
    for outer_index, inner_index in ((0, 1), (0, 2), (1, 2)):
        forward_sym = (
            forward_grad[inner_index][:, outer_index] + forward_grad[outer_index][:, inner_index]
        )
        adjoint_sym = (
            adjoint_grad[inner_index][:, outer_index] + adjoint_grad[outer_index][:, inner_index]
        )
        strain_product = strain_product + 0.5 * forward_sym * adjoint_sym
    inertia = (
        acceleration[:, 0] * adjoint[:, 0]
        + acceleration[:, 1] * adjoint[:, 1]
        + acceleration[:, 2] * adjoint[:, 2]
    )
    stacked = jnp.stack([forward_trace * adjoint_trace, 2.0 * strain_product, inertia], axis=1)
    return jnp.sum(stacked, axis=0) * volume_weights[:, :, :, None, None]


def body(
    forward_state,
    adjoint_state,
    materials,
    plane_neighbours,
    source_element,
    source_pulse,
    receiver_elements,
    receiver_residuals,
):
    derivative_table, volume_weights = gll_tables()
    plane_cells = plane_neighbours.shape[0]
    elements = materials.shape[-1]
    layers = elements // plane_cells
    shaped = materials.reshape(3, 5, 5, 5, layers, plane_cells)
    offset = lax.axis_index("slab") * elements
    element_ids = jnp.arange(elements, dtype=jnp.int32) + offset
    source_hits = (element_ids == source_element[0]).astype(jnp.float32)
    receiver_hits = (receiver_elements[:, None] == element_ids[None, :]).astype(jnp.float32)

    def x_sides(high_face, low_face):
        edge_shape = high_face.shape[:-2] + (1, plane_cells)
        leading = (high_face.shape[0], high_face.shape[1], -1)
        from_below = passed_along(high_face[..., -1, :].reshape(leading), "slab", 1)
        from_above = passed_along(low_face[..., 0, :].reshape(leading), "slab", -1)
        minus_side = jnp.concatenate(
            [from_below.reshape(edge_shape), high_face[..., :-1, :]], axis=-2
        )
        plus_side = jnp.concatenate([low_face[..., 1:, :], from_above.reshape(edge_shape)], axis=-2)
        return (minus_side, plus_side)

    forward_start = forward_state.reshape(1, 9, 5, 5, 5, layers, plane_cells)
    adjoint_start = adjoint_state.reshape(1, 9, 5, 5, 5, layers, plane_cells)
    forward_list = []
    accel_list = []
    adjoint_list = []
    forward_now = forward_start
    for step_index in range(STEPS):
        forward_now, acceleration = leap_step(
            forward_now,
            shaped,
            plane_neighbours,
            (source_pulse[0, step_index][:, None] * source_hits[None, :]).reshape(
                1, 3, layers, plane_cells
            ),
            derivative_table,
            x_sides,
        )
        forward_list.append(forward_now)
        accel_list.append(acceleration)
    adjoint_now = adjoint_start
    for step_index in range(STEPS):
        placed = jnp.dot(
            receiver_residuals[0, step_index], receiver_hits, precision=lax.Precision.HIGHEST
        )
        adjoint_now, unused_accel = leap_step(
            adjoint_now,
            shaped,
            plane_neighbours,
            placed.reshape(1, 3, layers, plane_cells),
            derivative_table,
            x_sides,
        )
        adjoint_list.append(adjoint_now)
    partial_terms = []
    for time_index in range(STEPS, 0, -1):
        adjoint_then = (
            adjoint_start if time_index == STEPS else adjoint_list[STEPS - 1 - time_index]
        )
        imaged = image_terms(
            forward_list[time_index - 1],
            adjoint_then,
            accel_list[time_index - 1],
            derivative_table,
            volume_weights,
        )
        partial_terms.append(imaged.reshape(3, 5, 5, 5, elements))
    local_total = partial_terms[0]
    for extra_part in partial_terms[1:]:
        local_total = local_total + extra_part
    whole_total = lax.psum(local_total, "shot")
    owned_width = elements // lax.axis_size("shot")
    gradient = lax.dynamic_slice_in_dim(
        whole_total, lax.axis_index("shot") * owned_width, owned_width, 4
    )
    return (gradient, adjoint_now.reshape(1, 9, 5, 5, 5, elements))


def solution(mesh):
    return jax.shard_map(
        body,
        mesh=mesh,
        in_specs=(
            P("shot", None, None, None, None, "slab"),
            P("shot", None, None, None, None, "slab"),
            P(None, None, None, None, "slab"),
            P(),
            P("shot"),
            P("shot", None, None),
            P(),
            P("shot", None, None, None),
        ),
        out_specs=(
            P(None, None, None, None, ("slab", "shot")),
            P("shot", None, None, None, None, "slab"),
        ),
        check_vma=False,
    )
```

profile of v0, /device:TPU:1, one launch (start us, length us, event | category | flops | bytes accessed | tf_op | source)
XLA Modules:
  0.0 709.6 jit_solution(2758858814178415271)
XLA Ops:
  79.8 5.8 gather_fusion.24
  91.0 5.8 gather_fusion.26
  102.2 5.8 gather_fusion.12
  113.4 5.8 gather_fusion.14
  126.7 5.8 gather_fusion.27
  139.9 5.8 gather_fusion.25
  175.2 5.7 gather_fusion.28
  186.3 5.7 gather_fusion.30
  204.1 5.8 gather_fusion.29
  215.3 5.8 gather_fusion.31
  238.2 5.7 gather_fusion.15
  248.7 5.7 gather_fusion.13
  282.2 5.8 gather_fusion.32
  292.7 5.8 gather_fusion.34
  305.3 5.7 gather_fusion.35
  320.6 5.7 gather_fusion.33
  330.7 4.0 collective-permute-start.11
  358.9 5.8 gather_fusion.36
  372.1 5.7 gather_fusion.37
  383.3 5.7 gather_fusion.38
  396.4 5.7 gather_fusion.39
  407.8 5.7 gather_fusion.16
  420.9 5.7 gather_fusion.17
  431.9 5.7 gather_fusion.18
  444.9 5.6 gather_fusion.19
  458.1 3.9 collective-permute-start.3
  490.4 5.6 gather_fusion.22
  500.3 5.6 gather_fusion.23
  510.0 5.6 gather_fusion.20
  526.7 5.7 gather_fusion.21
  536.4 3.8 collective-permute-start.5
  559.6 141.0 %all-reduce.2.cloned.1.call-done = f32[3,5,5,5,256]{4,0,3,2,1:T(4,128)} async-done(((f32[3,5,5,5,256]{4,0,3,2,1:T(4,128)}), f32[3,5,5,5,256]{4,0,3,2,1:T(4,128)}) %all-reduce.2.cloned.1.call-update) | async-done | bytes 384016 | tf_op jit(solution)/shard_map/psum | solution.py:225
  (470 shorter events, 380.3 us)
Async XLA Ops:
  7.2 693.5 %all-reduce.2.cloned.1.call-start = ((), (), s32[]{:S(2)}) async-start(), calls=%async_computation | async-start | bytes 1024000 | tf_op jit(solution)/shard_map/psum | solution.py:225
  14.2 142.7 %collective-permute-start = (f32[1,3,6400]{2,0,1:T(1,128)}, f32[1,3,6400]{2,0,1:T(1,128)}, u32[]{:S(2)}, u32[]{:S(2)}) collective-permute-start(f32[1,3,6400]{2,0,1:T(1,128)} %bitcast.7), channel_id=1, source_target_pairs={{0,16},{16,32},{32,48},{48,64},{64,80},{80,96},{96,112},{112,0},{1... | collective-permute-start | bytes 230408 | tf_op jit(solution)/shard_map/ppermute | solution.py:20
  18.1 12.5 %copy-start.20 = (f32[5,5,1,1,1]{1,0,4,3,2:T(8,128)S(1)}, f32[5,5,1,1,1]{1,0,4,3,2:T(8,128)}, u32[]{:S(2)}) copy-start(f32[5,5,1,1,1]{1,0,4,3,2:T(8,128)} %constant.1077) | copy-start | bytes 304
  24.3 128.1 %collective-permute-start.6 = (f32[1,3,6400]{2,0,1:T(1,128)}, f32[1,3,6400]{2,0,1:T(1,128)}, u32[]{:S(2)}, u32[]{:S(2)}) collective-permute-start(f32[1,3,6400]{2,0,1:T(1,128)} %bitcast.160), channel_id=1, source_target_pairs={{0,16},{16,32},{32,48},{48,64},{64,80},{80,96},{96,112},{112,0},{1... | collective-permute-start | bytes 230408 | tf_op jit(solution)/shard_map/ppermute | solution.py:20
  56.6 13.5 %copy-start.25 = (f32[3,5,5,256,5]{3,4,2,1,0:T(8,128)S(1)}, f32[3,5,5,256,5]{3,4,2,1,0:T(8,128)}, u32[]{:S(2)}) copy-start(f32[3,5,5,256,5]{3,4,2,1,0:T(8,128)} %fusion.232) | copy-start | bytes 1152004
  56.9 103.9 %copy-start.17 = (f32[1,5,5,5,256]{4,3,2,1,0:T(8,128)}, f32[1,5,5,5,256]{4,3,2,1,0:T(8,128)S(1)}, u32[]{:S(2)}) copy-start(f32[1,5,5,5,256]{4,3,2,1,0:T(8,128)S(1)} %copy.1356) | copy-start | bytes 384004
  61.9 13.5 %copy-start.24 = (f32[3,5,5,256,5]{3,4,2,1,0:T(8,128)S(1)}, f32[3,5,5,256,5]{3,4,2,1,0:T(8,128)}, u32[]{:S(2)}) copy-start(f32[3,5,5,256,5]{3,4,2,1,0:T(8,128)} %fusion.16) | copy-start | bytes 1152004
  154.2 4.8 collective-permute-start.7
  158.7 65.5 %collective-permute-start.1 = (f32[1,3,6400]{2,0,1:T(1,128)}, f32[1,3,6400]{2,0,1:T(1,128)}, u32[]{:S(2)}, u32[]{:S(2)}) collective-permute-start(f32[1,3,6400]{2,0,1:T(1,128)} %bitcast.9), channel_id=1, source_target_pairs={{0,112},{16,0},{32,16},{48,32},{64,48},{80,64},{96,80},{112,96},{1... | collective-permute-start | bytes 230408 | tf_op jit(solution)/shard_map/ppermute | solution.py:20
  167.2 62.8 %collective-permute-start.8 = (f32[1,3,6400]{2,0,1:T(1,128)}, f32[1,3,6400]{2,0,1:T(1,128)}, u32[]{:S(2)}, u32[]{:S(2)}) collective-permute-start(f32[1,3,6400]{2,0,1:T(1,128)} %bitcast.206), channel_id=1, source_target_pairs={{0,16},{16,32},{32,48},{48,64},{64,80},{80,96},{96,112},{112,0},{1... | collective-permute-start | bytes 230408 | tf_op jit(solution)/shard_map/ppermute | solution.py:20
  183.6 13.6 %copy-start.65 = (f32[1,3,5,5,1,1,256]{6,1,4,3,2,5,0:T(4,128)S(1)}, f32[1,3,5,5,1,1,256]{6,1,4,3,2,5,0:T(4,128)}, u32[]{:S(2)}) copy-start(f32[1,3,5,5,1,1,256]{6,1,4,3,2,5,0:T(4,128)} %get-tuple-element.624) | copy-start | bytes 230404
  231.9 25.3 %collective-permute-start.9 = (f32[1,3,6400]{2,0,1:T(1,128)S(1)}, f32[1,3,6400]{2,0,1:T(1,128)}, u32[]{:S(2)}, u32[]{:S(2)}) collective-permute-start(f32[1,3,6400]{2,0,1:T(1,128)S(1)} %bitcast.967), channel_id=1, source_target_pairs={{0,112},{16,0},{32,16},{48,32},{64,48},{80,64},{96,80},{112,96},{1... | collective-permute-start | bytes 230408 | tf_op jit(solution)/shard_map/ppermute | solution.py:20
  278.0 12.6 %copy-start.55 = (f32[1,3,1,5,5,1,256]{6,1,4,3,2,5,0:T(4,128)}, f32[1,3,1,5,5,1,256]{6,1,4,3,2,5,0:T(4,128)S(1)}, u32[]{:S(2)}) copy-start(f32[1,3,1,5,5,1,256]{6,1,4,3,2,5,0:T(4,128)S(1)} %get-tuple-element.611) | copy-start | bytes 230404
  278.7 50.2 %collective-permute-start.10 = (f32[1,3,6400]{2,0,1:T(1,128)}, f32[1,3,6400]{2,0,1:T(1,128)}, u32[]{:S(2)}, u32[]{:S(2)}) collective-permute-start(f32[1,3,6400]{2,0,1:T(1,128)} %bitcast.240), channel_id=1, source_target_pairs={{0,16},{16,32},{32,48},{48,64},{64,80},{80,96},{96,112},{112,0},{1... | collective-permute-start | bytes 230408 | tf_op jit(solution)/shard_map/ppermute | solution.py:20
  302.4 12.9 %copy-start.40 = (f32[1,3,5,5,5,1,256]{6,0,5,4,3,2,1:T(1,128)S(1)}, f32[1,3,5,5,5,1,256]{6,0,5,4,3,2,1:T(1,128)}, u32[]{:S(2)}) copy-start(f32[1,3,5,5,5,1,256]{6,0,5,4,3,2,1:T(1,128)} %get-tuple-element.653) | copy-start | bytes 1152004
  302.4 12.9 %copy-start.51 = (f32[1,3,5,5,1,1,256]{6,1,4,3,2,5,0:T(4,128)S(1)}, f32[1,3,5,5,1,1,256]{6,1,4,3,2,5,0:T(4,128)}, u32[]{:S(2)}) copy-start(f32[1,3,5,5,1,1,256]{6,1,4,3,2,5,0:T(4,128)} %copy-done.50) | copy-start | bytes 230404
  302.4 12.9 %copy-start.61 = (f32[1,3,5,5,1,1,256]{6,1,4,3,2,5,0:T(4,128)S(1)}, f32[1,3,5,5,1,1,256]{6,1,4,3,2,5,0:T(4,128)}, u32[]{:S(2)}) copy-start(f32[1,3,5,5,1,1,256]{6,1,4,3,2,5,0:T(4,128)} %copy-done.60) | copy-start | bytes 230404
  317.8 16.8 %copy-start.41 = (f32[1,3,5,5,5,1,256]{6,0,5,4,3,2,1:T(1,128)S(1)}, f32[1,3,5,5,5,1,256]{6,0,5,4,3,2,1:T(1,128)}, u32[]{:S(2)}) copy-start(f32[1,3,5,5,5,1,256]{6,0,5,4,3,2,1:T(1,128)} %get-tuple-element.655) | copy-start | bytes 1152004
  317.8 16.8 %copy-start.49 = (f32[1,3,5,1,5,1,256]{6,1,4,3,2,5,0:T(4,128)S(1)}, f32[1,3,5,1,5,1,256]{6,1,4,3,2,5,0:T(4,128)}, u32[]{:S(2)}) copy-start(f32[1,3,5,1,5,1,256]{6,1,4,3,2,5,0:T(4,128)} %copy-done.48) | copy-start | bytes 230404
  320.6 15.5 %copy-start.56 = (f32[1,3,1,5,5,1,256]{6,1,4,3,2,5,0:T(4,128)S(1)}, f32[1,3,1,5,5,1,256]{6,1,4,3,2,5,0:T(4,128)}, u32[]{:S(2)}) copy-start(f32[1,3,1,5,5,1,256]{6,1,4,3,2,5,0:T(4,128)} %copy-done.55) | copy-start | bytes 230404
  320.6 17.2 %copy-start.18 = (f32[1,5,5,5,256]{4,3,2,1,0:T(8,128)S(1)}, f32[1,5,5,5,256]{4,3,2,1,0:T(8,128)}, u32[]{:S(2)}) copy-start(f32[1,5,5,5,256]{4,3,2,1,0:T(8,128)} %copy-done.17) | copy-start | bytes 384004
  330.7 5.4 collective-permute-start.11
  354.4 102.4 %collective-permute-start.2 = (f32[1,3,6400]{2,0,1:T(1,128)}, f32[1,3,6400]{2,0,1:T(1,128)}, u32[]{:S(2)}, u32[]{:S(2)}) collective-permute-start(f32[1,3,6400]{2,0,1:T(1,128)} %bitcast.57), channel_id=1, source_target_pairs={{0,16},{16,32},{32,48},{48,64},{64,80},{80,96},{96,112},{112,0},{1... | collective-permute-start | bytes 230408 | tf_op jit(solution)/shard_map/ppermute | solution.py:20
  354.4 107.6 %collective-permute-start.12 = (f32[1,3,6400]{2,0,1:T(1,128)}, f32[1,3,6400]{2,0,1:T(1,128)}, u32[]{:S(2)}, u32[]{:S(2)}) collective-permute-start(f32[1,3,6400]{2,0,1:T(1,128)} %bitcast.281), channel_id=1, source_target_pairs={{0,16},{16,32},{32,48},{48,64},{64,80},{80,96},{96,112},{112,0},{1... | collective-permute-start | bytes 230408 | tf_op jit(solution)/shard_map/ppermute | solution.py:20
  456.4 13.5 %copy-start.36 = (f32[1,3,5,5,5,1,256]{6,0,5,4,3,2,1:T(1,128)S(1)}, f32[1,3,5,5,5,1,256]{6,0,5,4,3,2,1:T(1,128)}, u32[]{:S(2)}) copy-start(f32[1,3,5,5,5,1,256]{6,0,5,4,3,2,1:T(1,128)} %get-tuple-element.659) | copy-start | bytes 1152004
  458.1 6.9 collective-permute-start.3
  463.1 4.8 collective-permute-start.13
  487.1 47.3 %collective-permute-start.4 = (f32[1,3,6400]{2,0,1:T(1,128)S(1)}, f32[1,3,6400]{2,0,1:T(1,128)}, u32[]{:S(2)}, u32[]{:S(2)}) collective-permute-start(f32[1,3,6400]{2,0,1:T(1,128)S(1)} %reshape_squeeze_squeeze.48), channel_id=1, source_target_pairs={{0,16},{16,32},{32,48},{48,64},{64,80},{80,96},{96,112},{112,0},{1... | collective-permute-start | bytes 230408 | tf_op jit(solution)/shard_map/ppermute | solution.py:20
  508.0 13.0 %slice-start.1 = ((f32[3,5,5,256,5]{3,4,2,1,0:T(8,128)}), f32[3,5,5,256,1]{3,4,2,1,0:T(1,128)S(1)}, s32[]{:S(2)}) async-start(f32[3,5,5,256,5]{3,4,2,1,0:T(8,128)} %copy-done.32), calls=%async_computation.2 | async-start | bytes 153600 | tf_op jit(solution)/shard_map/slice.2062
  526.7 13.6 %copy-start.21 = (f32[1,3,5,5,5,1,256]{6,4,5,3,2,1,0:T(8,128)S(1)}, f32[1,3,5,5,5,1,256]{6,4,5,3,2,1,0:T(8,128)}, u32[]{:S(2)}) copy-start(f32[1,3,5,5,5,1,256]{6,4,5,3,2,1,0:T(8,128)} %fusion.92) | copy-start | bytes 1152004
  534.4 13.1 %copy-start.19 = (f32[1,5,5,5,256]{4,3,2,1,0:T(8,128)S(1)}, f32[1,5,5,5,256]{4,3,2,1,0:T(8,128)}, u32[]{:S(2)}) copy-start(f32[1,5,5,5,256]{4,3,2,1,0:T(8,128)} %copy-done.17) | copy-start | bytes 384004
  536.4 7.9 %collective-permute-start.5 = (f32[1,3,6400]{2,0,1:T(1,128)S(1)}, f32[1,3,6400]{2,0,1:T(1,128)S(1)}, u32[]{:S(2)}, u32[]{:S(2)}) collective-permute-start(f32[1,3,6400]{2,0,1:T(1,128)S(1)} %reshape_squeeze_squeeze.49), channel_id=1, source_target_pairs={{0,112},{16,0},{32,16},{48,32},{64,48},{80,64},{96,80},{112,96},{1... | collective-permute-start | bytes 230408 | tf_op jit(solution)/shard_map/ppermute | solution.py:20
  (68 other events, 339.3 us)
Sparse Core Ops, SparseCore 0:
  556.6 143.9 all-reduce.1
where the time goes:
time: 723 us; the launch traced here: 710 us
  local copies, waits for them, and re-layouts  406 us (56%)
  waiting for transfers between devices  144 us (20%)
  other arithmetic  85.8 us (12%)
  matrix products  33.6 us (5%)
  starting transfers between devices  24.2 us (3%)
  between operations  16.3 us (2%)
    psum x1, waiting for transfers between devices, body(): whole_total = lax.psum(local_total, 'shot')  141 us
    gather x28, local copies, waits for them, and re-layouts, neighbours_along(): jnp.take(face_of(wavefield, direction, 0), plane_neighbours[:, lower_colu...  116 us
    gather x28, local copies, waits for them, and re-layouts, neighbours_along(): jnp.take(face_of(wavefield, direction, 4), plane_neighbours[:, lower_colu...  115 us
    another operation x15, local copies, waits for them, and re-layouts, neighbours_along(): jnp.take(face_of(wavefield, direction, 0), plane_neighbours[:, lower_colu...  37.1 us
    another operation x14, local copies, waits for them, and re-layouts, neighbours_along(): jnp.take(face_of(wavefield, direction, 4), plane_neighbours[:, lower_colu...  36.3 us
    gather x22, local copies, waits for them, and re-layouts, leap_step(): subset = wavefield[:, list(stress_columns[direction])]  35.8 us
    scatter-add x24, other arithmetic, add_on_face(): return target.at[location].add(addend)  35 us
    dot_general x27, matrix products, node_derivative(): jnp.einsum(einsum_forms[direction], derivative_table, wavefield, precisio...  32.5 us
  transfers between devices with their start and end apart: 15, of which 3 were waited for; matrix products, arithmetic and copies ran while one was open for 61% of the time, Pallas kernels for 0%

commit v1 on v0

v1 whole, which is shorter than its diff:
```python
import math

import jax
import jax.numpy as jnp
import numpy as np
from jax import lax
from jax.experimental import pallas as pl
from jax.experimental.pallas import tpu as pltpu
from jax.sharding import PartitionSpec as P

f32 = jnp.float32
bf16 = jnp.bfloat16

time_step = 0.01
N = 256
STATE = (1, 9, 5, 5, 5, N)


def tables():
    root = math.sqrt(3.0 / 7.0)
    points = np.array([-1.0, -root, 0.0, root, 1.0])
    legendre = (35.0 * points**4 - 30.0 * points**2 + 3.0) / 8.0
    matrix = np.zeros((5, 5))
    for r in range(5):
        for c in range(5):
            if r != c:
                matrix[r, c] = legendre[r] / (legendre[c] * (points[r] - points[c]))
    matrix[0, 0] = -5.0
    matrix[4, 4] = 5.0
    quad = np.array([0.1, 49.0 / 90.0, 32.0 / 45.0, 49.0 / 90.0, 0.1])
    return matrix, quad


D_PLAIN, QUAD = tables()
D_LIFT = D_PLAIN.copy()
D_LIFT[0, 0] += 5.0
D_LIFT[4, 4] -= 5.0


def block_table(matrix):
    small = np.zeros((8, 8))
    small[:5, :5] = matrix
    whole = np.kron(np.eye(25), small).astype(np.float32)
    high = whole.astype(jnp.bfloat16)
    low = (whole - high.astype(np.float32)).astype(jnp.bfloat16)
    return np.stack([high, low])


def split(x):
    high = x.astype(bf16)
    return high, (x - high.astype(f32)).astype(bf16)


def dot(a, b):
    return lax.dot_general(a, b, (((1,), (0,)), ((), ())), preferred_element_type=f32)


def derive_rows(rows, matrix):
    even0, odd0 = rows[0] + rows[4], rows[0] - rows[4]
    even1, odd1 = rows[1] + rows[3], rows[1] - rows[3]
    out = [None] * 5
    for r in (0, 1):
        m = [float(v) for v in matrix[r]]
        p = 0.5 * (m[0] + m[4]) * even0 + 0.5 * (m[1] + m[3]) * even1 + m[2] * rows[2]
        q = 0.5 * (m[0] - m[4]) * odd0 + 0.5 * (m[1] - m[3]) * odd1
        out[r] = q + p
        out[4 - r] = q - p
    out[2] = float(matrix[2, 0]) * odd0 + float(matrix[2, 1]) * odd1
    return out


def derive_x(x, matrix):
    return jnp.stack(derive_rows([x[k] for k in range(5)], matrix), axis=0)


def derive_y(x, matrix):
    return jnp.stack(derive_rows([x[:, k] for k in range(5)], matrix), axis=1)


def derive_z(x, table):
    high, low = split(x.reshape(200, N))
    y = dot(table[0], high) + dot(table[0], low) + dot(table[1], high)
    return y.reshape(5, 5, 8, N)


def fill(dst, k, value):
    dst[k, :, :, 0:5, :] = value


def zero_pads(dst, count, value=0.0):
    for k in range(count):
        dst[k, :, :, 5:8, :] = jnp.full((5, 5, 3, N), value, f32)


def make_perms(nbr, perms):
    lane = lax.broadcasted_iota(jnp.int32, (N, N), 1)
    for k in range(4):
        sign = 5.0 if k % 2 == 0 else -5.0
        hit = nbr[:, k : k + 1] == lane
        perms[k] = jnp.where(hit, sign, 0.0).astype(bf16)


def permuted(face, matrix):
    high, low = split(face)
    return dot(high, matrix) + dot(low, matrix)


def jump_y(x, perms):
    at_low = permuted(x[:, 4].reshape(40, N), perms[1]).reshape(5, 8, N)
    at_high = permuted(x[:, 0].reshape(40, N), perms[0]).reshape(5, 8, N)
    return at_low, at_high


def jump_z(x, perms):
    rows = lax.broadcasted_iota(jnp.int32, (5, 5, 8, N), 2)
    turned = pltpu.roll(x.reshape(25, 8, N), 4, 1).reshape(5, 5, 8, N)
    down = jnp.where(rows == 0, turned, 0.0).reshape(200, N)
    up = jnp.where(rows == 4, turned, 0.0).reshape(200, N)
    return (permuted(down, perms[3]) + permuted(up, perms[2])).reshape(5, 5, 8, N)


def stress_of(i, d):
    return jnp.where(i == d, i, 6 - i - d)


def local_acceleration(stress, rinv, acc, table, perms):
    def one(i, carry):
        sx, sy, sz = stress[stress_of(i, 0)], stress[stress_of(i, 1)], stress[stress_of(i, 2)]
        total = derive_z(sz, table) + jump_z(sz, perms)
        total = total + derive_x(sx, D_LIFT)
        total = total + derive_y(sy, D_LIFT)
        acc[i] = total
        at_low, at_high = jump_y(sy, perms)
        acc[i, :, 0] += at_low
        acc[i, :, 4] += at_high
        acc[i] = acc[i] * rinv[...]
        return carry

    lax.fori_loop(0, 3, one, 0)


def pack_face(dst, k, value):
    for b in range(5):
        dst[k * 25 + 5 * b : k * 25 + 5 * b + 5, :] = value[b, 0:5]


def unpack_face(dst, k, src, j):
    for b in range(5):
        dst[k, b, 0:5, :] = src[j * 25 + 5 * b : j * 25 + 5 * b + 5, :]


def load_stress(state, stress):
    zero_pads(stress, 6)
    for k in range(6):
        fill(stress, k, state[0, 3 + k])


def load_material(mat, dst, k, pad):
    dst[:, :, 5:8, :] = jnp.full((5, 5, 3, N), pad, f32)
    dst[:, :, 0:5, :] = mat[k]


def inject_rows(kind, step, refs, base):
    if kind == "source":
        where_ref, pulse = refs
        lane = lax.broadcasted_iota(jnp.int32, (1, N), 1) + base
        hit = lane == where_ref[0]
        return [jnp.where(hit, pulse[0, step, i], 0.0) for i in range(3)]
    where_ref, residual = refs
    element = lax.broadcasted_iota(jnp.int32, (N, N), 0) + base
    hits = jnp.where(element == where_ref[...], 1.0, 0.0).astype(bf16)
    x = jnp.concatenate([residual[0, step], jnp.zeros((5, N), f32)], axis=0)
    total = None
    for part in range(3):
        high = x.astype(bf16)
        x = x - high.astype(f32)
        term = lax.dot_general(high, hits, (((1,), (1,)), ((), ())), preferred_element_type=f32)
        total = term if total is None else total + term
    return [total[i : i + 1] for i in range(3)]


def pack_sends(stress, acc, velocity, injected, rinv, up, down, first, with_v, with_r):
    for dst, a in ((up, 4), (down, 0)):
        for i in range(3):
            pack_face(dst, first + i, stress[(0, 5, 4)[i], a])
        if with_v:
            for i in range(3):
                pack_face(dst, first + 3 + i, velocity(i, a) + time_step * acc[i, a])
        if with_r:
            pack_face(dst, first + 6, 0.05 * rinv[a])


def start_kernel(fwd, adj, mat, nbr, table, f_up, f_down, a_up, a_down, f_acc, a_acc, stress, rinv, perms, vel):
    make_perms(nbr, perms)
    load_material(mat, rinv, 2, 1.0)
    rinv[...] = 1.0 / rinv[...]
    for state, acc, up, down, with_r in ((fwd, f_acc, f_up, f_down, True), (adj, a_acc, a_up, a_down, False)):
        load_stress(state, stress)
        local_acceleration(stress, rinv, acc, table, perms)
        vel[:, :, :, 5:8, :] = jnp.zeros((3, 2, 5, 3, N), f32)
        for i in range(3):
            vel[i, 0, :, 0:5, :] = state[0, i, 0]
            vel[i, 1, :, 0:5, :] = state[0, i, 4]
        pack_sends(
            stress, acc, lambda i, a: vel[i, a // 4], None, rinv, up, down, 0, True, with_r
        )


def finish_acceleration(acc, stress, rinv, halo, has_v):
    for i in range(3):
        k = (0, 5, 4)[i]
        acc[i, 0] = acc[i, 0] - 5.0 * rinv[0] * halo[0, i]
        acc[i, 4] = acc[i, 4] + 5.0 * rinv[4] * halo[1, i]
        if has_v:
            halo[0, 3 + i] = halo[0, 3 + i] + halo[0, 6] * stress[k, 0]
            halo[1, 3 + i] = halo[1, 3 + i] - halo[1, 6] * stress[k, 4]


def velocities(vel, acc, rows):
    mask = lax.broadcasted_iota(jnp.int32, (8, N), 0) == 2
    for i in range(3):
        vel[i] = vel[i] + time_step * acc[i]
        vel[i, 2, 2] = vel[i, 2, 2] + jnp.where(mask, rows[i], 0.0)


def jump_gradients(vel, halo, grads, table, perms):
    def one(i, carry):
        v = vel[i]
        gx = derive_x(v, D_LIFT)
        grads[i] = gx
        grads[i, 0] += -5.0 * halo[0, 3 + i]
        grads[i, 4] += 5.0 * halo[1, 3 + i]
        at_low, at_high = jump_y(v, perms)
        grads[3 + i] = derive_y(v, D_LIFT)
        grads[3 + i, :, 0] += at_low
        grads[3 + i, :, 4] += at_high
        grads[6 + i] = derive_z(v, table) + jump_z(v, perms)
        return carry

    lax.fori_loop(0, 3, one, 0)


def update_stress(stress, grads, lam, mu):
    def one(a, carry):
        g = lambda j, i: grads[3 * j + i, a]
        l, m = time_step * lam[a], time_step * mu[a]
        both = l * (g(0, 0) + g(1, 1) + g(2, 2))
        for i in range(3):
            stress[i, a] = stress[i, a] + (both + 2.0 * m * g(i, i))
        stress[3, a] = stress[3, a] + m * (g(2, 1) + g(1, 2))
        stress[4, a] = stress[4, a] + m * (g(2, 0) + g(0, 2))
        stress[5, a] = stress[5, a] + m * (g(1, 0) + g(0, 1))
        return carry

    lax.fori_loop(0, 5, one, 0)


def plain_gradients(vel, grads, table):
    def one(i, carry):
        v = vel[i]
        grads[i] = derive_x(v, D_PLAIN)
        grads[3 + i] = derive_y(v, D_PLAIN)
        grads[6 + i] = derive_z(v, table)
        return carry

    lax.fori_loop(0, 3, one, 0)


def load_halo(halo, below, above, plan, r_from):
    halo[:, :, :, 5:8, :] = jnp.zeros((2, 7, 5, 3, N), f32)
    for side, src in ((0, below), (1, above)):
        for slot, face in plan:
            unpack_face(halo.at[side], slot, src, face)
        if r_from is not None:
            unpack_face(halo.at[side], 6, r_from[side], 6)


def first_step_kernel(kind, base, state, mat, nbr, table, where_ref, strength, acc_in, below, above, r_below, r_above,
                      vel_out, stress_out, acc_out, next_acc, up, down,
                      rinv, lam, mu, halo, grads, perms):
    make_perms(nbr, perms)
    load_material(mat, rinv, 2, 1.0)
    rinv[...] = 1.0 / rinv[...]
    load_material(mat, lam, 0, 0.0)
    load_material(mat, mu, 1, 0.0)
    load_halo(halo, below, above, [(k, k) for k in range(6)], (r_below, r_above))
    load_stress(state, stress_out)
    zero_pads(vel_out, 3)
    for i in range(3):
        fill(vel_out, i, state[0, i])
    acc_out[...] = acc_in[...]
    finish_acceleration(acc_out, stress_out, rinv, halo, True)
    offset = base[0]
    velocities(vel_out, acc_out, inject_rows(kind, 0, (where_ref, strength), offset))
    jump_gradients(vel_out, halo, grads, table, perms)
    update_stress(stress_out, grads, lam, mu)
    local_acceleration(stress_out, rinv, next_acc, table, perms)
    adjoint = kind == "receiver"
    pack_sends(stress_out, next_acc, lambda i, a: vel_out[i, a], None, rinv, up, down, 0, adjoint, False)


def last_step_kernel(base, vel_in, stress_in, mat, nbr, table, where_ref, strength, acc_in, below, above, r_below, r_above,
                     out, rinv, lam, mu, halo, grads, perms, vel, stress, acc):
    make_perms(nbr, perms)
    load_material(mat, rinv, 2, 1.0)
    rinv[...] = 1.0 / rinv[...]
    load_material(mat, lam, 0, 0.0)
    load_material(mat, mu, 1, 0.0)
    load_halo(halo, below, above, [(k, k) for k in range(6)], (r_below, r_above))
    acc[...] = acc_in[...]
    vel[...] = vel_in[...]
    stress[...] = stress_in[...]
    finish_acceleration(acc, stress, rinv, halo, True)
    velocities(vel, acc, inject_rows("receiver", 1, (where_ref, strength), base[0]))
    jump_gradients(vel, halo, grads, table, perms)
    update_stress(stress, grads, lam, mu)
    for k in range(3):
        out[0, k] = vel[k, :, :, 0:5, :]
    for k in range(6):
        out[0, 3 + k] = stress[k, :, :, 0:5, :]


def image_kernel(base, adj, f_vel, f_acc, a_vel, mat, plain, where_ref, strength, acc_in, below, above,
                 out, rinv, halo, vel, acc, adj_vel, fg, ag, dense):
    load_material(mat, rinv, 2, 1.0)
    rinv[...] = 1.0 / rinv[...]
    load_halo(halo, below, above, [(k, k) for k in range(3)], None)
    acc[...] = acc_in[...]
    vel[...] = f_vel[...]
    finish_acceleration(acc, None, rinv, halo, False)
    velocities(vel, acc, inject_rows("source", 1, (where_ref, strength), base[0]))
    zero_pads(adj_vel, 3)
    for i in range(3):
        fill(adj_vel, i, adj[0, i])
    row = lax.broadcasted_iota(jnp.int32, (5, 8, N), 1)
    weight_c = jnp.zeros((5, 8, N), f32)
    for c in range(5):
        weight_c = jnp.where(row == c, float(QUAD[c]), weight_c)
    group = lax.broadcasted_iota(jnp.int32, (5, 8, N), 0)
    weight_b = jnp.zeros((5, 8, N), f32)
    for c in range(5):
        weight_b = jnp.where(group == c, float(QUAD[c]), weight_b)
    weight = weight_b * weight_c
    dense[368:384, :] = jnp.zeros((16, N), f32)
    for part in range(2):
        fv, av, fa = ((vel, adj_vel, acc), (f_vel, a_vel, f_acc))[part]
        plain_gradients(fv, fg, plain)
        plain_gradients(av, ag, plain)
        for a in range(5):
            f = lambda j, i: fg[3 * j + i, a]
            g = lambda j, i: ag[3 * j + i, a]
            w = weight * float(QUAD[a])
            f0, f1, f2 = f(0, 0), f(1, 1), f(2, 2)
            g0, g1, g2 = g(0, 0), g(1, 1), g(2, 2)
            first = (f0 + f1 + f2) * (g0 + g1 + g2) * w
            cross = None
            for i, j in ((0, 1), (0, 2), (1, 2)):
                term = (f(j, i) + f(i, j)) * (g(j, i) + g(i, j))
                cross = term if cross is None else cross + term
            second = (2.0 * (f0 * g0 + f1 * g1 + f2 * g2) + cross) * w
            third = (fa[0, a] * av[0, a] + fa[1, a] * av[1, a] + fa[2, a] * av[2, a]) * w
            for t, term in enumerate((first, second, third)):
                for b in range(5):
                    at = t * 125 + a * 25 + b * 5
                    if part == 0:
                        dense[at : at + 5, :] = term[b, 0:5]
                    else:
                        dense[at : at + 5, :] += term[b, 0:5]
    out[...] = dense[...].T


V = pl.BlockSpec(memory_space=pltpu.VMEM)
S = pl.BlockSpec(memory_space=pltpu.SMEM)


def field(count):
    return jax.ShapeDtypeStruct((count, 5, 5, 8, N), f32)


def sends(faces):
    return jax.ShapeDtypeStruct((faces * 25, N), f32)


def call(kernel, specs, outs, scratch, flops, moved):
    return pl.pallas_call(
        kernel,
        out_shape=outs,
        in_specs=specs,
        out_specs=jax.tree.map(lambda _: V, outs),
        scratch_shapes=scratch,
        compiler_params=pltpu.CompilerParams(vmem_limit_bytes=56 * 2**20),
        cost_estimate=pl.CostEstimate(flops=flops, bytes_accessed=moved, transcendentals=0),
    )


def scr(*shape):
    return pltpu.VMEM(shape, f32)


PERMS = pltpu.VMEM((4, N, N), bf16)
ONE = (5, 5, 8, N)


def passed_along(value, axis, steps):
    count = lax.axis_size(axis)
    pairs = [(source, (source + steps) % count) for source in range(count)]
    return lax.ppermute(value, axis, pairs)


def both_ways(up, down):
    return passed_along(up, "slab", 1), passed_along(down, "slab", -1)


def reduce_over_shots(x):
    x = x.reshape(4, 2, 2, 16, 384)
    place = lax.axis_index("shot")
    core, high, line = place % 2, (place // 2) % 2, place // 4
    pick = lambda v, k, axis: lax.dynamic_index_in_dim(v, k, axis, False)
    hop = lambda v, to: lax.ppermute(v, "shot", [(i, to(i)) for i in range(16)])
    x = pick(x, core, 2) + hop(pick(x, 1 - core, 2), lambda i: i ^ 1)
    total = pick(x, line, 0)
    for d in (1, 2, 3):
        total = total + hop(pick(x, (line + d) % 4, 0), lambda i: (i + 4 * d) % 16)
    return pick(total, high, 0) + hop(pick(total, 1 - high, 0), lambda i: i ^ 2)


def body(fwd, adj, materials, nbr, source_element, pulse, receivers, residuals):
    lift = jnp.asarray(block_table(D_LIFT))
    plain = jnp.asarray(block_table(D_PLAIN))
    base = (lax.axis_index("slab") * N).astype(jnp.int32).reshape(1)
    receivers = receivers.reshape(1, N)

    f_up, f_down, a_up, a_down, f_acc, a_acc = call(
        start_kernel,
        [V] * 5,
        (sends(7), sends(7), sends(6), sends(6), field(3), field(3)),
        [scr(6, *ONE), scr(*ONE), PERMS, scr(3, 2, 5, 8, N)],
        10**8, 4 * 10**6,
    )(fwd, adj, materials, nbr, lift)
    f_below, f_above = both_ways(f_up, f_down)
    a_below, a_above = both_ways(a_up, a_down)

    step_scratch = [scr(*ONE), scr(*ONE), scr(*ONE), scr(2, 7, 5, 8, N), scr(9, *ONE), PERMS]

    def first_step(kind, state, where_ref, strength, acc, below, above, faces):
        kernel = lambda base_ref, *refs: first_step_kernel(kind, base_ref, *refs)
        smem = S if kind == "source" else V
        return call(
            kernel,
            [S, V, V, V, V, smem, smem, V, V, V, V, V],
            (field(3), field(6), field(3), field(3), sends(faces), sends(faces)),
            step_scratch, 2 * 10**8, 10**7,
        )(base, state, materials, nbr, lift, where_ref, strength, acc, below, above, f_below, f_above)

    f_vel, _, f_acc1, f_acc2, f_up, f_down = first_step(
        "source", fwd, source_element, pulse, f_acc, f_below, f_above, 3
    )
    f_below2, f_above2 = both_ways(f_up, f_down)
    a_vel, a_stress, _, a_acc2, a_up, a_down = first_step(
        "receiver", adj, receivers, residuals, a_acc, a_below, a_above, 6
    )
    a_below2, a_above2 = both_ways(a_up, a_down)
    partial = call(
        image_kernel,
        [S, V, V, V, V, V, V, S, S, V, V, V],
        jax.ShapeDtypeStruct((N, 384), f32),
        [scr(*ONE), scr(2, 7, 5, 8, N), scr(3, *ONE), scr(3, *ONE), scr(3, *ONE), scr(9, *ONE), scr(9, *ONE), scr(384, N)],
        3 * 10**8, 10**7,
    )(base, adj, f_vel, f_acc1, a_vel, materials, plain, source_element, pulse, f_acc2, f_below2, f_above2)
    gradient = reduce_over_shots(partial)
    adjoint_end = call(
        last_step_kernel,
        [S, V, V, V, V, V, V, V, V, V, V, V, V],
        jax.ShapeDtypeStruct(STATE, f32),
        step_scratch + [scr(3, *ONE), scr(6, *ONE), scr(3, *ONE)],
        10**8, 10**7,
    )(base, a_vel, a_stress, materials, nbr, lift, receivers, residuals, a_acc2, a_below2, a_above2, f_below, f_above)
    return gradient[:, :375].T.reshape(3, 5, 5, 5, 16), adjoint_end


def solution(mesh):
    return jax.shard_map(
        body,
        mesh=mesh,
        in_specs=(
            P("shot", None, None, None, None, "slab"),
            P("shot", None, None, None, None, "slab"),
            P(None, None, None, None, "slab"),
            P(),
            P("shot"),
            P("shot", None, None),
            P(),
            P("shot", None, None, None),
        ),
        out_specs=(
            P(None, None, None, None, ("slab", "shot")),
            P("shot", None, None, None, None, "slab"),
        ),
        check_vma=False,
    )
```

time: 723 us -> 102 us (0.14)
  the two profiles are of different devices: /device:TPU:1 before, /device:TPU:0 now
where the time goes in v1:
time: 102 us; the launch traced here: 101 us
  Pallas kernels  34.8 us (34%)
  starting transfers between devices  25.4 us (25%)
  waiting for transfers between devices  23.2 us (23%)
  local copies, waits for them, and re-layouts  15.6 us (15%)
  between operations  1.54 us (2%)
  other arithmetic  1.05 us (1%)
    ppermute x8, starting transfers between devices, passed_along(): return lax.ppermute(value, axis, pairs)  17 us
    ppermute x5, waiting for transfers between devices, reduce_over_shots(): hop = lambda v, to: lax.ppermute(v, 'shot', [(i, to(i)) for i in range(16)])  15.9 us
    pallas_call x2, Pallas kernels, first_step(): call(kernel, [S, V, V, V, V, smem, smem, V, V, V, V, V], (field(3), field...  14.3 us
    unnamed x35, local copies, waits for them, and re-layouts  13.9 us
    ppermute x5, starting transfers between devices, reduce_over_shots(): hop = lambda v, to: lax.ppermute(v, 'shot', [(i, to(i)) for i in range(16)])  8.42 us
    pallas_call x1, Pallas kernels, body(): call(image_kernel, [S, V, V, V, V, V, V, S, S, V, V, V], jax.ShapeDtypeSt...  7.99 us
    ppermute x8, waiting for transfers between devices, passed_along(): return lax.ppermute(value, axis, pairs)  7.26 us
    pallas_call x1, Pallas kernels, body(): call(start_kernel, [V] * 5, (sends(7), sends(7), sends(6), sends(6), fiel...  6.71 us
  transfers between devices with their start and end apart: 13, of which 5 were waited for; matrix products, arithmetic and copies ran while one was open for 5% of the time, Pallas kernels for 20%

profile of v1, /device:TPU:0, one launch (start us, length us, event | category | flops | bytes accessed | tf_op | source)
XLA Modules:
  0.0 101.5 jit_solution(13345317414483583993)
XLA Ops:
  0.6 2.9 %copy.40.adj.refs_0_ = f32[1,9,5,5,5,256]{5,4,3,2,1,0:T(8,128)} copy(f32[1,9,5,5,5,256]{5,0,4,3,2,1:T(1,128)} %param.11) | data formatting | bytes 2304000 | tf_op args[1]
  3.5 1.5 %copy.33.fwd.refs_0_ = f32[1,9,5,5,5,256]{5,4,3,2,1,0:T(8,128)} copy(f32[1,9,5,5,5,256]{5,0,4,3,2,1:T(1,128)S(1)} %copy-done.2) | data formatting | bytes 2304000 | tf_op args[0]
  5.0 0.9 copy.34.mat.refs_1_
  5.9 0.8 copy.35.nbr.refs_2_
  6.7 6.7 %shard_map.113 = (f32[175,256]{1,0:T(8,128)}, f32[175,256]{1,0:T(8,128)}, f32[150,256]{1,0:T(8,128)}, f32[150,256]{1,0:T(8,128)}, f32[3,5,5,8,256]{4,3,2,1,0:T(8,128)}, /*index=5*/f32[3,5,5,8,256]{4,3,2,1,0:T(8,128)}) custom-call(f32[1,9,5,5,5,256]{5,4,3,2,1,0:T(8,128)} %copy.33.fwd.refs_0_, f32[1,9,5,5,5,256]{5,4,3,2,1,0:T(8,128)} %copy.40.adj.refs_0_, ...), custom_call_target="tpu_custom_call" | custom-call | flops 100000000 | bytes 4000000 | tf_op jit(solution)/shard_map/pallas_call | solution.py:433
  13.4 2.0 %collective-permute-start = (f32[175,256]{1,0:T(8,128)}, f32[175,256]{1,0:T(8,128)S(1)}, u32[]{:S(2)}, u32[]{:S(2)}) collective-permute-start(f32[175,256]{1,0:T(8,128)} %get-tuple-element.19), channel_id=1, source_target_pairs={{0,16},{16,32},{32,48},{48,64},{64,80},{80,96},{96,112},{112,0},{1... | collective-permute-start | bytes 537608 | tf_op jit(solution)/shard_map/ppermute | solution.py:407
  15.4 2.5 %collective-permute-start.1 = (f32[175,256]{1,0:T(8,128)}, f32[175,256]{1,0:T(8,128)S(1)}, u32[]{:S(2)}, u32[]{:S(2)}) collective-permute-start(f32[175,256]{1,0:T(8,128)} %get-tuple-element.20), channel_id=1, source_target_pairs={{0,112},{16,0},{32,16},{48,32},{64,48},{80,64},{96,80},{112,96},{1... | collective-permute-start | bytes 537608 | tf_op jit(solution)/shard_map/ppermute | solution.py:407
  17.9 4.1 %collective-permute-start.3 = (f32[150,256]{1,0:T(8,128)}, f32[150,256]{1,0:T(8,128)S(1)}, u32[]{:S(2)}, u32[]{:S(2)}) collective-permute-start(f32[150,256]{1,0:T(8,128)} %get-tuple-element.25), channel_id=1, source_target_pairs={{0,112},{16,0},{32,16},{48,32},{64,48},{80,64},{96,80},{112,96},{1... | collective-permute-start | bytes 460808 | tf_op jit(solution)/shard_map/ppermute | solution.py:407
  22.7 5.2 %collective-permute-done.refs_7_.refs_9_.r_below = f32[175,256]{1,0:T(8,128)S(1)} collective-permute-done((f32[175,256]{1,0:T(8,128)}, f32[175,256]{1,0:T(8,128)S(1)}, u32[]{:S(2)}, u32[]{:S(2)}) %collective-permute-start) | collective-permute-done | bytes 179232 | tf_op jit(solution)/shard_map/ppermute | solution.py:407
  27.9 2.1 %collective-permute-done.1.refs_8_.refs_10_.r_above = f32[175,256]{1,0:T(8,128)S(1)} collective-permute-done((f32[175,256]{1,0:T(8,128)}, f32[175,256]{1,0:T(8,128)S(1)}, u32[]{:S(2)}, u32[]{:S(2)}) %collective-permute-start.1) | collective-permute-done | bytes 179232 | tf_op jit(solution)/shard_map/ppermute | solution.py:407
  30.0 0.7 copy-done.1
  30.7 7.0 %shard_map.114 = (f32[3,5,5,8,256]{4,3,2,1,0:T(8,128)}, f32[6,5,5,8,256]{4,3,2,1,0:T(8,128)}, f32[3,5,5,8,256]{4,3,2,1,0:T(8,128)}, f32[3,5,5,8,256]{4,3,2,1,0:T...) custom-call(s32[1]{0:T(128)} %bitcast.base_ref.base, f32[1,9,5,5,5,256]{5,4,3,2,1,0:T(8,128)} %copy.33.fwd.refs_0_, ...), custom_call_target="tpu_custom_call" | custom-call | flops 200000000 | bytes 10000000 | tf_op jit(solution)/shard_map/pallas_call | solution.py:448
  38.0 3.8 %collective-permute-start.5 = (f32[75,256]{1,0:T(8,128)}, f32[75,256]{1,0:T(8,128)S(1)}, u32[]{:S(2)}, u32[]{:S(2)}) collective-permute-start(f32[75,256]{1,0:T(8,128)} %get-tuple-element.29), channel_id=1, source_target_pairs={{0,112},{16,0},{32,16},{48,32},{64,48},{80,64},{96,80},{112,96},{1... | collective-permute-start | bytes 230408 | tf_op jit(solution)/shard_map/ppermute | solution.py:407
  41.8 0.6 copy.39.refs_5_.strength
  42.4 0.7 copy-done.4
  43.1 7.3 %shard_map.115 = (f32[3,5,5,8,256]{4,3,2,1,0:T(8,128)}, f32[6,5,5,8,256]{4,3,2,1,0:T(8,128)}, f32[3,5,5,8,256]{4,3,2,1,0:T(8,128)}, f32[3,5,5,8,256]{4,3,2,1,0:T...) custom-call(s32[1]{0:T(128)} %bitcast.base_ref.base, f32[1,9,5,5,5,256]{5,4,3,2,1,0:T(8,128)} %copy.40.adj.refs_0_, ...), custom_call_target="tpu_custom_call" | custom-call | flops 200000000 | bytes 10000000 | tf_op jit(solution)/shard_map/pallas_call | solution.py:448
  50.5 0.6 copy-done.8
  51.1 8.0 %shard_map.116 = f32[256,384]{1,0:T(8,128)} custom-call(s32[1]{0:T(128)} %bitcast.base_ref.base, f32[1,9,5,5,5,256]{5,4,3,2,1,0:T(8,128)} %copy.40.adj.refs_0_, f32[3,5,5,8,256]{4,3,2,1,0:T(8,128)} %get-tuple-element.21.f_vel, f32[3,5,5,8,256]{4,3,2,1,0:T(8,128)} %get-tuple-element.22.f_acc, f32[3,5,5,8,256]{4,3,2,1,0:T(8,128)} %get-tuple-element.26.a_vel.vel_in, ...), custom_call_target="tpu_custom_call" | custom-call | flops 300000000 | bytes 10000000 | tf_op jit(solution)/shard_map/pallas_call | solution.py:463
  59.1 0.9 dynamic-slice_bitcast_fusion.2
  60.2 1.3 %collective-permute-done.6 = f32[4,2,16,384]{3,2,1,0:T(8,128)S(1)} collective-permute-done((f32[4,2,16,384]{3,2,1,0:T(8,128)S(1)}, f32[4,2,16,384]{3,2,1,0:T(8,128)S(1)}, u32[]{:S(2)}, u32[]{:S(2)}) %collective-permute-start.6) | collective-permute-done | bytes 196640 | tf_op jit(solution)/shard_map/ppermute | solution.py:419
  61.6 1.0 bitcast_add_fusion.1
  62.7 2.8 %collective-permute-start.9 = (f32[2,16,384]{1,2,0:T(8,128)S(1)}, f32[2,16,384]{1,2,0:T(8,128)S(1)}, u32[]{:S(2)}, u32[]{:S(2)}) collective-permute-start(f32[2,16,384]{1,2,0:T(8,128)S(1)} %bitcast.24), channel_id=1, source_target_pairs={{0,12},{1,13},{2,14},{3,15},{4,0},{5,1},{6,2},{7,3},{8,4},{9,5},{1... | collective-permute-start | bytes 147464 | tf_op jit(solution)/shard_map/ppermute | solution.py:419
  65.7 0.9 collective-permute-start.8
  66.8 1.0 collective-permute-start.7
  67.7 4.1 %collective-permute-start.12 = (f32[150,256]{1,0:T(8,128)S(1)}, f32[150,256]{1,0:T(8,128)S(1)}, u32[]{:S(2)}, u32[]{:S(2)}) collective-permute-start(f32[150,256]{1,0:T(8,128)S(1)} %copy-done.12), channel_id=1, source_target_pairs={{0,112},{16,0},{32,16},{48,32},{64,48},{80,64},{96,80},{112,96},{1... | collective-permute-start | bytes 460808 | tf_op jit(solution)/shard_map/ppermute | solution.py:407
  72.0 10.7 %collective-permute-done.9 = f32[2,16,384]{1,2,0:T(8,128)S(1)} collective-permute-done((f32[2,16,384]{1,2,0:T(8,128)S(1)}, f32[2,16,384]{1,2,0:T(8,128)S(1)}, u32[]{:S(2)}, u32[]{:S(2)}) %collective-permute-start.9) | collective-permute-done | bytes 49184 | tf_op jit(solution)/shard_map/ppermute | solution.py:419
  82.7 3.9 %collective-permute-done.7 = f32[2,16,384]{1,2,0:T(8,128)S(1)} collective-permute-done((f32[2,16,384]{1,2,0:T(8,128)S(1)}, f32[2,16,384]{1,2,0:T(8,128)S(1)}, u32[]{:S(2)}, u32[]{:S(2)}) %collective-permute-start.7) | collective-permute-done | bytes 49184 | tf_op jit(solution)/shard_map/ppermute | solution.py:419
  86.7 3.7 %collective-permute-start.10 = (f32[16,384]{0,1:T(8,128)S(1)}, f32[16,384]{0,1:T(8,128)S(1)}, u32[]{:S(2)}, u32[]{:S(2)}) collective-permute-start(f32[16,384]{0,1:T(8,128)S(1)} %get-tuple-element.39), channel_id=1, source_target_pairs={{0,2},{1,3},{2,0},{3,1},{4,6},{5,7},{6,4},{7,5},{8,10},{9,11},{10,... | collective-permute-start | bytes 73736 | tf_op jit(solution)/shard_map/ppermute | solution.py:419
  90.4 0.7 copy-done.6
  91.1 5.8 %shard_map.117 = f32[1,9,5,5,5,256]{5,4,3,2,1,0:T(8,128)} custom-call(s32[1]{0:T(128)} %bitcast.base_ref.base, f32[3,5,5,8,256]{4,3,2,1,0:T(8,128)} %get-tuple-element.26.a_vel.vel_in, f32[6,5,5,8,256]{4,3,2,1,0:T(8,128)} %get-tuple-element.30.stress_in, f32[3,5,5,5,256]{4,3,2,1,0:T(8,128)} %copy.34.mat.refs_1_, s32[256,4]{1,0:T(8,128)} %copy.35.nbr.refs_2_, ...), custom_call_target="tpu_custom_call" | custom-call | flops 100000000 | bytes 10000000 | tf_op jit(solution)/shard_map/pallas_call | solution.py:471
  96.9 3.7 %copy.50 = f32[1,9,5,5,5,256]{5,0,4,3,2,1:T(1,128)} copy(f32[1,9,5,5,5,256]{5,4,3,2,1,0:T(8,128)} %shard_map.117) | data formatting | bytes 2304000
  100.7 0.8 copy.49
  (45 shorter events, 1.5 us)
Async XLA Ops:
  0.6 2.9 %copy-start.2 = (f32[1,9,5,5,5,256]{5,0,4,3,2,1:T(1,128)S(1)}, f32[1,9,5,5,5,256]{5,0,4,3,2,1:T(1,128)}, u32[]{:S(2)}) copy-start(f32[1,9,5,5,5,256]{5,0,4,3,2,1:T(1,128)} %param.10) | copy-start | bytes 3456004
  3.5 1.5 %copy-start.3 = (f32[3,5,5,5,256]{4,0,3,2,1:T(4,128)S(1)}, f32[3,5,5,5,256]{4,0,3,2,1:T(4,128)}, u32[]{:S(2)}) copy-start(f32[3,5,5,5,256]{4,0,3,2,1:T(4,128)} %param.12) | copy-start | bytes 1152004
  3.5 2.4 %copy-start.11 = (s32[256,4]{0,1:T(4,128)S(1)}, s32[256,4]{0,1:T(4,128)}, u32[]{:S(2)}) copy-start(s32[256,4]{0,1:T(4,128)} %param.13) | copy-start | bytes 12292
  13.4 14.5 %collective-permute-start = (f32[175,256]{1,0:T(8,128)}, f32[175,256]{1,0:T(8,128)S(1)}, u32[]{:S(2)}, u32[]{:S(2)}) collective-permute-start(f32[175,256]{1,0:T(8,128)} %get-tuple-element.19), channel_id=1, source_target_pairs={{0,16},{16,32},{32,48},{48,64},{64,80},{80,96},{96,112},{112,0},{1... | collective-permute-start | bytes 537608 | tf_op jit(solution)/shard_map/ppermute | solution.py:407
  15.4 14.6 %collective-permute-start.1 = (f32[175,256]{1,0:T(8,128)}, f32[175,256]{1,0:T(8,128)S(1)}, u32[]{:S(2)}, u32[]{:S(2)}) collective-permute-start(f32[175,256]{1,0:T(8,128)} %get-tuple-element.20), channel_id=1, source_target_pairs={{0,112},{16,0},{32,16},{48,32},{64,48},{80,64},{96,80},{112,96},{1... | collective-permute-start | bytes 537608 | tf_op jit(solution)/shard_map/ppermute | solution.py:407
  17.9 24.5 %collective-permute-start.2 = (f32[150,256]{1,0:T(8,128)}, f32[150,256]{1,0:T(8,128)S(1)}, u32[]{:S(2)}, u32[]{:S(2)}) collective-permute-start(f32[150,256]{1,0:T(8,128)} %get-tuple-element.24), channel_id=1, source_target_pairs={{0,16},{16,32},{32,48},{48,64},{64,80},{80,96},{96,112},{112,0},{1... | collective-permute-start | bytes 460808 | tf_op jit(solution)/shard_map/ppermute | solution.py:407
  17.9 24.5 %collective-permute-start.3 = (f32[150,256]{1,0:T(8,128)}, f32[150,256]{1,0:T(8,128)S(1)}, u32[]{:S(2)}, u32[]{:S(2)}) collective-permute-start(f32[150,256]{1,0:T(8,128)} %get-tuple-element.25), channel_id=1, source_target_pairs={{0,112},{16,0},{32,16},{48,32},{64,48},{80,64},{96,80},{112,96},{1... | collective-permute-start | bytes 460808 | tf_op jit(solution)/shard_map/ppermute | solution.py:407
  27.9 2.1 %copy-start = (f32[175,256]{1,0:T(8,128)}, f32[175,256]{1,0:T(8,128)S(1)}, u32[]{:S(2)}) copy-start(f32[175,256]{1,0:T(8,128)S(1)} %collective-permute-done.refs_7_.refs_9_.r_below) | copy-start | bytes 537604
  30.0 0.7 copy-start.1
  30.7 11.1 %copy-start.10 = (f32[1,2,3,256]{3,1,2,0:T(2,128)S(1)}, f32[1,2,3,256]{3,1,2,0:T(2,128)}, u32[]{:S(2)}) copy-start(f32[1,2,3,256]{3,1,2,0:T(2,128)} %param.17) | copy-start | bytes 18436
  37.6 12.8 %collective-permute-start.4 = (f32[75,256]{1,0:T(8,128)}, f32[75,256]{1,0:T(8,128)S(1)}, u32[]{:S(2)}, u32[]{:S(2)}) collective-permute-start(f32[75,256]{1,0:T(8,128)} %get-tuple-element.28), channel_id=1, source_target_pairs={{0,16},{16,32},{32,48},{48,64},{64,80},{80,96},{96,112},{112,0},{1... | collective-permute-start | bytes 230408 | tf_op jit(solution)/shard_map/ppermute | solution.py:407
  38.0 12.4 %collective-permute-start.5 = (f32[75,256]{1,0:T(8,128)}, f32[75,256]{1,0:T(8,128)S(1)}, u32[]{:S(2)}, u32[]{:S(2)}) collective-permute-start(f32[75,256]{1,0:T(8,128)} %get-tuple-element.29), channel_id=1, source_target_pairs={{0,112},{16,0},{32,16},{48,32},{64,48},{80,64},{96,80},{112,96},{1... | collective-permute-start | bytes 230408 | tf_op jit(solution)/shard_map/ppermute | solution.py:407
  42.4 0.7 copy-start.4
  42.4 0.7 copy-start.5
  50.4 0.6 copy-start.8
  50.5 0.7 copy-start.9
  60.0 1.5 %collective-permute-start.6 = (f32[4,2,16,384]{3,2,1,0:T(8,128)S(1)}, f32[4,2,16,384]{3,2,1,0:T(8,128)S(1)}, u32[]{:S(2)}, u32[]{:S(2)}) collective-permute-start(f32[4,2,16,384]{3,2,1,0:T(8,128)S(1)} %dynamic-slice_bitcast_fusion.2), channel_id=1, source_target_pairs={{0,1},{1,0},{2,3},{3,2},{4,5},{5,4},{6,7},{7,6},{8,9},{9,8},{10,11... | collective-permute-start | bytes 589832 | tf_op jit(solution)/shard_map/ppermute | solution.py:419
  60.2 7.6 %copy-start.13 = (f32[150,256]{1,0:T(8,128)S(1)}, f32[150,256]{1,0:T(8,128)}, u32[]{:S(2)}) copy-start(f32[150,256]{1,0:T(8,128)} %get-tuple-element.32) | copy-start | bytes 460804
  60.2 7.6 %copy-start.12 = (f32[150,256]{1,0:T(8,128)S(1)}, f32[150,256]{1,0:T(8,128)}, u32[]{:S(2)}) copy-start(f32[150,256]{1,0:T(8,128)} %get-tuple-element.33) | copy-start | bytes 460804
  62.7 20.0 %collective-permute-start.9 = (f32[2,16,384]{1,2,0:T(8,128)S(1)}, f32[2,16,384]{1,2,0:T(8,128)S(1)}, u32[]{:S(2)}, u32[]{:S(2)}) collective-permute-start(f32[2,16,384]{1,2,0:T(8,128)S(1)} %bitcast.24), channel_id=1, source_target_pairs={{0,12},{1,13},{2,14},{3,15},{4,0},{5,1},{6,2},{7,3},{8,4},{9,5},{1... | collective-permute-start | bytes 147464 | tf_op jit(solution)/shard_map/ppermute | solution.py:419
  65.7 17.0 %collective-permute-start.8 = (f32[2,16,384]{1,2,0:T(8,128)S(1)}, f32[2,16,384]{1,2,0:T(8,128)S(1)}, u32[]{:S(2)}, u32[]{:S(2)}) collective-permute-start(f32[2,16,384]{1,2,0:T(8,128)S(1)} %bitcast.25), channel_id=1, source_target_pairs={{0,8},{1,9},{2,10},{3,11},{4,12},{5,13},{6,14},{7,15},{8,0},{9,1},... | collective-permute-start | bytes 147464 | tf_op jit(solution)/shard_map/ppermute | solution.py:419
  66.8 19.8 %collective-permute-start.7 = (f32[2,16,384]{1,2,0:T(8,128)S(1)}, f32[2,16,384]{1,2,0:T(8,128)S(1)}, u32[]{:S(2)}, u32[]{:S(2)}) collective-permute-start(f32[2,16,384]{1,2,0:T(8,128)S(1)} %bitcast.26), channel_id=1, source_target_pairs={{0,4},{1,5},{2,6},{3,7},{4,8},{5,9},{6,10},{7,11},{8,12},{9,13},{1... | collective-permute-start | bytes 147464 | tf_op jit(solution)/shard_map/ppermute | solution.py:419
  67.7 22.7 %collective-permute-start.11 = (f32[150,256]{1,0:T(8,128)S(1)}, f32[150,256]{1,0:T(8,128)S(1)}, u32[]{:S(2)}, u32[]{:S(2)}) collective-permute-start(f32[150,256]{1,0:T(8,128)S(1)} %copy-done.13), channel_id=1, source_target_pairs={{0,16},{16,32},{32,48},{48,64},{64,80},{80,96},{96,112},{112,0},{1... | collective-permute-start | bytes 460808 | tf_op jit(solution)/shard_map/ppermute | solution.py:407
  67.7 22.7 %collective-permute-start.12 = (f32[150,256]{1,0:T(8,128)S(1)}, f32[150,256]{1,0:T(8,128)S(1)}, u32[]{:S(2)}, u32[]{:S(2)}) collective-permute-start(f32[150,256]{1,0:T(8,128)S(1)} %copy-done.12), channel_id=1, source_target_pairs={{0,112},{16,0},{32,16},{48,32},{64,48},{80,64},{96,80},{112,96},{1... | collective-permute-start | bytes 460808 | tf_op jit(solution)/shard_map/ppermute | solution.py:407
  86.7 13.9 %collective-permute-start.10 = (f32[16,384]{0,1:T(8,128)S(1)}, f32[16,384]{0,1:T(8,128)S(1)}, u32[]{:S(2)}, u32[]{:S(2)}) collective-permute-start(f32[16,384]{0,1:T(8,128)S(1)} %get-tuple-element.39), channel_id=1, source_target_pairs={{0,2},{1,3},{2,0},{3,1},{4,6},{5,7},{6,4},{7,5},{8,10},{9,11},{10,... | collective-permute-start | bytes 73736 | tf_op jit(solution)/shard_map/ppermute | solution.py:419
  90.4 0.7 copy-start.6
  90.4 0.7 copy-start.7

commit v2 on v1

v2 whole, which is shorter than its diff:
```python
import math

import jax
import jax.numpy as jnp
import numpy as np
from jax import lax
from jax.experimental import pallas as pl
from jax.experimental.pallas import tpu as pltpu
from jax.sharding import PartitionSpec as P

f32 = jnp.float32
bf16 = jnp.bfloat16

time_step = 0.01
N = 256


def tables():
    root = math.sqrt(3.0 / 7.0)
    points = np.array([-1.0, -root, 0.0, root, 1.0])
    legendre = (35.0 * points**4 - 30.0 * points**2 + 3.0) / 8.0
    matrix = np.zeros((5, 5))
    for r in range(5):
        for c in range(5):
            if r != c:
                matrix[r, c] = legendre[r] / (legendre[c] * (points[r] - points[c]))
    matrix[0, 0] = -5.0
    matrix[4, 4] = 5.0
    quad = np.array([0.1, 49.0 / 90.0, 32.0 / 45.0, 49.0 / 90.0, 0.1])
    return matrix, quad


D_PLAIN, QUAD = tables()
D_LIFT = D_PLAIN.copy()
D_LIFT[0, 0] += 5.0
D_LIFT[4, 4] -= 5.0


def split(x):
    high = x.astype(bf16)
    return high, (x - high.astype(f32)).astype(bf16)


def dot(a, b):
    return lax.dot_general(a, b, (((1,), (0,)), ((), ())), preferred_element_type=f32)


def derive_rows(rows, matrix):
    even0, odd0 = rows[0] + rows[4], rows[0] - rows[4]
    even1, odd1 = rows[1] + rows[3], rows[1] - rows[3]
    out = [None] * 5
    for r in (0, 1):
        m = [float(v) for v in matrix[r]]
        p = 0.5 * (m[0] + m[4]) * even0 + 0.5 * (m[1] + m[3]) * even1 + m[2] * rows[2]
        q = 0.5 * (m[0] - m[4]) * odd0 + 0.5 * (m[1] - m[3]) * odd1
        out[r] = q + p
        out[4 - r] = q - p
    out[2] = float(matrix[2, 0]) * odd0 + float(matrix[2, 1]) * odd1
    return out


class Along:
    def __init__(self, matrix):
        row = lax.broadcasted_iota(jnp.int32, (8, 128), 0)
        self.places = [jnp.where(row < 5, lax.rem(row + m, 5), row) for m in range(1, 5)]
        self.factors = []
        for m in range(1, 5):
            self.factors.append(self.by_row(row, [matrix[c, (c + m) % 5] for c in range(5)]))
        own = [matrix[c, c] for c in range(5)]
        self.own = self.by_row(row, own) if any(own) else None

    @staticmethod
    def by_row(row, values):
        out = jnp.zeros((8, 128), f32)
        for c in range(5):
            out = jnp.where(row == c, float(values[c]), out)
        return out

    def __call__(self, tile):
        total = None if self.own is None else tile * self.own
        for place, factor in zip(self.places, self.factors):
            term = jnp.take_along_axis(tile, place, axis=0) * factor
            total = term if total is None else total + term
        return total


def flat(ref, rows):
    return ref.reshape(rows, 128)


def make_perms(nbr, perms):
    source = lax.broadcasted_iota(jnp.int32, (N, N), 0)
    for k in range(4):
        hit = source == nbr[k : k + 1, :]
        perms[k] = jnp.where(hit, -5.0 if k % 2 == 0 else 5.0, 0.0).astype(bf16)


def permuted(face, matrix):
    rows = face.shape[0]
    both = dot(jnp.concatenate(split(face), axis=0), matrix)
    return both[:rows] + both[rows:]


def jumps(field, ys, first_z, perms, yj, zj):
    count = field.shape[1]
    for side, b in ((0, 4), (1, 0)):
        face = jnp.concatenate(
            [
                jnp.concatenate([field[h, k, :, b].reshape(40, 128) for h in range(2)], axis=1)
                for k in ys
            ],
            axis=0,
        )
        got = permuted(face, perms[side])
        for h in range(2):
            for i in range(3):
                part = got[40 * i : 40 * i + 40, 128 * h : 128 * h + 128]
                yj[side, h, i] = part.reshape(5, 8, 128)
    rows = flat(field, 2 * count * 200)
    into = flat(zj, 1200)
    spare = jnp.zeros((5, N), f32)
    for side, c in ((0, 4), (1, 0)):
        face = jnp.concatenate(
            [rows[pl.ds((h * count + first_z) * 200 + c, 75, 8), :] for h in range(2)], axis=1
        )
        got = permuted(jnp.concatenate([face, spare], axis=0), perms[2 + side])
        for h in range(2):
            into[pl.ds(h * 600 + (0, 4)[side], 75, 8), :] = got[:75, 128 * h : 128 * h + 128]


def stress_of(i, d):
    return jnp.where(i == d, i, 6 - i - d)


def halves(count, one):
    def step(t, carry):
        one(lax.div(t, 2), lax.rem(t, 2))
        return carry

    lax.fori_loop(0, 2 * count, step, 0)


def local_acceleration(stress, rinv, acc, perms, yj, zj):
    along = Along(D_LIFT)
    jumps(stress, (5, 1, 3), 2, perms, yj, zj)

    def one(i, h):
        kx, ky, kz = stress_of(i, 0), stress_of(i, 1), stress_of(i, 2)
        for a in range(5):
            ys = derive_rows([stress[h, ky, a, b] for b in range(5)], D_LIFT)
            ys[0] = ys[0] + yj[0, h, i, a]
            ys[4] = ys[4] + yj[1, h, i, a]
            for b in range(5):
                acc[h, i, a, b] = ys[b] + (along(stress[h, kz, a, b]) + zj[h, 2 - i, a, b])
        for b in range(5):
            xs = derive_rows([stress[h, kx, a, b] for a in range(5)], D_LIFT)
            for a in range(5):
                acc[h, i, a, b] = (acc[h, i, a, b] + xs[a]) * rinv[h, a, b]

    halves(3, one)


def load_fields(src, first, dst, count):
    def one(k, carry):
        for g in range(25):
            for h in range(2):
                dst[h, k, g // 5, g % 5, 0:5, :] = src[pl.ds(250 * (first + k) + 10 * g + h, 5, 2), :]
        return carry

    lax.fori_loop(0, count, one, 0)


def pack_face(dst, k, value, h):
    for b in range(5):
        dst[pl.ds(50 * k + 10 * b + h, 5, 2), :] = value[b, 0:5]


def unpack_face(dst, side, k, src, j):
    for h in range(2):
        for b in range(5):
            dst[side, h, k, b, 0:5, :] = src[pl.ds(50 * j + 10 * b + h, 5, 2), :]


def load_halo(halo, below, above, r_below, r_above, count):
    for side, src in ((0, below), (1, above)):
        for k in range(count):
            unpack_face(halo, side, k, src, k)
    if r_below is not None:
        for side, src in ((0, r_below), (1, r_above)):
            unpack_face(halo, side, 6, src, 6)


def finish_acceleration(acc, stress, rinv, halo, has_v):
    for h in range(2):
        for i in range(3):
            k = (0, 5, 4)[i]
            acc[h, i, 0] = acc[h, i, 0] - 5.0 * rinv[h, 0] * halo[0, h, i]
            acc[h, i, 4] = acc[h, i, 4] + 5.0 * rinv[h, 4] * halo[1, h, i]
            if has_v:
                halo[0, h, 3 + i] = halo[0, h, 3 + i] + halo[0, h, 6] * stress[h, k, 0]
                halo[1, h, 3 + i] = halo[1, h, 3 + i] - halo[1, h, 6] * stress[h, k, 4]


def inject_rows(kind, step, where_ref, strength, base):
    if kind == "source":
        lane = lax.broadcasted_iota(jnp.int32, (1, N), 1) + base
        hit = lane == where_ref[0]
        return [jnp.where(hit, strength[0, step, i], 0.0) for i in range(3)]
    element = lax.broadcasted_iota(jnp.int32, (N, N), 0) + base
    hits = jnp.where(element == where_ref[...], 1.0, 0.0).astype(bf16)
    x = jnp.concatenate([strength[i, step : step + 1] for i in range(3)] + [jnp.zeros((13, N), f32)], axis=0)
    total = None
    for part in range(3):
        high = x.astype(bf16)
        x = x - high.astype(f32)
        term = lax.dot_general(high, hits, (((1,), (1,)), ((), ())), preferred_element_type=f32)
        total = term if total is None else total + term
    return [total[i : i + 1] for i in range(3)]


def velocities(vel_in, vel, acc, rows):
    def one(i, h):
        for a in range(5):
            vel[h, i, a] = vel_in[h, i, a] + time_step * acc[h, i, a]

    halves(3, one)
    mask = lax.broadcasted_iota(jnp.int32, (8, 128), 0) == 2
    for i in range(3):
        for h in range(2):
            vel[h, i, 2, 2] += jnp.where(mask, rows[i][:, 128 * h : 128 * h + 128], 0.0)


def jump_gradients(vel, halo, grads, perms, yj, zj):
    along = Along(D_LIFT)
    jumps(vel, (0, 1, 2), 0, perms, yj, zj)

    def one(i, h):
        for a in range(5):
            ys = derive_rows([vel[h, i, a, b] for b in range(5)], D_LIFT)
            ys[0] = ys[0] + yj[0, h, i, a]
            ys[4] = ys[4] + yj[1, h, i, a]
            for b in range(5):
                grads[h, 3 + i, a, b] = ys[b]
                grads[h, 6 + i, a, b] = along(vel[h, i, a, b]) + zj[h, i, a, b]
        for b in range(5):
            xs = derive_rows([vel[h, i, a, b] for a in range(5)], D_LIFT)
            xs[0] = xs[0] - 5.0 * halo[0, h, 3 + i, b]
            xs[4] = xs[4] + 5.0 * halo[1, h, 3 + i, b]
            for a in range(5):
                grads[h, i, a, b] = xs[a]

    halves(3, one)


def update_stress(stress_in, stress, grads, lam, mu):
    def one(a, h):
        g = lambda j, i: grads[h, 3 * j + i, a]
        l, m = lam[h, a], mu[h, a]
        both = l * (g(0, 0) + g(1, 1) + g(2, 2))
        for i in range(3):
            stress[h, i, a] = stress_in[h, i, a] + (both + 2.0 * m * g(i, i))
        stress[h, 3, a] = stress_in[h, 3, a] + m * (g(2, 1) + g(1, 2))
        stress[h, 4, a] = stress_in[h, 4, a] + m * (g(2, 0) + g(0, 2))
        stress[h, 5, a] = stress_in[h, 5, a] + m * (g(1, 0) + g(0, 1))

    halves(5, one)


def plain_gradients(vel, grads):
    along = Along(D_PLAIN)

    def one(i, h):
        for a in range(5):
            ys = derive_rows([vel[h, i, a, b] for b in range(5)], D_PLAIN)
            for b in range(5):
                grads[h, 3 + i, a, b] = ys[b]
                grads[h, 6 + i, a, b] = along(vel[h, i, a, b])
        for b in range(5):
            xs = derive_rows([vel[h, i, a, b] for a in range(5)], D_PLAIN)
            for a in range(5):
                grads[h, i, a, b] = xs[a]

    halves(3, one)


def image(fg, ag, acc, adj_vel, dense, first):
    row = lax.broadcasted_iota(jnp.int32, (8, 128), 0)
    weight = Along.by_row(row, QUAD)

    def one(k, h):
        for a in range(5):
            for b in range(5):
                f = lambda j, i: fg[h, 3 * j + i, a, b]
                g = lambda j, i: ag[h, 3 * j + i, a, b]
                w = weight * float(QUAD[a] * QUAD[b])
                f0, f1, f2 = f(0, 0), f(1, 1), f(2, 2)
                g0, g1, g2 = g(0, 0), g(1, 1), g(2, 2)
                trace = (f0 + f1 + f2) * (g0 + g1 + g2) * w
                cross = None
                for i, j in ((0, 1), (0, 2), (1, 2)):
                    term = (f(j, i) + f(i, j)) * (g(j, i) + g(i, j))
                    cross = term if cross is None else cross + term
                strain = (2.0 * (f0 * g0 + f1 * g1 + f2 * g2) + cross) * w
                inertia = None
                for i in range(3):
                    term = acc[h, i, a, b] * adj_vel[h, i, a, b]
                    inertia = term if inertia is None else inertia + term
                for t, term in enumerate((trace, strain, inertia * w)):
                    at = t * 125 + a * 25 + b * 5
                    if first is None:
                        dense[h, at : at + 5, :] = term[0:5]
                    else:
                        dense[h, at : at + 5, :] = first[h, at : at + 5, :] + term[0:5]

    halves(1, one)


def start_common(state, rinv, perms, acc, vel, stress, up, down, yj, zj, with_r):
    src = flat(state, 2250)
    up, down = (flat(r, r.shape[0] * 2) for r in (up, down))
    load_fields(src, 0, vel, 3)
    load_fields(src, 3, stress, 6)
    local_acceleration(stress, rinv, acc, perms, yj, zj)
    for dst, a in ((up, 4), (down, 0)):
        for i in range(3):
            dst[50 * i : 50 * i + 50, :] = src[250 * (3, 8, 7)[i] + 50 * a : 250 * (3, 8, 7)[i] + 50 * a + 50, :]
            for h in range(2):
                pack_face(dst, 3 + i, vel[h, i, a] + time_step * acc[h, i, a], h)
        if with_r:
            for h in range(2):
                pack_face(dst, 6, 0.05 * rinv[h, a], h)


def load_material(mat, k, dst):
    for g in range(25):
        for h in range(2):
            dst[h, g // 5, g % 5, 0:5, :] = mat[5 * g : 5 * g + 5, k, 128 * h : 128 * h + 128]


def forward_start_kernel(state, mat, nbr, up, down, acc, vel, stress, rinv, perms, yj, zj):
    make_perms(nbr, perms)
    load_material(mat, 2, rinv)
    for h in range(2):
        for a in range(5):
            rinv[h, a] = 1.0 / rinv[h, a]
    zj[...] = jnp.zeros(zj.shape, f32)
    start_common(state, rinv, perms, acc, vel, stress, up, down, yj, zj, True)


def adjoint_start_kernel(state, mat, rinv, perms, up, down, acc, vel, stress, lam, mu, yj, zj):
    zj[...] = jnp.zeros(zj.shape, f32)
    start_common(state, rinv, perms, acc, vel, stress, up, down, yj, zj, False)
    for k, dst in ((0, lam), (1, mu)):
        load_material(mat, k, dst)
        for h in range(2):
            for a in range(5):
                dst[h, a] = time_step * dst[h, a]


def finish_step(kind, step, base, vel_in, stress_in, lam, mu, rinv, perms, where_ref, strength,
                vel, stress, acc, halo, grads, yj, zj):
    finish_acceleration(acc, stress_in, rinv, halo, True)
    velocities(vel_in, vel, acc, inject_rows(kind, step, where_ref, strength, base))
    jump_gradients(vel, halo, grads, perms, yj, zj)
    update_stress(stress_in, stress, grads, lam, mu)


def middle_kernel(kind, base, vel_in, stress_in, acc_in, lam, mu, rinv, perms, where_ref, strength,
                  below, above, r_below, r_above, up, down, vel, stress, acc, next_acc, halo, grads, yj, zj):
    zj[...] = jnp.zeros(zj.shape, f32)
    load_halo(halo, *(flat(r, r.shape[0] * 2) for r in (below, above, r_below, r_above)), 6)
    acc[...] = acc_in[...]
    finish_step(kind, 0, base[0], vel_in, stress_in, lam, mu, rinv, perms, where_ref, strength,
                vel, stress, acc, halo, grads, yj, zj)
    local_acceleration(stress, rinv, next_acc, perms, yj, zj)
    for dst, a in ((up, 4), (down, 0)):
        dst = flat(dst, dst.shape[0] * 2)
        for i in range(3):
            for h in range(2):
                pack_face(dst, i, stress[h, (0, 5, 4)[i], a], h)
                if kind == "receiver":
                    pack_face(dst, 3 + i, vel[h, i, a] + time_step * next_acc[h, i, a], h)


def last_kernel(base, vel_in, stress_in, acc_in, lam, mu, rinv, perms, where_ref, strength,
                below, above, r_below, r_above, out, vel, stress, acc, halo, grads, yj, zj):
    zj[...] = jnp.zeros(zj.shape, f32)
    load_halo(halo, *(flat(r, r.shape[0] * 2) for r in (below, above, r_below, r_above)), 6)
    acc[...] = acc_in[...]
    finish_step("receiver", 1, base[0], vel_in, stress_in, lam, mu, rinv, perms, where_ref, strength,
                vel, stress, acc, halo, grads, yj, zj)
    dst = flat(out, 2250)
    for first, field, count in ((0, vel, 3), (3, stress, 6)):

        def one(k, carry):
            for g in range(25):
                for h in range(2):
                    dst[pl.ds(250 * (first + k) + 10 * g + h, 5, 2), :] = field[h, k, g // 5, g % 5, 0:5, :]
            return carry

        lax.fori_loop(0, count, one, 0)


def first_image_kernel(adj_vel_end, f_vel, f_acc, a_vel, dense, end_grads, fg, ag):
    plain_gradients(f_vel, fg)
    plain_gradients(a_vel, ag)
    image(fg, ag, f_acc, a_vel, dense, None)
    plain_gradients(adj_vel_end, end_grads)


def last_image_kernel(base, f_vel, acc_in, adj_vel, end_grads, first, rinv, where_ref, strength, below, above,
                      keep, send, halo, vel, acc, fg, dense):
    load_halo(halo, flat(below, 150), flat(above, 150), None, None, 3)
    acc[...] = acc_in[...]
    finish_acceleration(acc, None, rinv, halo, False)
    velocities(f_vel, vel, acc, inject_rows("source", 1, where_ref, strength, base[0]))
    plain_gradients(vel, fg)
    for h in range(2):
        dense[h, 368:384, :] = jnp.zeros((16, 128), f32)
    image(fg, end_grads, acc, adj_vel, dense, first)
    core = base[1]
    turned = [dense[h].T for h in range(2)]
    for parity, (mine, other) in ((0, (keep, send)), (1, (send, keep))):

        @pl.when(core == parity)
        def _():
            for s in range(16):
                piece = turned[s // 8][16 * (s % 8) : 16 * (s % 8) + 16]
                (mine if s % 2 == 0 else other)[s // 2] = piece


V = pl.BlockSpec(memory_space=pltpu.VMEM)
S = pl.BlockSpec(memory_space=pltpu.SMEM)


def shape(*dims):
    return jax.ShapeDtypeStruct(dims, f32)


def field(count):
    return shape(2, count, 5, 5, 8, 128)


ONE = shape(2, 5, 5, 8, 128)
PERMS = jax.ShapeDtypeStruct((4, N, N), bf16)


def sends(faces):
    return shape(faces * 25, 2, 128)


def scr(s):
    return pltpu.VMEM(s.shape, s.dtype)


JUMPS = [pltpu.VMEM((2, 2, 3, 5, 8, 128), f32), pltpu.VMEM((2, 3, 5, 5, 8, 128), f32)]
HALO = pltpu.VMEM((2, 2, 7, 5, 8, 128), f32)


def call(kernel, specs, outs, scratch, flops, moved):
    return pl.pallas_call(
        kernel,
        out_shape=outs,
        in_specs=specs,
        out_specs=jax.tree.map(lambda _: V, outs),
        scratch_shapes=scratch,
        compiler_params=pltpu.CompilerParams(vmem_limit_bytes=20 * 2**20),
        cost_estimate=pl.CostEstimate(flops=flops, bytes_accessed=moved, transcendentals=0),
    )


def passed_along(value, axis, steps):
    count = lax.axis_size(axis)
    pairs = [(source, (source + steps) % count) for source in range(count)]
    return lax.ppermute(value, axis, pairs)


def both_ways(up, down):
    return passed_along(up, "slab", 1), passed_along(down, "slab", -1)


def reduce_over_shots(keep, send):
    place = lax.axis_index("shot")
    high, line = (place // 2) % 2, place // 4
    pick = lambda v, k, axis: lax.dynamic_index_in_dim(v, k, axis, False)
    hop = lambda v, to: lax.ppermute(v, "shot", [(i, to(i)) for i in range(16)])
    x = (keep + hop(send, lambda i: i ^ 1)).reshape(4, 2, 16, 384)
    total = pick(x, line, 0)
    for d in (1, 2, 3):
        total = total + hop(pick(x, (line + d) % 4, 0), lambda i: (i + 4 * d) % 16)
    return pick(total, high, 0) + hop(pick(total, 1 - high, 0), lambda i: i ^ 2)


def body(fwd, adj, materials, nbr, source_element, pulse, receivers, residuals):
    base = jnp.stack([lax.axis_index("slab") * N, lax.axis_index("shot") % 2]).astype(jnp.int32)
    receivers = receivers.reshape(1, N)
    fwd, adj = (x.reshape(1125, 2, 128) for x in (fwd, adj))
    mat = materials.transpose(1, 2, 3, 0, 4).reshape(125, 3, N)
    nbr = nbr.T
    residuals = residuals.transpose(0, 2, 1, 3).reshape(3, 2, N)

    f_up, f_down, f_acc, f_vel, f_stress, rinv, perms = call(
        forward_start_kernel,
        [V] * 3,
        (sends(7), sends(7), field(3), field(3), field(6), ONE, PERMS),
        JUMPS,
        10**8, 4 * 10**6,
    )(fwd, mat, nbr)
    f_below, f_above = both_ways(f_up, f_down)
    a_up, a_down, a_acc, a_vel, a_stress, lam, mu = call(
        adjoint_start_kernel,
        [V] * 4,
        (sends(6), sends(6), field(3), field(3), field(6), ONE, ONE),
        JUMPS,
        10**8, 4 * 10**6,
    )(adj, mat, rinv, perms)
    a_below, a_above = both_ways(a_up, a_down)
    adj_vel_end = a_vel

    def middle(kind, vel, stress, acc, where_ref, strength, below, above, faces):
        kernel = lambda base_ref, *refs: middle_kernel(kind, base_ref, *refs)
        held = S if kind == "source" else V
        return call(
            kernel,
            [S] + [V] * 7 + [held] * 2 + [V] * 4,
            (sends(faces), sends(faces), field(3), field(6), field(3), field(3)),
            [HALO, scr(field(9))] + JUMPS,
            2 * 10**8, 8 * 10**6,
        )(base, vel, stress, acc, lam, mu, rinv, perms, where_ref, strength, below, above, f_below, f_above)

    f_up, f_down, f_vel1, _, f_acc1, f_acc2 = middle(
        "source", f_vel, f_stress, f_acc, source_element, pulse, f_below, f_above, 3
    )
    f_below2, f_above2 = both_ways(f_up, f_down)
    a_up, a_down, a_vel1, a_stress1, _, a_acc2 = middle(
        "receiver", a_vel, a_stress, a_acc, receivers, residuals, a_below, a_above, 6
    )
    a_below2, a_above2 = both_ways(a_up, a_down)
    first, end_grads = call(
        first_image_kernel,
        [V] * 4,
        (shape(2, 384, 128), field(9)),
        [scr(field(9)), scr(field(9))],
        10**8, 8 * 10**6,
    )(adj_vel_end, f_vel1, f_acc1, a_vel1)
    keep, send = call(
        last_image_kernel,
        [S] + [V] * 6 + [S] * 2 + [V] * 2,
        (shape(8, 16, 384), shape(8, 16, 384)),
        [HALO, scr(field(3)), scr(field(3)), scr(field(9)), scr(shape(2, 384, 128))],
        10**8, 8 * 10**6,
    )(base, f_vel1, f_acc2, adj_vel_end, end_grads, first, rinv, source_element, pulse, f_below2, f_above2)
    gradient = reduce_over_shots(keep, send)
    adjoint_end = call(
        last_kernel,
        [S] + [V] * 13,
        shape(1125, 2, 128),
        [scr(field(3)), scr(field(6)), scr(field(3)), HALO, scr(field(9))] + JUMPS,
        10**8, 8 * 10**6,
    )(base, a_vel1, a_stress1, a_acc2, lam, mu, rinv, perms, receivers, residuals, a_below2, a_above2, f_below, f_above)
    return gradient[:, :375].T.reshape(3, 5, 5, 5, 16), adjoint_end.reshape(1, 9, 5, 5, 5, N)


def solution(mesh):
    return jax.shard_map(
        body,
        mesh=mesh,
        in_specs=(
            P("shot", None, None, None, None, "slab"),
            P("shot", None, None, None, None, "slab"),
            P(None, None, None, None, "slab"),
            P(),
            P("shot"),
            P("shot", None, None),
            P(),
            P("shot", None, None, None),
        ),
        out_specs=(
            P(None, None, None, None, ("slab", "shot")),
            P("shot", None, None, None, None, "slab"),
        ),
        check_vma=False,
    )
```

time: 102 us -> 67.7 us (0.66)
  waiting for transfers between devices: 23.2 us -> 6.78 us
  Pallas kernels: 34.8 us -> 20.4 us
  local copies, waits for them, and re-layouts: 15.6 us -> 13.3 us
    pallas_call x5 -> x7, Pallas kernels: 34.8 us -> 20.4 us  [the longest x2 8.14 us: middle(): call(kernel, [S] + [V] * 7 + [held] * 2 + [V] * 4, (sends(faces), sends(f...]
    ppermute x5, waiting for transfers between devices: 15.9 us -> 1.96 us  [reduce_over_shots(): hop = lambda v, to: lax.ppermute(v, 'shot', [(i, to(i)) for i in range(16)])]
    ppermute x8, waiting for transfers between devices: 7.26 us -> 4.82 us  [passed_along(): return lax.ppermute(value, axis, pairs)]
    unnamed x35 -> x43, local copies, waits for them, and re-layouts: 13.9 us -> 13.1 us
  transfers between devices with their start and end apart: 13 -> 13, of which waited for: 5 -> 5; matrix products, arithmetic and copies ran while one was open for 5% -> 0% of each run, Pallas kernels for 20% -> 23%
where the time goes in v2:
time: 67.7 us; the launch traced here: 67.1 us
  starting transfers between devices  25 us (37%)
  Pallas kernels  20.4 us (30%)
  local copies, waits for them, and re-layouts  13.3 us (20%)
  waiting for transfers between devices  6.78 us (10%)
  between operations  1.43 us (2%)
    ppermute x8, starting transfers between devices, passed_along(): return lax.ppermute(value, axis, pairs)  16.9 us
    unnamed x43, local copies, waits for them, and re-layouts  13.1 us
    ppermute x5, starting transfers between devices, reduce_over_shots(): hop = lambda v, to: lax.ppermute(v, 'shot', [(i, to(i)) for i in range(16)])  8.18 us
    pallas_call x2, Pallas kernels, middle(): call(kernel, [S] + [V] * 7 + [held] * 2 + [V] * 4, (sends(faces), sends(f...  8.14 us
    ppermute x8, waiting for transfers between devices, passed_along(): return lax.ppermute(value, axis, pairs)  4.82 us
    pallas_call x1, Pallas kernels, body(): call(last_kernel, [S] + [V] * 13, shape(1125, 2, 128), [scr(field(3)), sc...  3.55 us
    pallas_call x1, Pallas kernels, body(): call(last_image_kernel, [S] + [V] * 6 + [S] * 2 + [V] * 2, (shape(8, 16,...  2.56 us
    pallas_call x1, Pallas kernels, body(): call(forward_start_kernel, [V] * 3, (sends(7), sends(7), field(3), field(...  2.24 us
  transfers between devices with their start and end apart: 13, of which 5 were waited for; matrix products, arithmetic and copies ran while one was open for 0% of the time, Pallas kernels for 23%

profile of v2, /device:TPU:0, one launch (start us, length us, event | category | flops | bytes accessed | tf_op | source)
XLA Modules:
  0.0 67.1 jit_solution(11762800177708252882)
XLA Ops:
  0.6 1.0 %copy-done = f32[3,5,5,5,256]{4,0,3,2,1:T(4,128)S(1)} copy-done((f32[3,5,5,5,256]{4,0,3,2,1:T(4,128)S(1)}, f32[3,5,5,5,256]{4,0,3,2,1:T(4,128)}, u32[]{:S(2)}) %copy-start) | copy-done | bytes 384024
  1.7 1.3 %copy-done.8 = f32[1,9,5,5,5,256]{5,0,4,3,2,1:T(1,128)S(1)} copy-done((f32[1,9,5,5,5,256]{5,0,4,3,2,1:T(1,128)S(1)}, f32[1,9,5,5,5,256]{5,0,4,3,2,1:T(1,128)}, u32[]{:S(2)}) %copy-start.8) | copy-done | bytes 1152024
  2.9 0.7 %copy-done.15 = s32[256,4]{0,1:T(4,128)S(1)} copy-done((s32[256,4]{0,1:T(4,128)S(1)}, s32[256,4]{0,1:T(4,128)}, u32[]{:S(2)}) %copy-start.15) | copy-done | bytes 4120
  3.6 2.2 %shard_map.95 = (f32[175,2,128]{2,1,0:T(2,128)}, f32[175,2,128]{2,1,0:T(2,128)}, f32[2,3,5,5,8,128]{5,4,3,2,1,0:T(8,128)S(1)}, f32[2,3,5,5,8,128]{5,4,3,2,1,0:T(...) custom-call(f32[1125,2,128]{2,1,0:T(2,128)S(1)} %bitcast.34, ...), custom_call_target="tpu_custom_call" | custom-call | flops 100000000 | bytes 4000000 | tf_op jit(solution)/shard_map/pallas_call | solution.py:502
  5.9 1.0 %copy-done.4 = f32[2,6,5,5,8,128]{5,4,3,2,1,0:T(8,128)} copy-done((f32[2,6,5,5,8,128]{5,4,3,2,1,0:T(8,128)}, f32[2,6,5,5,8,128]{5,4,3,2,1,0:T(8,128)S(1)}, u32[]{:S(2)}) %copy-start.4) | copy-done | bytes 1228824
  6.9 0.8 %copy-done.12 = f32[2,3,5,5,8,128]{5,4,3,2,1,0:T(8,128)} copy-done((f32[2,3,5,5,8,128]{5,4,3,2,1,0:T(8,128)}, f32[2,3,5,5,8,128]{5,4,3,2,1,0:T(8,128)S(1)}, u32[]{:S(2)}) %copy-start.12) | copy-done | bytes 614424
  7.7 2.0 %collective-permute-start = (f32[175,2,128]{2,1,0:T(2,128)}, f32[175,2,128]{2,1,0:T(2,128)S(1)}, u32[]{:S(2)}, u32[]{:S(2)}) collective-permute-start(f32[175,2,128]{2,1,0:T(2,128)} %get-tuple-element.37), channel_id=1, source_target_pairs={{0,16},{16,32},{32,48},{48,64},{64,80},{80,96},{96,112},{112,0},{1... | collective-permute-start | bytes 537608 | tf_op jit(solution)/shard_map/ppermute | solution.py:475
  9.7 2.5 %collective-permute-start.1 = (f32[175,2,128]{2,1,0:T(2,128)}, f32[175,2,128]{2,1,0:T(2,128)S(1)}, u32[]{:S(2)}, u32[]{:S(2)}) collective-permute-start(f32[175,2,128]{2,1,0:T(2,128)} %get-tuple-element.38), channel_id=1, source_target_pairs={{0,112},{16,0},{32,16},{48,32},{64,48},{80,64},{96,80},{112,96},{1... | collective-permute-start | bytes 537608 | tf_op jit(solution)/shard_map/ppermute | solution.py:475
  12.2 2.1 %shard_map.96 = (f32[150,2,128]{2,1,0:T(2,128)}, f32[150,2,128]{2,1,0:T(2,128)}, f32[2,3,5,5,8,128]{5,4,3,2,1,0:T(8,128)S(1)}, f32[2,3,5,5,8,128]{5,4,3,2,1,0:T(...) custom-call(f32[1125,2,128]{2,1,0:T(2,128)S(1)} %bitcast.35, ...), custom_call_target="tpu_custom_call" | custom-call | flops 100000000 | bytes 4000000 | tf_op jit(solution)/shard_map/pallas_call | solution.py:510
  14.3 1.1 %copy-done.2 = f32[2,6,5,5,8,128]{5,4,3,2,1,0:T(8,128)} copy-done((f32[2,6,5,5,8,128]{5,4,3,2,1,0:T(8,128)}, f32[2,6,5,5,8,128]{5,4,3,2,1,0:T(8,128)S(1)}, u32[]{:S(2)}) %copy-start.2) | copy-done | bytes 1228824
  15.3 4.1 %collective-permute-start.3 = (f32[150,2,128]{2,1,0:T(2,128)}, f32[150,2,128]{2,1,0:T(2,128)}, u32[]{:S(2)}, u32[]{:S(2)}) collective-permute-start(f32[150,2,128]{2,1,0:T(2,128)} %get-tuple-element.46), channel_id=1, source_target_pairs={{0,112},{16,0},{32,16},{48,32},{64,48},{80,64},{96,80},{112,96},{1... | collective-permute-start | bytes 460808 | tf_op jit(solution)/shard_map/ppermute | solution.py:475
  20.2 1.9 %collective-permute-done.refs_9_.refs_11_.r_below = f32[175,2,128]{2,1,0:T(2,128)S(1)} collective-permute-done((f32[175,2,128]{2,1,0:T(2,128)}, f32[175,2,128]{2,1,0:T(2,128)S(1)}, u32[]{:S(2)}, u32[]{:S(2)}) %collective-permute-start) | collective-permute-done | bytes 179232 | tf_op jit(solution)/shard_map/ppermute | solution.py:475
  22.1 2.1 %collective-permute-done.1.refs_10_.refs_12_.r_above = f32[175,2,128]{2,1,0:T(2,128)S(1)} collective-permute-done((f32[175,2,128]{2,1,0:T(2,128)}, f32[175,2,128]{2,1,0:T(2,128)S(1)}, u32[]{:S(2)}, u32[]{:S(2)}) %collective-permute-start.1) | collective-permute-done | bytes 179232 | tf_op jit(solution)/shard_map/ppermute | solution.py:475
  24.2 1.3 %copy-done.5 = f32[2,6,5,5,8,128]{5,4,3,2,1,0:T(8,128)S(1)} copy-done((f32[2,6,5,5,8,128]{5,4,3,2,1,0:T(8,128)S(1)}, f32[2,6,5,5,8,128]{5,4,3,2,1,0:T(8,128)}, u32[]{:S(2)}) %copy-start.5) | copy-done | bytes 1228824
  25.5 1.1 %copy-done.13 = f32[2,3,5,5,8,128]{5,4,3,2,1,0:T(8,128)S(1)} copy-done((f32[2,3,5,5,8,128]{5,4,3,2,1,0:T(8,128)S(1)}, f32[2,3,5,5,8,128]{5,4,3,2,1,0:T(8,128)}, u32[]{:S(2)}) %copy-start.13) | copy-done | bytes 614424
  26.6 3.8 %shard_map.97 = (f32[75,2,128]{2,1,0:T(2,128)S(1)}, f32[75,2,128]{2,1,0:T(2,128)S(1)}, f32[2,3,5,5,8,128]{5,4,3,2,1,0:T(8,128)S(1)}, f32[2,6,5,5,8,128]{5,4,3,2,...) custom-call(s32[2]{0:T(128)S(1)} %pad_add_fusion.base_ref.base, ...), custom_call_target="tpu_custom_call" | custom-call | flops 200000000 | bytes 8000000 | tf_op jit(solution)/shard_map/pallas_call | solution.py:523
  30.6 3.8 %collective-permute-start.5 = (f32[75,2,128]{2,1,0:T(2,128)S(1)}, f32[75,2,128]{2,1,0:T(2,128)S(1)}, u32[]{:S(2)}, u32[]{:S(2)}) collective-permute-start(f32[75,2,128]{2,1,0:T(2,128)S(1)} %get-tuple-element.51), channel_id=1, source_target_pairs={{0,112},{16,0},{32,16},{48,32},{64,48},{80,64},{96,80},{112,96},{1... | collective-permute-start | bytes 230408 | tf_op jit(solution)/shard_map/ppermute | solution.py:475
  34.5 1.1 %copy-done.11 = f32[2,3,5,5,8,128]{5,4,3,2,1,0:T(8,128)S(1)} copy-done((f32[2,3,5,5,8,128]{5,4,3,2,1,0:T(8,128)S(1)}, f32[2,3,5,5,8,128]{5,4,3,2,1,0:T(8,128)}, u32[]{:S(2)}) %copy-start.11) | copy-done | bytes 614424
  35.6 4.4 %shard_map.98 = (f32[150,2,128]{2,1,0:T(2,128)S(1)}, f32[150,2,128]{2,1,0:T(2,128)S(1)}, f32[2,3,5,5,8,128]{5,4,3,2,1,0:T(8,128)S(1)}, f32[2,6,5,5,8,128]{5,4,3,...) custom-call(s32[2]{0:T(128)S(1)} %pad_add_fusion.base_ref.base, ...), custom_call_target="tpu_custom_call" | custom-call | flops 200000000 | bytes 8000000 | tf_op jit(solution)/shard_map/pallas_call | solution.py:523
  40.0 1.1 %copy-done.6 = f32[2,6,5,5,8,128]{5,4,3,2,1,0:T(8,128)} copy-done((f32[2,6,5,5,8,128]{5,4,3,2,1,0:T(8,128)}, f32[2,6,5,5,8,128]{5,4,3,2,1,0:T(8,128)S(1)}, u32[]{:S(2)}) %copy-start.6) | copy-done | bytes 1228824
  41.7 1.8 %shard_map.99 = (f32[2,384,128]{2,1,0:T(8,128)S(1)}, f32[2,9,5,5,8,128]{5,4,3,2,1,0:T(8,128)S(1)}) custom-call(f32[2,3,5,5,8,128]{5,4,3,2,1,0:T(8,128)S(1)} %get-tuple-element.41.refs_0_.adj_vel_end.adj_vel, f32[2,3,5,5,8,128]{5,4,3,2,1,0:T(8,128)S(1)} %get-tuple-element.39.f_vel, f32[2,3,5,5,8,128]{5,4,3,2,1,0:T(8,128)S(1)} %get-tuple-element.42.f_acc, ...), custom_call_target="tpu_custom_call" | custom-call | flops 100000000 | bytes 8000000 | tf_op jit(solution)/shard_map/pallas_call | solution.py:539
  43.5 2.6 %shard_map.100 = (f32[8,16,384]{2,1,0:T(8,128)S(1)}, f32[8,16,384]{2,1,0:T(8,128)}) custom-call(s32[2]{0:T(128)S(1)} %pad_add_fusion.base_ref.base, f32[2,3,5,5,8,128]{5,4,3,2,1,0:T(8,128)S(1)} %get-tuple-element.39.f_vel, f32[2,3,5,5,8,128]{5,4,3,2,1,0:T(8,128)S(1)} %get-tuple-element.40.acc_in, ...), custom_call_target="tpu_custom_call" | custom-call | flops 100000000 | bytes 8000000 | tf_op jit(solution)/shard_map/pallas_call | solution.py:546
  46.1 1.6 %collective-permute-done.6 = f32[8,16,384]{2,1,0:T(8,128)S(1)} collective-permute-done((f32[8,16,384]{2,1,0:T(8,128)}, f32[8,16,384]{2,1,0:T(8,128)S(1)}, u32[]{:S(2)}, u32[]{:S(2)}) %collective-permute-start.6) | collective-permute-done | bytes 196640 | tf_op jit(solution)/shard_map/ppermute | solution.py:486
  47.8 2.8 %collective-permute-start.9 = (f32[2,16,384]{2,1,0:T(8,128)S(1)}, f32[2,16,384]{2,1,0:T(8,128)S(1)}, u32[]{:S(2)}, u32[]{:S(2)}) collective-permute-start(f32[2,16,384]{2,1,0:T(8,128)S(1)} %get-tuple-element.67), channel_id=1, source_target_pairs={{0,12},{1,13},{2,14},{3,15},{4,0},{5,1},{6,2},{7,3},{8,4},{9,5},{1... | collective-permute-start | bytes 147464 | tf_op jit(solution)/shard_map/ppermute | solution.py:486
  50.6 0.8 %collective-permute-start.8 = (f32[2,16,384]{2,1,0:T(8,128)S(1)}, f32[2,16,384]{2,1,0:T(8,128)S(1)}, u32[]{:S(2)}, u32[]{:S(2)}) collective-permute-start(f32[2,16,384]{2,1,0:T(8,128)S(1)} %get-tuple-element.68), channel_id=1, source_target_pairs={{0,8},{1,9},{2,10},{3,11},{4,12},{5,13},{6,14},{7,15},{8,0},{9,1},... | collective-permute-start | bytes 147464 | tf_op jit(solution)/shard_map/ppermute | solution.py:486
  51.4 0.9 %collective-permute-start.7 = (f32[2,16,384]{2,1,0:T(8,128)S(1)}, f32[2,16,384]{2,1,0:T(8,128)S(1)}, u32[]{:S(2)}, u32[]{:S(2)}) collective-permute-start(f32[2,16,384]{2,1,0:T(8,128)S(1)} %get-tuple-element.66), channel_id=1, source_target_pairs={{0,4},{1,5},{2,6},{3,7},{4,8},{5,9},{6,10},{7,11},{8,12},{9,13},{1... | collective-permute-start | bytes 147464 | tf_op jit(solution)/shard_map/ppermute | solution.py:486
  52.3 4.1 %collective-permute-start.12 = (f32[150,2,128]{2,1,0:T(2,128)}, f32[150,2,128]{2,1,0:T(2,128)S(1)}, u32[]{:S(2)}, u32[]{:S(2)}) collective-permute-start(f32[150,2,128]{2,1,0:T(2,128)} %copy-done.19), channel_id=1, source_target_pairs={{0,112},{16,0},{32,16},{48,32},{64,48},{80,64},{96,80},{112,96},{1... | collective-permute-start | bytes 460808 | tf_op jit(solution)/shard_map/ppermute | solution.py:475
  56.8 3.7 %collective-permute-start.10 = (f32[16,384]{1,0:T(8,128)S(1)}, f32[16,384]{1,0:T(8,128)S(1)}, u32[]{:S(2)}, u32[]{:S(2)}) collective-permute-start(f32[16,384]{1,0:T(8,128)S(1)} %get-tuple-element.70), channel_id=1, source_target_pairs={{0,2},{1,3},{2,0},{3,1},{4,6},{5,7},{6,4},{7,5},{8,10},{9,11},{10,... | collective-permute-start | bytes 73736 | tf_op jit(solution)/shard_map/ppermute | solution.py:486
  60.5 0.8 %collective-permute-done.12.above = f32[150,2,128]{2,1,0:T(2,128)S(1)} collective-permute-done((f32[150,2,128]{2,1,0:T(2,128)}, f32[150,2,128]{2,1,0:T(2,128)S(1)}, u32[]{:S(2)}, u32[]{:S(2)}) %collective-permute-start.12) | collective-permute-done | bytes 153632 | tf_op jit(solution)/shard_map/ppermute | solution.py:475
  61.3 1.3 %copy-done.7 = f32[2,6,5,5,8,128]{5,4,3,2,1,0:T(8,128)S(1)} copy-done((f32[2,6,5,5,8,128]{5,4,3,2,1,0:T(8,128)S(1)}, f32[2,6,5,5,8,128]{5,4,3,2,1,0:T(8,128)}, u32[]{:S(2)}) %copy-start.7) | copy-done | bytes 1228824
  62.6 3.6 %shard_map.101 = f32[1125,2,128]{2,1,0:T(2,128)} custom-call(s32[2]{0:T(128)S(1)} %pad_add_fusion.base_ref.base, f32[2,3,5,5,8,128]{5,4,3,2,1,0:T(8,128)S(1)} %get-tuple-element.47.a_vel.vel_in, f32[2,6,5,5,8,128]{5,4,3,2,1,0:T(8,128)S(1)} %copy-done.7, f32[2,3,5,5,8,128]{5,4,3,2,1,0:T(8,128)S(1)} %get-tuple-element.55.acc_in, ...), custom_call_target="tpu_custom_call" | custom-call | flops 100000000 | bytes 8000000 | tf_op jit(solution)/shard_map/pallas_call | solution.py:554
  66.3 0.8 %copy.16 = f32[3,5,5,5,16]{4,0,3,2,1:T(4,128)} copy(f32[3,5,5,5,16]{4,3,2,1,0:T(8,128)S(1)} %reshape.34) | data formatting | bytes 48000
  (52 shorter events, 1.6 us)
Async XLA Ops:
  0.6 1.0 %copy-start = (f32[3,5,5,5,256]{4,0,3,2,1:T(4,128)S(1)}, f32[3,5,5,5,256]{4,0,3,2,1:T(4,128)}, u32[]{:S(2)}) copy-start(f32[3,5,5,5,256]{4,0,3,2,1:T(4,128)} %param.10) | copy-start | bytes 1152004
  1.7 1.3 %copy-start.8 = (f32[1,9,5,5,5,256]{5,0,4,3,2,1:T(1,128)S(1)}, f32[1,9,5,5,5,256]{5,0,4,3,2,1:T(1,128)}, u32[]{:S(2)}) copy-start(f32[1,9,5,5,5,256]{5,0,4,3,2,1:T(1,128)} %param.8) | copy-start | bytes 3456004
  3.6 8.6 %copy-start.1 = (f32[3,5,5,5,256]{4,0,3,2,1:T(4,128)S(1)}, f32[3,5,5,5,256]{4,0,3,2,1:T(4,128)}, u32[]{:S(2)}) copy-start(f32[3,5,5,5,256]{4,0,3,2,1:T(4,128)} %param.10) | copy-start | bytes 1152004
  3.6 8.6 %copy-start.9 = (f32[1,9,5,5,5,256]{5,0,4,3,2,1:T(1,128)S(1)}, f32[1,9,5,5,5,256]{5,0,4,3,2,1:T(1,128)}, u32[]{:S(2)}) copy-start(f32[1,9,5,5,5,256]{5,0,4,3,2,1:T(1,128)} %param.9) | copy-start | bytes 3456004
  5.9 1.0 %copy-start.4 = (f32[2,6,5,5,8,128]{5,4,3,2,1,0:T(8,128)}, f32[2,6,5,5,8,128]{5,4,3,2,1,0:T(8,128)S(1)}, u32[]{:S(2)}) copy-start(f32[2,6,5,5,8,128]{5,4,3,2,1,0:T(8,128)S(1)} %get-tuple-element.31.refs_1_) | copy-start | bytes 3686404
  6.9 0.8 %copy-start.12 = (f32[2,3,5,5,8,128]{5,4,3,2,1,0:T(8,128)}, f32[2,3,5,5,8,128]{5,4,3,2,1,0:T(8,128)S(1)}, u32[]{:S(2)}) copy-start(f32[2,3,5,5,8,128]{5,4,3,2,1,0:T(8,128)S(1)} %get-tuple-element.30.refs_0_) | copy-start | bytes 1843204
  7.7 16.5 %copy-start.16 = (f32[1,2,3]{2,1,0:T(2,128)S(1)}, f32[1,2,3]{2,1,0:T(2,128)}, u32[]{:S(2)}) copy-start(f32[1,2,3]{2,1,0:T(2,128)} %strength.1) | copy-start | bytes 76
  7.7 14.4 %collective-permute-start = (f32[175,2,128]{2,1,0:T(2,128)}, f32[175,2,128]{2,1,0:T(2,128)S(1)}, u32[]{:S(2)}, u32[]{:S(2)}) collective-permute-start(f32[175,2,128]{2,1,0:T(2,128)} %get-tuple-element.37), channel_id=1, source_target_pairs={{0,16},{16,32},{32,48},{48,64},{64,80},{80,96},{96,112},{112,0},{1... | collective-permute-start | bytes 537608 | tf_op jit(solution)/shard_map/ppermute | solution.py:475
  9.7 14.5 %collective-permute-start.1 = (f32[175,2,128]{2,1,0:T(2,128)}, f32[175,2,128]{2,1,0:T(2,128)S(1)}, u32[]{:S(2)}, u32[]{:S(2)}) collective-permute-start(f32[175,2,128]{2,1,0:T(2,128)} %get-tuple-element.38), channel_id=1, source_target_pairs={{0,112},{16,0},{32,16},{48,32},{64,48},{80,64},{96,80},{112,96},{1... | collective-permute-start | bytes 537608 | tf_op jit(solution)/shard_map/ppermute | solution.py:475
  14.3 1.1 %copy-start.2 = (f32[2,6,5,5,8,128]{5,4,3,2,1,0:T(8,128)}, f32[2,6,5,5,8,128]{5,4,3,2,1,0:T(8,128)S(1)}, u32[]{:S(2)}) copy-start(f32[2,6,5,5,8,128]{5,4,3,2,1,0:T(8,128)S(1)} %get-tuple-element.43.refs_1_) | copy-start | bytes 3686404
  15.3 15.0 %copy-start.10 = (f32[2,3,5,5,8,128]{5,4,3,2,1,0:T(8,128)}, f32[2,3,5,5,8,128]{5,4,3,2,1,0:T(8,128)S(1)}, u32[]{:S(2)}) copy-start(f32[2,3,5,5,8,128]{5,4,3,2,1,0:T(8,128)S(1)} %get-tuple-element.44.refs_2_) | copy-start | bytes 1843204
  15.3 19.2 %collective-permute-start.2 = (f32[150,2,128]{2,1,0:T(2,128)}, f32[150,2,128]{2,1,0:T(2,128)S(1)}, u32[]{:S(2)}, u32[]{:S(2)}) collective-permute-start(f32[150,2,128]{2,1,0:T(2,128)} %get-tuple-element.45), channel_id=1, source_target_pairs={{0,16},{16,32},{32,48},{48,64},{64,80},{80,96},{96,112},{112,0},{1... | collective-permute-start | bytes 460808 | tf_op jit(solution)/shard_map/ppermute | solution.py:475
  15.3 19.2 %collective-permute-start.3 = (f32[150,2,128]{2,1,0:T(2,128)}, f32[150,2,128]{2,1,0:T(2,128)}, u32[]{:S(2)}, u32[]{:S(2)}) collective-permute-start(f32[150,2,128]{2,1,0:T(2,128)} %get-tuple-element.46), channel_id=1, source_target_pairs={{0,112},{16,0},{32,16},{48,32},{64,48},{80,64},{96,80},{112,96},{1... | collective-permute-start | bytes 460808 | tf_op jit(solution)/shard_map/ppermute | solution.py:475
  24.2 1.3 %copy-start.5 = (f32[2,6,5,5,8,128]{5,4,3,2,1,0:T(8,128)S(1)}, f32[2,6,5,5,8,128]{5,4,3,2,1,0:T(8,128)}, u32[]{:S(2)}) copy-start(f32[2,6,5,5,8,128]{5,4,3,2,1,0:T(8,128)} %copy-done.4) | copy-start | bytes 3686404
  25.5 1.1 %copy-start.13 = (f32[2,3,5,5,8,128]{5,4,3,2,1,0:T(8,128)S(1)}, f32[2,3,5,5,8,128]{5,4,3,2,1,0:T(8,128)}, u32[]{:S(2)}) copy-start(f32[2,3,5,5,8,128]{5,4,3,2,1,0:T(8,128)} %copy-done.12) | copy-start | bytes 1843204
  26.6 7.9 %copy-start.3 = (f32[2,6,5,5,8,128]{5,4,3,2,1,0:T(8,128)S(1)}, f32[2,6,5,5,8,128]{5,4,3,2,1,0:T(8,128)}, u32[]{:S(2)}) copy-start(f32[2,6,5,5,8,128]{5,4,3,2,1,0:T(8,128)} %copy-done.2) | copy-start | bytes 3686404
  26.6 7.9 %copy-start.14 = (f32[1,2,3,256]{3,1,2,0:T(2,128)S(1)}, f32[1,2,3,256]{3,1,2,0:T(2,128)}, u32[]{:S(2)}) copy-start(f32[1,2,3,256]{3,1,2,0:T(2,128)} %param.15) | copy-start | bytes 18436
  26.6 7.9 %copy-start.17 = (s32[256]{0:T(256)S(1)}, s32[256]{0:T(256)}, u32[]{:S(2)}) copy-start(s32[256]{0:T(256)} %param.14) | copy-start | bytes 3076
  30.4 13.2 %collective-permute-start.4 = (f32[75,2,128]{2,1,0:T(2,128)S(1)}, f32[75,2,128]{2,1,0:T(2,128)S(1)}, u32[]{:S(2)}, u32[]{:S(2)}) collective-permute-start(f32[75,2,128]{2,1,0:T(2,128)S(1)} %get-tuple-element.50), channel_id=1, source_target_pairs={{0,16},{16,32},{32,48},{48,64},{64,80},{80,96},{96,112},{112,0},{1... | collective-permute-start | bytes 230408 | tf_op jit(solution)/shard_map/ppermute | solution.py:475
  30.6 12.9 %collective-permute-start.5 = (f32[75,2,128]{2,1,0:T(2,128)S(1)}, f32[75,2,128]{2,1,0:T(2,128)S(1)}, u32[]{:S(2)}, u32[]{:S(2)}) collective-permute-start(f32[75,2,128]{2,1,0:T(2,128)S(1)} %get-tuple-element.51), channel_id=1, source_target_pairs={{0,112},{16,0},{32,16},{48,32},{64,48},{80,64},{96,80},{112,96},{1... | collective-permute-start | bytes 230408 | tf_op jit(solution)/shard_map/ppermute | solution.py:475
  34.5 1.1 %copy-start.11 = (f32[2,3,5,5,8,128]{5,4,3,2,1,0:T(8,128)S(1)}, f32[2,3,5,5,8,128]{5,4,3,2,1,0:T(8,128)}, u32[]{:S(2)}) copy-start(f32[2,3,5,5,8,128]{5,4,3,2,1,0:T(8,128)} %copy-done.10) | copy-start | bytes 1843204
  40.0 1.1 %copy-start.6 = (f32[2,6,5,5,8,128]{5,4,3,2,1,0:T(8,128)}, f32[2,6,5,5,8,128]{5,4,3,2,1,0:T(8,128)S(1)}, u32[]{:S(2)}) copy-start(f32[2,6,5,5,8,128]{5,4,3,2,1,0:T(8,128)S(1)} %get-tuple-element.54.stress_in) | copy-start | bytes 3686404
  41.7 1.8 %copy-start.19 = (f32[150,2,128]{2,1,0:T(2,128)}, f32[150,2,128]{2,1,0:T(2,128)S(1)}, u32[]{:S(2)}) copy-start(f32[150,2,128]{2,1,0:T(2,128)S(1)} %get-tuple-element.57) | copy-start | bytes 460804
  46.1 15.2 %copy-start.18 = (s32[256]{0:T(256)S(1)}, s32[256]{0:T(256)}, u32[]{:S(2)}) copy-start(s32[256]{0:T(256)} %param.14) | copy-start | bytes 3076
  46.1 1.7 %collective-permute-start.6 = (f32[8,16,384]{2,1,0:T(8,128)}, f32[8,16,384]{2,1,0:T(8,128)S(1)}, u32[]{:S(2)}, u32[]{:S(2)}) collective-permute-start(f32[8,16,384]{2,1,0:T(8,128)} %get-tuple-element.53), channel_id=1, source_target_pairs={{0,1},{1,0},{2,3},{3,2},{4,5},{5,4},{6,7},{7,6},{8,9},{9,8},{10,11... | collective-permute-start | bytes 589832 | tf_op jit(solution)/shard_map/ppermute | solution.py:486
  47.8 8.6 %collective-permute-start.9 = (f32[2,16,384]{2,1,0:T(8,128)S(1)}, f32[2,16,384]{2,1,0:T(8,128)S(1)}, u32[]{:S(2)}, u32[]{:S(2)}) collective-permute-start(f32[2,16,384]{2,1,0:T(8,128)S(1)} %get-tuple-element.67), channel_id=1, source_target_pairs={{0,12},{1,13},{2,14},{3,15},{4,0},{5,1},{6,2},{7,3},{8,4},{9,5},{1... | collective-permute-start | bytes 147464 | tf_op jit(solution)/shard_map/ppermute | solution.py:486
  50.6 5.8 %collective-permute-start.8 = (f32[2,16,384]{2,1,0:T(8,128)S(1)}, f32[2,16,384]{2,1,0:T(8,128)S(1)}, u32[]{:S(2)}, u32[]{:S(2)}) collective-permute-start(f32[2,16,384]{2,1,0:T(8,128)S(1)} %get-tuple-element.68), channel_id=1, source_target_pairs={{0,8},{1,9},{2,10},{3,11},{4,12},{5,13},{6,14},{7,15},{8,0},{9,1},... | collective-permute-start | bytes 147464 | tf_op jit(solution)/shard_map/ppermute | solution.py:486
  51.4 5.3 %collective-permute-start.7 = (f32[2,16,384]{2,1,0:T(8,128)S(1)}, f32[2,16,384]{2,1,0:T(8,128)S(1)}, u32[]{:S(2)}, u32[]{:S(2)}) collective-permute-start(f32[2,16,384]{2,1,0:T(8,128)S(1)} %get-tuple-element.66), channel_id=1, source_target_pairs={{0,4},{1,5},{2,6},{3,7},{4,8},{5,9},{6,10},{7,11},{8,12},{9,13},{1... | collective-permute-start | bytes 147464 | tf_op jit(solution)/shard_map/ppermute | solution.py:486
  52.3 8.2 %collective-permute-start.11 = (f32[150,2,128]{2,1,0:T(2,128)}, f32[150,2,128]{2,1,0:T(2,128)S(1)}, u32[]{:S(2)}, u32[]{:S(2)}) collective-permute-start(f32[150,2,128]{2,1,0:T(2,128)} %copy-done.20), channel_id=1, source_target_pairs={{0,16},{16,32},{32,48},{48,64},{64,80},{80,96},{96,112},{112,0},{1... | collective-permute-start | bytes 460808 | tf_op jit(solution)/shard_map/ppermute | solution.py:475
  52.3 9.0 %collective-permute-start.12 = (f32[150,2,128]{2,1,0:T(2,128)}, f32[150,2,128]{2,1,0:T(2,128)S(1)}, u32[]{:S(2)}, u32[]{:S(2)}) collective-permute-start(f32[150,2,128]{2,1,0:T(2,128)} %copy-done.19), channel_id=1, source_target_pairs={{0,112},{16,0},{32,16},{48,32},{64,48},{80,64},{96,80},{112,96},{1... | collective-permute-start | bytes 460808 | tf_op jit(solution)/shard_map/ppermute | solution.py:475
  56.8 9.3 %collective-permute-start.10 = (f32[16,384]{1,0:T(8,128)S(1)}, f32[16,384]{1,0:T(8,128)S(1)}, u32[]{:S(2)}, u32[]{:S(2)}) collective-permute-start(f32[16,384]{1,0:T(8,128)S(1)} %get-tuple-element.70), channel_id=1, source_target_pairs={{0,2},{1,3},{2,0},{3,1},{4,6},{5,7},{6,4},{7,5},{8,10},{9,11},{10,... | collective-permute-start | bytes 73736 | tf_op jit(solution)/shard_map/ppermute | solution.py:486
  61.3 1.3 %copy-start.7 = (f32[2,6,5,5,8,128]{5,4,3,2,1,0:T(8,128)S(1)}, f32[2,6,5,5,8,128]{5,4,3,2,1,0:T(8,128)}, u32[]{:S(2)}) copy-start(f32[2,6,5,5,8,128]{5,4,3,2,1,0:T(8,128)} %copy-done.6) | copy-start | bytes 3686404
  (2 other events, 1.3 us)

commit v3 on v2

--- a/solution.py
+++ b/solution.py
@@ -218,6 +218,10 @@
     return [total[i : i + 1] for i in range(3)]
 
 
+def slab_base():
+    return lax.axis_index("slab") * N
+
+
 def velocities(vel_in, vel, acc, rows):
     def one(i, h):
         for a in range(5):
@@ -315,8 +319,14 @@
     halves(1, one)
 
 
-def start_common(state, rinv, perms, acc, vel, stress, up, down, yj, zj, with_r):
-    src = flat(state, 2250)
+def fetch(src, dst, sem):
+    copy = pltpu.make_async_copy(src, dst, sem)
+    copy.start()
+    return copy
+
+
+def start_common(src, rinv, perms, acc, vel, stress, up, down, yj, zj, with_r):
+    src = flat(src, 2250)
     up, down = (flat(r, r.shape[0] * 2) for r in (up, down))
     load_fields(src, 0, vel, 3)
     load_fields(src, 3, stress, 6)
@@ -337,13 +347,19 @@
             dst[h, g // 5, g % 5, 0:5, :] = mat[5 * g : 5 * g + 5, k, 128 * h : 128 * h + 128]
 
 
-def forward_start_kernel(state, mat, nbr, up, down, acc, vel, stress, rinv, perms, yj, zj):
+def forward_start_kernel(state_hbm, mat_hbm, nbr_hbm, up, down, acc, vel, stress, rinv, perms, yj, zj, state, mat, nbr, sems):
+    first = fetch(nbr_hbm, nbr, sems.at[0])
+    second = fetch(mat_hbm, mat, sems.at[1])
+    third = fetch(state_hbm, state, sems.at[2])
+    first.wait()
     make_perms(nbr, perms)
+    second.wait()
     load_material(mat, 2, rinv)
     for h in range(2):
         for a in range(5):
             rinv[h, a] = 1.0 / rinv[h, a]
     zj[...] = jnp.zeros(zj.shape, f32)
+    third.wait()
     start_common(state, rinv, perms, acc, vel, stress, up, down, yj, zj, True)
 
 
@@ -365,14 +381,16 @@
     update_stress(stress_in, stress, grads, lam, mu)
 
 
-def middle_kernel(kind, base, vel_in, stress_in, acc_in, lam, mu, rinv, perms, where_ref, strength,
-                  below, above, r_below, r_above, up, down, vel, stress, acc, next_acc, halo, grads, yj, zj):
+def middle_kernel(kind, vel_in, stress_in, acc_in, lam, mu, rinv, perms, where_ref, strength,
+                  below, above, r_below, r_above, up, down, vel, stress, acc, *rest):
+    next_acc, (halo, grads, yj, zj) = (rest[0], rest[1:]) if kind == "receiver" else (None, rest)
     zj[...] = jnp.zeros(zj.shape, f32)
     load_halo(halo, *(flat(r, r.shape[0] * 2) for r in (below, above, r_below, r_above)), 6)
     acc[...] = acc_in[...]
-    finish_step(kind, 0, base[0], vel_in, stress_in, lam, mu, rinv, perms, where_ref, strength,
+    finish_step(kind, 0, slab_base(), vel_in, stress_in, lam, mu, rinv, perms, where_ref, strength,
                 vel, stress, acc, halo, grads, yj, zj)
-    local_acceleration(stress, rinv, next_acc, perms, yj, zj)
+    if kind == "receiver":
+        local_acceleration(stress, rinv, next_acc, perms, yj, zj)
     for dst, a in ((up, 4), (down, 0)):
         dst = flat(dst, dst.shape[0] * 2)
         for i in range(3):
@@ -382,12 +400,12 @@
                     pack_face(dst, 3 + i, vel[h, i, a] + time_step * next_acc[h, i, a], h)
 
 
-def last_kernel(base, vel_in, stress_in, acc_in, lam, mu, rinv, perms, where_ref, strength,
+def last_kernel(vel_in, stress_in, acc_in, lam, mu, rinv, perms, where_ref, strength,
                 below, above, r_below, r_above, out, vel, stress, acc, halo, grads, yj, zj):
     zj[...] = jnp.zeros(zj.shape, f32)
     load_halo(halo, *(flat(r, r.shape[0] * 2) for r in (below, above, r_below, r_above)), 6)
     acc[...] = acc_in[...]
-    finish_step("receiver", 1, base[0], vel_in, stress_in, lam, mu, rinv, perms, where_ref, strength,
+    finish_step("receiver", 1, slab_base(), vel_in, stress_in, lam, mu, rinv, perms, where_ref, strength,
                 vel, stress, acc, halo, grads, yj, zj)
     dst = flat(out, 2250)
     for first, field, count in ((0, vel, 3), (3, stress, 6)):
@@ -401,24 +419,26 @@
         lax.fori_loop(0, count, one, 0)
 
 
-def first_image_kernel(adj_vel_end, f_vel, f_acc, a_vel, dense, end_grads, fg, ag):
+def first_image_kernel(adj_vel_end, f_vel, f_acc, a_vel, f_stress, rinv, perms, dense, end_grads, next_acc, fg, ag, yj, zj):
+    zj[...] = jnp.zeros(zj.shape, f32)
+    local_acceleration(f_stress, rinv, next_acc, perms, yj, zj)
     plain_gradients(f_vel, fg)
     plain_gradients(a_vel, ag)
     image(fg, ag, f_acc, a_vel, dense, None)
     plain_gradients(adj_vel_end, end_grads)
 
 
-def last_image_kernel(base, f_vel, acc_in, adj_vel, end_grads, first, rinv, where_ref, strength, below, above,
+def last_image_kernel(f_vel, acc_in, adj_vel, end_grads, first, rinv, where_ref, strength, below, above,
                       keep, send, halo, vel, acc, fg, dense):
     load_halo(halo, flat(below, 150), flat(above, 150), None, None, 3)
     acc[...] = acc_in[...]
     finish_acceleration(acc, None, rinv, halo, False)
-    velocities(f_vel, vel, acc, inject_rows("source", 1, where_ref, strength, base[0]))
+    velocities(f_vel, vel, acc, inject_rows("source", 1, where_ref, strength, slab_base()))
     plain_gradients(vel, fg)
     for h in range(2):
         dense[h, 368:384, :] = jnp.zeros((16, 128), f32)
     image(fg, end_grads, acc, adj_vel, dense, first)
-    core = base[1]
+    core = lax.rem(lax.axis_index("shot"), 2)
     turned = [dense[h].T for h in range(2)]
     for parity, (mine, other) in ((0, (keep, send)), (1, (send, keep))):
 
@@ -464,7 +484,7 @@
         in_specs=specs,
         out_specs=jax.tree.map(lambda _: V, outs),
         scratch_shapes=scratch,
-        compiler_params=pltpu.CompilerParams(vmem_limit_bytes=20 * 2**20),
+        compiler_params=pltpu.CompilerParams(vmem_limit_bytes=8 * 2**20),
         cost_estimate=pl.CostEstimate(flops=flops, bytes_accessed=moved, transcendentals=0),
     )
 
@@ -492,7 +512,6 @@
 
 
 def body(fwd, adj, materials, nbr, source_element, pulse, receivers, residuals):
-    base = jnp.stack([lax.axis_index("slab") * N, lax.axis_index("shot") % 2]).astype(jnp.int32)
     receivers = receivers.reshape(1, N)
     fwd, adj = (x.reshape(1125, 2, 128) for x in (fwd, adj))
     mat = materials.transpose(1, 2, 3, 0, 4).reshape(125, 3, N)
@@ -501,9 +520,9 @@
 
     f_up, f_down, f_acc, f_vel, f_stress, rinv, perms = call(
         forward_start_kernel,
-        [V] * 3,
+        [pl.BlockSpec(memory_space=pltpu.HBM)] * 3,
         (sends(7), sends(7), field(3), field(3), field(6), ONE, PERMS),
-        JUMPS,
+        JUMPS + [scr(shape(1125, 2, 128)), scr(shape(125, 3, N)), pltpu.VMEM((4, N), jnp.int32), pltpu.SemaphoreType.DMA((3,))],
         10**8, 4 * 10**6,
     )(fwd, mat, nbr)
     f_below, f_above = both_ways(f_up, f_down)
@@ -518,17 +537,17 @@
     adj_vel_end = a_vel
 
     def middle(kind, vel, stress, acc, where_ref, strength, below, above, faces):
-        kernel = lambda base_ref, *refs: middle_kernel(kind, base_ref, *refs)
+        kernel = lambda *refs: middle_kernel(kind, *refs)
         held = S if kind == "source" else V
         return call(
             kernel,
-            [S] + [V] * 7 + [held] * 2 + [V] * 4,
-            (sends(faces), sends(faces), field(3), field(6), field(3), field(3)),
+            [V] * 7 + [held] * 2 + [V] * 4,
+            (sends(faces), sends(faces), field(3), field(6), field(3)) + (() if kind == "source" else (field(3),)),
             [HALO, scr(field(9))] + JUMPS,
             2 * 10**8, 8 * 10**6,
-        )(base, vel, stress, acc, lam, mu, rinv, perms, where_ref, strength, below, above, f_below, f_above)
-
-    f_up, f_down, f_vel1, _, f_acc1, f_acc2 = middle(
+        )(vel, stress, acc, lam, mu, rinv, perms, where_ref, strength, below, above, f_below, f_above)
+
+    f_up, f_down, f_vel1, f_stress1, f_acc1 = middle(
         "source", f_vel, f_stress, f_acc, source_element, pulse, f_below, f_above, 3
     )
     f_below2, f_above2 = both_ways(f_up, f_down)
@@ -536,28 +555,28 @@
         "receiver", a_vel, a_stress, a_acc, receivers, residuals, a_below, a_above, 6
     )
     a_below2, a_above2 = both_ways(a_up, a_down)
-    first, end_grads = call(
+    first, end_grads, f_acc2 = call(
         first_image_kernel,
-        [V] * 4,
-        (shape(2, 384, 128), field(9)),
-        [scr(field(9)), scr(field(9))],
-        10**8, 8 * 10**6,
-    )(adj_vel_end, f_vel1, f_acc1, a_vel1)
+        [V] * 7,
+        (shape(2, 384, 128), field(9), field(3)),
+        [scr(field(9)), scr(field(9))] + JUMPS,
+        1000, 1000,
+    )(adj_vel_end, f_vel1, f_acc1, a_vel1, f_stress1, rinv, perms)
     keep, send = call(
         last_image_kernel,
-        [S] + [V] * 6 + [S] * 2 + [V] * 2,
+        [V] * 6 + [S] * 2 + [V] * 2,
         (shape(8, 16, 384), shape(8, 16, 384)),
         [HALO, scr(field(3)), scr(field(3)), scr(field(9)), scr(shape(2, 384, 128))],
-        10**8, 8 * 10**6,
-    )(base, f_vel1, f_acc2, adj_vel_end, end_grads, first, rinv, source_element, pulse, f_below2, f_above2)
+        1000, 1000,
+    )(f_vel1, f_acc2, adj_vel_end, end_grads, first, rinv, source_element, pulse, f_below2, f_above2)
     gradient = reduce_over_shots(keep, send)
     adjoint_end = call(
         last_kernel,
-        [S] + [V] * 13,
+        [V] * 13,
         shape(1125, 2, 128),
         [scr(field(3)), scr(field(6)), scr(field(3)), HALO, scr(field(9))] + JUMPS,
         10**8, 8 * 10**6,
-    )(base, a_vel1, a_stress1, a_acc2, lam, mu, rinv, perms, receivers, residuals, a_below2, a_above2, f_below, f_above)
+    )(a_vel1, a_stress1, a_acc2, lam, mu, rinv, perms, receivers, residuals, a_below2, a_above2, f_below, f_above)
     return gradient[:, :375].T.reshape(3, 5, 5, 5, 16), adjoint_end.reshape(1, 9, 5, 5, 5, N)
 
 

time: 67.7 us -> 62.5 us (0.923)
  local copies, waits for them, and re-layouts: 13.3 us -> 7.82 us
  Pallas kernels: 20.4 us -> 17 us
  other arithmetic: 0.12 us -> 1.84 us
  starting transfers between devices: 25 us -> 26.5 us
  waiting for transfers between devices: 6.78 us -> 7.54 us
    unnamed x43 -> x27, local copies, waits for them, and re-layouts: 13.1 us -> 7.65 us
    pallas_call x6, Pallas kernels: 18.3 us -> 15.6 us  [the longest x2 5.4 us: middle(): call(kernel, [V] * 7 + [held] * 2 + [V] * 4, (sends(faces), sends(faces),...]
    ppermute x5, starting transfers between devices: 8.18 us -> 9.39 us  [reduce_over_shots(): hop = lambda v, to: lax.ppermute(v, 'shot', [(i, to(i)) for i in range(16)])]
    add x1, other arithmetic: 0.02 us -> 0.96 us  [reduce_over_shots(): x = (keep + hop(send, lambda i: i ^ 1)).reshape(4, 2, 16, 384)]
    ppermute x8, waiting for transfers between devices: 4.82 us -> 5.75 us  [passed_along(): return lax.ppermute(value, axis, pairs)]
    add x1, other arithmetic: 0.01 us -> 0.87 us  [reduce_over_shots(): total = total + hop(pick(x, (line + d) % 4, 0), lambda i: (i + 4 * d) % 16)]
    pallas_call x1, Pallas kernels: 2.09 us -> 1.4 us  [body(): call(adjoint_start_kernel, [V] * 4, (sends(6), sends(6), field(3), field(...]
  transfers between devices with their start and end apart: 13 -> 13, of which waited for: 5 -> 4; matrix products, arithmetic and copies ran while one was open for 0% -> 1% of each run, Pallas kernels for 23% -> 20%
where the time goes in v3:
time: 62.5 us; the launch traced here: 62.1 us
  starting transfers between devices  26.5 us (42%)
  Pallas kernels  17 us (27%)
  local copies, waits for them, and re-layouts  7.82 us (13%)
  waiting for transfers between devices  7.54 us (12%)
  other arithmetic  1.84 us (3%)
  between operations  1.42 us (2%)
    ppermute x8, starting transfers between devices, passed_along(): return lax.ppermute(value, axis, pairs)  17.1 us
    ppermute x5, starting transfers between devices, reduce_over_shots(): hop = lambda v, to: lax.ppermute(v, 'shot', [(i, to(i)) for i in range(16)])  9.39 us
    unnamed x27, local copies, waits for them, and re-layouts  7.65 us
    ppermute x8, waiting for transfers between devices, passed_along(): return lax.ppermute(value, axis, pairs)  5.75 us
    pallas_call x2, Pallas kernels, middle(): call(kernel, [V] * 7 + [held] * 2 + [V] * 4, (sends(faces), sends(faces),...  5.4 us
    pallas_call x1, Pallas kernels, body(): call(last_kernel, [V] * 13, shape(1125, 2, 128), [scr(field(3)), scr(fiel...  3.01 us
    pallas_call x1, Pallas kernels, body(): call(first_image_kernel, [V] * 7, (shape(2, 384, 128), field(9), field(3)...  2.72 us
    pallas_call x1, Pallas kernels, body(): call(last_image_kernel, [V] * 6 + [S] * 2 + [V] * 2, (shape(8, 16, 384),...  2.47 us
  transfers between devices with their start and end apart: 13, of which 4 were waited for; matrix products, arithmetic and copies ran while one was open for 1% of the time, Pallas kernels for 20%

profile of v3, /device:TPU:0, one launch (start us, length us, event | category | flops | bytes accessed | tf_op | source)
XLA Modules:
  0.0 62.1 jit_solution(9330780664494799577)
XLA Ops:
  0.6 1.0 %copy-done = f32[3,5,5,5,256]{4,0,3,2,1:T(4,128)S(1)} copy-done((f32[3,5,5,5,256]{4,0,3,2,1:T(4,128)S(1)}, f32[3,5,5,5,256]{4,0,3,2,1:T(4,128)}, u32[]{:S(2)}) %copy-start) | copy-done | bytes 384024
  1.7 1.3 %copy-done.2 = f32[1,9,5,5,5,256]{5,0,4,3,2,1:T(1,128)S(1)} copy-done((f32[1,9,5,5,5,256]{5,0,4,3,2,1:T(1,128)S(1)}, f32[1,9,5,5,5,256]{5,0,4,3,2,1:T(1,128)}, u32[]{:S(2)}) %copy-start.2) | copy-done | bytes 1152024
  2.9 0.7 %copy-done.7 = s32[256,4]{0,1:T(4,128)S(1)} copy-done((s32[256,4]{0,1:T(4,128)S(1)}, s32[256,4]{0,1:T(4,128)}, u32[]{:S(2)}) %copy-start.7) | copy-done | bytes 4120
  3.6 2.0 %shard_map.95 = (f32[175,2,128]{2,1,0:T(2,128)S(1)}, f32[175,2,128]{2,1,0:T(2,128)S(1)}, f32[2,3,5,5,8,128]{5,4,3,2,1,0:T(8,128)S(1)}, f32[2,3,5,5,8,128]{5,4,3,...) custom-call(f32[1125,2,128]{2,1,0:T(2,128)S(1)} %bitcast.32, ...), custom_call_target="tpu_custom_call" | custom-call | flops 100000000 | bytes 4000000 | tf_op jit(solution)/shard_map/pallas_call | solution.py:521
  5.6 2.1 %collective-permute-start = (f32[175,2,128]{2,1,0:T(2,128)S(1)}, f32[175,2,128]{2,1,0:T(2,128)S(1)}, u32[]{:S(2)}, u32[]{:S(2)}) collective-permute-start(f32[175,2,128]{2,1,0:T(2,128)S(1)} %get-tuple-element.38), channel_id=1, source_target_pairs={{0,16},{16,32},{32,48},{48,64},{64,80},{80,96},{96,112},{112,0},{1... | collective-permute-start | bytes 537608 | tf_op jit(solution)/shard_map/ppermute | solution.py:495
  7.7 2.5 %collective-permute-start.1 = (f32[175,2,128]{2,1,0:T(2,128)S(1)}, f32[175,2,128]{2,1,0:T(2,128)S(1)}, u32[]{:S(2)}, u32[]{:S(2)}) collective-permute-start(f32[175,2,128]{2,1,0:T(2,128)S(1)} %get-tuple-element.39), channel_id=1, source_target_pairs={{0,112},{16,0},{32,16},{48,32},{64,48},{80,64},{96,80},{112,96},{1... | collective-permute-start | bytes 537608 | tf_op jit(solution)/shard_map/ppermute | solution.py:495
  10.2 1.4 %shard_map.96 = (f32[150,2,128]{2,1,0:T(2,128)S(1)}, f32[150,2,128]{2,1,0:T(2,128)S(1)}, f32[2,3,5,5,8,128]{5,4,3,2,1,0:T(8,128)S(1)}, f32[2,3,5,5,8,128]{5,4,3,...) custom-call(f32[1125,2,128]{2,1,0:T(2,128)S(1)} %bitcast.33, ...), custom_call_target="tpu_custom_call" | custom-call | flops 100000000 | bytes 4000000 | tf_op jit(solution)/shard_map/pallas_call | solution.py:529
  11.7 4.1 %collective-permute-start.3 = (f32[150,2,128]{2,1,0:T(2,128)S(1)}, f32[150,2,128]{2,1,0:T(2,128)S(1)}, u32[]{:S(2)}, u32[]{:S(2)}) collective-permute-start(f32[150,2,128]{2,1,0:T(2,128)S(1)} %get-tuple-element.46), channel_id=1, source_target_pairs={{0,112},{16,0},{32,16},{48,32},{64,48},{80,64},{96,80},{112,96},{1... | collective-permute-start | bytes 460808 | tf_op jit(solution)/shard_map/ppermute | solution.py:495
  16.5 3.3 %collective-permute-done.refs_9_.refs_11_.r_below = f32[175,2,128]{2,1,0:T(2,128)S(1)} collective-permute-done((f32[175,2,128]{2,1,0:T(2,128)S(1)}, f32[175,2,128]{2,1,0:T(2,128)S(1)}, u32[]{:S(2)}, u32[]{:S(2)}) %collective-permute-start) | collective-permute-done | bytes 179232 | tf_op jit(solution)/shard_map/ppermute | solution.py:495
  19.8 2.2 %collective-permute-done.1.refs_10_.refs_12_.r_above = f32[175,2,128]{2,1,0:T(2,128)S(1)} collective-permute-done((f32[175,2,128]{2,1,0:T(2,128)S(1)}, f32[175,2,128]{2,1,0:T(2,128)S(1)}, u32[]{:S(2)}, u32[]{:S(2)}) %collective-permute-start.1) | collective-permute-done | bytes 179232 | tf_op jit(solution)/shard_map/ppermute | solution.py:495
  22.0 2.0 %shard_map.97 = (f32[75,2,128]{2,1,0:T(2,128)S(1)}, f32[75,2,128]{2,1,0:T(2,128)S(1)}, f32[2,3,5,5,8,128]{5,4,3,2,1,0:T(8,128)S(1)}, f32[2,6,5,5,8,128]{5,4,3,2,1,0:T(8,128)S(1)}, f32[2,3,5,5,8,128]{5,4,3,2,1,0:T(8,128)S(1)}) custom-call(f32[2,3,5,5,8,128]{5,4,3,2,1,0:T(8,128)S(1)} %get-tuple-element.31.refs_0_, ...), custom_call_target="tpu_custom_call" | custom-call | flops 200000000 | bytes 8000000 | tf_op jit(solution)/shard_map/pallas_call | solution.py:542
  23.9 0.4 collective-permute-start.4
  24.3 3.8 %collective-permute-start.5 = (f32[75,2,128]{2,1,0:T(2,128)S(1)}, f32[75,2,128]{2,1,0:T(2,128)S(1)}, u32[]{:S(2)}, u32[]{:S(2)}) collective-permute-start(f32[75,2,128]{2,1,0:T(2,128)S(1)} %get-tuple-element.53), channel_id=1, source_target_pairs={{0,112},{16,0},{32,16},{48,32},{64,48},{80,64},{96,80},{112,96},{1... | collective-permute-start | bytes 230408 | tf_op jit(solution)/shard_map/ppermute | solution.py:495
  28.2 3.4 %shard_map.98 = (f32[150,2,128]{2,1,0:T(2,128)S(1)}, f32[150,2,128]{2,1,0:T(2,128)S(1)}, f32[2,3,5,5,8,128]{5,4,3,2,1,0:T(8,128)S(1)}, f32[2,6,5,5,8,128]{5,4,3,...) custom-call(f32[2,3,5,5,8,128]{5,4,3,2,1,0:T(8,128)S(1)} %get-tuple-element.41.refs_0_.adj_vel_en, ...), custom_call_target="tpu_custom_call" | custom-call | flops 200000000 | bytes 8000000 | tf_op jit(solution)/shard_map/pallas_call | solution.py:542
  31.6 0.8 %copy-done.4 = f32[2,3,5,5,8,128]{5,4,3,2,1,0:T(8,128)} copy-done((f32[2,3,5,5,8,128]{5,4,3,2,1,0:T(8,128)}, f32[2,3,5,5,8,128]{5,4,3,2,1,0:T(8,128)S(1)}, u32[]{:S(2)}) %copy-start.4) | copy-done | bytes 614424
  32.4 0.7 %copy-done.10 = f32[150,2,128]{2,1,0:T(2,128)} copy-done((f32[150,2,128]{2,1,0:T(2,128)}, f32[150,2,128]{2,1,0:T(2,128)S(1)}, u32[]{:S(2)}) %copy-start.10) | copy-done | bytes 153624
  33.1 0.7 %copy-done.11 = f32[150,2,128]{2,1,0:T(2,128)} copy-done((f32[150,2,128]{2,1,0:T(2,128)}, f32[150,2,128]{2,1,0:T(2,128)S(1)}, u32[]{:S(2)}) %copy-start.11) | copy-done | bytes 153624
  33.7 2.7 %shard_map.99 = (f32[2,384,128]{2,1,0:T(8,128)S(1)}, f32[2,9,5,5,8,128]{5,4,3,2,1,0:T(8,128)S(1)}, f32[2,3,5,5,8,128]{5,4,3,2,1,0:T(8,128)S(1)}) custom-call(f32[2,3,5,5,8,128]{5,4,3,2,1,0:T(8,128)S(1)} %get-tuple-element.41.refs_0_.adj_vel_end.adj_vel, f32[2,3,5,5,8,128]{5,4,3,2,1,0:T(8,128)S(1)} %get-tuple-element.40.f_vel, ...), custom_call_target="tpu_custom_call" | custom-call | flops 1000 | bytes 1000 | tf_op jit(solution)/shard_map/pallas_call | solution.py:558
  36.5 2.5 %shard_map.100 = (f32[8,16,384]{2,1,0:T(8,128)S(1)}, f32[8,16,384]{2,1,0:T(8,128)}) custom-call(f32[2,3,5,5,8,128]{5,4,3,2,1,0:T(8,128)S(1)} %get-tuple-element.40.f_vel, f32[2,3,5,5,8,128]{5,4,3,2,1,0:T(8,128)S(1)} %get-tuple-element.49.acc_in, f32[2,3,5,5,8,128]{5,4,3,2,1,0:T(8,128)S(1)} %get-tuple-element.41.refs_0_.adj_vel_end.adj_vel, ...), custom_call_target="tpu_custom_call" | custom-call | flops 1000 | bytes 1000 | tf_op jit(solution)/shard_map/pallas_call | solution.py:565
  39.0 1.8 %collective-permute-done.6 = f32[8,16,384]{2,1,0:T(8,128)} collective-permute-done((f32[8,16,384]{2,1,0:T(8,128)}, f32[8,16,384]{2,1,0:T(8,128)}, u32[]{:S(2)}, u32[]{:S(2)}) %collective-permute-start.6) | collective-permute-done | bytes 196640 | tf_op jit(solution)/shard_map/ppermute | solution.py:506
  40.8 1.0 %add.60 = f32[8,16,384]{2,1,0:T(8,128)S(1)} add(f32[8,16,384]{2,1,0:T(8,128)S(1)} %get-tuple-element.54, f32[8,16,384]{2,1,0:T(8,128)} %collective-permute-done.6) | non-fusion elementwise | flops 49152 | bytes 589824 | tf_op jit(solution)/shard_map/add | solution.py:507
  41.7 0.7 %copy-done.12 = f32[8,16,384]{2,1,0:T(8,128)} copy-done((f32[8,16,384]{2,1,0:T(8,128)}, f32[8,16,384]{2,1,0:T(8,128)S(1)}, u32[]{:S(2)}) %copy-start.12) | copy-done | bytes 196632
  42.4 1.6 %collective-permute-start.7 = (f32[2,16,384]{2,1,0:T(8,128)S(1)}, f32[2,16,384]{2,1,0:T(8,128)S(1)}, u32[]{:S(2)}, u32[]{:S(2)}) collective-permute-start(f32[2,16,384]{2,1,0:T(8,128)S(1)} %get-tuple-element.68), channel_id=1, source_target_pairs={{0,4},{1,5},{2,6},{3,7},{4,8},{5,9},{6,10},{7,11},{8,12},{9,13},{1... | collective-permute-start | bytes 147464 | tf_op jit(solution)/shard_map/ppermute | solution.py:506
  44.0 2.7 %collective-permute-start.8 = (f32[2,16,384]{2,1,0:T(8,128)S(1)}, f32[2,16,384]{2,1,0:T(8,128)}, u32[]{:S(2)}, u32[]{:S(2)}) collective-permute-start(f32[2,16,384]{2,1,0:T(8,128)S(1)} %get-tuple-element.70), channel_id=1, source_target_pairs={{0,8},{1,9},{2,10},{3,11},{4,12},{5,13},{6,14},{7,15},{8,0},{9,1},... | collective-permute-start | bytes 147464 | tf_op jit(solution)/shard_map/ppermute | solution.py:506
  46.7 1.4 %collective-permute-start.9 = (f32[2,16,384]{2,1,0:T(8,128)S(1)}, f32[2,16,384]{2,1,0:T(8,128)}, u32[]{:S(2)}, u32[]{:S(2)}) collective-permute-start(f32[2,16,384]{2,1,0:T(8,128)S(1)} %get-tuple-element.69), channel_id=1, source_target_pairs={{0,12},{1,13},{2,14},{3,15},{4,0},{5,1},{6,2},{7,3},{8,4},{9,5},{1... | collective-permute-start | bytes 147464 | tf_op jit(solution)/shard_map/ppermute | solution.py:506
  48.1 4.1 %collective-permute-start.12 = (f32[150,2,128]{2,1,0:T(2,128)}, f32[150,2,128]{2,1,0:T(2,128)S(1)}, u32[]{:S(2)}, u32[]{:S(2)}) collective-permute-start(f32[150,2,128]{2,1,0:T(2,128)} %copy-done.10), channel_id=1, source_target_pairs={{0,112},{16,0},{32,16},{48,32},{64,48},{80,64},{96,80},{112,96},{1... | collective-permute-start | bytes 460808 | tf_op jit(solution)/shard_map/ppermute | solution.py:495
  52.3 0.9 %fusion.1 = f32[2,16,384]{2,1,0:T(8,128)S(1)} fusion(f32[2,16,384]{2,1,0:T(8,128)} %collective-permute-done.9, f32[2,16,384]{2,1,0:T(8,128)} %collective-permute-done.8, f32[2,16,384]{2,1,0:T(8,128)S(1)} %collective-permute-done.7, f32[4,2,16,384]{3,2,1,0:T(8,128)} %bitcast.41, s32[]{:T(128)S(6)} %select_n.47), kind=kLoop, calls=%fused_computation.2 | loop fusion | flops 36864 | bytes 245764 | tf_op jit(solution)/shard_map/add | solution.py:510
  53.2 3.7 %collective-permute-start.10 = (f32[16,384]{1,0:T(8,128)S(1)}, f32[16,384]{1,0:T(8,128)S(1)}, u32[]{:S(2)}, u32[]{:S(2)}) collective-permute-start(f32[16,384]{1,0:T(8,128)S(1)} %get-tuple-element.72), channel_id=1, source_target_pairs={{0,2},{1,3},{2,0},{3,1},{4,6},{5,7},{6,4},{7,5},{8,10},{9,11},{10,... | collective-permute-start | bytes 73736 | tf_op jit(solution)/shard_map/ppermute | solution.py:506
  56.8 0.3 collective-permute-done.12.above
  57.1 1.1 %copy-done.5 = f32[2,3,5,5,8,128]{5,4,3,2,1,0:T(8,128)S(1)} copy-done((f32[2,3,5,5,8,128]{5,4,3,2,1,0:T(8,128)S(1)}, f32[2,3,5,5,8,128]{5,4,3,2,1,0:T(8,128)}, u32[]{:S(2)}) %copy-start.5) | copy-done | bytes 614424
  58.2 3.0 %shard_map.101 = f32[1125,2,128]{2,1,0:T(2,128)} custom-call(f32[2,3,5,5,8,128]{5,4,3,2,1,0:T(8,128)S(1)} %get-tuple-element.47.a_vel.vel_in, f32[2,6,5,5,8,128]{5,4,3,2,1,0:T(8,128)S(1)} %get-tuple-element.56.stress_in, f32[2,3,5,5,8,128]{5,4,3,2,1,0:T(8,128)S(1)} %copy-done.5, f32[2,5,5,8,128]{4,3,2,1,0:T(8,128)S(1)} %get-tuple-element.36.refs_3_.lam, ...), custom_call_target="tpu_custom_call" | custom-call | flops 100000000 | bytes 8000000 | tf_op jit(solution)/shard_map/pallas_call | solution.py:573
  61.4 0.8 %copy.16 = f32[3,5,5,5,16]{4,0,3,2,1:T(4,128)} copy(f32[3,5,5,5,16]{4,3,2,1,0:T(8,128)S(1)} %reshape.34) | data formatting | bytes 48000
  (35 shorter events, 0.3 us)
Async XLA Ops:
  0.6 1.0 %copy-start = (f32[3,5,5,5,256]{4,0,3,2,1:T(4,128)S(1)}, f32[3,5,5,5,256]{4,0,3,2,1:T(4,128)}, u32[]{:S(2)}) copy-start(f32[3,5,5,5,256]{4,0,3,2,1:T(4,128)} %param.10) | copy-start | bytes 1152004
  1.7 1.3 %copy-start.2 = (f32[1,9,5,5,5,256]{5,0,4,3,2,1:T(1,128)S(1)}, f32[1,9,5,5,5,256]{5,0,4,3,2,1:T(1,128)}, u32[]{:S(2)}) copy-start(f32[1,9,5,5,5,256]{5,0,4,3,2,1:T(1,128)} %param.8) | copy-start | bytes 3456004
  2.9 0.7 %copy-start.7 = (s32[256,4]{0,1:T(4,128)S(1)}, s32[256,4]{0,1:T(4,128)}, u32[]{:S(2)}) copy-start(s32[256,4]{0,1:T(4,128)} %param.11) | copy-start | bytes 12292
  3.6 6.6 %copy-start.1 = (f32[3,5,5,5,256]{4,0,3,2,1:T(4,128)S(1)}, f32[3,5,5,5,256]{4,0,3,2,1:T(4,128)}, u32[]{:S(2)}) copy-start(f32[3,5,5,5,256]{4,0,3,2,1:T(4,128)} %param.10) | copy-start | bytes 1152004
  3.6 6.6 %copy-start.3 = (f32[1,9,5,5,5,256]{5,0,4,3,2,1:T(1,128)S(1)}, f32[1,9,5,5,5,256]{5,0,4,3,2,1:T(1,128)}, u32[]{:S(2)}) copy-start(f32[1,9,5,5,5,256]{5,0,4,3,2,1:T(1,128)} %param.9) | copy-start | bytes 3456004
  5.6 16.3 %copy-start.8 = (f32[1,2,3]{2,1,0:T(2,128)S(1)}, f32[1,2,3]{2,1,0:T(2,128)}, u32[]{:S(2)}) copy-start(f32[1,2,3]{2,1,0:T(2,128)} %strength.1) | copy-start | bytes 76
  5.6 14.1 %collective-permute-start = (f32[175,2,128]{2,1,0:T(2,128)S(1)}, f32[175,2,128]{2,1,0:T(2,128)S(1)}, u32[]{:S(2)}, u32[]{:S(2)}) collective-permute-start(f32[175,2,128]{2,1,0:T(2,128)S(1)} %get-tuple-element.38), channel_id=1, source_target_pairs={{0,16},{16,32},{32,48},{48,64},{64,80},{80,96},{96,112},{112,0},{1... | collective-permute-start | bytes 537608 | tf_op jit(solution)/shard_map/ppermute | solution.py:495
  7.7 14.3 %collective-permute-start.1 = (f32[175,2,128]{2,1,0:T(2,128)S(1)}, f32[175,2,128]{2,1,0:T(2,128)S(1)}, u32[]{:S(2)}, u32[]{:S(2)}) collective-permute-start(f32[175,2,128]{2,1,0:T(2,128)S(1)} %get-tuple-element.39), channel_id=1, source_target_pairs={{0,112},{16,0},{32,16},{48,32},{64,48},{80,64},{96,80},{112,96},{1... | collective-permute-start | bytes 537608 | tf_op jit(solution)/shard_map/ppermute | solution.py:495
  11.6 16.5 %collective-permute-start.2 = (f32[150,2,128]{2,1,0:T(2,128)S(1)}, f32[150,2,128]{2,1,0:T(2,128)S(1)}, u32[]{:S(2)}, u32[]{:S(2)}) collective-permute-start(f32[150,2,128]{2,1,0:T(2,128)S(1)} %get-tuple-element.45), channel_id=1, source_target_pairs={{0,16},{16,32},{32,48},{48,64},{64,80},{80,96},{96,112},{112,0},{1... | collective-permute-start | bytes 460808 | tf_op jit(solution)/shard_map/ppermute | solution.py:495
  11.7 16.4 %collective-permute-start.3 = (f32[150,2,128]{2,1,0:T(2,128)S(1)}, f32[150,2,128]{2,1,0:T(2,128)S(1)}, u32[]{:S(2)}, u32[]{:S(2)}) collective-permute-start(f32[150,2,128]{2,1,0:T(2,128)S(1)} %get-tuple-element.46), channel_id=1, source_target_pairs={{0,112},{16,0},{32,16},{48,32},{64,48},{80,64},{96,80},{112,96},{1... | collective-permute-start | bytes 460808 | tf_op jit(solution)/shard_map/ppermute | solution.py:495
  22.0 6.2 %copy-start.6 = (f32[1,2,3,256]{3,1,2,0:T(2,128)S(1)}, f32[1,2,3,256]{3,1,2,0:T(2,128)}, u32[]{:S(2)}) copy-start(f32[1,2,3,256]{3,1,2,0:T(2,128)} %param.15) | copy-start | bytes 18436
  22.0 6.2 %copy-start.9 = (s32[256]{0:T(256)S(1)}, s32[256]{0:T(256)}, u32[]{:S(2)}) copy-start(s32[256]{0:T(256)} %param.14) | copy-start | bytes 3076
  23.9 12.6 %collective-permute-start.4 = (f32[75,2,128]{2,1,0:T(2,128)S(1)}, f32[75,2,128]{2,1,0:T(2,128)S(1)}, u32[]{:S(2)}, u32[]{:S(2)}) collective-permute-start(f32[75,2,128]{2,1,0:T(2,128)S(1)} %get-tuple-element.52), channel_id=1, source_target_pairs={{0,16},{16,32},{32,48},{48,64},{64,80},{80,96},{96,112},{112,0},{1... | collective-permute-start | bytes 230408 | tf_op jit(solution)/shard_map/ppermute | solution.py:495
  24.3 12.2 %collective-permute-start.5 = (f32[75,2,128]{2,1,0:T(2,128)S(1)}, f32[75,2,128]{2,1,0:T(2,128)S(1)}, u32[]{:S(2)}, u32[]{:S(2)}) collective-permute-start(f32[75,2,128]{2,1,0:T(2,128)S(1)} %get-tuple-element.53), channel_id=1, source_target_pairs={{0,112},{16,0},{32,16},{48,32},{64,48},{80,64},{96,80},{112,96},{1... | collective-permute-start | bytes 230408 | tf_op jit(solution)/shard_map/ppermute | solution.py:495
  31.6 0.8 %copy-start.4 = (f32[2,3,5,5,8,128]{5,4,3,2,1,0:T(8,128)}, f32[2,3,5,5,8,128]{5,4,3,2,1,0:T(8,128)S(1)}, u32[]{:S(2)}) copy-start(f32[2,3,5,5,8,128]{5,4,3,2,1,0:T(8,128)S(1)} %get-tuple-element.57.acc_in) | copy-start | bytes 1843204
  32.4 0.7 %copy-start.10 = (f32[150,2,128]{2,1,0:T(2,128)}, f32[150,2,128]{2,1,0:T(2,128)S(1)}, u32[]{:S(2)}) copy-start(f32[150,2,128]{2,1,0:T(2,128)S(1)} %get-tuple-element.59) | copy-start | bytes 460804
  33.1 0.7 %copy-start.11 = (f32[150,2,128]{2,1,0:T(2,128)}, f32[150,2,128]{2,1,0:T(2,128)S(1)}, u32[]{:S(2)}) copy-start(f32[150,2,128]{2,1,0:T(2,128)S(1)} %get-tuple-element.58) | copy-start | bytes 460804
  39.0 1.8 %collective-permute-start.6 = (f32[8,16,384]{2,1,0:T(8,128)}, f32[8,16,384]{2,1,0:T(8,128)}, u32[]{:S(2)}, u32[]{:S(2)}) collective-permute-start(f32[8,16,384]{2,1,0:T(8,128)} %get-tuple-element.55), channel_id=1, source_target_pairs={{0,1},{1,0},{2,3},{3,2},{4,5},{5,4},{6,7},{7,6},{8,9},{9,8},{10,11... | collective-permute-start | bytes 589832 | tf_op jit(solution)/shard_map/ppermute | solution.py:506
  41.7 0.7 %copy-start.12 = (f32[8,16,384]{2,1,0:T(8,128)}, f32[8,16,384]{2,1,0:T(8,128)S(1)}, u32[]{:S(2)}) copy-start(f32[8,16,384]{2,1,0:T(8,128)S(1)} %add.60) | copy-start | bytes 589828
  42.4 9.9 %collective-permute-start.7 = (f32[2,16,384]{2,1,0:T(8,128)S(1)}, f32[2,16,384]{2,1,0:T(8,128)S(1)}, u32[]{:S(2)}, u32[]{:S(2)}) collective-permute-start(f32[2,16,384]{2,1,0:T(8,128)S(1)} %get-tuple-element.68), channel_id=1, source_target_pairs={{0,4},{1,5},{2,6},{3,7},{4,8},{5,9},{6,10},{7,11},{8,12},{9,13},{1... | collective-permute-start | bytes 147464 | tf_op jit(solution)/shard_map/ppermute | solution.py:506
  44.0 8.3 %collective-permute-start.8 = (f32[2,16,384]{2,1,0:T(8,128)S(1)}, f32[2,16,384]{2,1,0:T(8,128)}, u32[]{:S(2)}, u32[]{:S(2)}) collective-permute-start(f32[2,16,384]{2,1,0:T(8,128)S(1)} %get-tuple-element.70), channel_id=1, source_target_pairs={{0,8},{1,9},{2,10},{3,11},{4,12},{5,13},{6,14},{7,15},{8,0},{9,1},... | collective-permute-start | bytes 147464 | tf_op jit(solution)/shard_map/ppermute | solution.py:506
  46.7 5.6 %collective-permute-start.9 = (f32[2,16,384]{2,1,0:T(8,128)S(1)}, f32[2,16,384]{2,1,0:T(8,128)}, u32[]{:S(2)}, u32[]{:S(2)}) collective-permute-start(f32[2,16,384]{2,1,0:T(8,128)S(1)} %get-tuple-element.69), channel_id=1, source_target_pairs={{0,12},{1,13},{2,14},{3,15},{4,0},{5,1},{6,2},{7,3},{8,4},{9,5},{1... | collective-permute-start | bytes 147464 | tf_op jit(solution)/shard_map/ppermute | solution.py:506
  48.1 8.7 %collective-permute-start.11 = (f32[150,2,128]{2,1,0:T(2,128)}, f32[150,2,128]{2,1,0:T(2,128)S(1)}, u32[]{:S(2)}, u32[]{:S(2)}) collective-permute-start(f32[150,2,128]{2,1,0:T(2,128)} %copy-done.11), channel_id=1, source_target_pairs={{0,16},{16,32},{32,48},{48,64},{64,80},{80,96},{96,112},{112,0},{1... | collective-permute-start | bytes 460808 | tf_op jit(solution)/shard_map/ppermute | solution.py:495
  48.1 9.0 %collective-permute-start.12 = (f32[150,2,128]{2,1,0:T(2,128)}, f32[150,2,128]{2,1,0:T(2,128)S(1)}, u32[]{:S(2)}, u32[]{:S(2)}) collective-permute-start(f32[150,2,128]{2,1,0:T(2,128)} %copy-done.10), channel_id=1, source_target_pairs={{0,112},{16,0},{32,16},{48,32},{64,48},{80,64},{96,80},{112,96},{1... | collective-permute-start | bytes 460808 | tf_op jit(solution)/shard_map/ppermute | solution.py:495
  53.2 8.0 %collective-permute-start.10 = (f32[16,384]{1,0:T(8,128)S(1)}, f32[16,384]{1,0:T(8,128)S(1)}, u32[]{:S(2)}, u32[]{:S(2)}) collective-permute-start(f32[16,384]{1,0:T(8,128)S(1)} %get-tuple-element.72), channel_id=1, source_target_pairs={{0,2},{1,3},{2,0},{3,1},{4,6},{5,7},{6,4},{7,5},{8,10},{9,11},{10,... | collective-permute-start | bytes 73736 | tf_op jit(solution)/shard_map/ppermute | solution.py:506
  57.1 1.1 %copy-start.5 = (f32[2,3,5,5,8,128]{5,4,3,2,1,0:T(8,128)S(1)}, f32[2,3,5,5,8,128]{5,4,3,2,1,0:T(8,128)}, u32[]{:S(2)}) copy-start(f32[2,3,5,5,8,128]{5,4,3,2,1,0:T(8,128)} %copy-done.4) | copy-start | bytes 1843204

commit v4 on v3

--- a/solution.py
+++ b/solution.py
@@ -201,21 +201,24 @@
                 halo[1, h, 3 + i] = halo[1, h, 3 + i] - halo[1, h, 6] * stress[h, k, 4]
 
 
-def inject_rows(kind, step, where_ref, strength, base):
-    if kind == "source":
-        lane = lax.broadcasted_iota(jnp.int32, (1, N), 1) + base
-        hit = lane == where_ref[0]
-        return [jnp.where(hit, strength[0, step, i], 0.0) for i in range(3)]
-    element = lax.broadcasted_iota(jnp.int32, (N, N), 0) + base
+def source_rows(step, where_ref, pulse):
+    lane = lax.broadcasted_iota(jnp.int32, (1, N), 1) + slab_base()
+    hit = lane == where_ref[0]
+    return [jnp.where(hit, pulse[0, step, i], 0.0) for i in range(3)]
+
+
+def receiver_rows(where_ref, residual):
+    element = lax.broadcasted_iota(jnp.int32, (N, N), 0) + slab_base()
     hits = jnp.where(element == where_ref[...], 1.0, 0.0).astype(bf16)
-    x = jnp.concatenate([strength[i, step : step + 1] for i in range(3)] + [jnp.zeros((13, N), f32)], axis=0)
+    spare = jnp.zeros((5, N), f32)
+    x = jnp.concatenate([r for step in range(2) for r in [residual[i, step : step + 1] for i in range(3)] + [spare]], axis=0)
     total = None
     for part in range(3):
         high = x.astype(bf16)
         x = x - high.astype(f32)
         term = lax.dot_general(high, hits, (((1,), (1,)), ((), ())), preferred_element_type=f32)
         total = term if total is None else total + term
-    return [total[i : i + 1] for i in range(3)]
+    return total
 
 
 def slab_base():
@@ -363,32 +366,34 @@
     start_common(state, rinv, perms, acc, vel, stress, up, down, yj, zj, True)
 
 
-def adjoint_start_kernel(state, mat, rinv, perms, up, down, acc, vel, stress, lam, mu, yj, zj):
+def adjoint_start_kernel(state, mat, rinv, perms, receivers, residuals, up, down, acc, vel, stress, lam, mu,
+                         end_grads, injected, yj, zj):
     zj[...] = jnp.zeros(zj.shape, f32)
+    injected[...] = receiver_rows(receivers, residuals)
     start_common(state, rinv, perms, acc, vel, stress, up, down, yj, zj, False)
     for k, dst in ((0, lam), (1, mu)):
         load_material(mat, k, dst)
         for h in range(2):
             for a in range(5):
                 dst[h, a] = time_step * dst[h, a]
-
-
-def finish_step(kind, step, base, vel_in, stress_in, lam, mu, rinv, perms, where_ref, strength,
-                vel, stress, acc, halo, grads, yj, zj):
+    plain_gradients(vel, end_grads)
+
+
+def finish_step(rows, vel_in, stress_in, lam, mu, rinv, perms, vel, stress, acc, halo, grads, yj, zj):
     finish_acceleration(acc, stress_in, rinv, halo, True)
-    velocities(vel_in, vel, acc, inject_rows(kind, step, where_ref, strength, base))
+    velocities(vel_in, vel, acc, rows)
     jump_gradients(vel, halo, grads, perms, yj, zj)
     update_stress(stress_in, stress, grads, lam, mu)
 
 
-def middle_kernel(kind, vel_in, stress_in, acc_in, lam, mu, rinv, perms, where_ref, strength,
+def middle_kernel(kind, vel_in, stress_in, acc_in, lam, mu, rinv, perms, inject,
                   below, above, r_below, r_above, up, down, vel, stress, acc, *rest):
     next_acc, (halo, grads, yj, zj) = (rest[0], rest[1:]) if kind == "receiver" else (None, rest)
+    rows = [inject[i : i + 1] for i in range(3)] if kind == "receiver" else source_rows(0, *inject)
     zj[...] = jnp.zeros(zj.shape, f32)
     load_halo(halo, *(flat(r, r.shape[0] * 2) for r in (below, above, r_below, r_above)), 6)
     acc[...] = acc_in[...]
-    finish_step(kind, 0, slab_base(), vel_in, stress_in, lam, mu, rinv, perms, where_ref, strength,
-                vel, stress, acc, halo, grads, yj, zj)
+    finish_step(rows, vel_in, stress_in, lam, mu, rinv, perms, vel, stress, acc, halo, grads, yj, zj)
     if kind == "receiver":
         local_acceleration(stress, rinv, next_acc, perms, yj, zj)
     for dst, a in ((up, 4), (down, 0)):
@@ -400,13 +405,13 @@
                     pack_face(dst, 3 + i, vel[h, i, a] + time_step * next_acc[h, i, a], h)
 
 
-def last_kernel(vel_in, stress_in, acc_in, lam, mu, rinv, perms, where_ref, strength,
+def last_kernel(vel_in, stress_in, acc_in, lam, mu, rinv, perms, inject,
                 below, above, r_below, r_above, out, vel, stress, acc, halo, grads, yj, zj):
     zj[...] = jnp.zeros(zj.shape, f32)
     load_halo(halo, *(flat(r, r.shape[0] * 2) for r in (below, above, r_below, r_above)), 6)
     acc[...] = acc_in[...]
-    finish_step("receiver", 1, slab_base(), vel_in, stress_in, lam, mu, rinv, perms, where_ref, strength,
-                vel, stress, acc, halo, grads, yj, zj)
+    rows = [inject[8 + i : 9 + i] for i in range(3)]
+    finish_step(rows, vel_in, stress_in, lam, mu, rinv, perms, vel, stress, acc, halo, grads, yj, zj)
     dst = flat(out, 2250)
     for first, field, count in ((0, vel, 3), (3, stress, 6)):
 
@@ -419,13 +424,12 @@
         lax.fori_loop(0, count, one, 0)
 
 
-def first_image_kernel(adj_vel_end, f_vel, f_acc, a_vel, f_stress, rinv, perms, dense, end_grads, next_acc, fg, ag, yj, zj):
+def first_image_kernel(f_vel, f_acc, a_vel, f_stress, rinv, perms, dense, next_acc, fg, ag, yj, zj):
     zj[...] = jnp.zeros(zj.shape, f32)
     local_acceleration(f_stress, rinv, next_acc, perms, yj, zj)
     plain_gradients(f_vel, fg)
     plain_gradients(a_vel, ag)
     image(fg, ag, f_acc, a_vel, dense, None)
-    plain_gradients(adj_vel_end, end_grads)
 
 
 def last_image_kernel(f_vel, acc_in, adj_vel, end_grads, first, rinv, where_ref, strength, below, above,
@@ -433,7 +437,7 @@
     load_halo(halo, flat(below, 150), flat(above, 150), None, None, 3)
     acc[...] = acc_in[...]
     finish_acceleration(acc, None, rinv, halo, False)
-    velocities(f_vel, vel, acc, inject_rows("source", 1, where_ref, strength, slab_base()))
+    velocities(f_vel, vel, acc, source_rows(1, where_ref, strength))
     plain_gradients(vel, fg)
     for h in range(2):
         dense[h, 368:384, :] = jnp.zeros((16, 128), f32)
@@ -499,16 +503,33 @@
     return passed_along(up, "slab", 1), passed_along(down, "slab", -1)
 
 
+def core_sum_kernel(keep, got, mine, *others):
+    line = lax.div(lax.axis_index("shot"), 4)
+    for d, dst in enumerate((mine, *others)):
+        to = lax.rem(line + d, 4)
+        for high in range(2):
+            dst[high] = keep[2 * to + high] + got[2 * to + high]
+
+
+def line_sum_kernel(mine, one, two, three, keep, send):
+    high = lax.rem(lax.div(lax.axis_index("shot"), 2), 2)
+    for dst, k in ((keep, high), (send, 1 - high)):
+        dst[...] = (mine[k] + one[k]) + (two[k] + three[k])
+
+
+def last_sum_kernel(keep, got, out):
+    turned = (keep[...] + got[...]).T
+    for t in range(3):
+        out[:, t, :] = turned[125 * t : 125 * t + 125]
+
+
 def reduce_over_shots(keep, send):
-    place = lax.axis_index("shot")
-    high, line = (place // 2) % 2, place // 4
-    pick = lambda v, k, axis: lax.dynamic_index_in_dim(v, k, axis, False)
     hop = lambda v, to: lax.ppermute(v, "shot", [(i, to(i)) for i in range(16)])
-    x = (keep + hop(send, lambda i: i ^ 1)).reshape(4, 2, 16, 384)
-    total = pick(x, line, 0)
-    for d in (1, 2, 3):
-        total = total + hop(pick(x, (line + d) % 4, 0), lambda i: (i + 4 * d) % 16)
-    return pick(total, high, 0) + hop(pick(total, 1 - high, 0), lambda i: i ^ 2)
+    pair, chunk = shape(2, 16, 384), shape(16, 384)
+    mine, *others = call(core_sum_kernel, [V] * 2, (pair,) * 4, [], 1000, 1000)(keep, hop(send, lambda i: i ^ 1))
+    got = [hop(x, lambda i: (i + 4 * d) % 16) for d, x in enumerate(others, 1)]
+    keep, send = call(line_sum_kernel, [V] * 4, (chunk,) * 2, [], 1000, 1000)(mine, *got)
+    return call(last_sum_kernel, [V] * 2, shape(125, 3, 16), [], 1000, 1000)(keep, hop(send, lambda i: i ^ 2))
 
 
 def body(fwd, adj, materials, nbr, source_element, pulse, receivers, residuals):
@@ -524,44 +545,48 @@
         (sends(7), sends(7), field(3), field(3), field(6), ONE, PERMS),
         JUMPS + [scr(shape(1125, 2, 128)), scr(shape(125, 3, N)), pltpu.VMEM((4, N), jnp.int32), pltpu.SemaphoreType.DMA((3,))],
         10**8, 4 * 10**6,
-    )(fwd, mat, nbr)
+    )(*(pltpu.with_memory_space_constraint(x, pltpu.HBM) for x in (fwd, mat, nbr)))
     f_below, f_above = both_ways(f_up, f_down)
-    a_up, a_down, a_acc, a_vel, a_stress, lam, mu = call(
+    a_up, a_down, a_acc, a_vel, a_stress, lam, mu, end_grads, injected = call(
         adjoint_start_kernel,
-        [V] * 4,
-        (sends(6), sends(6), field(3), field(3), field(6), ONE, ONE),
+        [V] * 6,
+        (sends(6), sends(6), field(3), field(3), field(6), ONE, ONE, field(9), shape(16, N)),
         JUMPS,
         10**8, 4 * 10**6,
-    )(adj, mat, rinv, perms)
+    )(adj, mat, rinv, perms, receivers, residuals)
     a_below, a_above = both_ways(a_up, a_down)
     adj_vel_end = a_vel
 
-    def middle(kind, vel, stress, acc, where_ref, strength, below, above, faces):
-        kernel = lambda *refs: middle_kernel(kind, *refs)
-        held = S if kind == "source" else V
+    def middle(kind, vel, stress, acc, inject, below, above, faces):
+        if kind == "source":
+            kernel = lambda *refs: middle_kernel(kind, *refs[:7], refs[7:9], *refs[9:])
+            held = [S] * 2
+        else:
+            kernel = lambda *refs: middle_kernel(kind, *refs)
+            held = [V]
         return call(
             kernel,
-            [V] * 7 + [held] * 2 + [V] * 4,
+            [V] * 7 + held + [V] * 4,
             (sends(faces), sends(faces), field(3), field(6), field(3)) + (() if kind == "source" else (field(3),)),
             [HALO, scr(field(9))] + JUMPS,
             2 * 10**8, 8 * 10**6,
-        )(vel, stress, acc, lam, mu, rinv, perms, where_ref, strength, below, above, f_below, f_above)
+        )(vel, stress, acc, lam, mu, rinv, perms, *inject, below, above, f_below, f_above)
 
     f_up, f_down, f_vel1, f_stress1, f_acc1 = middle(
-        "source", f_vel, f_stress, f_acc, source_element, pulse, f_below, f_above, 3
+        "source", f_vel, f_stress, f_acc, (source_element, pulse), f_below, f_above, 3
     )
     f_below2, f_above2 = both_ways(f_up, f_down)
     a_up, a_down, a_vel1, a_stress1, _, a_acc2 = middle(
-        "receiver", a_vel, a_stress, a_acc, receivers, residuals, a_below, a_above, 6
+        "receiver", a_vel, a_stress, a_acc, (injected,), a_below, a_above, 6
     )
     a_below2, a_above2 = both_ways(a_up, a_down)
-    first, end_grads, f_acc2 = call(
+    first, f_acc2 = call(
         first_image_kernel,
-        [V] * 7,
-        (shape(2, 384, 128), field(9), field(3)),
+        [V] * 6,
+        (shape(2, 384, 128), field(3)),
         [scr(field(9)), scr(field(9))] + JUMPS,
         1000, 1000,
-    )(adj_vel_end, f_vel1, f_acc1, a_vel1, f_stress1, rinv, perms)
+    )(f_vel1, f_acc1, a_vel1, f_stress1, rinv, perms)
     keep, send = call(
         last_image_kernel,
         [V] * 6 + [S] * 2 + [V] * 2,
@@ -572,12 +597,12 @@
     gradient = reduce_over_shots(keep, send)
     adjoint_end = call(
         last_kernel,
-        [V] * 13,
+        [V] * 12,
         shape(1125, 2, 128),
         [scr(field(3)), scr(field(6)), scr(field(3)), HALO, scr(field(9))] + JUMPS,
         10**8, 8 * 10**6,
-    )(a_vel1, a_stress1, a_acc2, lam, mu, rinv, perms, receivers, residuals, a_below2, a_above2, f_below, f_above)
-    return gradient[:, :375].T.reshape(3, 5, 5, 5, 16), adjoint_end.reshape(1, 9, 5, 5, 5, N)
+    )(a_vel1, a_stress1, a_acc2, lam, mu, rinv, perms, injected, a_below2, a_above2, f_below, f_above)
+    return gradient.reshape(5, 5, 5, 3, 16).transpose(3, 0, 1, 2, 4), adjoint_end.reshape(1, 9, 5, 5, 5, N)
 
 
 def solution(mesh):

time: 62.5 us -> 53.1 us (0.85)
  local copies, waits for them, and re-layouts: 7.82 us -> 0.02 us
  other arithmetic: 1.84 us -> 0 us
    unnamed x27 -> x10, local copies, waits for them, and re-layouts: 7.65 us -> 0.02 us
    add x2 -> x0, other arithmetic: 1.83 us -> none  [the longest x1 0.96 us: reduce_over_shots(): x = (keep + hop(send, lambda i: i ^ 1)).reshape(4, 2, 16, 384)]
    ppermute x8, waiting for transfers between devices: 5.75 us -> 4.56 us  [passed_along(): return lax.ppermute(value, axis, pairs)]
    ppermute x5, waiting for transfers between devices: 1.79 us -> 2.67 us  [reduce_over_shots(): hop = lambda v, to: lax.ppermute(v, 'shot', [(i, to(i)) for i in range(16)])]
    pallas_call x1, Pallas kernels: 1.99 us -> 2.77 us  [body(): call(forward_start_kernel, [pl.BlockSpec(memory_space=pltpu.HBM)] * 3, (s...]
    pallas_call x1, Pallas kernels: 2.47 us -> 1.81 us  [body(): call(last_image_kernel, [V] * 6 + [S] * 2 + [V] * 2, (shape(8, 16, 384),...]
    pallas_call x5 -> x8, Pallas kernels: 12.5 us -> 13.1 us  [the longest x2 5.03 us: middle(): call(kernel, [V] * 7 + held + [V] * 4, (sends(faces), sends(faces), field...]
  transfers between devices with their start and end apart: 13 -> 13, of which waited for: 4 -> 4; matrix products, arithmetic and copies ran while one was open for 1% -> 0% of each run, Pallas kernels for 20% -> 23%
where the time goes in v4:
time: 53.1 us; the launch traced here: 53 us
  starting transfers between devices  26.7 us (50%)
  Pallas kernels  17.6 us (33%)
  waiting for transfers between devices  7.23 us (14%)
  between operations  1.42 us (3%)
    ppermute x8, starting transfers between devices, passed_along(): return lax.ppermute(value, axis, pairs)  17.2 us
    ppermute x5, starting transfers between devices, reduce_over_shots(): hop = lambda v, to: lax.ppermute(v, 'shot', [(i, to(i)) for i in range(16)])  9.46 us
    pallas_call x2, Pallas kernels, middle(): call(kernel, [V] * 7 + held + [V] * 4, (sends(faces), sends(faces), field...  5.03 us
    ppermute x8, waiting for transfers between devices, passed_along(): return lax.ppermute(value, axis, pairs)  4.56 us
    pallas_call x1, Pallas kernels, body(): call(forward_start_kernel, [pl.BlockSpec(memory_space=pltpu.HBM)] * 3, (s...  2.77 us
    ppermute x5, waiting for transfers between devices, reduce_over_shots(): hop = lambda v, to: lax.ppermute(v, 'shot', [(i, to(i)) for i in range(16)])  2.67 us
    pallas_call x1, Pallas kernels, body(): call(last_kernel, [V] * 12, shape(1125, 2, 128), [scr(field(3)), scr(fiel...  2.61 us
    pallas_call x1, Pallas kernels, body(): call(adjoint_start_kernel, [V] * 6, (sends(6), sends(6), field(3), field(...  2.31 us
  transfers between devices with their start and end apart: 13, of which 4 were waited for; matrix products, arithmetic and copies ran while one was open for 0% of the time, Pallas kernels for 23%

profile of v4, /device:TPU:0, one launch (start us, length us, event | category | flops | bytes accessed | tf_op | source)
XLA Modules:
  0.0 53.0 jit_solution(3640270088939864106)
XLA Ops:
  0.7 2.8 %shard_map.95 = (f32[175,2,128]{2,1,0:T(2,128)S(1)}, f32[175,2,128]{2,1,0:T(2,128)S(1)}, f32[2,3,5,5,8,128]{5,4,3,2,1,0:T(8,128)S(1)}, f32[2,3,5,5,8,128]{5,4,3,...) custom-call(f32[1125,2,128]{2,1,0:T(2,128)} %bitcast.20, ...), custom_call_target="tpu_custom_call" | custom-call | flops 100000000 | bytes 4000000 | tf_op jit(solution)/shard_map/pallas_call | solution.py:542
  3.4 0.0 copy-start.3
  3.5 2.1 %collective-permute-start = (f32[175,2,128]{2,1,0:T(2,128)S(1)}, f32[175,2,128]{2,1,0:T(2,128)S(1)}, u32[]{:S(2)}, u32[]{:S(2)}) collective-permute-start(f32[175,2,128]{2,1,0:T(2,128)S(1)} %get-tuple-element.45), channel_id=1, source_target_pairs={{0,16},{16,32},{32,48},{48,64},{64,80},{80,96},{96,112},{112,0},{1... | collective-permute-start | bytes 537608 | tf_op jit(solution)/shard_map/ppermute | solution.py:499
  5.5 2.5 %collective-permute-start.1 = (f32[175,2,128]{2,1,0:T(2,128)S(1)}, f32[175,2,128]{2,1,0:T(2,128)S(1)}, u32[]{:S(2)}, u32[]{:S(2)}) collective-permute-start(f32[175,2,128]{2,1,0:T(2,128)S(1)} %get-tuple-element.46), channel_id=1, source_target_pairs={{0,112},{16,0},{32,16},{48,32},{64,48},{80,64},{96,80},{112,96},{1... | collective-permute-start | bytes 537608 | tf_op jit(solution)/shard_map/ppermute | solution.py:499
  8.1 2.3 %shard_map.96 = (f32[150,2,128]{2,1,0:T(2,128)S(1)}, f32[150,2,128]{2,1,0:T(2,128)S(1)}, f32[2,3,5,5,8,128]{5,4,3,2,1,0:T(8,128)S(1)}, f32[2,3,5,5,8,128]{5,4,3,...) custom-call(f32[1125,2,128]{2,1,0:T(2,128)S(1)} %bitcast.16, ...), custom_call_target="tpu_custom_call" | custom-call | flops 100000000 | bytes 4000000 | tf_op jit(solution)/shard_map/pallas_call | solution.py:550
  10.4 0.1 collective-permute-start.2
  10.5 4.1 %collective-permute-start.3 = (f32[150,2,128]{2,1,0:T(2,128)S(1)}, f32[150,2,128]{2,1,0:T(2,128)S(1)}, u32[]{:S(2)}, u32[]{:S(2)}) collective-permute-start(f32[150,2,128]{2,1,0:T(2,128)S(1)} %get-tuple-element.54), channel_id=1, source_target_pairs={{0,112},{16,0},{32,16},{48,32},{64,48},{80,64},{96,80},{112,96},{1... | collective-permute-start | bytes 460808 | tf_op jit(solution)/shard_map/ppermute | solution.py:499
  15.2 2.3 %collective-permute-done.refs_9_.refs_11_.refs_10_.r_below = f32[175,2,128]{2,1,0:T(2,128)S(1)} collective-permute-done((f32[175,2,128]{2,1,0:T(2,128)S(1)}, f32[175,2,128]{2,1,0:T(2,128)S(1)}, u32[]{:S(2)}, u32[]{:S(2)}) %collective-permute-start) | collective-permute-done | bytes 179232 | tf_op jit(solution)/shard_map/ppermute | solution.py:499
  17.6 2.2 %collective-permute-done.1.refs_10_.refs_12_.refs_11_.r_above = f32[175,2,128]{2,1,0:T(2,128)S(1)} collective-permute-done((f32[175,2,128]{2,1,0:T(2,128)S(1)}, f32[175,2,128]{2,1,0:T(2,128)S(1)}, u32[]{:S(2)}, u32[]{:S(2)}) %collective-permute-start.1) | collective-permute-done | bytes 179232 | tf_op jit(solution)/shard_map/ppermute | solution.py:499
  19.8 2.0 %shard_map.97 = (f32[75,2,128]{2,1,0:T(2,128)S(1)}, f32[75,2,128]{2,1,0:T(2,128)S(1)}, f32[2,3,5,5,8,128]{5,4,3,2,1,0:T(8,128)S(1)}, f32[2,6,5,5,8,128]{5,4,3,2,1,0:T(8,128)S(1)}, f32[2,3,5,5,8,128]{5,4,3,2,1,0:T(8,128)S(1)}) custom-call(f32[2,3,5,5,8,128]{5,4,3,2,1,0:T(8,128)S(1)} %get-tuple-element.38.refs_0_, ...), custom_call_target="tpu_custom_call" | custom-call | flops 200000000 | bytes 8000000 | tf_op jit(solution)/shard_map/pallas_call | solution.py:567
  21.8 0.4 collective-permute-start.4
  22.1 3.8 %collective-permute-start.5 = (f32[75,2,128]{2,1,0:T(2,128)S(1)}, f32[75,2,128]{2,1,0:T(2,128)S(1)}, u32[]{:S(2)}, u32[]{:S(2)}) collective-permute-start(f32[75,2,128]{2,1,0:T(2,128)S(1)} %get-tuple-element.61), channel_id=1, source_target_pairs={{0,112},{16,0},{32,16},{48,32},{64,48},{80,64},{96,80},{112,96},{1... | collective-permute-start | bytes 230408 | tf_op jit(solution)/shard_map/ppermute | solution.py:499
  26.0 0.0 collective-permute-done.2.refs_8_
  26.0 0.0 collective-permute-done.3.refs_9_
  26.0 3.1 %shard_map.98 = (f32[150,2,128]{2,1,0:T(2,128)S(1)}, f32[150,2,128]{2,1,0:T(2,128)S(1)}, f32[2,3,5,5,8,128]{5,4,3,2,1,0:T(8,128)S(1)}, f32[2,6,5,5,8,128]{5,4,3,...) custom-call(f32[2,3,5,5,8,128]{5,4,3,2,1,0:T(8,128)S(1)} %get-tuple-element.49.refs_0_.adj_vel, ...), custom_call_target="tpu_custom_call" | custom-call | flops 200000000 | bytes 8000000 | tf_op jit(solution)/shard_map/pallas_call | solution.py:567
  29.0 2.2 %shard_map.99 = (f32[2,384,128]{2,1,0:T(8,128)S(1)}, f32[2,3,5,5,8,128]{5,4,3,2,1,0:T(8,128)S(1)}) custom-call(f32[2,3,5,5,8,128]{5,4,3,2,1,0:T(8,128)S(1)} %get-tuple-element.47.f_vel, f32[2,3,5,5,8,128]{5,4,3,2,1,0:T(8,128)S(1)} %get-tuple-element.48.f_acc, f32[2,3,5,5,8,128]{5,4,3,2,1,0:T(8,128)S(1)} %get-tuple-element.55.a_vel.vel_in, ...), custom_call_target="tpu_custom_call" | custom-call | flops 1000 | bytes 1000 | tf_op jit(solution)/shard_map/pallas_call | solution.py:583
  31.2 0.0 collective-permute-done.4.below
  31.2 0.0 collective-permute-done.5.above
  31.3 1.8 %shard_map.100 = (f32[8,16,384]{2,1,0:T(8,128)S(1)}, f32[8,16,384]{2,1,0:T(8,128)S(1)}) custom-call(f32[2,3,5,5,8,128]{5,4,3,2,1,0:T(8,128)S(1)} %get-tuple-element.47.f_vel, f32[2,3,5,5,8,128]{5,4,3,2,1,0:T(8,128)S(1)} %get-tuple-element.57.acc_in, f32[2,3,5,5,8,128]{5,4,3,2,1,0:T(8,128)S(1)} %get-tuple-element.49.refs_0_.adj_vel, ...), custom_call_target="tpu_custom_call" | custom-call | flops 1000 | bytes 1000 | tf_op jit(solution)/shard_map/pallas_call | solution.py:590
  33.1 0.1 collective-permute-start.6
  33.2 0.1 collective-permute-start.11
  33.2 4.1 %collective-permute-start.12 = (f32[150,2,128]{2,1,0:T(2,128)S(1)}, f32[150,2,128]{2,1,0:T(2,128)S(1)}, u32[]{:S(2)}, u32[]{:S(2)}) collective-permute-start(f32[150,2,128]{2,1,0:T(2,128)S(1)} %get-tuple-element.73), channel_id=1, source_target_pairs={{0,112},{16,0},{32,16},{48,32},{64,48},{80,64},{96,80},{112,96},{1... | collective-permute-start | bytes 460808 | tf_op jit(solution)/shard_map/ppermute | solution.py:499
  37.4 0.0 collective-permute-done.6.got
  37.4 1.6 %collective-permute-start.7 = (f32[2,16,384]{2,1,0:T(8,128)S(1)}, f32[2,16,384]{2,1,0:T(8,128)S(1)}, u32[]{:S(2)}, u32[]{:S(2)}) collective-permute-start(f32[2,16,384]{2,1,0:T(8,128)S(1)} %get-tuple-element.65), channel_id=1, source_target_pairs={{0,4},{1,5},{2,6},{3,7},{4,8},{5,9},{6,10},{7,11},{8,12},{9,13},{1... | collective-permute-start | bytes 147464 | tf_op jit(solution)/shard_map/ppermute | solution.py:527
  39.0 2.7 %collective-permute-start.8 = (f32[2,16,384]{2,1,0:T(8,128)S(1)}, f32[2,16,384]{2,1,0:T(8,128)S(1)}, u32[]{:S(2)}, u32[]{:S(2)}) collective-permute-start(f32[2,16,384]{2,1,0:T(8,128)S(1)} %get-tuple-element.66), channel_id=1, source_target_pairs={{0,8},{1,9},{2,10},{3,11},{4,12},{5,13},{6,14},{7,15},{8,0},{9,1},... | collective-permute-start | bytes 147464 | tf_op jit(solution)/shard_map/ppermute | solution.py:527
  41.7 1.4 %collective-permute-start.9 = (f32[2,16,384]{2,1,0:T(8,128)S(1)}, f32[2,16,384]{2,1,0:T(8,128)S(1)}, u32[]{:S(2)}, u32[]{:S(2)}) collective-permute-start(f32[2,16,384]{2,1,0:T(8,128)S(1)} %get-tuple-element.67), channel_id=1, source_target_pairs={{0,12},{1,13},{2,14},{3,15},{4,0},{5,1},{6,2},{7,3},{8,4},{9,5},{1... | collective-permute-start | bytes 147464 | tf_op jit(solution)/shard_map/ppermute | solution.py:527
  43.1 1.4 %collective-permute-done.8.two = f32[2,16,384]{2,1,0:T(8,128)S(1)} collective-permute-done((f32[2,16,384]{2,1,0:T(8,128)S(1)}, f32[2,16,384]{2,1,0:T(8,128)S(1)}, u32[]{:S(2)}, u32[]{:S(2)}) %collective-permute-start.8) | collective-permute-done | bytes 49184 | tf_op jit(solution)/shard_map/ppermute | solution.py:527
  44.6 1.2 %collective-permute-done.9.three = f32[2,16,384]{2,1,0:T(8,128)S(1)} collective-permute-done((f32[2,16,384]{2,1,0:T(8,128)S(1)}, f32[2,16,384]{2,1,0:T(8,128)S(1)}, u32[]{:S(2)}, u32[]{:S(2)}) %collective-permute-start.9) | collective-permute-done | bytes 49184 | tf_op jit(solution)/shard_map/ppermute | solution.py:527
  45.8 3.7 %collective-permute-start.10 = (f32[16,384]{1,0:T(8,128)S(1)}, f32[16,384]{1,0:T(8,128)S(1)}, u32[]{:S(2)}, u32[]{:S(2)}) collective-permute-start(f32[16,384]{1,0:T(8,128)S(1)} %get-tuple-element.69), channel_id=1, source_target_pairs={{0,2},{1,3},{2,0},{3,1},{4,6},{5,7},{6,4},{7,5},{8,10},{9,11},{10,... | collective-permute-start | bytes 73736 | tf_op jit(solution)/shard_map/ppermute | solution.py:527
  49.5 2.6 %shard_map.104 = f32[1125,2,128]{2,1,0:T(2,128)} custom-call(f32[2,3,5,5,8,128]{5,4,3,2,1,0:T(8,128)S(1)} %get-tuple-element.55.a_vel.vel_in, f32[2,6,5,5,8,128]{5,4,3,2,1,0:T(8,128)S(1)} %get-tuple-element.70.stress_in, f32[2,3,5,5,8,128]{5,4,3,2,1,0:T(8,128)S(1)} %get-tuple-element.71.acc_in, f32[2,5,5,8,128]{4,3,2,1,0:T(8,128)S(1)} %get-tuple-element.43.refs_3_.lam, ...), custom_call_target="tpu_custom_call" | custom-call | flops 100000000 | bytes 8000000 | tf_op jit(solution)/shard_map/pallas_call | solution.py:598
  52.1 0.0 collective-permute-done.10.got
  52.1 0.9 %shard_map.103 = f32[125,3,16]{2,1,0:T(4,128)} custom-call(f32[16,384]{1,0:T(8,128)S(1)} %get-tuple-element.68.keep, f32[16,384]{1,0:T(8,128)S(1)} %collective-permute-done.10.got), custom_call_target="tpu_custom_call" | custom-call | flops 1000 | bytes 1000 | tf_op jit(solution)/shard_map/pallas_call | solution.py:532
  (14 shorter events, 0.1 us)
Async XLA Ops:
  0.6 7.4 %copy-start = (f32[3,5,5,5,256]{4,0,3,2,1:T(4,128)S(1)}, f32[3,5,5,5,256]{4,0,3,2,1:T(4,128)}, u32[]{:S(2)}) copy-start(f32[3,5,5,5,256]{4,0,3,2,1:T(4,128)} %param.10) | copy-start | bytes 1152004
  0.6 7.4 %copy-start.1 = (f32[1,9,5,5,5,256]{5,0,4,3,2,1:T(1,128)S(1)}, f32[1,9,5,5,5,256]{5,0,4,3,2,1:T(1,128)}, u32[]{:S(2)}) copy-start(f32[1,9,5,5,5,256]{5,0,4,3,2,1:T(1,128)} %param.9) | copy-start | bytes 3456004
  0.7 7.4 %copy-start.4 = (s32[256]{0:T(256)S(1)}, s32[256]{0:T(256)}, u32[]{:S(2)}) copy-start(s32[256]{0:T(256)} %param.14) | copy-start | bytes 3076
  0.7 7.4 %copy-start.2 = (f32[1,2,3,256]{3,1,2,0:T(2,128)S(1)}, f32[1,2,3,256]{3,1,2,0:T(2,128)}, u32[]{:S(2)}) copy-start(f32[1,2,3,256]{3,1,2,0:T(2,128)} %param.15) | copy-start | bytes 18436
  3.4 16.3 %copy-start.3 = (f32[1,2,3]{2,1,0:T(2,128)S(1)}, f32[1,2,3]{2,1,0:T(2,128)}, u32[]{:S(2)}) copy-start(f32[1,2,3]{2,1,0:T(2,128)} %strength.1) | copy-start | bytes 76
  3.5 14.1 %collective-permute-start = (f32[175,2,128]{2,1,0:T(2,128)S(1)}, f32[175,2,128]{2,1,0:T(2,128)S(1)}, u32[]{:S(2)}, u32[]{:S(2)}) collective-permute-start(f32[175,2,128]{2,1,0:T(2,128)S(1)} %get-tuple-element.45), channel_id=1, source_target_pairs={{0,16},{16,32},{32,48},{48,64},{64,80},{80,96},{96,112},{112,0},{1... | collective-permute-start | bytes 537608 | tf_op jit(solution)/shard_map/ppermute | solution.py:499
  5.5 14.3 %collective-permute-start.1 = (f32[175,2,128]{2,1,0:T(2,128)S(1)}, f32[175,2,128]{2,1,0:T(2,128)S(1)}, u32[]{:S(2)}, u32[]{:S(2)}) collective-permute-start(f32[175,2,128]{2,1,0:T(2,128)S(1)} %get-tuple-element.46), channel_id=1, source_target_pairs={{0,112},{16,0},{32,16},{48,32},{64,48},{80,64},{96,80},{112,96},{1... | collective-permute-start | bytes 537608 | tf_op jit(solution)/shard_map/ppermute | solution.py:499
  10.4 15.6 %collective-permute-start.2 = (f32[150,2,128]{2,1,0:T(2,128)S(1)}, f32[150,2,128]{2,1,0:T(2,128)S(1)}, u32[]{:S(2)}, u32[]{:S(2)}) collective-permute-start(f32[150,2,128]{2,1,0:T(2,128)S(1)} %get-tuple-element.53), channel_id=1, source_target_pairs={{0,16},{16,32},{32,48},{48,64},{64,80},{80,96},{96,112},{112,0},{1... | collective-permute-start | bytes 460808 | tf_op jit(solution)/shard_map/ppermute | solution.py:499
  10.5 15.5 %collective-permute-start.3 = (f32[150,2,128]{2,1,0:T(2,128)S(1)}, f32[150,2,128]{2,1,0:T(2,128)S(1)}, u32[]{:S(2)}, u32[]{:S(2)}) collective-permute-start(f32[150,2,128]{2,1,0:T(2,128)S(1)} %get-tuple-element.54), channel_id=1, source_target_pairs={{0,112},{16,0},{32,16},{48,32},{64,48},{80,64},{96,80},{112,96},{1... | collective-permute-start | bytes 460808 | tf_op jit(solution)/shard_map/ppermute | solution.py:499
  21.8 9.5 %collective-permute-start.4 = (f32[75,2,128]{2,1,0:T(2,128)S(1)}, f32[75,2,128]{2,1,0:T(2,128)S(1)}, u32[]{:S(2)}, u32[]{:S(2)}) collective-permute-start(f32[75,2,128]{2,1,0:T(2,128)S(1)} %get-tuple-element.60), channel_id=1, source_target_pairs={{0,16},{16,32},{32,48},{48,64},{64,80},{80,96},{96,112},{112,0},{1... | collective-permute-start | bytes 230408 | tf_op jit(solution)/shard_map/ppermute | solution.py:499
  22.1 9.1 %collective-permute-start.5 = (f32[75,2,128]{2,1,0:T(2,128)S(1)}, f32[75,2,128]{2,1,0:T(2,128)S(1)}, u32[]{:S(2)}, u32[]{:S(2)}) collective-permute-start(f32[75,2,128]{2,1,0:T(2,128)S(1)} %get-tuple-element.61), channel_id=1, source_target_pairs={{0,112},{16,0},{32,16},{48,32},{64,48},{80,64},{96,80},{112,96},{1... | collective-permute-start | bytes 230408 | tf_op jit(solution)/shard_map/ppermute | solution.py:499
  33.1 4.3 %collective-permute-start.6 = (f32[8,16,384]{2,1,0:T(8,128)S(1)}, f32[8,16,384]{2,1,0:T(8,128)S(1)}, u32[]{:S(2)}, u32[]{:S(2)}) collective-permute-start(f32[8,16,384]{2,1,0:T(8,128)S(1)} %get-tuple-element.63), channel_id=1, source_target_pairs={{0,1},{1,0},{2,3},{3,2},{4,5},{5,4},{6,7},{7,6},{8,9},{9,8},{10,11... | collective-permute-start | bytes 589832 | tf_op jit(solution)/shard_map/ppermute | solution.py:527
  33.2 16.3 %collective-permute-start.11 = (f32[150,2,128]{2,1,0:T(2,128)S(1)}, f32[150,2,128]{2,1,0:T(2,128)S(1)}, u32[]{:S(2)}, u32[]{:S(2)}) collective-permute-start(f32[150,2,128]{2,1,0:T(2,128)S(1)} %get-tuple-element.72), channel_id=1, source_target_pairs={{0,16},{16,32},{32,48},{48,64},{64,80},{80,96},{96,112},{112,0},{1... | collective-permute-start | bytes 460808 | tf_op jit(solution)/shard_map/ppermute | solution.py:499
  33.2 16.2 %collective-permute-start.12 = (f32[150,2,128]{2,1,0:T(2,128)S(1)}, f32[150,2,128]{2,1,0:T(2,128)S(1)}, u32[]{:S(2)}, u32[]{:S(2)}) collective-permute-start(f32[150,2,128]{2,1,0:T(2,128)S(1)} %get-tuple-element.73), channel_id=1, source_target_pairs={{0,112},{16,0},{32,16},{48,32},{64,48},{80,64},{96,80},{112,96},{1... | collective-permute-start | bytes 460808 | tf_op jit(solution)/shard_map/ppermute | solution.py:499
  37.4 5.7 %collective-permute-start.7 = (f32[2,16,384]{2,1,0:T(8,128)S(1)}, f32[2,16,384]{2,1,0:T(8,128)S(1)}, u32[]{:S(2)}, u32[]{:S(2)}) collective-permute-start(f32[2,16,384]{2,1,0:T(8,128)S(1)} %get-tuple-element.65), channel_id=1, source_target_pairs={{0,4},{1,5},{2,6},{3,7},{4,8},{5,9},{6,10},{7,11},{8,12},{9,13},{1... | collective-permute-start | bytes 147464 | tf_op jit(solution)/shard_map/ppermute | solution.py:527
  39.0 5.6 %collective-permute-start.8 = (f32[2,16,384]{2,1,0:T(8,128)S(1)}, f32[2,16,384]{2,1,0:T(8,128)S(1)}, u32[]{:S(2)}, u32[]{:S(2)}) collective-permute-start(f32[2,16,384]{2,1,0:T(8,128)S(1)} %get-tuple-element.66), channel_id=1, source_target_pairs={{0,8},{1,9},{2,10},{3,11},{4,12},{5,13},{6,14},{7,15},{8,0},{9,1},... | collective-permute-start | bytes 147464 | tf_op jit(solution)/shard_map/ppermute | solution.py:527
  41.7 4.1 %collective-permute-start.9 = (f32[2,16,384]{2,1,0:T(8,128)S(1)}, f32[2,16,384]{2,1,0:T(8,128)S(1)}, u32[]{:S(2)}, u32[]{:S(2)}) collective-permute-start(f32[2,16,384]{2,1,0:T(8,128)S(1)} %get-tuple-element.67), channel_id=1, source_target_pairs={{0,12},{1,13},{2,14},{3,15},{4,0},{5,1},{6,2},{7,3},{8,4},{9,5},{1... | collective-permute-start | bytes 147464 | tf_op jit(solution)/shard_map/ppermute | solution.py:527
  45.8 6.3 %collective-permute-start.10 = (f32[16,384]{1,0:T(8,128)S(1)}, f32[16,384]{1,0:T(8,128)S(1)}, u32[]{:S(2)}, u32[]{:S(2)}) collective-permute-start(f32[16,384]{1,0:T(8,128)S(1)} %get-tuple-element.69), channel_id=1, source_target_pairs={{0,2},{1,3},{2,0},{3,1},{4,6},{5,7},{6,4},{7,5},{8,10},{9,11},{10,... | collective-permute-start | bytes 73736 | tf_op jit(solution)/shard_map/ppermute | solution.py:527

commit v5 on v4

--- a/solution.py
+++ b/solution.py
@@ -181,13 +181,23 @@
             dst[side, h, k, b, 0:5, :] = src[pl.ds(50 * j + 10 * b + h, 5, 2), :]
 
 
-def load_halo(halo, below, above, r_below, r_above, count):
-    for side, src in ((0, below), (1, above)):
+def load_halo(halo, first, second, r_first, r_second, count):
+    odd = lax.rem(lax.axis_index("slab"), 2)
+    for side, src in ((1 - odd, first), (odd, second)):
         for k in range(count):
             unpack_face(halo, side, k, src, k)
-    if r_below is not None:
-        for side, src in ((0, r_below), (1, r_above)):
+    if r_first is not None:
+        for side, src in ((1 - odd, r_first), (odd, r_second)):
             unpack_face(halo, side, 6, src, 6)
+
+
+def pack_faces(first, second, values):
+    odd = lax.rem(lax.axis_index("slab"), 2)
+    for dst, a in ((first, 4 * (1 - odd)), (second, 4 * odd)):
+        dst = flat(dst, dst.shape[0] * 2)
+        for h in range(2):
+            for k, value in enumerate(values(a, h)):
+                pack_face(dst, k, value, h)
 
 
 def finish_acceleration(acc, stress, rinv, halo, has_v):
@@ -328,20 +338,17 @@
     return copy
 
 
-def start_common(src, rinv, perms, acc, vel, stress, up, down, yj, zj, with_r):
+def start_common(src, rinv, perms, acc, vel, stress, one, two, yj, zj, with_r):
     src = flat(src, 2250)
-    up, down = (flat(r, r.shape[0] * 2) for r in (up, down))
     load_fields(src, 0, vel, 3)
     load_fields(src, 3, stress, 6)
     local_acceleration(stress, rinv, acc, perms, yj, zj)
-    for dst, a in ((up, 4), (down, 0)):
-        for i in range(3):
-            dst[50 * i : 50 * i + 50, :] = src[250 * (3, 8, 7)[i] + 50 * a : 250 * (3, 8, 7)[i] + 50 * a + 50, :]
-            for h in range(2):
-                pack_face(dst, 3 + i, vel[h, i, a] + time_step * acc[h, i, a], h)
-        if with_r:
-            for h in range(2):
-                pack_face(dst, 6, 0.05 * rinv[h, a], h)
+
+    def values(a, h):
+        out = [stress[h, k, a] for k in (0, 5, 4)] + [vel[h, i, a] + time_step * acc[h, i, a] for i in range(3)]
+        return out + ([0.05 * rinv[h, a]] if with_r else [])
+
+    pack_faces(one, two, values)
 
 
 def load_material(mat, k, dst):
@@ -350,7 +357,7 @@
             dst[h, g // 5, g % 5, 0:5, :] = mat[5 * g : 5 * g + 5, k, 128 * h : 128 * h + 128]
 
 
-def forward_start_kernel(state_hbm, mat_hbm, nbr_hbm, up, down, acc, vel, stress, rinv, perms, yj, zj, state, mat, nbr, sems):
+def forward_start_kernel(state_hbm, mat_hbm, nbr_hbm, one, two, acc, vel, stress, rinv, perms, yj, zj, state, mat, nbr, sems):
     first = fetch(nbr_hbm, nbr, sems.at[0])
     second = fetch(mat_hbm, mat, sems.at[1])
     third = fetch(state_hbm, state, sems.at[2])
@@ -363,14 +370,14 @@
             rinv[h, a] = 1.0 / rinv[h, a]
     zj[...] = jnp.zeros(zj.shape, f32)
     third.wait()
-    start_common(state, rinv, perms, acc, vel, stress, up, down, yj, zj, True)
-
-
-def adjoint_start_kernel(state, mat, rinv, perms, receivers, residuals, up, down, acc, vel, stress, lam, mu,
+    start_common(state, rinv, perms, acc, vel, stress, one, two, yj, zj, True)
+
+
+def adjoint_start_kernel(state, mat, rinv, perms, receivers, residuals, one, two, acc, vel, stress, lam, mu,
                          end_grads, injected, yj, zj):
     zj[...] = jnp.zeros(zj.shape, f32)
     injected[...] = receiver_rows(receivers, residuals)
-    start_common(state, rinv, perms, acc, vel, stress, up, down, yj, zj, False)
+    start_common(state, rinv, perms, acc, vel, stress, one, two, yj, zj, False)
     for k, dst in ((0, lam), (1, mu)):
         load_material(mat, k, dst)
         for h in range(2):
@@ -387,28 +394,29 @@
 
 
 def middle_kernel(kind, vel_in, stress_in, acc_in, lam, mu, rinv, perms, inject,
-                  below, above, r_below, r_above, up, down, vel, stress, acc, *rest):
+                  near, far, r_near, r_far, one, two, vel, stress, acc, *rest):
     next_acc, (halo, grads, yj, zj) = (rest[0], rest[1:]) if kind == "receiver" else (None, rest)
     rows = [inject[i : i + 1] for i in range(3)] if kind == "receiver" else source_rows(0, *inject)
     zj[...] = jnp.zeros(zj.shape, f32)
-    load_halo(halo, *(flat(r, r.shape[0] * 2) for r in (below, above, r_below, r_above)), 6)
+    load_halo(halo, *(flat(r, r.shape[0] * 2) for r in (near, far, r_near, r_far)), 6)
     acc[...] = acc_in[...]
     finish_step(rows, vel_in, stress_in, lam, mu, rinv, perms, vel, stress, acc, halo, grads, yj, zj)
     if kind == "receiver":
         local_acceleration(stress, rinv, next_acc, perms, yj, zj)
-    for dst, a in ((up, 4), (down, 0)):
-        dst = flat(dst, dst.shape[0] * 2)
-        for i in range(3):
-            for h in range(2):
-                pack_face(dst, i, stress[h, (0, 5, 4)[i], a], h)
-                if kind == "receiver":
-                    pack_face(dst, 3 + i, vel[h, i, a] + time_step * next_acc[h, i, a], h)
+
+    def values(a, h):
+        out = [stress[h, k, a] for k in (0, 5, 4)]
+        if kind == "receiver":
+            out += [vel[h, i, a] + time_step * next_acc[h, i, a] for i in range(3)]
+        return out
+
+    pack_faces(one, two, values)
 
 
 def last_kernel(vel_in, stress_in, acc_in, lam, mu, rinv, perms, inject,
-                below, above, r_below, r_above, out, vel, stress, acc, halo, grads, yj, zj):
+                near, far, r_near, r_far, out, vel, stress, acc, halo, grads, yj, zj):
     zj[...] = jnp.zeros(zj.shape, f32)
-    load_halo(halo, *(flat(r, r.shape[0] * 2) for r in (below, above, r_below, r_above)), 6)
+    load_halo(halo, *(flat(r, r.shape[0] * 2) for r in (near, far, r_near, r_far)), 6)
     acc[...] = acc_in[...]
     rows = [inject[8 + i : 9 + i] for i in range(3)]
     finish_step(rows, vel_in, stress_in, lam, mu, rinv, perms, vel, stress, acc, halo, grads, yj, zj)
@@ -432,9 +440,9 @@
     image(fg, ag, f_acc, a_vel, dense, None)
 
 
-def last_image_kernel(f_vel, acc_in, adj_vel, end_grads, first, rinv, where_ref, strength, below, above,
+def last_image_kernel(f_vel, acc_in, adj_vel, end_grads, first, rinv, where_ref, strength, near, far,
                       keep, send, halo, vel, acc, fg, dense):
-    load_halo(halo, flat(below, 150), flat(above, 150), None, None, 3)
+    load_halo(halo, flat(near, 150), flat(far, 150), None, None, 3)
     acc[...] = acc_in[...]
     finish_acceleration(acc, None, rinv, halo, False)
     velocities(f_vel, vel, acc, source_rows(1, where_ref, strength))
@@ -493,14 +501,11 @@
     )
 
 
-def passed_along(value, axis, steps):
-    count = lax.axis_size(axis)
-    pairs = [(source, (source + steps) % count) for source in range(count)]
-    return lax.ppermute(value, axis, pairs)
-
-
-def both_ways(up, down):
-    return passed_along(up, "slab", 1), passed_along(down, "slab", -1)
+def both_ways(first, second):
+    count = lax.axis_size("slab")
+    near = [(i, i ^ 1) for i in range(count)]
+    far = [(i, (i + (1 if i % 2 else -1)) % count) for i in range(count)]
+    return lax.ppermute(first, "slab", near), lax.ppermute(second, "slab", far)
 
 
 def core_sum_kernel(keep, got, mine, *others):
@@ -517,10 +522,11 @@
         dst[...] = (mine[k] + one[k]) + (two[k] + three[k])
 
 
-def last_sum_kernel(keep, got, out):
+def last_sum_kernel(keep, got, out, rows):
     turned = (keep[...] + got[...]).T
     for t in range(3):
-        out[:, t, :] = turned[125 * t : 125 * t + 125]
+        rows[pl.ds(t, 125, 4), 0:16] = turned[125 * t : 125 * t + 125]
+    out[...] = rows.reshape(125, 4, 128)[:, 0:3, 0:16]
 
 
 def reduce_over_shots(keep, send):
@@ -529,7 +535,7 @@
     mine, *others = call(core_sum_kernel, [V] * 2, (pair,) * 4, [], 1000, 1000)(keep, hop(send, lambda i: i ^ 1))
     got = [hop(x, lambda i: (i + 4 * d) % 16) for d, x in enumerate(others, 1)]
     keep, send = call(line_sum_kernel, [V] * 4, (chunk,) * 2, [], 1000, 1000)(mine, *got)
-    return call(last_sum_kernel, [V] * 2, shape(125, 3, 16), [], 1000, 1000)(keep, hop(send, lambda i: i ^ 2))
+    return call(last_sum_kernel, [V] * 2, shape(125, 3, 16), [scr(shape(500, 128))], 1000, 1000)(keep, hop(send, lambda i: i ^ 2))
 
 
 def body(fwd, adj, materials, nbr, source_element, pulse, receivers, residuals):
@@ -539,25 +545,25 @@
     nbr = nbr.T
     residuals = residuals.transpose(0, 2, 1, 3).reshape(3, 2, N)
 
-    f_up, f_down, f_acc, f_vel, f_stress, rinv, perms = call(
+    f_one, f_two, f_acc, f_vel, f_stress, rinv, perms = call(
         forward_start_kernel,
         [pl.BlockSpec(memory_space=pltpu.HBM)] * 3,
         (sends(7), sends(7), field(3), field(3), field(6), ONE, PERMS),
         JUMPS + [scr(shape(1125, 2, 128)), scr(shape(125, 3, N)), pltpu.VMEM((4, N), jnp.int32), pltpu.SemaphoreType.DMA((3,))],
         10**8, 4 * 10**6,
     )(*(pltpu.with_memory_space_constraint(x, pltpu.HBM) for x in (fwd, mat, nbr)))
-    f_below, f_above = both_ways(f_up, f_down)
-    a_up, a_down, a_acc, a_vel, a_stress, lam, mu, end_grads, injected = call(
+    f_near, f_far = both_ways(f_one, f_two)
+    a_one, a_two, a_acc, a_vel, a_stress, lam, mu, end_grads, injected = call(
         adjoint_start_kernel,
         [V] * 6,
         (sends(6), sends(6), field(3), field(3), field(6), ONE, ONE, field(9), shape(16, N)),
         JUMPS,
         10**8, 4 * 10**6,
     )(adj, mat, rinv, perms, receivers, residuals)
-    a_below, a_above = both_ways(a_up, a_down)
+    a_near, a_far = both_ways(a_one, a_two)
     adj_vel_end = a_vel
 
-    def middle(kind, vel, stress, acc, inject, below, above, faces):
+    def middle(kind, vel, stress, acc, inject, near, far, faces):
         if kind == "source":
             kernel = lambda *refs: middle_kernel(kind, *refs[:7], refs[7:9], *refs[9:])
             held = [S] * 2
@@ -570,16 +576,16 @@
             (sends(faces), sends(faces), field(3), field(6), field(3)) + (() if kind == "source" else (field(3),)),
             [HALO, scr(field(9))] + JUMPS,
             2 * 10**8, 8 * 10**6,
-        )(vel, stress, acc, lam, mu, rinv, perms, *inject, below, above, f_below, f_above)
-
-    f_up, f_down, f_vel1, f_stress1, f_acc1 = middle(
-        "source", f_vel, f_stress, f_acc, (source_element, pulse), f_below, f_above, 3
+        )(vel, stress, acc, lam, mu, rinv, perms, *inject, near, far, f_near, f_far)
+
+    f_one, f_two, f_vel1, f_stress1, f_acc1 = middle(
+        "source", f_vel, f_stress, f_acc, (source_element, pulse), f_near, f_far, 3
     )
-    f_below2, f_above2 = both_ways(f_up, f_down)
-    a_up, a_down, a_vel1, a_stress1, _, a_acc2 = middle(
-        "receiver", a_vel, a_stress, a_acc, (injected,), a_below, a_above, 6
+    f_near2, f_far2 = both_ways(f_one, f_two)
+    a_one, a_two, a_vel1, a_stress1, _, a_acc2 = middle(
+        "receiver", a_vel, a_stress, a_acc, (injected,), a_near, a_far, 6
     )
-    a_below2, a_above2 = both_ways(a_up, a_down)
+    a_near2, a_far2 = both_ways(a_one, a_two)
     first, f_acc2 = call(
         first_image_kernel,
         [V] * 6,
@@ -593,7 +599,7 @@
         (shape(8, 16, 384), shape(8, 16, 384)),
         [HALO, scr(field(3)), scr(field(3)), scr(field(9)), scr(shape(2, 384, 128))],
         1000, 1000,
-    )(f_vel1, f_acc2, adj_vel_end, end_grads, first, rinv, source_element, pulse, f_below2, f_above2)
+    )(f_vel1, f_acc2, adj_vel_end, end_grads, first, rinv, source_element, pulse, f_near2, f_far2)
     gradient = reduce_over_shots(keep, send)
     adjoint_end = call(
         last_kernel,
@@ -601,7 +607,7 @@
         shape(1125, 2, 128),
         [scr(field(3)), scr(field(6)), scr(field(3)), HALO, scr(field(9))] + JUMPS,
         10**8, 8 * 10**6,
-    )(a_vel1, a_stress1, a_acc2, lam, mu, rinv, perms, injected, a_below2, a_above2, f_below, f_above)
+    )(a_vel1, a_stress1, a_acc2, lam, mu, rinv, perms, injected, a_near2, a_far2, f_near, f_far)
     return gradient.reshape(5, 5, 5, 3, 16).transpose(3, 0, 1, 2, 4), adjoint_end.reshape(1, 9, 5, 5, 5, N)
 
 

time: 53.1 us -> 50.3 us (0.947)
  starting transfers between devices: 26.7 us -> 24.1 us
    ppermute x8, starting transfers between devices: 17.2 us -> 14.3 us  [the longest x4 8.57 us: both_ways(): lax.ppermute(second, 'slab', far)]
  transfers between devices with their start and end apart: 13 -> 13, of which waited for: 4 -> 4; matrix products, arithmetic and copies ran while one was open for 0% -> 0% of each run, Pallas kernels for 23% -> 25%
where the time goes in v5:
time: 50.3 us; the launch traced here: 50.2 us
  starting transfers between devices  24.1 us (48%)
  Pallas kernels  17.8 us (35%)
  waiting for transfers between devices  6.87 us (14%)
  between operations  1.4 us (3%)
    ppermute x5, starting transfers between devices, reduce_over_shots(): hop = lambda v, to: lax.ppermute(v, 'shot', [(i, to(i)) for i in range(16)])  9.81 us
    ppermute x4, starting transfers between devices, both_ways(): lax.ppermute(second, 'slab', far)  8.57 us
    ppermute x4, starting transfers between devices, both_ways(): lax.ppermute(first, 'slab', near)  5.75 us
    pallas_call x2, Pallas kernels, middle(): call(kernel, [V] * 7 + held + [V] * 4, (sends(faces), sends(faces), field...  5.15 us
    ppermute x4, waiting for transfers between devices, both_ways(): lax.ppermute(first, 'slab', near)  4.21 us
    pallas_call x1, Pallas kernels, body(): call(forward_start_kernel, [pl.BlockSpec(memory_space=pltpu.HBM)] * 3, (s...  2.78 us
    ppermute x5, waiting for transfers between devices, reduce_over_shots(): hop = lambda v, to: lax.ppermute(v, 'shot', [(i, to(i)) for i in range(16)])  2.65 us
    pallas_call x1, Pallas kernels, body(): call(last_kernel, [V] * 12, shape(1125, 2, 128), [scr(field(3)), scr(fiel...  2.61 us
  transfers between devices with their start and end apart: 13, of which 4 were waited for; matrix products, arithmetic and copies ran while one was open for 0% of the time, Pallas kernels for 25%

profile of v5, /device:TPU:0, one launch (start us, length us, event | category | flops | bytes accessed | tf_op | source)
XLA Modules:
  0.0 50.2 jit_solution(2636279546195932223)
XLA Ops:
  0.7 2.8 %shard_map.95 = (f32[175,2,128]{2,1,0:T(2,128)S(1)}, f32[175,2,128]{2,1,0:T(2,128)S(1)}, f32[2,3,5,5,8,128]{5,4,3,2,1,0:T(8,128)S(1)}, f32[2,3,5,5,8,128]{5,4,3,...) custom-call(f32[1125,2,128]{2,1,0:T(2,128)} %bitcast.20, ...), custom_call_target="tpu_custom_call" | custom-call | flops 100000000 | bytes 4000000 | tf_op jit(solution)/shard_map/pallas_call | solution.py:548
  3.5 0.0 copy-start.3
  3.5 2.1 %collective-permute-start = (f32[175,2,128]{2,1,0:T(2,128)S(1)}, f32[175,2,128]{2,1,0:T(2,128)S(1)}, u32[]{:S(2)}, u32[]{:S(2)}) collective-permute-start(f32[175,2,128]{2,1,0:T(2,128)S(1)} %get-tuple-element.45), channel_id=1, source_target_pairs={{0,16},{16,0},{32,48},{48,32},{64,80},{80,64},{96,112},{112,96},{1... | collective-permute-start | bytes 537608 | tf_op jit(solution)/shard_map/ppermute | solution.py:508
  5.6 2.6 %collective-permute-start.1 = (f32[175,2,128]{2,1,0:T(2,128)S(1)}, f32[175,2,128]{2,1,0:T(2,128)S(1)}, u32[]{:S(2)}, u32[]{:S(2)}) collective-permute-start(f32[175,2,128]{2,1,0:T(2,128)S(1)} %get-tuple-element.46), channel_id=1, source_target_pairs={{0,112},{16,32},{32,16},{48,64},{64,48},{80,96},{96,80},{112,0},{1... | collective-permute-start | bytes 537608 | tf_op jit(solution)/shard_map/ppermute | solution.py:508
  8.1 2.3 %shard_map.96 = (f32[150,2,128]{2,1,0:T(2,128)S(1)}, f32[150,2,128]{2,1,0:T(2,128)S(1)}, f32[2,3,5,5,8,128]{5,4,3,2,1,0:T(8,128)S(1)}, f32[2,3,5,5,8,128]{5,4,3,...) custom-call(f32[1125,2,128]{2,1,0:T(2,128)S(1)} %bitcast.16, ...), custom_call_target="tpu_custom_call" | custom-call | flops 100000000 | bytes 4000000 | tf_op jit(solution)/shard_map/pallas_call | solution.py:556
  10.5 0.6 %collective-permute-start.2 = (f32[150,2,128]{2,1,0:T(2,128)S(1)}, f32[150,2,128]{2,1,0:T(2,128)S(1)}, u32[]{:S(2)}, u32[]{:S(2)}) collective-permute-start(f32[150,2,128]{2,1,0:T(2,128)S(1)} %get-tuple-element.53), channel_id=1, source_target_pairs={{0,16},{16,0},{32,48},{48,32},{64,80},{80,64},{96,112},{112,96},{1... | collective-permute-start | bytes 460808 | tf_op jit(solution)/shard_map/ppermute | solution.py:508
  11.0 1.7 %collective-permute-start.3 = (f32[150,2,128]{2,1,0:T(2,128)S(1)}, f32[150,2,128]{2,1,0:T(2,128)S(1)}, u32[]{:S(2)}, u32[]{:S(2)}) collective-permute-start(f32[150,2,128]{2,1,0:T(2,128)S(1)} %get-tuple-element.54), channel_id=1, source_target_pairs={{0,112},{16,32},{32,16},{48,64},{64,48},{80,96},{96,80},{112,0},{1... | collective-permute-start | bytes 460808 | tf_op jit(solution)/shard_map/ppermute | solution.py:508
  13.4 4.2 %collective-permute-done.refs_9_.refs_11_.refs_10_.r_near = f32[175,2,128]{2,1,0:T(2,128)S(1)} collective-permute-done((f32[175,2,128]{2,1,0:T(2,128)S(1)}, f32[175,2,128]{2,1,0:T(2,128)S(1)}, u32[]{:S(2)}, u32[]{:S(2)}) %collective-permute-start) | collective-permute-done | bytes 179232 | tf_op jit(solution)/shard_map/ppermute | solution.py:508
  17.6 0.0 collective-permute-done.1.refs_10_.refs_12_.refs_11_.r_far
  17.6 2.0 %shard_map.97 = (f32[75,2,128]{2,1,0:T(2,128)S(1)}, f32[75,2,128]{2,1,0:T(2,128)S(1)}, f32[2,3,5,5,8,128]{5,4,3,2,1,0:T(8,128)S(1)}, f32[2,6,5,5,8,128]{5,4,3,2,1,0:T(8,128)S(1)}, f32[2,3,5,5,8,128]{5,4,3,2,1,0:T(8,128)S(1)}) custom-call(f32[2,3,5,5,8,128]{5,4,3,2,1,0:T(8,128)S(1)} %get-tuple-element.38.refs_0_, ...), custom_call_target="tpu_custom_call" | custom-call | flops 200000000 | bytes 8000000 | tf_op jit(solution)/shard_map/pallas_call | solution.py:573
  19.6 2.6 %collective-permute-start.4 = (f32[75,2,128]{2,1,0:T(2,128)S(1)}, f32[75,2,128]{2,1,0:T(2,128)S(1)}, u32[]{:S(2)}, u32[]{:S(2)}) collective-permute-start(f32[75,2,128]{2,1,0:T(2,128)S(1)} %get-tuple-element.60), channel_id=1, source_target_pairs={{0,16},{16,0},{32,48},{48,32},{64,80},{80,64},{96,112},{112,96},{1... | collective-permute-start | bytes 230408 | tf_op jit(solution)/shard_map/ppermute | solution.py:508
  22.1 2.6 %collective-permute-start.5 = (f32[75,2,128]{2,1,0:T(2,128)S(1)}, f32[75,2,128]{2,1,0:T(2,128)S(1)}, u32[]{:S(2)}, u32[]{:S(2)}) collective-permute-start(f32[75,2,128]{2,1,0:T(2,128)S(1)} %get-tuple-element.61), channel_id=1, source_target_pairs={{0,112},{16,32},{32,16},{48,64},{64,48},{80,96},{96,80},{112,0},{1... | collective-permute-start | bytes 230408 | tf_op jit(solution)/shard_map/ppermute | solution.py:508
  24.7 0.0 collective-permute-done.2.refs_8_
  24.7 3.2 %shard_map.98 = (f32[150,2,128]{2,1,0:T(2,128)S(1)}, f32[150,2,128]{2,1,0:T(2,128)S(1)}, f32[2,3,5,5,8,128]{5,4,3,2,1,0:T(8,128)S(1)}, f32[2,6,5,5,8,128]{5,4,3,...) custom-call(f32[2,3,5,5,8,128]{5,4,3,2,1,0:T(8,128)S(1)} %get-tuple-element.49.refs_0_.adj_vel, ...), custom_call_target="tpu_custom_call" | custom-call | flops 200000000 | bytes 8000000 | tf_op jit(solution)/shard_map/pallas_call | solution.py:573
  27.9 2.2 %shard_map.99 = (f32[2,384,128]{2,1,0:T(8,128)S(1)}, f32[2,3,5,5,8,128]{5,4,3,2,1,0:T(8,128)S(1)}) custom-call(f32[2,3,5,5,8,128]{5,4,3,2,1,0:T(8,128)S(1)} %get-tuple-element.47.f_vel, f32[2,3,5,5,8,128]{5,4,3,2,1,0:T(8,128)S(1)} %get-tuple-element.48.f_acc, f32[2,3,5,5,8,128]{5,4,3,2,1,0:T(8,128)S(1)} %get-tuple-element.55.a_vel.vel_in, ...), custom_call_target="tpu_custom_call" | custom-call | flops 1000 | bytes 1000 | tf_op jit(solution)/shard_map/pallas_call | solution.py:589
  30.1 1.8 %shard_map.100 = (f32[8,16,384]{2,1,0:T(8,128)S(1)}, f32[8,16,384]{2,1,0:T(8,128)S(1)}) custom-call(f32[2,3,5,5,8,128]{5,4,3,2,1,0:T(8,128)S(1)} %get-tuple-element.47.f_vel, f32[2,3,5,5,8,128]{5,4,3,2,1,0:T(8,128)S(1)} %get-tuple-element.57.acc_in, f32[2,3,5,5,8,128]{5,4,3,2,1,0:T(8,128)S(1)} %get-tuple-element.49.refs_0_.adj_vel, ...), custom_call_target="tpu_custom_call" | custom-call | flops 1000 | bytes 1000 | tf_op jit(solution)/shard_map/pallas_call | solution.py:596
  31.9 0.1 collective-permute-start.6
  32.0 0.6 %collective-permute-start.11 = (f32[150,2,128]{2,1,0:T(2,128)S(1)}, f32[150,2,128]{2,1,0:T(2,128)S(1)}, u32[]{:S(2)}, u32[]{:S(2)}) collective-permute-start(f32[150,2,128]{2,1,0:T(2,128)S(1)} %get-tuple-element.72), channel_id=1, source_target_pairs={{0,16},{16,0},{32,48},{48,32},{64,80},{80,64},{96,112},{112,96},{1... | collective-permute-start | bytes 460808 | tf_op jit(solution)/shard_map/ppermute | solution.py:508
  32.6 1.7 %collective-permute-start.12 = (f32[150,2,128]{2,1,0:T(2,128)S(1)}, f32[150,2,128]{2,1,0:T(2,128)S(1)}, u32[]{:S(2)}, u32[]{:S(2)}) collective-permute-start(f32[150,2,128]{2,1,0:T(2,128)S(1)} %get-tuple-element.73), channel_id=1, source_target_pairs={{0,112},{16,32},{32,16},{48,64},{64,48},{80,96},{96,80},{112,0},{1... | collective-permute-start | bytes 460808 | tf_op jit(solution)/shard_map/ppermute | solution.py:508
  34.3 0.0 collective-permute-done.6.got
  34.3 1.6 %collective-permute-start.7 = (f32[2,16,384]{2,1,0:T(8,128)S(1)}, f32[2,16,384]{2,1,0:T(8,128)S(1)}, u32[]{:S(2)}, u32[]{:S(2)}) collective-permute-start(f32[2,16,384]{2,1,0:T(8,128)S(1)} %get-tuple-element.65), channel_id=1, source_target_pairs={{0,4},{1,5},{2,6},{3,7},{4,8},{5,9},{6,10},{7,11},{8,12},{9,13},{1... | collective-permute-start | bytes 147464 | tf_op jit(solution)/shard_map/ppermute | solution.py:533
  35.9 2.7 %collective-permute-start.8 = (f32[2,16,384]{2,1,0:T(8,128)S(1)}, f32[2,16,384]{2,1,0:T(8,128)S(1)}, u32[]{:S(2)}, u32[]{:S(2)}) collective-permute-start(f32[2,16,384]{2,1,0:T(8,128)S(1)} %get-tuple-element.66), channel_id=1, source_target_pairs={{0,8},{1,9},{2,10},{3,11},{4,12},{5,13},{6,14},{7,15},{8,0},{9,1},... | collective-permute-start | bytes 147464 | tf_op jit(solution)/shard_map/ppermute | solution.py:533
  38.6 1.4 %collective-permute-start.9 = (f32[2,16,384]{2,1,0:T(8,128)S(1)}, f32[2,16,384]{2,1,0:T(8,128)S(1)}, u32[]{:S(2)}, u32[]{:S(2)}) collective-permute-start(f32[2,16,384]{2,1,0:T(8,128)S(1)} %get-tuple-element.67), channel_id=1, source_target_pairs={{0,12},{1,13},{2,14},{3,15},{4,0},{5,1},{6,2},{7,3},{8,4},{9,5},{1... | collective-permute-start | bytes 147464 | tf_op jit(solution)/shard_map/ppermute | solution.py:533
  40.1 0.2 collective-permute-done.7.one
  40.2 1.3 %collective-permute-done.8.two = f32[2,16,384]{2,1,0:T(8,128)S(1)} collective-permute-done((f32[2,16,384]{2,1,0:T(8,128)S(1)}, f32[2,16,384]{2,1,0:T(8,128)S(1)}, u32[]{:S(2)}, u32[]{:S(2)}) %collective-permute-start.8) | collective-permute-done | bytes 49184 | tf_op jit(solution)/shard_map/ppermute | solution.py:533
  41.5 1.2 %collective-permute-done.9.three = f32[2,16,384]{2,1,0:T(8,128)S(1)} collective-permute-done((f32[2,16,384]{2,1,0:T(8,128)S(1)}, f32[2,16,384]{2,1,0:T(8,128)S(1)}, u32[]{:S(2)}, u32[]{:S(2)}) %collective-permute-start.9) | collective-permute-done | bytes 49184 | tf_op jit(solution)/shard_map/ppermute | solution.py:533
  42.7 4.0 %collective-permute-start.10 = (f32[16,384]{1,0:T(8,128)S(1)}, f32[16,384]{1,0:T(8,128)S(1)}, u32[]{:S(2)}, u32[]{:S(2)}) collective-permute-start(f32[16,384]{1,0:T(8,128)S(1)} %get-tuple-element.69), channel_id=1, source_target_pairs={{0,2},{1,3},{2,0},{3,1},{4,6},{5,7},{6,4},{7,5},{8,10},{9,11},{10,... | collective-permute-start | bytes 73736 | tf_op jit(solution)/shard_map/ppermute | solution.py:533
  46.7 0.0 collective-permute-done.11.near
  46.7 0.0 collective-permute-done.12.far
  46.7 2.6 %shard_map.104 = f32[1125,2,128]{2,1,0:T(2,128)} custom-call(f32[2,3,5,5,8,128]{5,4,3,2,1,0:T(8,128)S(1)} %get-tuple-element.55.a_vel.vel_in, f32[2,6,5,5,8,128]{5,4,3,2,1,0:T(8,128)S(1)} %get-tuple-element.70.stress_in, f32[2,3,5,5,8,128]{5,4,3,2,1,0:T(8,128)S(1)} %get-tuple-element.71.acc_in, f32[2,5,5,8,128]{4,3,2,1,0:T(8,128)S(1)} %get-tuple-element.43.refs_3_.lam, ...), custom_call_target="tpu_custom_call" | custom-call | flops 100000000 | bytes 8000000 | tf_op jit(solution)/shard_map/pallas_call | solution.py:604
  49.3 0.0 collective-permute-done.10.got
  49.3 0.9 %shard_map.103 = f32[125,3,16]{2,1,0:T(4,128)} custom-call(f32[16,384]{1,0:T(8,128)S(1)} %get-tuple-element.68.keep, f32[16,384]{1,0:T(8,128)S(1)} %collective-permute-done.10.got), custom_call_target="tpu_custom_call" | custom-call | flops 1000 | bytes 1000 | tf_op jit(solution)/shard_map/pallas_call | solution.py:538
  (14 shorter events, 0.1 us)
Async XLA Ops:
  0.6 7.5 %copy-start = (f32[3,5,5,5,256]{4,0,3,2,1:T(4,128)S(1)}, f32[3,5,5,5,256]{4,0,3,2,1:T(4,128)}, u32[]{:S(2)}) copy-start(f32[3,5,5,5,256]{4,0,3,2,1:T(4,128)} %param.10) | copy-start | bytes 1152004
  0.6 7.5 %copy-start.1 = (f32[1,9,5,5,5,256]{5,0,4,3,2,1:T(1,128)S(1)}, f32[1,9,5,5,5,256]{5,0,4,3,2,1:T(1,128)}, u32[]{:S(2)}) copy-start(f32[1,9,5,5,5,256]{5,0,4,3,2,1:T(1,128)} %param.9) | copy-start | bytes 3456004
  0.7 7.5 %copy-start.4 = (s32[256]{0:T(256)S(1)}, s32[256]{0:T(256)}, u32[]{:S(2)}) copy-start(s32[256]{0:T(256)} %param.14) | copy-start | bytes 3076
  0.7 7.5 %copy-start.2 = (f32[1,2,3,256]{3,1,2,0:T(2,128)S(1)}, f32[1,2,3,256]{3,1,2,0:T(2,128)}, u32[]{:S(2)}) copy-start(f32[1,2,3,256]{3,1,2,0:T(2,128)} %param.15) | copy-start | bytes 18436
  3.5 14.1 %copy-start.3 = (f32[1,2,3]{2,1,0:T(2,128)S(1)}, f32[1,2,3]{2,1,0:T(2,128)}, u32[]{:S(2)}) copy-start(f32[1,2,3]{2,1,0:T(2,128)} %strength.1) | copy-start | bytes 76
  3.5 14.1 %collective-permute-start = (f32[175,2,128]{2,1,0:T(2,128)S(1)}, f32[175,2,128]{2,1,0:T(2,128)S(1)}, u32[]{:S(2)}, u32[]{:S(2)}) collective-permute-start(f32[175,2,128]{2,1,0:T(2,128)S(1)} %get-tuple-element.45), channel_id=1, source_target_pairs={{0,16},{16,0},{32,48},{48,32},{64,80},{80,64},{96,112},{112,96},{1... | collective-permute-start | bytes 537608 | tf_op jit(solution)/shard_map/ppermute | solution.py:508
  5.6 12.1 %collective-permute-start.1 = (f32[175,2,128]{2,1,0:T(2,128)S(1)}, f32[175,2,128]{2,1,0:T(2,128)S(1)}, u32[]{:S(2)}, u32[]{:S(2)}) collective-permute-start(f32[175,2,128]{2,1,0:T(2,128)S(1)} %get-tuple-element.46), channel_id=1, source_target_pairs={{0,112},{16,32},{32,16},{48,64},{64,48},{80,96},{96,80},{112,0},{1... | collective-permute-start | bytes 537608 | tf_op jit(solution)/shard_map/ppermute | solution.py:508
  10.5 14.3 %collective-permute-start.2 = (f32[150,2,128]{2,1,0:T(2,128)S(1)}, f32[150,2,128]{2,1,0:T(2,128)S(1)}, u32[]{:S(2)}, u32[]{:S(2)}) collective-permute-start(f32[150,2,128]{2,1,0:T(2,128)S(1)} %get-tuple-element.53), channel_id=1, source_target_pairs={{0,16},{16,0},{32,48},{48,32},{64,80},{80,64},{96,112},{112,96},{1... | collective-permute-start | bytes 460808 | tf_op jit(solution)/shard_map/ppermute | solution.py:508
  11.0 13.7 %collective-permute-start.3 = (f32[150,2,128]{2,1,0:T(2,128)S(1)}, f32[150,2,128]{2,1,0:T(2,128)S(1)}, u32[]{:S(2)}, u32[]{:S(2)}) collective-permute-start(f32[150,2,128]{2,1,0:T(2,128)S(1)} %get-tuple-element.54), channel_id=1, source_target_pairs={{0,112},{16,32},{32,16},{48,64},{64,48},{80,96},{96,80},{112,0},{1... | collective-permute-start | bytes 460808 | tf_op jit(solution)/shard_map/ppermute | solution.py:508
  19.6 10.5 %collective-permute-start.4 = (f32[75,2,128]{2,1,0:T(2,128)S(1)}, f32[75,2,128]{2,1,0:T(2,128)S(1)}, u32[]{:S(2)}, u32[]{:S(2)}) collective-permute-start(f32[75,2,128]{2,1,0:T(2,128)S(1)} %get-tuple-element.60), channel_id=1, source_target_pairs={{0,16},{16,0},{32,48},{48,32},{64,80},{80,64},{96,112},{112,96},{1... | collective-permute-start | bytes 230408 | tf_op jit(solution)/shard_map/ppermute | solution.py:508
  22.1 8.0 %collective-permute-start.5 = (f32[75,2,128]{2,1,0:T(2,128)S(1)}, f32[75,2,128]{2,1,0:T(2,128)S(1)}, u32[]{:S(2)}, u32[]{:S(2)}) collective-permute-start(f32[75,2,128]{2,1,0:T(2,128)S(1)} %get-tuple-element.61), channel_id=1, source_target_pairs={{0,112},{16,32},{32,16},{48,64},{64,48},{80,96},{96,80},{112,0},{1... | collective-permute-start | bytes 230408 | tf_op jit(solution)/shard_map/ppermute | solution.py:508
  31.9 2.4 %collective-permute-start.6 = (f32[8,16,384]{2,1,0:T(8,128)S(1)}, f32[8,16,384]{2,1,0:T(8,128)S(1)}, u32[]{:S(2)}, u32[]{:S(2)}) collective-permute-start(f32[8,16,384]{2,1,0:T(8,128)S(1)} %get-tuple-element.63), channel_id=1, source_target_pairs={{0,1},{1,0},{2,3},{3,2},{4,5},{5,4},{6,7},{7,6},{8,9},{9,8},{10,11... | collective-permute-start | bytes 589832 | tf_op jit(solution)/shard_map/ppermute | solution.py:533
  32.0 14.7 %collective-permute-start.11 = (f32[150,2,128]{2,1,0:T(2,128)S(1)}, f32[150,2,128]{2,1,0:T(2,128)S(1)}, u32[]{:S(2)}, u32[]{:S(2)}) collective-permute-start(f32[150,2,128]{2,1,0:T(2,128)S(1)} %get-tuple-element.72), channel_id=1, source_target_pairs={{0,16},{16,0},{32,48},{48,32},{64,80},{80,64},{96,112},{112,96},{1... | collective-permute-start | bytes 460808 | tf_op jit(solution)/shard_map/ppermute | solution.py:508
  32.6 14.1 %collective-permute-start.12 = (f32[150,2,128]{2,1,0:T(2,128)S(1)}, f32[150,2,128]{2,1,0:T(2,128)S(1)}, u32[]{:S(2)}, u32[]{:S(2)}) collective-permute-start(f32[150,2,128]{2,1,0:T(2,128)S(1)} %get-tuple-element.73), channel_id=1, source_target_pairs={{0,112},{16,32},{32,16},{48,64},{64,48},{80,96},{96,80},{112,0},{1... | collective-permute-start | bytes 460808 | tf_op jit(solution)/shard_map/ppermute | solution.py:508
  34.3 5.9 %collective-permute-start.7 = (f32[2,16,384]{2,1,0:T(8,128)S(1)}, f32[2,16,384]{2,1,0:T(8,128)S(1)}, u32[]{:S(2)}, u32[]{:S(2)}) collective-permute-start(f32[2,16,384]{2,1,0:T(8,128)S(1)} %get-tuple-element.65), channel_id=1, source_target_pairs={{0,4},{1,5},{2,6},{3,7},{4,8},{5,9},{6,10},{7,11},{8,12},{9,13},{1... | collective-permute-start | bytes 147464 | tf_op jit(solution)/shard_map/ppermute | solution.py:533
  35.9 5.6 %collective-permute-start.8 = (f32[2,16,384]{2,1,0:T(8,128)S(1)}, f32[2,16,384]{2,1,0:T(8,128)S(1)}, u32[]{:S(2)}, u32[]{:S(2)}) collective-permute-start(f32[2,16,384]{2,1,0:T(8,128)S(1)} %get-tuple-element.66), channel_id=1, source_target_pairs={{0,8},{1,9},{2,10},{3,11},{4,12},{5,13},{6,14},{7,15},{8,0},{9,1},... | collective-permute-start | bytes 147464 | tf_op jit(solution)/shard_map/ppermute | solution.py:533
  38.6 4.1 %collective-permute-start.9 = (f32[2,16,384]{2,1,0:T(8,128)S(1)}, f32[2,16,384]{2,1,0:T(8,128)S(1)}, u32[]{:S(2)}, u32[]{:S(2)}) collective-permute-start(f32[2,16,384]{2,1,0:T(8,128)S(1)} %get-tuple-element.67), channel_id=1, source_target_pairs={{0,12},{1,13},{2,14},{3,15},{4,0},{5,1},{6,2},{7,3},{8,4},{9,5},{1... | collective-permute-start | bytes 147464 | tf_op jit(solution)/shard_map/ppermute | solution.py:533
  42.7 6.6 %collective-permute-start.10 = (f32[16,384]{1,0:T(8,128)S(1)}, f32[16,384]{1,0:T(8,128)S(1)}, u32[]{:S(2)}, u32[]{:S(2)}) collective-permute-start(f32[16,384]{1,0:T(8,128)S(1)} %get-tuple-element.69), channel_id=1, source_target_pairs={{0,2},{1,3},{2,0},{3,1},{4,6},{5,7},{6,4},{7,5},{8,10},{9,11},{10,... | collective-permute-start | bytes 73736 | tf_op jit(solution)/shard_map/ppermute | solution.py:533

commit v6 on v5

--- a/solution.py
+++ b/solution.py
@@ -247,20 +247,31 @@
             vel[h, i, 2, 2] += jnp.where(mask, rows[i][:, 128 * h : 128 * h + 128], 0.0)
 
 
-def jump_gradients(vel, halo, grads, perms, yj, zj):
+def jump_gradients(vel, halo, grads, plain, perms, yj, zj):
     along = Along(D_LIFT)
     jumps(vel, (0, 1, 2), 0, perms, yj, zj)
+    own = Along.by_row(lax.broadcasted_iota(jnp.int32, (8, 128), 0), [-5.0, 0.0, 0.0, 0.0, 5.0])
 
     def one(i, h):
         for a in range(5):
-            ys = derive_rows([vel[h, i, a, b] for b in range(5)], D_LIFT)
+            v = [vel[h, i, a, b] for b in range(5)]
+            ys = derive_rows(v, D_LIFT)
+            zs = [along(v[b]) for b in range(5)]
+            if plain is not None:
+                for b in range(5):
+                    plain[h, 3 + i, a, b] = ys[b] + {0: -5.0, 4: 5.0}[b] * v[b] if b in (0, 4) else ys[b]
+                    plain[h, 6 + i, a, b] = zs[b] + own * v[b]
             ys[0] = ys[0] + yj[0, h, i, a]
             ys[4] = ys[4] + yj[1, h, i, a]
             for b in range(5):
                 grads[h, 3 + i, a, b] = ys[b]
-                grads[h, 6 + i, a, b] = along(vel[h, i, a, b]) + zj[h, i, a, b]
+                grads[h, 6 + i, a, b] = zs[b] + zj[h, i, a, b]
         for b in range(5):
-            xs = derive_rows([vel[h, i, a, b] for a in range(5)], D_LIFT)
+            v = [vel[h, i, a, b] for a in range(5)]
+            xs = derive_rows(v, D_LIFT)
+            if plain is not None:
+                for a in range(5):
+                    plain[h, i, a, b] = xs[a] + {0: -5.0, 4: 5.0}[a] * v[a] if a in (0, 4) else xs[a]
             xs[0] = xs[0] - 5.0 * halo[0, h, 3 + i, b]
             xs[4] = xs[4] + 5.0 * halo[1, h, 3 + i, b]
             for a in range(5):
@@ -359,8 +370,8 @@
 
 def forward_start_kernel(state_hbm, mat_hbm, nbr_hbm, one, two, acc, vel, stress, rinv, perms, yj, zj, state, mat, nbr, sems):
     first = fetch(nbr_hbm, nbr, sems.at[0])
+    third = fetch(state_hbm, state, sems.at[2])
     second = fetch(mat_hbm, mat, sems.at[1])
-    third = fetch(state_hbm, state, sems.at[2])
     first.wait()
     make_perms(nbr, perms)
     second.wait()
@@ -386,58 +397,75 @@
     plain_gradients(vel, end_grads)
 
 
-def finish_step(rows, vel_in, stress_in, lam, mu, rinv, perms, vel, stress, acc, halo, grads, yj, zj):
+def complete_step(rows, vel_in, stress_in, lam, mu, rinv, perms, vel, stress, acc, halo, grads, plain, yj, zj):
     finish_acceleration(acc, stress_in, rinv, halo, True)
     velocities(vel_in, vel, acc, rows)
-    jump_gradients(vel, halo, grads, perms, yj, zj)
+    jump_gradients(vel, halo, grads, plain, perms, yj, zj)
     update_stress(stress_in, stress, grads, lam, mu)
 
 
-def middle_kernel(kind, vel_in, stress_in, acc_in, lam, mu, rinv, perms, inject,
-                  near, far, r_near, r_far, one, two, vel, stress, acc, *rest):
-    next_acc, (halo, grads, yj, zj) = (rest[0], rest[1:]) if kind == "receiver" else (None, rest)
-    rows = [inject[i : i + 1] for i in range(3)] if kind == "receiver" else source_rows(0, *inject)
+def middle_common(rows, vel_in, stress_in, acc_in, lam, mu, rinv, perms, near, far, r_near, r_far,
+                  one, two, vel, stress, acc, next_acc, plain, halo, grads, yj, zj, with_v):
     zj[...] = jnp.zeros(zj.shape, f32)
     load_halo(halo, *(flat(r, r.shape[0] * 2) for r in (near, far, r_near, r_far)), 6)
     acc[...] = acc_in[...]
-    finish_step(rows, vel_in, stress_in, lam, mu, rinv, perms, vel, stress, acc, halo, grads, yj, zj)
-    if kind == "receiver":
-        local_acceleration(stress, rinv, next_acc, perms, yj, zj)
+    complete_step(rows, vel_in, stress_in, lam, mu, rinv, perms, vel, stress, acc, halo, grads, plain, yj, zj)
+    local_acceleration(stress, rinv, next_acc, perms, yj, zj)
 
     def values(a, h):
         out = [stress[h, k, a] for k in (0, 5, 4)]
-        if kind == "receiver":
+        if with_v:
             out += [vel[h, i, a] + time_step * next_acc[h, i, a] for i in range(3)]
         return out
 
     pack_faces(one, two, values)
 
 
-def last_kernel(vel_in, stress_in, acc_in, lam, mu, rinv, perms, inject,
-                near, far, r_near, r_far, out, vel, stress, acc, halo, grads, yj, zj):
+def forward_middle_kernel(vel_in, stress_in, acc_in, lam, mu, rinv, perms, where_ref, strength, near, far,
+                          one, two, vel, acc, next_acc, plain, stress, halo, grads, yj, zj):
+    middle_common(source_rows(0, where_ref, strength), vel_in, stress_in, acc_in, lam, mu, rinv, perms, near, far, near, far,
+                  one, two, vel, stress, acc, next_acc, plain, halo, grads, yj, zj, False)
+
+
+def adjoint_middle_kernel(vel_in, stress_in, acc_in, lam, mu, rinv, perms, inject, near, far, r_near, r_far, f_plain, f_acc,
+                          one, two, vel, stress, next_acc, dense, acc, plain, halo, grads, yj, zj):
+    rows = [inject[i : i + 1] for i in range(3)]
+    middle_common(rows, vel_in, stress_in, acc_in, lam, mu, rinv, perms, near, far, r_near, r_far,
+                  one, two, vel, stress, acc, next_acc, plain, halo, grads, yj, zj, True)
+    image(f_plain, plain, f_acc, vel, dense, None)
+
+
+def last_kernel(vel_in, stress_in, acc_in, lam, mu, rinv, perms, inject, near, far, r_near, r_far,
+                out, vel, stress, acc, halo, grads, yj, zj, rows_out, sems):
     zj[...] = jnp.zeros(zj.shape, f32)
     load_halo(halo, *(flat(r, r.shape[0] * 2) for r in (near, far, r_near, r_far)), 6)
     acc[...] = acc_in[...]
     rows = [inject[8 + i : 9 + i] for i in range(3)]
-    finish_step(rows, vel_in, stress_in, lam, mu, rinv, perms, vel, stress, acc, halo, grads, yj, zj)
-    dst = flat(out, 2250)
-    for first, field, count in ((0, vel, 3), (3, stress, 6)):
-
+    finish_acceleration(acc, stress_in, rinv, halo, True)
+    velocities(vel_in, vel, acc, rows)
+    dst = flat(rows_out, 2250)
+
+    def leave(first, k, field):
+        for g in range(25):
+            for h in range(2):
+                dst[pl.ds(250 * (first + k) + 10 * g + h, 5, 2), :] = field[h, k, g // 5, g % 5, 0:5, :]
+        there = pl.ds(125 * (first + k), 125)
+        return pltpu.make_async_copy(rows_out.at[there], out.at[there], sems.at[first + k])
+
+    def leave_all(first, count, field):
         def one(k, carry):
-            for g in range(25):
-                for h in range(2):
-                    dst[pl.ds(250 * (first + k) + 10 * g + h, 5, 2), :] = field[h, k, g // 5, g % 5, 0:5, :]
+            leave(first, k, field).start()
             return carry
 
         lax.fori_loop(0, count, one, 0)
 
-
-def first_image_kernel(f_vel, f_acc, a_vel, f_stress, rinv, perms, dense, next_acc, fg, ag, yj, zj):
-    zj[...] = jnp.zeros(zj.shape, f32)
-    local_acceleration(f_stress, rinv, next_acc, perms, yj, zj)
-    plain_gradients(f_vel, fg)
-    plain_gradients(a_vel, ag)
-    image(fg, ag, f_acc, a_vel, dense, None)
+    leave_all(0, 3, vel)
+    jump_gradients(vel, halo, grads, None, perms, yj, zj)
+    update_stress(stress_in, stress, grads, lam, mu)
+    leave_all(3, 6, stress)
+    for k in range(9):
+        there = pl.ds(125 * k, 125)
+        pltpu.make_async_copy(rows_out.at[there], out.at[there], sems.at[k]).wait()
 
 
 def last_image_kernel(f_vel, acc_in, adj_vel, end_grads, first, rinv, where_ref, strength, near, far,
@@ -489,12 +517,12 @@
 HALO = pltpu.VMEM((2, 2, 7, 5, 8, 128), f32)
 
 
-def call(kernel, specs, outs, scratch, flops, moved):
+def call(kernel, specs, outs, scratch, flops, moved, where=V):
     return pl.pallas_call(
         kernel,
         out_shape=outs,
         in_specs=specs,
-        out_specs=jax.tree.map(lambda _: V, outs),
+        out_specs=jax.tree.map(lambda _: where, outs),
         scratch_shapes=scratch,
         compiler_params=pltpu.CompilerParams(vmem_limit_bytes=8 * 2**20),
         cost_estimate=pl.CostEstimate(flops=flops, bytes_accessed=moved, transcendentals=0),
@@ -563,36 +591,22 @@
     a_near, a_far = both_ways(a_one, a_two)
     adj_vel_end = a_vel
 
-    def middle(kind, vel, stress, acc, inject, near, far, faces):
-        if kind == "source":
-            kernel = lambda *refs: middle_kernel(kind, *refs[:7], refs[7:9], *refs[9:])
-            held = [S] * 2
-        else:
-            kernel = lambda *refs: middle_kernel(kind, *refs)
-            held = [V]
-        return call(
-            kernel,
-            [V] * 7 + held + [V] * 4,
-            (sends(faces), sends(faces), field(3), field(6), field(3)) + (() if kind == "source" else (field(3),)),
-            [HALO, scr(field(9))] + JUMPS,
-            2 * 10**8, 8 * 10**6,
-        )(vel, stress, acc, lam, mu, rinv, perms, *inject, near, far, f_near, f_far)
-
-    f_one, f_two, f_vel1, f_stress1, f_acc1 = middle(
-        "source", f_vel, f_stress, f_acc, (source_element, pulse), f_near, f_far, 3
-    )
+    f_one, f_two, f_vel1, f_acc1, f_acc2, f_plain = call(
+        forward_middle_kernel,
+        [V] * 7 + [S] * 2 + [V] * 2,
+        (sends(3), sends(3), field(3), field(3), field(3), field(9)),
+        [scr(field(6)), HALO, scr(field(9))] + JUMPS,
+        2 * 10**8, 8 * 10**6,
+    )(f_vel, f_stress, f_acc, lam, mu, rinv, perms, source_element, pulse, f_near, f_far)
     f_near2, f_far2 = both_ways(f_one, f_two)
-    a_one, a_two, a_vel1, a_stress1, _, a_acc2 = middle(
-        "receiver", a_vel, a_stress, a_acc, (injected,), a_near, a_far, 6
-    )
+    a_one, a_two, a_vel1, a_stress1, a_acc2, first = call(
+        adjoint_middle_kernel,
+        [V] * 14,
+        (sends(6), sends(6), field(3), field(6), field(3), shape(2, 384, 128)),
+        [scr(field(3)), scr(field(9)), HALO, scr(field(9))] + JUMPS,
+        2 * 10**8, 8 * 10**6,
+    )(a_vel, a_stress, a_acc, lam, mu, rinv, perms, injected, a_near, a_far, f_near, f_far, f_plain, f_acc1)
     a_near2, a_far2 = both_ways(a_one, a_two)
-    first, f_acc2 = call(
-        first_image_kernel,
-        [V] * 6,
-        (shape(2, 384, 128), field(3)),
-        [scr(field(9)), scr(field(9))] + JUMPS,
-        1000, 1000,
-    )(f_vel1, f_acc1, a_vel1, f_stress1, rinv, perms)
     keep, send = call(
         last_image_kernel,
         [V] * 6 + [S] * 2 + [V] * 2,
@@ -605,8 +619,10 @@
         last_kernel,
         [V] * 12,
         shape(1125, 2, 128),
-        [scr(field(3)), scr(field(6)), scr(field(3)), HALO, scr(field(9))] + JUMPS,
+        [scr(field(3)), scr(field(6)), scr(field(3)), HALO, scr(field(9))] + JUMPS
+        + [scr(shape(1125, 2, 128)), pltpu.SemaphoreType.DMA((9,))],
         10**8, 8 * 10**6,
+        pl.BlockSpec(memory_space=pltpu.HBM),
     )(a_vel1, a_stress1, a_acc2, lam, mu, rinv, perms, injected, a_near2, a_far2, f_near, f_far)
     return gradient.reshape(5, 5, 5, 3, 16).transpose(3, 0, 1, 2, 4), adjoint_end.reshape(1, 9, 5, 5, 5, N)
 

time: 50.3 us -> 50.6 us (level)
  Pallas kernels: 17.8 us -> 16 us
  waiting for transfers between devices: 6.87 us -> 8.11 us
  starting transfers between devices: 24.1 us -> 24.9 us
    pallas_call x3 -> x2, Pallas kernels: 7.34 us -> 5.61 us  [the longest x1 2.93 us: body(): call(forward_middle_kernel, [V] * 7 + [S] * 2 + [V] * 2, (sends(3), sends...]
    ppermute x4, starting transfers between devices: 8.57 us -> 10.1 us  [both_ways(): lax.ppermute(second, 'slab', far)]
    ppermute x4, waiting for transfers between devices: 0.01 us -> 1.24 us  [both_ways(): lax.ppermute(second, 'slab', far)]
  transfers between devices with their start and end apart: 13 -> 13, of which waited for: 4 -> 5; matrix products, arithmetic and copies ran while one was open for 0% -> 0% of each run, Pallas kernels for 25% -> 21%
where the time goes in v6:
time: 50.6 us; the launch traced here: 50.4 us
  starting transfers between devices  24.9 us (49%)
  Pallas kernels  16 us (32%)
  waiting for transfers between devices  8.11 us (16%)
  between operations  1.42 us (3%)
    ppermute x4, starting transfers between devices, both_ways(): lax.ppermute(second, 'slab', far)  10.1 us
    ppermute x5, starting transfers between devices, reduce_over_shots(): hop = lambda v, to: lax.ppermute(v, 'shot', [(i, to(i)) for i in range(16)])  9.47 us
    ppermute x4, starting transfers between devices, both_ways(): lax.ppermute(first, 'slab', near)  5.29 us
    ppermute x4, waiting for transfers between devices, both_ways(): lax.ppermute(first, 'slab', near)  4.22 us
    pallas_call x1, Pallas kernels, body(): call(forward_middle_kernel, [V] * 7 + [S] * 2 + [V] * 2, (sends(3), sends...  2.93 us
    pallas_call x1, Pallas kernels, body(): call(forward_start_kernel, [pl.BlockSpec(memory_space=pltpu.HBM)] * 3, (s...  2.88 us
    pallas_call x1, Pallas kernels, body(): call(adjoint_middle_kernel, [V] * 14, (sends(6), sends(6), field(3), fiel...  2.68 us
    ppermute x5, waiting for transfers between devices, reduce_over_shots(): hop = lambda v, to: lax.ppermute(v, 'shot', [(i, to(i)) for i in range(16)])  2.66 us
  transfers between devices with their start and end apart: 13, of which 5 were waited for; matrix products, arithmetic and copies ran while one was open for 0% of the time, Pallas kernels for 21%

profile of v6, /device:TPU:0, one launch (start us, length us, event | category | flops | bytes accessed | tf_op | source)
XLA Modules:
  0.0 50.4 jit_solution(13323646977809122868)
XLA Ops:
  0.7 2.9 %shard_map.95 = (f32[175,2,128]{2,1,0:T(2,128)S(1)}, f32[175,2,128]{2,1,0:T(2,128)S(1)}, f32[2,3,5,5,8,128]{5,4,3,2,1,0:T(8,128)S(1)}, f32[2,3,5,5,8,128]{5,4,3,...) custom-call(f32[1125,2,128]{2,1,0:T(2,128)} %bitcast.20, ...), custom_call_target="tpu_custom_call" | custom-call | flops 100000000 | bytes 4000000 | tf_op jit(solution)/shard_map/pallas_call | solution.py:576
  3.6 0.0 copy-start.3
  3.6 2.1 %collective-permute-start = (f32[175,2,128]{2,1,0:T(2,128)S(1)}, f32[175,2,128]{2,1,0:T(2,128)S(1)}, u32[]{:S(2)}, u32[]{:S(2)}) collective-permute-start(f32[175,2,128]{2,1,0:T(2,128)S(1)} %get-tuple-element.45), channel_id=1, source_target_pairs={{0,16},{16,0},{32,48},{48,32},{64,80},{80,64},{96,112},{112,96},{1... | collective-permute-start | bytes 537608 | tf_op jit(solution)/shard_map/ppermute | solution.py:536
  5.7 2.6 %collective-permute-start.1 = (f32[175,2,128]{2,1,0:T(2,128)S(1)}, f32[175,2,128]{2,1,0:T(2,128)S(1)}, u32[]{:S(2)}, u32[]{:S(2)}) collective-permute-start(f32[175,2,128]{2,1,0:T(2,128)S(1)} %get-tuple-element.46), channel_id=1, source_target_pairs={{0,112},{16,32},{32,16},{48,64},{64,48},{80,96},{96,80},{112,0},{1... | collective-permute-start | bytes 537608 | tf_op jit(solution)/shard_map/ppermute | solution.py:536
  8.2 2.3 %shard_map.96 = (f32[150,2,128]{2,1,0:T(2,128)S(1)}, f32[150,2,128]{2,1,0:T(2,128)S(1)}, f32[2,3,5,5,8,128]{5,4,3,2,1,0:T(8,128)S(1)}, f32[2,3,5,5,8,128]{5,4,3,...) custom-call(f32[1125,2,128]{2,1,0:T(2,128)S(1)} %bitcast.16, ...), custom_call_target="tpu_custom_call" | custom-call | flops 100000000 | bytes 4000000 | tf_op jit(solution)/shard_map/pallas_call | solution.py:584
  10.6 0.6 %collective-permute-start.2 = (f32[150,2,128]{2,1,0:T(2,128)S(1)}, f32[150,2,128]{2,1,0:T(2,128)S(1)}, u32[]{:S(2)}, u32[]{:S(2)}) collective-permute-start(f32[150,2,128]{2,1,0:T(2,128)S(1)} %get-tuple-element.54), channel_id=1, source_target_pairs={{0,16},{16,0},{32,48},{48,32},{64,80},{80,64},{96,112},{112,96},{1... | collective-permute-start | bytes 460808 | tf_op jit(solution)/shard_map/ppermute | solution.py:536
  11.1 1.7 %collective-permute-start.3 = (f32[150,2,128]{2,1,0:T(2,128)S(1)}, f32[150,2,128]{2,1,0:T(2,128)S(1)}, u32[]{:S(2)}, u32[]{:S(2)}) collective-permute-start(f32[150,2,128]{2,1,0:T(2,128)S(1)} %get-tuple-element.55), channel_id=1, source_target_pairs={{0,112},{16,32},{32,16},{48,64},{64,48},{80,96},{96,80},{112,0},{1... | collective-permute-start | bytes 460808 | tf_op jit(solution)/shard_map/ppermute | solution.py:536
  13.5 4.2 %collective-permute-done.near.r_near = f32[175,2,128]{2,1,0:T(2,128)S(1)} collective-permute-done((f32[175,2,128]{2,1,0:T(2,128)S(1)}, f32[175,2,128]{2,1,0:T(2,128)S(1)}, u32[]{:S(2)}, u32[]{:S(2)}) %collective-permute-start) | collective-permute-done | bytes 179232 | tf_op jit(solution)/shard_map/ppermute | solution.py:536
  17.7 0.0 collective-permute-done.1.far.r_far
  17.7 2.9 %shard_map.97 = (f32[75,2,128]{2,1,0:T(2,128)S(1)}, f32[75,2,128]{2,1,0:T(2,128)S(1)}, f32[2,3,5,5,8,128]{5,4,3,2,1,0:T(8,128)S(1)}, f32[2,3,5,5,8,128]{5,4,3,2,...) custom-call(f32[2,3,5,5,8,128]{5,4,3,2,1,0:T(8,128)S(1)} %get-tuple-element.38.vel_in, ...), custom_call_target="tpu_custom_call" | custom-call | flops 200000000 | bytes 8000000 | tf_op jit(solution)/shard_map/pallas_call | solution.py:594
  20.6 2.6 %collective-permute-start.4 = (f32[75,2,128]{2,1,0:T(2,128)S(1)}, f32[75,2,128]{2,1,0:T(2,128)S(1)}, u32[]{:S(2)}, u32[]{:S(2)}) collective-permute-start(f32[75,2,128]{2,1,0:T(2,128)S(1)} %get-tuple-element.59), channel_id=1, source_target_pairs={{0,16},{16,0},{32,48},{48,32},{64,80},{80,64},{96,112},{112,96},{1... | collective-permute-start | bytes 230408 | tf_op jit(solution)/shard_map/ppermute | solution.py:536
  23.2 2.6 %collective-permute-start.5 = (f32[75,2,128]{2,1,0:T(2,128)S(1)}, f32[75,2,128]{2,1,0:T(2,128)S(1)}, u32[]{:S(2)}, u32[]{:S(2)}) collective-permute-start(f32[75,2,128]{2,1,0:T(2,128)S(1)} %get-tuple-element.60), channel_id=1, source_target_pairs={{0,112},{16,32},{32,16},{48,64},{64,48},{80,96},{96,80},{112,0},{1... | collective-permute-start | bytes 230408 | tf_op jit(solution)/shard_map/ppermute | solution.py:536
  25.8 0.0 collective-permute-done.2.near
  25.8 0.0 collective-permute-done.3.far
  25.8 2.7 %shard_map.98 = (f32[150,2,128]{2,1,0:T(2,128)S(1)}, f32[150,2,128]{2,1,0:T(2,128)S(1)}, f32[2,3,5,5,8,128]{5,4,3,2,1,0:T(8,128)S(1)}, f32[2,6,5,5,8,128]{5,4,3,...) custom-call(f32[2,3,5,5,8,128]{5,4,3,2,1,0:T(8,128)S(1)} %get-tuple-element.49.vel_in.adj_vel, ...), custom_call_target="tpu_custom_call" | custom-call | flops 200000000 | bytes 8000000 | tf_op jit(solution)/shard_map/pallas_call | solution.py:602
  28.5 0.0 collective-permute-done.4.near
  28.5 1.2 %collective-permute-done.5.far = f32[75,2,128]{2,1,0:T(2,128)S(1)} collective-permute-done((f32[75,2,128]{2,1,0:T(2,128)S(1)}, f32[75,2,128]{2,1,0:T(2,128)S(1)}, u32[]{:S(2)}, u32[]{:S(2)}) %collective-permute-start.5) | collective-permute-done | bytes 76832 | tf_op jit(solution)/shard_map/ppermute | solution.py:536
  29.7 1.8 %shard_map.99 = (f32[8,16,384]{2,1,0:T(8,128)S(1)}, f32[8,16,384]{2,1,0:T(8,128)S(1)}) custom-call(f32[2,3,5,5,8,128]{5,4,3,2,1,0:T(8,128)S(1)} %get-tuple-element.47.f_vel, f32[2,3,5,5,8,128]{5,4,3,2,1,0:T(8,128)S(1)} %get-tuple-element.48.acc_in, f32[2,3,5,5,8,128]{5,4,3,2,1,0:T(8,128)S(1)} %get-tuple-element.49.vel_in.adj_vel, ...), custom_call_target="tpu_custom_call" | custom-call | flops 1000 | bytes 1000 | tf_op jit(solution)/shard_map/pallas_call | solution.py:610
  31.5 0.1 collective-permute-start.6
  31.6 0.1 collective-permute-start.11
  31.7 3.3 %collective-permute-start.12 = (f32[150,2,128]{2,1,0:T(2,128)S(1)}, f32[150,2,128]{2,1,0:T(2,128)S(1)}, u32[]{:S(2)}, u32[]{:S(2)}) collective-permute-start(f32[150,2,128]{2,1,0:T(2,128)S(1)} %get-tuple-element.73), channel_id=1, source_target_pairs={{0,112},{16,32},{32,16},{48,64},{64,48},{80,96},{96,80},{112,0},{1... | collective-permute-start | bytes 460808 | tf_op jit(solution)/shard_map/ppermute | solution.py:536
  35.0 0.0 collective-permute-done.6.got
  35.0 1.6 %collective-permute-start.7 = (f32[2,16,384]{2,1,0:T(8,128)S(1)}, f32[2,16,384]{2,1,0:T(8,128)S(1)}, u32[]{:S(2)}, u32[]{:S(2)}) collective-permute-start(f32[2,16,384]{2,1,0:T(8,128)S(1)} %get-tuple-element.64), channel_id=1, source_target_pairs={{0,4},{1,5},{2,6},{3,7},{4,8},{5,9},{6,10},{7,11},{8,12},{9,13},{1... | collective-permute-start | bytes 147464 | tf_op jit(solution)/shard_map/ppermute | solution.py:561
  36.6 2.7 %collective-permute-start.8 = (f32[2,16,384]{2,1,0:T(8,128)S(1)}, f32[2,16,384]{2,1,0:T(8,128)S(1)}, u32[]{:S(2)}, u32[]{:S(2)}) collective-permute-start(f32[2,16,384]{2,1,0:T(8,128)S(1)} %get-tuple-element.65), channel_id=1, source_target_pairs={{0,8},{1,9},{2,10},{3,11},{4,12},{5,13},{6,14},{7,15},{8,0},{9,1},... | collective-permute-start | bytes 147464 | tf_op jit(solution)/shard_map/ppermute | solution.py:561
  39.3 1.4 %collective-permute-start.9 = (f32[2,16,384]{2,1,0:T(8,128)S(1)}, f32[2,16,384]{2,1,0:T(8,128)S(1)}, u32[]{:S(2)}, u32[]{:S(2)}) collective-permute-start(f32[2,16,384]{2,1,0:T(8,128)S(1)} %get-tuple-element.66), channel_id=1, source_target_pairs={{0,12},{1,13},{2,14},{3,15},{4,0},{5,1},{6,2},{7,3},{8,4},{9,5},{1... | collective-permute-start | bytes 147464 | tf_op jit(solution)/shard_map/ppermute | solution.py:561
  40.8 0.2 collective-permute-done.7.one
  40.9 1.3 %collective-permute-done.8.two = f32[2,16,384]{2,1,0:T(8,128)S(1)} collective-permute-done((f32[2,16,384]{2,1,0:T(8,128)S(1)}, f32[2,16,384]{2,1,0:T(8,128)S(1)}, u32[]{:S(2)}, u32[]{:S(2)}) %collective-permute-start.8) | collective-permute-done | bytes 49184 | tf_op jit(solution)/shard_map/ppermute | solution.py:561
  42.2 1.2 %collective-permute-done.9.three = f32[2,16,384]{2,1,0:T(8,128)S(1)} collective-permute-done((f32[2,16,384]{2,1,0:T(8,128)S(1)}, f32[2,16,384]{2,1,0:T(8,128)S(1)}, u32[]{:S(2)}, u32[]{:S(2)}) %collective-permute-start.9) | collective-permute-done | bytes 49184 | tf_op jit(solution)/shard_map/ppermute | solution.py:561
  43.4 3.7 %collective-permute-start.10 = (f32[16,384]{1,0:T(8,128)S(1)}, f32[16,384]{1,0:T(8,128)S(1)}, u32[]{:S(2)}, u32[]{:S(2)}) collective-permute-start(f32[16,384]{1,0:T(8,128)S(1)} %get-tuple-element.68), channel_id=1, source_target_pairs={{0,2},{1,3},{2,0},{3,1},{4,6},{5,7},{6,4},{7,5},{8,10},{9,11},{10,... | collective-permute-start | bytes 73736 | tf_op jit(solution)/shard_map/ppermute | solution.py:561
  47.1 2.4 %shard_map.103 = f32[1125,2,128]{2,1,0:T(2,128)} custom-call(f32[2,3,5,5,8,128]{5,4,3,2,1,0:T(8,128)S(1)} %get-tuple-element.69.vel_in, f32[2,6,5,5,8,128]{5,4,3,2,1,0:T(8,128)S(1)} %get-tuple-element.70.stress_in, f32[2,3,5,5,8,128]{5,4,3,2,1,0:T(8,128)S(1)} %get-tuple-element.71.acc_in, f32[2,5,5,8,128]{4,3,2,1,0:T(8,128)S(1)} %get-tuple-element.43.lam, ...), custom_call_target="tpu_custom_call" | custom-call | flops 100000000 | bytes 8000000 | tf_op jit(solution)/shard_map/pallas_call | solution.py:618
  49.5 0.0 collective-permute-done.10.got
  49.6 0.9 %shard_map.102 = f32[125,3,16]{2,1,0:T(4,128)} custom-call(f32[16,384]{1,0:T(8,128)S(1)} %get-tuple-element.67.keep, f32[16,384]{1,0:T(8,128)S(1)} %collective-permute-done.10.got), custom_call_target="tpu_custom_call" | custom-call | flops 1000 | bytes 1000 | tf_op jit(solution)/shard_map/pallas_call | solution.py:566
  (13 shorter events, 0.1 us)
Async XLA Ops:
  0.6 7.6 %copy-start = (f32[3,5,5,5,256]{4,0,3,2,1:T(4,128)S(1)}, f32[3,5,5,5,256]{4,0,3,2,1:T(4,128)}, u32[]{:S(2)}) copy-start(f32[3,5,5,5,256]{4,0,3,2,1:T(4,128)} %param.10) | copy-start | bytes 1152004
  0.6 7.6 %copy-start.2 = (f32[1,2,3,256]{3,1,2,0:T(2,128)S(1)}, f32[1,2,3,256]{3,1,2,0:T(2,128)}, u32[]{:S(2)}) copy-start(f32[1,2,3,256]{3,1,2,0:T(2,128)} %param.15) | copy-start | bytes 18436
  0.7 7.6 %copy-start.4 = (s32[256]{0:T(256)S(1)}, s32[256]{0:T(256)}, u32[]{:S(2)}) copy-start(s32[256]{0:T(256)} %param.14) | copy-start | bytes 3076
  0.7 7.6 %copy-start.1 = (f32[1,9,5,5,5,256]{5,0,4,3,2,1:T(1,128)S(1)}, f32[1,9,5,5,5,256]{5,0,4,3,2,1:T(1,128)}, u32[]{:S(2)}) copy-start(f32[1,9,5,5,5,256]{5,0,4,3,2,1:T(1,128)} %param.9) | copy-start | bytes 3456004
  3.6 14.1 %copy-start.3 = (f32[1,2,3]{2,1,0:T(2,128)S(1)}, f32[1,2,3]{2,1,0:T(2,128)}, u32[]{:S(2)}) copy-start(f32[1,2,3]{2,1,0:T(2,128)} %strength.3) | copy-start | bytes 76
  3.6 14.1 %collective-permute-start = (f32[175,2,128]{2,1,0:T(2,128)S(1)}, f32[175,2,128]{2,1,0:T(2,128)S(1)}, u32[]{:S(2)}, u32[]{:S(2)}) collective-permute-start(f32[175,2,128]{2,1,0:T(2,128)S(1)} %get-tuple-element.45), channel_id=1, source_target_pairs={{0,16},{16,0},{32,48},{48,32},{64,80},{80,64},{96,112},{112,96},{1... | collective-permute-start | bytes 537608 | tf_op jit(solution)/shard_map/ppermute | solution.py:536
  5.7 12.1 %collective-permute-start.1 = (f32[175,2,128]{2,1,0:T(2,128)S(1)}, f32[175,2,128]{2,1,0:T(2,128)S(1)}, u32[]{:S(2)}, u32[]{:S(2)}) collective-permute-start(f32[175,2,128]{2,1,0:T(2,128)S(1)} %get-tuple-element.46), channel_id=1, source_target_pairs={{0,112},{16,32},{32,16},{48,64},{64,48},{80,96},{96,80},{112,0},{1... | collective-permute-start | bytes 537608 | tf_op jit(solution)/shard_map/ppermute | solution.py:536
  10.6 15.2 %collective-permute-start.2 = (f32[150,2,128]{2,1,0:T(2,128)S(1)}, f32[150,2,128]{2,1,0:T(2,128)S(1)}, u32[]{:S(2)}, u32[]{:S(2)}) collective-permute-start(f32[150,2,128]{2,1,0:T(2,128)S(1)} %get-tuple-element.54), channel_id=1, source_target_pairs={{0,16},{16,0},{32,48},{48,32},{64,80},{80,64},{96,112},{112,96},{1... | collective-permute-start | bytes 460808 | tf_op jit(solution)/shard_map/ppermute | solution.py:536
  11.1 14.7 %collective-permute-start.3 = (f32[150,2,128]{2,1,0:T(2,128)S(1)}, f32[150,2,128]{2,1,0:T(2,128)S(1)}, u32[]{:S(2)}, u32[]{:S(2)}) collective-permute-start(f32[150,2,128]{2,1,0:T(2,128)S(1)} %get-tuple-element.55), channel_id=1, source_target_pairs={{0,112},{16,32},{32,16},{48,64},{64,48},{80,96},{96,80},{112,0},{1... | collective-permute-start | bytes 460808 | tf_op jit(solution)/shard_map/ppermute | solution.py:536
  20.6 7.8 %collective-permute-start.4 = (f32[75,2,128]{2,1,0:T(2,128)S(1)}, f32[75,2,128]{2,1,0:T(2,128)S(1)}, u32[]{:S(2)}, u32[]{:S(2)}) collective-permute-start(f32[75,2,128]{2,1,0:T(2,128)S(1)} %get-tuple-element.59), channel_id=1, source_target_pairs={{0,16},{16,0},{32,48},{48,32},{64,80},{80,64},{96,112},{112,96},{1... | collective-permute-start | bytes 230408 | tf_op jit(solution)/shard_map/ppermute | solution.py:536
  23.2 6.5 %collective-permute-start.5 = (f32[75,2,128]{2,1,0:T(2,128)S(1)}, f32[75,2,128]{2,1,0:T(2,128)S(1)}, u32[]{:S(2)}, u32[]{:S(2)}) collective-permute-start(f32[75,2,128]{2,1,0:T(2,128)S(1)} %get-tuple-element.60), channel_id=1, source_target_pairs={{0,112},{16,32},{32,16},{48,64},{64,48},{80,96},{96,80},{112,0},{1... | collective-permute-start | bytes 230408 | tf_op jit(solution)/shard_map/ppermute | solution.py:536
  31.5 3.5 %collective-permute-start.6 = (f32[8,16,384]{2,1,0:T(8,128)S(1)}, f32[8,16,384]{2,1,0:T(8,128)S(1)}, u32[]{:S(2)}, u32[]{:S(2)}) collective-permute-start(f32[8,16,384]{2,1,0:T(8,128)S(1)} %get-tuple-element.62), channel_id=1, source_target_pairs={{0,1},{1,0},{2,3},{3,2},{4,5},{5,4},{6,7},{7,6},{8,9},{9,8},{10,11... | collective-permute-start | bytes 589832 | tf_op jit(solution)/shard_map/ppermute | solution.py:561
  31.6 15.5 %collective-permute-start.11 = (f32[150,2,128]{2,1,0:T(2,128)S(1)}, f32[150,2,128]{2,1,0:T(2,128)S(1)}, u32[]{:S(2)}, u32[]{:S(2)}) collective-permute-start(f32[150,2,128]{2,1,0:T(2,128)S(1)} %get-tuple-element.72), channel_id=1, source_target_pairs={{0,16},{16,0},{32,48},{48,32},{64,80},{80,64},{96,112},{112,96},{1... | collective-permute-start | bytes 460808 | tf_op jit(solution)/shard_map/ppermute | solution.py:536
  31.7 15.4 %collective-permute-start.12 = (f32[150,2,128]{2,1,0:T(2,128)S(1)}, f32[150,2,128]{2,1,0:T(2,128)S(1)}, u32[]{:S(2)}, u32[]{:S(2)}) collective-permute-start(f32[150,2,128]{2,1,0:T(2,128)S(1)} %get-tuple-element.73), channel_id=1, source_target_pairs={{0,112},{16,32},{32,16},{48,64},{64,48},{80,96},{96,80},{112,0},{1... | collective-permute-start | bytes 460808 | tf_op jit(solution)/shard_map/ppermute | solution.py:536
  35.0 5.9 %collective-permute-start.7 = (f32[2,16,384]{2,1,0:T(8,128)S(1)}, f32[2,16,384]{2,1,0:T(8,128)S(1)}, u32[]{:S(2)}, u32[]{:S(2)}) collective-permute-start(f32[2,16,384]{2,1,0:T(8,128)S(1)} %get-tuple-element.64), channel_id=1, source_target_pairs={{0,4},{1,5},{2,6},{3,7},{4,8},{5,9},{6,10},{7,11},{8,12},{9,13},{1... | collective-permute-start | bytes 147464 | tf_op jit(solution)/shard_map/ppermute | solution.py:561
  36.6 5.6 %collective-permute-start.8 = (f32[2,16,384]{2,1,0:T(8,128)S(1)}, f32[2,16,384]{2,1,0:T(8,128)S(1)}, u32[]{:S(2)}, u32[]{:S(2)}) collective-permute-start(f32[2,16,384]{2,1,0:T(8,128)S(1)} %get-tuple-element.65), channel_id=1, source_target_pairs={{0,8},{1,9},{2,10},{3,11},{4,12},{5,13},{6,14},{7,15},{8,0},{9,1},... | collective-permute-start | bytes 147464 | tf_op jit(solution)/shard_map/ppermute | solution.py:561
  39.3 4.1 %collective-permute-start.9 = (f32[2,16,384]{2,1,0:T(8,128)S(1)}, f32[2,16,384]{2,1,0:T(8,128)S(1)}, u32[]{:S(2)}, u32[]{:S(2)}) collective-permute-start(f32[2,16,384]{2,1,0:T(8,128)S(1)} %get-tuple-element.66), channel_id=1, source_target_pairs={{0,12},{1,13},{2,14},{3,15},{4,0},{5,1},{6,2},{7,3},{8,4},{9,5},{1... | collective-permute-start | bytes 147464 | tf_op jit(solution)/shard_map/ppermute | solution.py:561
  43.4 6.1 %collective-permute-start.10 = (f32[16,384]{1,0:T(8,128)S(1)}, f32[16,384]{1,0:T(8,128)S(1)}, u32[]{:S(2)}, u32[]{:S(2)}) collective-permute-start(f32[16,384]{1,0:T(8,128)S(1)} %get-tuple-element.68), channel_id=1, source_target_pairs={{0,2},{1,3},{2,0},{3,1},{4,6},{5,7},{6,4},{7,5},{8,10},{9,11},{10,... | collective-permute-start | bytes 73736 | tf_op jit(solution)/shard_map/ppermute | solution.py:561

commit v7 on v6

--- a/solution.py
+++ b/solution.py
@@ -129,10 +129,18 @@
 
 
 def stress_of(i, d):
+    if isinstance(i, int):
+        return i if i == d else 6 - i - d
     return jnp.where(i == d, i, 6 - i - d)
 
 
-def halves(count, one):
+def halves(count, one, unrolled=False):
+    if unrolled:
+        for k in range(count):
+            for h in range(2):
+                one(k, h)
+        return
+
     def step(t, carry):
         one(lax.div(t, 2), lax.rem(t, 2))
         return carry
@@ -157,7 +165,7 @@
             for a in range(5):
                 acc[h, i, a, b] = (acc[h, i, a, b] + xs[a]) * rinv[h, a, b]
 
-    halves(3, one)
+    halves(3, one, True)
 
 
 def load_fields(src, first, dst, count):
@@ -240,7 +248,7 @@
         for a in range(5):
             vel[h, i, a] = vel_in[h, i, a] + time_step * acc[h, i, a]
 
-    halves(3, one)
+    halves(3, one, True)
     mask = lax.broadcasted_iota(jnp.int32, (8, 128), 0) == 2
     for i in range(3):
         for h in range(2):
@@ -277,7 +285,7 @@
             for a in range(5):
                 grads[h, i, a, b] = xs[a]
 
-    halves(3, one)
+    halves(3, one, True)
 
 
 def update_stress(stress_in, stress, grads, lam, mu):
@@ -291,7 +299,7 @@
         stress[h, 4, a] = stress_in[h, 4, a] + m * (g(2, 0) + g(0, 2))
         stress[h, 5, a] = stress_in[h, 5, a] + m * (g(1, 0) + g(0, 1))
 
-    halves(5, one)
+    halves(5, one, True)
 
 
 def plain_gradients(vel, grads):
@@ -308,7 +316,7 @@
             for a in range(5):
                 grads[h, i, a, b] = xs[a]
 
-    halves(3, one)
+    halves(3, one, True)
 
 
 def image(fg, ag, acc, adj_vel, dense, first):
@@ -405,16 +413,17 @@
 
 
 def middle_common(rows, vel_in, stress_in, acc_in, lam, mu, rinv, perms, near, far, r_near, r_far,
-                  one, two, vel, stress, acc, next_acc, plain, halo, grads, yj, zj, with_v):
+                  one, two, vel, stress, acc, next_acc, plain, halo, grads, yj, zj):
     zj[...] = jnp.zeros(zj.shape, f32)
     load_halo(halo, *(flat(r, r.shape[0] * 2) for r in (near, far, r_near, r_far)), 6)
     acc[...] = acc_in[...]
     complete_step(rows, vel_in, stress_in, lam, mu, rinv, perms, vel, stress, acc, halo, grads, plain, yj, zj)
-    local_acceleration(stress, rinv, next_acc, perms, yj, zj)
+    if next_acc is not None:
+        local_acceleration(stress, rinv, next_acc, perms, yj, zj)
 
     def values(a, h):
         out = [stress[h, k, a] for k in (0, 5, 4)]
-        if with_v:
+        if next_acc is not None:
             out += [vel[h, i, a] + time_step * next_acc[h, i, a] for i in range(3)]
         return out
 
@@ -422,17 +431,18 @@
 
 
 def forward_middle_kernel(vel_in, stress_in, acc_in, lam, mu, rinv, perms, where_ref, strength, near, far,
-                          one, two, vel, acc, next_acc, plain, stress, halo, grads, yj, zj):
+                          one, two, vel, acc, plain, stress, halo, grads, yj, zj):
     middle_common(source_rows(0, where_ref, strength), vel_in, stress_in, acc_in, lam, mu, rinv, perms, near, far, near, far,
-                  one, two, vel, stress, acc, next_acc, plain, halo, grads, yj, zj, False)
-
-
-def adjoint_middle_kernel(vel_in, stress_in, acc_in, lam, mu, rinv, perms, inject, near, far, r_near, r_far, f_plain, f_acc,
-                          one, two, vel, stress, next_acc, dense, acc, plain, halo, grads, yj, zj):
+                  one, two, vel, stress, acc, None, plain, halo, grads, yj, zj)
+
+
+def adjoint_middle_kernel(vel_in, stress_in, acc_in, lam, mu, rinv, perms, inject, near, far, r_near, r_far, f_plain, f_acc, f_stress,
+                          one, two, vel, stress, next_acc, dense, f_next_acc, acc, plain, halo, grads, yj, zj):
     rows = [inject[i : i + 1] for i in range(3)]
     middle_common(rows, vel_in, stress_in, acc_in, lam, mu, rinv, perms, near, far, r_near, r_far,
-                  one, two, vel, stress, acc, next_acc, plain, halo, grads, yj, zj, True)
+                  one, two, vel, stress, acc, next_acc, plain, halo, grads, yj, zj)
     image(f_plain, plain, f_acc, vel, dense, None)
+    local_acceleration(f_stress, rinv, f_next_acc, perms, yj, zj)
 
 
 def last_kernel(vel_in, stress_in, acc_in, lam, mu, rinv, perms, inject, near, far, r_near, r_far,
@@ -591,21 +601,21 @@
     a_near, a_far = both_ways(a_one, a_two)
     adj_vel_end = a_vel
 
-    f_one, f_two, f_vel1, f_acc1, f_acc2, f_plain = call(
+    f_one, f_two, f_vel1, f_acc1, f_plain, f_stress1 = call(
         forward_middle_kernel,
         [V] * 7 + [S] * 2 + [V] * 2,
-        (sends(3), sends(3), field(3), field(3), field(3), field(9)),
-        [scr(field(6)), HALO, scr(field(9))] + JUMPS,
+        (sends(3), sends(3), field(3), field(3), field(9), field(6)),
+        [HALO, scr(field(9))] + JUMPS,
         2 * 10**8, 8 * 10**6,
     )(f_vel, f_stress, f_acc, lam, mu, rinv, perms, source_element, pulse, f_near, f_far)
     f_near2, f_far2 = both_ways(f_one, f_two)
-    a_one, a_two, a_vel1, a_stress1, a_acc2, first = call(
+    a_one, a_two, a_vel1, a_stress1, a_acc2, first, f_acc2 = call(
         adjoint_middle_kernel,
-        [V] * 14,
-        (sends(6), sends(6), field(3), field(6), field(3), shape(2, 384, 128)),
+        [V] * 15,
+        (sends(6), sends(6), field(3), field(6), field(3), shape(2, 384, 128), field(3)),
         [scr(field(3)), scr(field(9)), HALO, scr(field(9))] + JUMPS,
         2 * 10**8, 8 * 10**6,
-    )(a_vel, a_stress, a_acc, lam, mu, rinv, perms, injected, a_near, a_far, f_near, f_far, f_plain, f_acc1)
+    )(a_vel, a_stress, a_acc, lam, mu, rinv, perms, injected, a_near, a_far, f_near, f_far, f_plain, f_acc1, f_stress1)
     a_near2, a_far2 = both_ways(a_one, a_two)
     keep, send = call(
         last_image_kernel,

time: 50.6 us -> 49 us (0.968)
  Pallas kernels: 16 us -> 14.4 us
    pallas_call x1, Pallas kernels: 2.93 us -> 1.85 us  [body(): call(forward_middle_kernel, [V] * 7 + [S] * 2 + [V] * 2, (sends(3), sends...]
  transfers between devices with their start and end apart: 13 -> 13, of which waited for: 5 -> 5; matrix products, arithmetic and copies ran while one was open for 0% -> 0% of each run, Pallas kernels for 21% -> 19%
where the time goes in v7:
time: 49 us; the launch traced here: 48.8 us
  starting transfers between devices  24.9 us (51%)
  Pallas kernels  14.4 us (29%)
  waiting for transfers between devices  8.04 us (16%)
  between operations  1.42 us (3%)
    ppermute x4, starting transfers between devices, both_ways(): lax.ppermute(second, 'slab', far)  10.2 us
    ppermute x5, starting transfers between devices, reduce_over_shots(): hop = lambda v, to: lax.ppermute(v, 'shot', [(i, to(i)) for i in range(16)])  9.49 us
    ppermute x4, starting transfers between devices, both_ways(): lax.ppermute(first, 'slab', near)  5.24 us
    ppermute x4, waiting for transfers between devices, both_ways(): lax.ppermute(first, 'slab', near)  4.47 us
    pallas_call x1, Pallas kernels, body(): call(adjoint_middle_kernel, [V] * 15, (sends(6), sends(6), field(3), fiel...  2.98 us
    pallas_call x1, Pallas kernels, body(): call(forward_start_kernel, [pl.BlockSpec(memory_space=pltpu.HBM)] * 3, (s...  2.72 us
    ppermute x5, waiting for transfers between devices, reduce_over_shots(): hop = lambda v, to: lax.ppermute(v, 'shot', [(i, to(i)) for i in range(16)])  2.65 us
    pallas_call x1, Pallas kernels, body(): call(last_kernel, [V] * 12, shape(1125, 2, 128), [scr(field(3)), scr(fiel...  2.23 us
  transfers between devices with their start and end apart: 13, of which 5 were waited for; matrix products, arithmetic and copies ran while one was open for 0% of the time, Pallas kernels for 19%

profile of v7, /device:TPU:0, one launch (start us, length us, event | category | flops | bytes accessed | tf_op | source)
XLA Modules:
  0.0 48.8 jit_solution(7852258267946667783)
XLA Ops:
  0.7 2.7 %shard_map.95 = (f32[175,2,128]{2,1,0:T(2,128)S(1)}, f32[175,2,128]{2,1,0:T(2,128)S(1)}, f32[2,3,5,5,8,128]{5,4,3,2,1,0:T(8,128)S(1)}, f32[2,3,5,5,8,128]{5,4,3,...) custom-call(f32[1125,2,128]{2,1,0:T(2,128)} %bitcast.20, ...), custom_call_target="tpu_custom_call" | custom-call | flops 100000000 | bytes 4000000 | tf_op jit(solution)/shard_map/pallas_call | solution.py:586
  3.4 0.0 copy-start.3
  3.4 2.1 %collective-permute-start = (f32[175,2,128]{2,1,0:T(2,128)S(1)}, f32[175,2,128]{2,1,0:T(2,128)S(1)}, u32[]{:S(2)}, u32[]{:S(2)}) collective-permute-start(f32[175,2,128]{2,1,0:T(2,128)S(1)} %get-tuple-element.46), channel_id=1, source_target_pairs={{0,16},{16,0},{32,48},{48,32},{64,80},{80,64},{96,112},{112,96},{1... | collective-permute-start | bytes 537608 | tf_op jit(solution)/shard_map/ppermute | solution.py:546
  5.5 2.6 %collective-permute-start.1 = (f32[175,2,128]{2,1,0:T(2,128)S(1)}, f32[175,2,128]{2,1,0:T(2,128)S(1)}, u32[]{:S(2)}, u32[]{:S(2)}) collective-permute-start(f32[175,2,128]{2,1,0:T(2,128)S(1)} %get-tuple-element.47), channel_id=1, source_target_pairs={{0,112},{16,32},{32,16},{48,64},{64,48},{80,96},{96,80},{112,0},{1... | collective-permute-start | bytes 537608 | tf_op jit(solution)/shard_map/ppermute | solution.py:546
  8.1 2.0 %shard_map.96 = (f32[150,2,128]{2,1,0:T(2,128)S(1)}, f32[150,2,128]{2,1,0:T(2,128)S(1)}, f32[2,3,5,5,8,128]{5,4,3,2,1,0:T(8,128)S(1)}, f32[2,3,5,5,8,128]{5,4,3,...) custom-call(f32[1125,2,128]{2,1,0:T(2,128)S(1)} %bitcast.16, ...), custom_call_target="tpu_custom_call" | custom-call | flops 100000000 | bytes 4000000 | tf_op jit(solution)/shard_map/pallas_call | solution.py:594
  10.1 0.5 %collective-permute-start.2 = (f32[150,2,128]{2,1,0:T(2,128)S(1)}, f32[150,2,128]{2,1,0:T(2,128)S(1)}, u32[]{:S(2)}, u32[]{:S(2)}) collective-permute-start(f32[150,2,128]{2,1,0:T(2,128)S(1)} %get-tuple-element.53), channel_id=1, source_target_pairs={{0,16},{16,0},{32,48},{48,32},{64,80},{80,64},{96,112},{112,96},{1... | collective-permute-start | bytes 460808 | tf_op jit(solution)/shard_map/ppermute | solution.py:546
  10.7 1.8 %collective-permute-start.3 = (f32[150,2,128]{2,1,0:T(2,128)S(1)}, f32[150,2,128]{2,1,0:T(2,128)S(1)}, u32[]{:S(2)}, u32[]{:S(2)}) collective-permute-start(f32[150,2,128]{2,1,0:T(2,128)S(1)} %get-tuple-element.54), channel_id=1, source_target_pairs={{0,112},{16,32},{32,16},{48,64},{64,48},{80,96},{96,80},{112,0},{1... | collective-permute-start | bytes 460808 | tf_op jit(solution)/shard_map/ppermute | solution.py:546
  13.1 4.5 %collective-permute-done.near.r_near = f32[175,2,128]{2,1,0:T(2,128)S(1)} collective-permute-done((f32[175,2,128]{2,1,0:T(2,128)S(1)}, f32[175,2,128]{2,1,0:T(2,128)S(1)}, u32[]{:S(2)}, u32[]{:S(2)}) %collective-permute-start) | collective-permute-done | bytes 179232 | tf_op jit(solution)/shard_map/ppermute | solution.py:546
  17.5 0.0 collective-permute-done.1.far.r_far
  17.5 1.8 %shard_map.97 = (f32[75,2,128]{2,1,0:T(2,128)S(1)}, f32[75,2,128]{2,1,0:T(2,128)S(1)}, f32[2,3,5,5,8,128]{5,4,3,2,1,0:T(8,128)S(1)}, f32[2,3,5,5,8,128]{5,4,3,2,...) custom-call(f32[2,3,5,5,8,128]{5,4,3,2,1,0:T(8,128)S(1)} %get-tuple-element.39.vel_in, ...), custom_call_target="tpu_custom_call" | custom-call | flops 200000000 | bytes 8000000 | tf_op jit(solution)/shard_map/pallas_call | solution.py:604
  19.4 2.6 %collective-permute-start.4 = (f32[75,2,128]{2,1,0:T(2,128)S(1)}, f32[75,2,128]{2,1,0:T(2,128)S(1)}, u32[]{:S(2)}, u32[]{:S(2)}) collective-permute-start(f32[75,2,128]{2,1,0:T(2,128)S(1)} %get-tuple-element.61), channel_id=1, source_target_pairs={{0,16},{16,0},{32,48},{48,32},{64,80},{80,64},{96,112},{112,96},{1... | collective-permute-start | bytes 230408 | tf_op jit(solution)/shard_map/ppermute | solution.py:546
  21.9 2.6 %collective-permute-start.5 = (f32[75,2,128]{2,1,0:T(2,128)S(1)}, f32[75,2,128]{2,1,0:T(2,128)S(1)}, u32[]{:S(2)}, u32[]{:S(2)}) collective-permute-start(f32[75,2,128]{2,1,0:T(2,128)S(1)} %get-tuple-element.62), channel_id=1, source_target_pairs={{0,112},{16,32},{32,16},{48,64},{64,48},{80,96},{96,80},{112,0},{1... | collective-permute-start | bytes 230408 | tf_op jit(solution)/shard_map/ppermute | solution.py:546
  24.5 0.0 collective-permute-done.2.near
  24.5 0.0 collective-permute-done.3.far
  24.5 3.0 %shard_map.98 = (f32[150,2,128]{2,1,0:T(2,128)S(1)}, f32[150,2,128]{2,1,0:T(2,128)S(1)}, f32[2,3,5,5,8,128]{5,4,3,2,1,0:T(8,128)S(1)}, f32[2,6,5,5,8,128]{5,4,3,...) custom-call(f32[2,3,5,5,8,128]{5,4,3,2,1,0:T(8,128)S(1)} %get-tuple-, ...), custom_call_target="tpu_custom_call" | custom-call | flops 200000000 | bytes 8000000 | tf_op jit(solution)/shard_map/pallas_call | solution.py:612
  27.5 0.0 collective-permute-done.4.near
  27.5 0.9 %collective-permute-done.5.far = f32[75,2,128]{2,1,0:T(2,128)S(1)} collective-permute-done((f32[75,2,128]{2,1,0:T(2,128)S(1)}, f32[75,2,128]{2,1,0:T(2,128)S(1)}, u32[]{:S(2)}, u32[]{:S(2)}) %collective-permute-start.5) | collective-permute-done | bytes 76832 | tf_op jit(solution)/shard_map/ppermute | solution.py:546
  28.4 1.7 %shard_map.99 = (f32[8,16,384]{2,1,0:T(8,128)S(1)}, f32[8,16,384]{2,1,0:T(8,128)S(1)}) custom-call(f32[2,3,5,5,8,128]{5,4,3,2,1,0:T(8,128)S(1)} %get-tuple-element.48.f_vel, f32[2,3,5,5,8,128]{5,4,3,2,1,0:T(8,128)S(1)} %get-tuple-element.58.acc_in, f32[2,3,5,5,8,128]{5,4,3,2,1,0:T(8,128)S(1)} %get-tuple-element.49.vel_in.adj_vel, ...), custom_call_target="tpu_custom_call" | custom-call | flops 1000 | bytes 1000 | tf_op jit(solution)/shard_map/pallas_call | solution.py:620
  30.2 0.1 collective-permute-start.6
  30.2 0.1 collective-permute-start.11
  30.3 3.3 %collective-permute-start.12 = (f32[150,2,128]{2,1,0:T(2,128)S(1)}, f32[150,2,128]{2,1,0:T(2,128)S(1)}, u32[]{:S(2)}, u32[]{:S(2)}) collective-permute-start(f32[150,2,128]{2,1,0:T(2,128)S(1)} %get-tuple-element.75), channel_id=1, source_target_pairs={{0,112},{16,32},{32,16},{48,64},{64,48},{80,96},{96,80},{112,0},{1... | collective-permute-start | bytes 460808 | tf_op jit(solution)/shard_map/ppermute | solution.py:546
  33.6 1.6 %collective-permute-start.7 = (f32[2,16,384]{2,1,0:T(8,128)S(1)}, f32[2,16,384]{2,1,0:T(8,128)S(1)}, u32[]{:S(2)}, u32[]{:S(2)}) collective-permute-start(f32[2,16,384]{2,1,0:T(8,128)S(1)} %get-tuple-element.66), channel_id=1, source_target_pairs={{0,4},{1,5},{2,6},{3,7},{4,8},{5,9},{6,10},{7,11},{8,12},{9,13},{1... | collective-permute-start | bytes 147464 | tf_op jit(solution)/shard_map/ppermute | solution.py:571
  35.2 2.7 %collective-permute-start.8 = (f32[2,16,384]{2,1,0:T(8,128)S(1)}, f32[2,16,384]{2,1,0:T(8,128)S(1)}, u32[]{:S(2)}, u32[]{:S(2)}) collective-permute-start(f32[2,16,384]{2,1,0:T(8,128)S(1)} %get-tuple-element.67), channel_id=1, source_target_pairs={{0,8},{1,9},{2,10},{3,11},{4,12},{5,13},{6,14},{7,15},{8,0},{9,1},... | collective-permute-start | bytes 147464 | tf_op jit(solution)/shard_map/ppermute | solution.py:571
  37.9 1.4 %collective-permute-start.9 = (f32[2,16,384]{2,1,0:T(8,128)S(1)}, f32[2,16,384]{2,1,0:T(8,128)S(1)}, u32[]{:S(2)}, u32[]{:S(2)}) collective-permute-start(f32[2,16,384]{2,1,0:T(8,128)S(1)} %get-tuple-element.68), channel_id=1, source_target_pairs={{0,12},{1,13},{2,14},{3,15},{4,0},{5,1},{6,2},{7,3},{8,4},{9,5},{1... | collective-permute-start | bytes 147464 | tf_op jit(solution)/shard_map/ppermute | solution.py:571
  39.4 0.2 collective-permute-done.7.one
  39.5 1.3 %collective-permute-done.8.two = f32[2,16,384]{2,1,0:T(8,128)S(1)} collective-permute-done((f32[2,16,384]{2,1,0:T(8,128)S(1)}, f32[2,16,384]{2,1,0:T(8,128)S(1)}, u32[]{:S(2)}, u32[]{:S(2)}) %collective-permute-start.8) | collective-permute-done | bytes 49184 | tf_op jit(solution)/shard_map/ppermute | solution.py:571
  40.8 1.2 %collective-permute-done.9.three = f32[2,16,384]{2,1,0:T(8,128)S(1)} collective-permute-done((f32[2,16,384]{2,1,0:T(8,128)S(1)}, f32[2,16,384]{2,1,0:T(8,128)S(1)}, u32[]{:S(2)}, u32[]{:S(2)}) %collective-permute-start.9) | collective-permute-done | bytes 49184 | tf_op jit(solution)/shard_map/ppermute | solution.py:571
  42.0 3.7 %collective-permute-start.10 = (f32[16,384]{1,0:T(8,128)S(1)}, f32[16,384]{1,0:T(8,128)S(1)}, u32[]{:S(2)}, u32[]{:S(2)}) collective-permute-start(f32[16,384]{1,0:T(8,128)S(1)} %get-tuple-element.70), channel_id=1, source_target_pairs={{0,2},{1,3},{2,0},{3,1},{4,6},{5,7},{6,4},{7,5},{8,10},{9,11},{10,... | collective-permute-start | bytes 73736 | tf_op jit(solution)/shard_map/ppermute | solution.py:571
  45.7 0.0 collective-permute-done.11.near
  45.7 0.0 collective-permute-done.12.far
  45.7 2.2 %shard_map.103 = f32[1125,2,128]{2,1,0:T(2,128)} custom-call(f32[2,3,5,5,8,128]{5,4,3,2,1,0:T(8,128)S(1)} %get-tuple-element.71.vel_in, f32[2,6,5,5,8,128]{5,4,3,2,1,0:T(8,128)S(1)} %get-tuple-element.72.stress_in, f32[2,3,5,5,8,128]{5,4,3,2,1,0:T(8,128)S(1)} %get-tuple-element.73.acc_in, f32[2,5,5,8,128]{4,3,2,1,0:T(8,128)S(1)} %get-tuple-element.44.lam, ...), custom_call_target="tpu_custom_call" | custom-call | flops 100000000 | bytes 8000000 | tf_op jit(solution)/shard_map/pallas_call | solution.py:628
  48.0 0.9 %shard_map.102 = f32[125,3,16]{2,1,0:T(4,128)} custom-call(f32[16,384]{1,0:T(8,128)S(1)} %get-tuple-element.69.keep, f32[16,384]{1,0:T(8,128)S(1)} %collective-permute-done.10.got), custom_call_target="tpu_custom_call" | custom-call | flops 1000 | bytes 1000 | tf_op jit(solution)/shard_map/pallas_call | solution.py:576
  (13 shorter events, 0.1 us)
Async XLA Ops:
  0.6 7.4 %copy-start = (f32[3,5,5,5,256]{4,0,3,2,1:T(4,128)S(1)}, f32[3,5,5,5,256]{4,0,3,2,1:T(4,128)}, u32[]{:S(2)}) copy-start(f32[3,5,5,5,256]{4,0,3,2,1:T(4,128)} %param.10) | copy-start | bytes 1152004
  0.6 7.4 %copy-start.2 = (f32[1,2,3,256]{3,1,2,0:T(2,128)S(1)}, f32[1,2,3,256]{3,1,2,0:T(2,128)}, u32[]{:S(2)}) copy-start(f32[1,2,3,256]{3,1,2,0:T(2,128)} %param.15) | copy-start | bytes 18436
  0.7 7.4 %copy-start.4 = (s32[256]{0:T(256)S(1)}, s32[256]{0:T(256)}, u32[]{:S(2)}) copy-start(s32[256]{0:T(256)} %param.14) | copy-start | bytes 3076
  0.7 7.4 %copy-start.1 = (f32[1,9,5,5,5,256]{5,0,4,3,2,1:T(1,128)S(1)}, f32[1,9,5,5,5,256]{5,0,4,3,2,1:T(1,128)}, u32[]{:S(2)}) copy-start(f32[1,9,5,5,5,256]{5,0,4,3,2,1:T(1,128)} %param.9) | copy-start | bytes 3456004
  3.4 14.1 %copy-start.3 = (f32[1,2,3]{2,1,0:T(2,128)S(1)}, f32[1,2,3]{2,1,0:T(2,128)}, u32[]{:S(2)}) copy-start(f32[1,2,3]{2,1,0:T(2,128)} %strength.3) | copy-start | bytes 76
  3.4 14.1 %collective-permute-start = (f32[175,2,128]{2,1,0:T(2,128)S(1)}, f32[175,2,128]{2,1,0:T(2,128)S(1)}, u32[]{:S(2)}, u32[]{:S(2)}) collective-permute-start(f32[175,2,128]{2,1,0:T(2,128)S(1)} %get-tuple-element.46), channel_id=1, source_target_pairs={{0,16},{16,0},{32,48},{48,32},{64,80},{80,64},{96,112},{112,96},{1... | collective-permute-start | bytes 537608 | tf_op jit(solution)/shard_map/ppermute | solution.py:546
  5.5 12.1 %collective-permute-start.1 = (f32[175,2,128]{2,1,0:T(2,128)S(1)}, f32[175,2,128]{2,1,0:T(2,128)S(1)}, u32[]{:S(2)}, u32[]{:S(2)}) collective-permute-start(f32[175,2,128]{2,1,0:T(2,128)S(1)} %get-tuple-element.47), channel_id=1, source_target_pairs={{0,112},{16,32},{32,16},{48,64},{64,48},{80,96},{96,80},{112,0},{1... | collective-permute-start | bytes 537608 | tf_op jit(solution)/shard_map/ppermute | solution.py:546
  10.1 14.4 %collective-permute-start.2 = (f32[150,2,128]{2,1,0:T(2,128)S(1)}, f32[150,2,128]{2,1,0:T(2,128)S(1)}, u32[]{:S(2)}, u32[]{:S(2)}) collective-permute-start(f32[150,2,128]{2,1,0:T(2,128)S(1)} %get-tuple-element.53), channel_id=1, source_target_pairs={{0,16},{16,0},{32,48},{48,32},{64,80},{80,64},{96,112},{112,96},{1... | collective-permute-start | bytes 460808 | tf_op jit(solution)/shard_map/ppermute | solution.py:546
  10.7 13.9 %collective-permute-start.3 = (f32[150,2,128]{2,1,0:T(2,128)S(1)}, f32[150,2,128]{2,1,0:T(2,128)S(1)}, u32[]{:S(2)}, u32[]{:S(2)}) collective-permute-start(f32[150,2,128]{2,1,0:T(2,128)S(1)} %get-tuple-element.54), channel_id=1, source_target_pairs={{0,112},{16,32},{32,16},{48,64},{64,48},{80,96},{96,80},{112,0},{1... | collective-permute-start | bytes 460808 | tf_op jit(solution)/shard_map/ppermute | solution.py:546
  19.4 8.1 %collective-permute-start.4 = (f32[75,2,128]{2,1,0:T(2,128)S(1)}, f32[75,2,128]{2,1,0:T(2,128)S(1)}, u32[]{:S(2)}, u32[]{:S(2)}) collective-permute-start(f32[75,2,128]{2,1,0:T(2,128)S(1)} %get-tuple-element.61), channel_id=1, source_target_pairs={{0,16},{16,0},{32,48},{48,32},{64,80},{80,64},{96,112},{112,96},{1... | collective-permute-start | bytes 230408 | tf_op jit(solution)/shard_map/ppermute | solution.py:546
  21.9 6.5 %collective-permute-start.5 = (f32[75,2,128]{2,1,0:T(2,128)S(1)}, f32[75,2,128]{2,1,0:T(2,128)S(1)}, u32[]{:S(2)}, u32[]{:S(2)}) collective-permute-start(f32[75,2,128]{2,1,0:T(2,128)S(1)} %get-tuple-element.62), channel_id=1, source_target_pairs={{0,112},{16,32},{32,16},{48,64},{64,48},{80,96},{96,80},{112,0},{1... | collective-permute-start | bytes 230408 | tf_op jit(solution)/shard_map/ppermute | solution.py:546
  30.2 3.5 %collective-permute-start.6 = (f32[8,16,384]{2,1,0:T(8,128)S(1)}, f32[8,16,384]{2,1,0:T(8,128)S(1)}, u32[]{:S(2)}, u32[]{:S(2)}) collective-permute-start(f32[8,16,384]{2,1,0:T(8,128)S(1)} %get-tuple-element.64), channel_id=1, source_target_pairs={{0,1},{1,0},{2,3},{3,2},{4,5},{5,4},{6,7},{7,6},{8,9},{9,8},{10,11... | collective-permute-start | bytes 589832 | tf_op jit(solution)/shard_map/ppermute | solution.py:571
  30.2 15.5 %collective-permute-start.11 = (f32[150,2,128]{2,1,0:T(2,128)S(1)}, f32[150,2,128]{2,1,0:T(2,128)S(1)}, u32[]{:S(2)}, u32[]{:S(2)}) collective-permute-start(f32[150,2,128]{2,1,0:T(2,128)S(1)} %get-tuple-element.74), channel_id=1, source_target_pairs={{0,16},{16,0},{32,48},{48,32},{64,80},{80,64},{96,112},{112,96},{1... | collective-permute-start | bytes 460808 | tf_op jit(solution)/shard_map/ppermute | solution.py:546
  30.3 15.4 %collective-permute-start.12 = (f32[150,2,128]{2,1,0:T(2,128)S(1)}, f32[150,2,128]{2,1,0:T(2,128)S(1)}, u32[]{:S(2)}, u32[]{:S(2)}) collective-permute-start(f32[150,2,128]{2,1,0:T(2,128)S(1)} %get-tuple-element.75), channel_id=1, source_target_pairs={{0,112},{16,32},{32,16},{48,64},{64,48},{80,96},{96,80},{112,0},{1... | collective-permute-start | bytes 460808 | tf_op jit(solution)/shard_map/ppermute | solution.py:546
  33.6 5.9 %collective-permute-start.7 = (f32[2,16,384]{2,1,0:T(8,128)S(1)}, f32[2,16,384]{2,1,0:T(8,128)S(1)}, u32[]{:S(2)}, u32[]{:S(2)}) collective-permute-start(f32[2,16,384]{2,1,0:T(8,128)S(1)} %get-tuple-element.66), channel_id=1, source_target_pairs={{0,4},{1,5},{2,6},{3,7},{4,8},{5,9},{6,10},{7,11},{8,12},{9,13},{1... | collective-permute-start | bytes 147464 | tf_op jit(solution)/shard_map/ppermute | solution.py:571
  35.2 5.6 %collective-permute-start.8 = (f32[2,16,384]{2,1,0:T(8,128)S(1)}, f32[2,16,384]{2,1,0:T(8,128)S(1)}, u32[]{:S(2)}, u32[]{:S(2)}) collective-permute-start(f32[2,16,384]{2,1,0:T(8,128)S(1)} %get-tuple-element.67), channel_id=1, source_target_pairs={{0,8},{1,9},{2,10},{3,11},{4,12},{5,13},{6,14},{7,15},{8,0},{9,1},... | collective-permute-start | bytes 147464 | tf_op jit(solution)/shard_map/ppermute | solution.py:571
  37.9 4.1 %collective-permute-start.9 = (f32[2,16,384]{2,1,0:T(8,128)S(1)}, f32[2,16,384]{2,1,0:T(8,128)S(1)}, u32[]{:S(2)}, u32[]{:S(2)}) collective-permute-start(f32[2,16,384]{2,1,0:T(8,128)S(1)} %get-tuple-element.68), channel_id=1, source_target_pairs={{0,12},{1,13},{2,14},{3,15},{4,0},{5,1},{6,2},{7,3},{8,4},{9,5},{1... | collective-permute-start | bytes 147464 | tf_op jit(solution)/shard_map/ppermute | solution.py:571
  42.0 5.9 %collective-permute-start.10 = (f32[16,384]{1,0:T(8,128)S(1)}, f32[16,384]{1,0:T(8,128)S(1)}, u32[]{:S(2)}, u32[]{:S(2)}) collective-permute-start(f32[16,384]{1,0:T(8,128)S(1)} %get-tuple-element.70), channel_id=1, source_target_pairs={{0,2},{1,3},{2,0},{3,1},{4,6},{5,7},{6,4},{7,5},{8,10},{9,11},{10,... | collective-permute-start | bytes 73736 | tf_op jit(solution)/shard_map/ppermute | solution.py:571

commit v8 on v7

--- a/solution.py
+++ b/solution.py
@@ -319,15 +319,20 @@
     halves(3, one, True)
 
 
-def image(fg, ag, acc, adj_vel, dense, first):
+def reader(field, count):
+    return lambda h, a, b: [field[h, k, a, b] for k in range(count)]
+
+
+def image(f_read, g_read, acc_read, adj_vel, dense, first):
     row = lax.broadcasted_iota(jnp.int32, (8, 128), 0)
     weight = Along.by_row(row, QUAD)
 
     def one(k, h):
         for a in range(5):
             for b in range(5):
-                f = lambda j, i: fg[h, 3 * j + i, a, b]
-                g = lambda j, i: ag[h, 3 * j + i, a, b]
+                fs, gs, accs = f_read(h, a, b), g_read(h, a, b), acc_read(h, a, b)
+                f = lambda j, i: fs[3 * j + i]
+                g = lambda j, i: gs[3 * j + i]
                 w = weight * float(QUAD[a] * QUAD[b])
                 f0, f1, f2 = f(0, 0), f(1, 1), f(2, 2)
                 g0, g1, g2 = g(0, 0), g(1, 1), g(2, 2)
@@ -339,7 +344,7 @@
                 strain = (2.0 * (f0 * g0 + f1 * g1 + f2 * g2) + cross) * w
                 inertia = None
                 for i in range(3):
-                    term = acc[h, i, a, b] * adj_vel[h, i, a, b]
+                    term = accs[i] * adj_vel[h, i, a, b]
                     inertia = term if inertia is None else inertia + term
                 for t, term in enumerate((trace, strain, inertia * w)):
                     at = t * 125 + a * 25 + b * 5
@@ -437,12 +442,15 @@
 
 
 def adjoint_middle_kernel(vel_in, stress_in, acc_in, lam, mu, rinv, perms, inject, near, far, r_near, r_far, f_plain, f_acc, f_stress,
-                          one, two, vel, stress, next_acc, dense, f_next_acc, acc, plain, halo, grads, yj, zj):
+                          f_vel, where_ref, pulse,
+                          one, two, vel, stress, next_acc, dense, f_next_acc, f_early, acc, plain, halo, grads, yj, zj):
     rows = [inject[i : i + 1] for i in range(3)]
     middle_common(rows, vel_in, stress_in, acc_in, lam, mu, rinv, perms, near, far, r_near, r_far,
                   one, two, vel, stress, acc, next_acc, plain, halo, grads, yj, zj)
-    image(f_plain, plain, f_acc, vel, dense, None)
+    image(reader(f_plain, 9), reader(plain, 9), reader(f_acc, 3), vel, dense, None)
     local_acceleration(f_stress, rinv, f_next_acc, perms, yj, zj)
+    velocities(f_vel, acc, f_next_acc, source_rows(1, where_ref, pulse))
+    plain_gradients(acc, f_early)
 
 
 def last_kernel(vel_in, stress_in, acc_in, lam, mu, rinv, perms, inject, near, far, r_near, r_far,
@@ -478,16 +486,37 @@
         pltpu.make_async_copy(rows_out.at[there], out.at[there], sems.at[k]).wait()
 
 
-def last_image_kernel(f_vel, acc_in, adj_vel, end_grads, first, rinv, where_ref, strength, near, far,
-                      keep, send, halo, vel, acc, fg, dense):
+def last_image_kernel(acc, early, adj_vel, end_grads, first, rinv, near, far, keep, send, halo, change, turn, dense):
     load_halo(halo, flat(near, 150), flat(far, 150), None, None, 3)
-    acc[...] = acc_in[...]
-    finish_acceleration(acc, None, rinv, halo, False)
-    velocities(f_vel, vel, acc, source_rows(1, where_ref, strength))
-    plain_gradients(vel, fg)
+    along = Along(D_PLAIN)
+    for h in range(2):
+        for i in range(3):
+            for side, a in ((0, 0), (1, 4)):
+                d = (5.0 if side else -5.0) * rinv[h, a] * halo[side, h, i]
+                change[side, h, i] = d
+                ys = derive_rows([time_step * d[b] for b in range(5)], D_PLAIN)
+                for b in range(5):
+                    turn[side, h, i, b] = ys[b]
+                    turn[side, h, 3 + i, b] = along(time_step * d[b])
+
+    def f_read(h, a, b):
+        out = [early[h, k, a, b] for k in range(9)]
+        low, high = float(time_step * D_PLAIN[a, 0]), float(time_step * D_PLAIN[a, 4])
+        for i in range(3):
+            out[i] = out[i] + (low * change[0, h, i, b] + high * change[1, h, i, b])
+        if a in (0, 4):
+            for k in range(6):
+                out[3 + k] = out[3 + k] + turn[a // 4, h, k, b]
+        return out
+
+    def acc_read(h, a, b):
+        if a in (0, 4):
+            return [acc[h, i, a, b] + change[a // 4, h, i, b] for i in range(3)]
+        return [acc[h, i, a, b] for i in range(3)]
+
     for h in range(2):
         dense[h, 368:384, :] = jnp.zeros((16, 128), f32)
-    image(fg, end_grads, acc, adj_vel, dense, first)
+    image(f_read, reader(end_grads, 9), acc_read, adj_vel, dense, first)
     core = lax.rem(lax.axis_index("shot"), 2)
     turned = [dense[h].T for h in range(2)]
     for parity, (mine, other) in ((0, (keep, send)), (1, (send, keep))):
@@ -609,21 +638,21 @@
         2 * 10**8, 8 * 10**6,
     )(f_vel, f_stress, f_acc, lam, mu, rinv, perms, source_element, pulse, f_near, f_far)
     f_near2, f_far2 = both_ways(f_one, f_two)
-    a_one, a_two, a_vel1, a_stress1, a_acc2, first, f_acc2 = call(
+    a_one, a_two, a_vel1, a_stress1, a_acc2, first, f_acc2, f_early = call(
         adjoint_middle_kernel,
-        [V] * 15,
-        (sends(6), sends(6), field(3), field(6), field(3), shape(2, 384, 128), field(3)),
+        [V] * 16 + [S] * 2,
+        (sends(6), sends(6), field(3), field(6), field(3), shape(2, 384, 128), field(3), field(9)),
         [scr(field(3)), scr(field(9)), HALO, scr(field(9))] + JUMPS,
         2 * 10**8, 8 * 10**6,
-    )(a_vel, a_stress, a_acc, lam, mu, rinv, perms, injected, a_near, a_far, f_near, f_far, f_plain, f_acc1, f_stress1)
+    )(a_vel, a_stress, a_acc, lam, mu, rinv, perms, injected, a_near, a_far, f_near, f_far, f_plain, f_acc1, f_stress1, f_vel1, source_element, pulse)
     a_near2, a_far2 = both_ways(a_one, a_two)
     keep, send = call(
         last_image_kernel,
-        [V] * 6 + [S] * 2 + [V] * 2,
+        [V] * 8,
         (shape(8, 16, 384), shape(8, 16, 384)),
-        [HALO, scr(field(3)), scr(field(3)), scr(field(9)), scr(shape(2, 384, 128))],
+        [HALO, pltpu.VMEM((2, 2, 3, 5, 8, 128), f32), pltpu.VMEM((2, 2, 6, 5, 8, 128), f32), scr(shape(2, 384, 128))],
         1000, 1000,
-    )(f_vel1, f_acc2, adj_vel_end, end_grads, first, rinv, source_element, pulse, f_near2, f_far2)
+    )(f_acc2, f_early, adj_vel_end, end_grads, first, rinv, f_near2, f_far2)
     gradient = reduce_over_shots(keep, send)
     adjoint_end = call(
         last_kernel,

time: 49 us -> 48.1 us (0.982)
  waiting for transfers between devices: 8.04 us -> 7.12 us
    ppermute x4, waiting for transfers between devices: 0.92 us -> 0.01 us  [both_ways(): lax.ppermute(second, 'slab', far)]
    ppermute x4, starting transfers between devices: 10.2 us -> 9.44 us  [both_ways(): lax.ppermute(second, 'slab', far)]
  transfers between devices with their start and end apart: 13 -> 13, of which waited for: 5 -> 3; matrix products, arithmetic and copies ran while one was open for 0% -> 0% of each run, Pallas kernels for 19% -> 22%
where the time goes in v8:
time: 48.1 us; the launch traced here: 48 us
  starting transfers between devices  24.6 us (51%)
  Pallas kernels  14.8 us (31%)
  waiting for transfers between devices  7.12 us (15%)
  between operations  1.42 us (3%)
    ppermute x5, starting transfers between devices, reduce_over_shots(): hop = lambda v, to: lax.ppermute(v, 'shot', [(i, to(i)) for i in range(16)])  9.47 us
    ppermute x4, starting transfers between devices, both_ways(): lax.ppermute(second, 'slab', far)  9.44 us
    ppermute x4, starting transfers between devices, both_ways(): lax.ppermute(first, 'slab', near)  5.7 us
    ppermute x4, waiting for transfers between devices, both_ways(): lax.ppermute(first, 'slab', near)  4.44 us
    pallas_call x1, Pallas kernels, body(): call(adjoint_middle_kernel, [V] * 16 + [S] * 2, (sends(6), sends(6), fiel...  4.16 us
    pallas_call x1, Pallas kernels, body(): call(forward_start_kernel, [pl.BlockSpec(memory_space=pltpu.HBM)] * 3, (s...  2.74 us
    ppermute x5, waiting for transfers between devices, reduce_over_shots(): hop = lambda v, to: lax.ppermute(v, 'shot', [(i, to(i)) for i in range(16)])  2.67 us
    pallas_call x1, Pallas kernels, body(): call(last_kernel, [V] * 12, shape(1125, 2, 128), [scr(field(3)), scr(fiel...  2.3 us
  transfers between devices with their start and end apart: 13, of which 3 were waited for; matrix products, arithmetic and copies ran while one was open for 0% of the time, Pallas kernels for 22%

profile of v8, /device:TPU:0, one launch (start us, length us, event | category | flops | bytes accessed | tf_op | source)
XLA Modules:
  0.0 48.0 jit_solution(1950007203738348095)
XLA Ops:
  0.7 2.7 %shard_map.95 = (f32[175,2,128]{2,1,0:T(2,128)S(1)}, f32[175,2,128]{2,1,0:T(2,128)S(1)}, f32[2,3,5,5,8,128]{5,4,3,2,1,0:T(8,128)S(1)}, f32[2,3,5,5,8,128]{5,4,3,...) custom-call(f32[1125,2,128]{2,1,0:T(2,128)} %bitcast.20, ...), custom_call_target="tpu_custom_call" | custom-call | flops 100000000 | bytes 4000000 | tf_op jit(solution)/shard_map/pallas_call | solution.py:615
  3.4 0.0 copy-start.3
  3.4 2.1 %collective-permute-start.2 = (f32[175,2,128]{2,1,0:T(2,128)S(1)}, f32[175,2,128]{2,1,0:T(2,128)S(1)}, u32[]{:S(2)}, u32[]{:S(2)}) collective-permute-start(f32[175,2,128]{2,1,0:T(2,128)S(1)} %get-tuple-element.50), channel_id=1, source_target_pairs={{0,16},{16,0},{32,48},{48,32},{64,80},{80,64},{96,112},{112,96},{1... | collective-permute-start | bytes 537608 | tf_op jit(solution)/shard_map/ppermute | solution.py:575
  5.5 2.6 %collective-permute-start.3 = (f32[175,2,128]{2,1,0:T(2,128)S(1)}, f32[175,2,128]{2,1,0:T(2,128)S(1)}, u32[]{:S(2)}, u32[]{:S(2)}) collective-permute-start(f32[175,2,128]{2,1,0:T(2,128)S(1)} %get-tuple-element.51), channel_id=1, source_target_pairs={{0,112},{16,32},{32,16},{48,64},{64,48},{80,96},{96,80},{112,0},{1... | collective-permute-start | bytes 537608 | tf_op jit(solution)/shard_map/ppermute | solution.py:575
  8.1 2.1 %shard_map.96 = (f32[150,2,128]{2,1,0:T(2,128)S(1)}, f32[150,2,128]{2,1,0:T(2,128)S(1)}, f32[2,3,5,5,8,128]{5,4,3,2,1,0:T(8,128)S(1)}, f32[2,3,5,5,8,128]{5,4,3,...) custom-call(f32[1125,2,128]{2,1,0:T(2,128)S(1)} %bitcast.16, ...), custom_call_target="tpu_custom_call" | custom-call | flops 100000000 | bytes 4000000 | tf_op jit(solution)/shard_map/pallas_call | solution.py:623
  10.2 0.5 %collective-permute-start = (f32[150,2,128]{2,1,0:T(2,128)S(1)}, f32[150,2,128]{2,1,0:T(2,128)S(1)}, u32[]{:S(2)}, u32[]{:S(2)}) collective-permute-start(f32[150,2,128]{2,1,0:T(2,128)S(1)} %get-tuple-element.48), channel_id=1, source_target_pairs={{0,16},{16,0},{32,48},{48,32},{64,80},{80,64},{96,112},{112,96},{1... | collective-permute-start | bytes 460808 | tf_op jit(solution)/shard_map/ppermute | solution.py:575
  10.7 1.7 %collective-permute-start.1 = (f32[150,2,128]{2,1,0:T(2,128)S(1)}, f32[150,2,128]{2,1,0:T(2,128)S(1)}, u32[]{:S(2)}, u32[]{:S(2)}) collective-permute-start(f32[150,2,128]{2,1,0:T(2,128)S(1)} %get-tuple-element.49), channel_id=1, source_target_pairs={{0,112},{16,32},{32,16},{48,64},{64,48},{80,96},{96,80},{112,0},{1... | collective-permute-start | bytes 460808 | tf_op jit(solution)/shard_map/ppermute | solution.py:575
  13.1 4.4 %collective-permute-done.2.near.r_near = f32[175,2,128]{2,1,0:T(2,128)S(1)} collective-permute-done((f32[175,2,128]{2,1,0:T(2,128)S(1)}, f32[175,2,128]{2,1,0:T(2,128)S(1)}, u32[]{:S(2)}, u32[]{:S(2)}) %collective-permute-start.2) | collective-permute-done | bytes 179232 | tf_op jit(solution)/shard_map/ppermute | solution.py:575
  17.6 0.0 collective-permute-done.3.far.r_far
  17.6 1.8 %shard_map.97 = (f32[75,2,128]{2,1,0:T(2,128)S(1)}, f32[75,2,128]{2,1,0:T(2,128)S(1)}, f32[2,3,5,5,8,128]{5,4,3,2,1,0:T(8,128)S(1)}, f32[2,3,5,5,8,128]{5,4,3,2,...) custom-call(f32[2,3,5,5,8,128]{5,4,3,2,1,0:T(8,128)S(1)} %get-tuple-element.52.vel_in, ...), custom_call_target="tpu_custom_call" | custom-call | flops 200000000 | bytes 8000000 | tf_op jit(solution)/shard_map/pallas_call | solution.py:633
  19.4 2.6 %collective-permute-start.4 = (f32[75,2,128]{2,1,0:T(2,128)S(1)}, f32[75,2,128]{2,1,0:T(2,128)S(1)}, u32[]{:S(2)}, u32[]{:S(2)}) collective-permute-start(f32[75,2,128]{2,1,0:T(2,128)S(1)} %get-tuple-element.63), channel_id=1, source_target_pairs={{0,16},{16,0},{32,48},{48,32},{64,80},{80,64},{96,112},{112,96},{1... | collective-permute-start | bytes 230408 | tf_op jit(solution)/shard_map/ppermute | solution.py:575
  21.9 2.6 %collective-permute-start.5 = (f32[75,2,128]{2,1,0:T(2,128)S(1)}, f32[75,2,128]{2,1,0:T(2,128)S(1)}, u32[]{:S(2)}, u32[]{:S(2)}) collective-permute-start(f32[75,2,128]{2,1,0:T(2,128)S(1)} %get-tuple-element.64), channel_id=1, source_target_pairs={{0,112},{16,32},{32,16},{48,64},{64,48},{80,96},{96,80},{112,0},{1... | collective-permute-start | bytes 230408 | tf_op jit(solution)/shard_map/ppermute | solution.py:575
  24.5 0.0 collective-permute-done.near
  24.5 0.0 collective-permute-done.1.far
  24.5 4.2 %shard_map.98 = (f32[150,2,128]{2,1,0:T(2,128)S(1)}, f32[150,2,128]{2,1,0:T(2,128)S(1)}, f32[2,3,5,5,8,128]{5,4,3,2,1,0:T(8,128)S(1)}, f32[2,6,5,5,8,128]{5,4,3,...) custom-call(f32[2,3,5,5,8,128]{5,4,3,2,1,0:T(8,128)S(1)} %get-tuple-, ...), custom_call_target="tpu_custom_call" | custom-call | flops 200000000 | bytes 8000000 | tf_op jit(solution)/shard_map/pallas_call | solution.py:641
  28.7 0.0 collective-permute-done.4.near
  28.7 0.0 collective-permute-done.5.far
  28.7 0.8 %shard_map.99 = (f32[8,16,384]{2,1,0:T(8,128)S(1)}, f32[8,16,384]{2,1,0:T(8,128)S(1)}) custom-call(f32[2,3,5,5,8,128]{5,4,3,2,1,0:T(8,128)S(1)} %get-tuple-element.59.acc, f32[2,9,5,5,8,128]{5,4,3,2,1,0:T(8,128)S(1)} %get-tuple-element.60.early, f32[2,3,5,5,8,128]{5,4,3,2,1,0:T(8,128)S(1)} %get-tuple-element.42.vel_in.adj_vel, ...), custom_call_target="tpu_custom_call" | custom-call | flops 1000 | bytes 1000 | tf_op jit(solution)/shard_map/pallas_call | solution.py:649
  29.6 0.1 collective-permute-start.6
  29.7 0.5 %collective-permute-start.11 = (f32[150,2,128]{2,1,0:T(2,128)S(1)}, f32[150,2,128]{2,1,0:T(2,128)S(1)}, u32[]{:S(2)}, u32[]{:S(2)}) collective-permute-start(f32[150,2,128]{2,1,0:T(2,128)S(1)} %get-tuple-element.76), channel_id=1, source_target_pairs={{0,16},{16,0},{32,48},{48,32},{64,80},{80,64},{96,112},{112,96},{1... | collective-permute-start | bytes 460808 | tf_op jit(solution)/shard_map/ppermute | solution.py:575
  30.2 2.6 %collective-permute-start.12 = (f32[150,2,128]{2,1,0:T(2,128)S(1)}, f32[150,2,128]{2,1,0:T(2,128)S(1)}, u32[]{:S(2)}, u32[]{:S(2)}) collective-permute-start(f32[150,2,128]{2,1,0:T(2,128)S(1)} %get-tuple-element.77), channel_id=1, source_target_pairs={{0,112},{16,32},{32,16},{48,64},{64,48},{80,96},{96,80},{112,0},{1... | collective-permute-start | bytes 460808 | tf_op jit(solution)/shard_map/ppermute | solution.py:575
  32.7 0.0 collective-permute-done.6.got
  32.8 1.6 %collective-permute-start.7 = (f32[2,16,384]{2,1,0:T(8,128)S(1)}, f32[2,16,384]{2,1,0:T(8,128)S(1)}, u32[]{:S(2)}, u32[]{:S(2)}) collective-permute-start(f32[2,16,384]{2,1,0:T(8,128)S(1)} %get-tuple-element.68), channel_id=1, source_target_pairs={{0,4},{1,5},{2,6},{3,7},{4,8},{5,9},{6,10},{7,11},{8,12},{9,13},{1... | collective-permute-start | bytes 147464 | tf_op jit(solution)/shard_map/ppermute | solution.py:600
  34.3 2.7 %collective-permute-start.8 = (f32[2,16,384]{2,1,0:T(8,128)S(1)}, f32[2,16,384]{2,1,0:T(8,128)S(1)}, u32[]{:S(2)}, u32[]{:S(2)}) collective-permute-start(f32[2,16,384]{2,1,0:T(8,128)S(1)} %get-tuple-element.69), channel_id=1, source_target_pairs={{0,8},{1,9},{2,10},{3,11},{4,12},{5,13},{6,14},{7,15},{8,0},{9,1},... | collective-permute-start | bytes 147464 | tf_op jit(solution)/shard_map/ppermute | solution.py:600
  37.1 1.4 %collective-permute-start.9 = (f32[2,16,384]{2,1,0:T(8,128)S(1)}, f32[2,16,384]{2,1,0:T(8,128)S(1)}, u32[]{:S(2)}, u32[]{:S(2)}) collective-permute-start(f32[2,16,384]{2,1,0:T(8,128)S(1)} %get-tuple-element.70), channel_id=1, source_target_pairs={{0,12},{1,13},{2,14},{3,15},{4,0},{5,1},{6,2},{7,3},{8,4},{9,5},{1... | collective-permute-start | bytes 147464 | tf_op jit(solution)/shard_map/ppermute | solution.py:600
  38.5 0.0 collective-permute-done.7.one
  38.5 1.4 %collective-permute-done.8.two = f32[2,16,384]{2,1,0:T(8,128)S(1)} collective-permute-done((f32[2,16,384]{2,1,0:T(8,128)S(1)}, f32[2,16,384]{2,1,0:T(8,128)S(1)}, u32[]{:S(2)}, u32[]{:S(2)}) %collective-permute-start.8) | collective-permute-done | bytes 49184 | tf_op jit(solution)/shard_map/ppermute | solution.py:600
  39.9 1.2 %collective-permute-done.9.three = f32[2,16,384]{2,1,0:T(8,128)S(1)} collective-permute-done((f32[2,16,384]{2,1,0:T(8,128)S(1)}, f32[2,16,384]{2,1,0:T(8,128)S(1)}, u32[]{:S(2)}, u32[]{:S(2)}) %collective-permute-start.9) | collective-permute-done | bytes 49184 | tf_op jit(solution)/shard_map/ppermute | solution.py:600
  41.2 3.7 %collective-permute-start.10 = (f32[16,384]{1,0:T(8,128)S(1)}, f32[16,384]{1,0:T(8,128)S(1)}, u32[]{:S(2)}, u32[]{:S(2)}) collective-permute-start(f32[16,384]{1,0:T(8,128)S(1)} %get-tuple-element.72), channel_id=1, source_target_pairs={{0,2},{1,3},{2,0},{3,1},{4,6},{5,7},{6,4},{7,5},{8,10},{9,11},{10,... | collective-permute-start | bytes 73736 | tf_op jit(solution)/shard_map/ppermute | solution.py:600
  44.8 0.0 collective-permute-done.11.near
  44.8 2.3 %shard_map.103 = f32[1125,2,128]{2,1,0:T(2,128)} custom-call(f32[2,3,5,5,8,128]{5,4,3,2,1,0:T(8,128)S(1)} %get-tuple-element.73.vel_in, f32[2,6,5,5,8,128]{5,4,3,2,1,0:T(8,128)S(1)} %get-tuple-element.74.stress_in, f32[2,3,5,5,8,128]{5,4,3,2,1,0:T(8,128)S(1)} %get-tuple-element.75.acc_in, f32[2,5,5,8,128]{4,3,2,1,0:T(8,128)S(1)} %get-tuple-element.45.lam, ...), custom_call_target="tpu_custom_call" | custom-call | flops 100000000 | bytes 8000000 | tf_op jit(solution)/shard_map/pallas_call | solution.py:657
  47.1 0.9 %shard_map.102 = f32[125,3,16]{2,1,0:T(4,128)} custom-call(f32[16,384]{1,0:T(8,128)S(1)} %get-tuple-element.71.keep, f32[16,384]{1,0:T(8,128)S(1)} %collective-permute-done.10.got), custom_call_target="tpu_custom_call" | custom-call | flops 1000 | bytes 1000 | tf_op jit(solution)/shard_map/pallas_call | solution.py:605
  (13 shorter events, 0.1 us)
Async XLA Ops:
  0.6 7.4 %copy-start = (f32[3,5,5,5,256]{4,0,3,2,1:T(4,128)S(1)}, f32[3,5,5,5,256]{4,0,3,2,1:T(4,128)}, u32[]{:S(2)}) copy-start(f32[3,5,5,5,256]{4,0,3,2,1:T(4,128)} %param.10) | copy-start | bytes 1152004
  0.6 7.4 %copy-start.2 = (f32[1,2,3,256]{3,1,2,0:T(2,128)S(1)}, f32[1,2,3,256]{3,1,2,0:T(2,128)}, u32[]{:S(2)}) copy-start(f32[1,2,3,256]{3,1,2,0:T(2,128)} %param.15) | copy-start | bytes 18436
  0.7 7.4 %copy-start.4 = (s32[256]{0:T(256)S(1)}, s32[256]{0:T(256)}, u32[]{:S(2)}) copy-start(s32[256]{0:T(256)} %param.14) | copy-start | bytes 3076
  0.7 7.4 %copy-start.1 = (f32[1,9,5,5,5,256]{5,0,4,3,2,1:T(1,128)S(1)}, f32[1,9,5,5,5,256]{5,0,4,3,2,1:T(1,128)}, u32[]{:S(2)}) copy-start(f32[1,9,5,5,5,256]{5,0,4,3,2,1:T(1,128)} %param.9) | copy-start | bytes 3456004
  3.4 14.1 %copy-start.3 = (f32[1,2,3]{2,1,0:T(2,128)S(1)}, f32[1,2,3]{2,1,0:T(2,128)}, u32[]{:S(2)}) copy-start(f32[1,2,3]{2,1,0:T(2,128)} %pulse.1) | copy-start | bytes 76
  3.4 14.1 %collective-permute-start.2 = (f32[175,2,128]{2,1,0:T(2,128)S(1)}, f32[175,2,128]{2,1,0:T(2,128)S(1)}, u32[]{:S(2)}, u32[]{:S(2)}) collective-permute-start(f32[175,2,128]{2,1,0:T(2,128)S(1)} %get-tuple-element.50), channel_id=1, source_target_pairs={{0,16},{16,0},{32,48},{48,32},{64,80},{80,64},{96,112},{112,96},{1... | collective-permute-start | bytes 537608 | tf_op jit(solution)/shard_map/ppermute | solution.py:575
  5.5 12.1 %collective-permute-start.3 = (f32[175,2,128]{2,1,0:T(2,128)S(1)}, f32[175,2,128]{2,1,0:T(2,128)S(1)}, u32[]{:S(2)}, u32[]{:S(2)}) collective-permute-start(f32[175,2,128]{2,1,0:T(2,128)S(1)} %get-tuple-element.51), channel_id=1, source_target_pairs={{0,112},{16,32},{32,16},{48,64},{64,48},{80,96},{96,80},{112,0},{1... | collective-permute-start | bytes 537608 | tf_op jit(solution)/shard_map/ppermute | solution.py:575
  10.2 14.3 %collective-permute-start = (f32[150,2,128]{2,1,0:T(2,128)S(1)}, f32[150,2,128]{2,1,0:T(2,128)S(1)}, u32[]{:S(2)}, u32[]{:S(2)}) collective-permute-start(f32[150,2,128]{2,1,0:T(2,128)S(1)} %get-tuple-element.48), channel_id=1, source_target_pairs={{0,16},{16,0},{32,48},{48,32},{64,80},{80,64},{96,112},{112,96},{1... | collective-permute-start | bytes 460808 | tf_op jit(solution)/shard_map/ppermute | solution.py:575
  10.7 13.8 %collective-permute-start.1 = (f32[150,2,128]{2,1,0:T(2,128)S(1)}, f32[150,2,128]{2,1,0:T(2,128)S(1)}, u32[]{:S(2)}, u32[]{:S(2)}) collective-permute-start(f32[150,2,128]{2,1,0:T(2,128)S(1)} %get-tuple-element.49), channel_id=1, source_target_pairs={{0,112},{16,32},{32,16},{48,64},{64,48},{80,96},{96,80},{112,0},{1... | collective-permute-start | bytes 460808 | tf_op jit(solution)/shard_map/ppermute | solution.py:575
  19.4 9.3 %collective-permute-start.4 = (f32[75,2,128]{2,1,0:T(2,128)S(1)}, f32[75,2,128]{2,1,0:T(2,128)S(1)}, u32[]{:S(2)}, u32[]{:S(2)}) collective-permute-start(f32[75,2,128]{2,1,0:T(2,128)S(1)} %get-tuple-element.63), channel_id=1, source_target_pairs={{0,16},{16,0},{32,48},{48,32},{64,80},{80,64},{96,112},{112,96},{1... | collective-permute-start | bytes 230408 | tf_op jit(solution)/shard_map/ppermute | solution.py:575
  21.9 6.8 %collective-permute-start.5 = (f32[75,2,128]{2,1,0:T(2,128)S(1)}, f32[75,2,128]{2,1,0:T(2,128)S(1)}, u32[]{:S(2)}, u32[]{:S(2)}) collective-permute-start(f32[75,2,128]{2,1,0:T(2,128)S(1)} %get-tuple-element.64), channel_id=1, source_target_pairs={{0,112},{16,32},{32,16},{48,64},{64,48},{80,96},{96,80},{112,0},{1... | collective-permute-start | bytes 230408 | tf_op jit(solution)/shard_map/ppermute | solution.py:575
  29.6 3.2 %collective-permute-start.6 = (f32[8,16,384]{2,1,0:T(8,128)S(1)}, f32[8,16,384]{2,1,0:T(8,128)S(1)}, u32[]{:S(2)}, u32[]{:S(2)}) collective-permute-start(f32[8,16,384]{2,1,0:T(8,128)S(1)} %get-tuple-element.66), channel_id=1, source_target_pairs={{0,1},{1,0},{2,3},{3,2},{4,5},{5,4},{6,7},{7,6},{8,9},{9,8},{10,11... | collective-permute-start | bytes 589832 | tf_op jit(solution)/shard_map/ppermute | solution.py:600
  29.7 15.2 %collective-permute-start.11 = (f32[150,2,128]{2,1,0:T(2,128)S(1)}, f32[150,2,128]{2,1,0:T(2,128)S(1)}, u32[]{:S(2)}, u32[]{:S(2)}) collective-permute-start(f32[150,2,128]{2,1,0:T(2,128)S(1)} %get-tuple-element.76), channel_id=1, source_target_pairs={{0,16},{16,0},{32,48},{48,32},{64,80},{80,64},{96,112},{112,96},{1... | collective-permute-start | bytes 460808 | tf_op jit(solution)/shard_map/ppermute | solution.py:575
  30.2 14.7 %collective-permute-start.12 = (f32[150,2,128]{2,1,0:T(2,128)S(1)}, f32[150,2,128]{2,1,0:T(2,128)S(1)}, u32[]{:S(2)}, u32[]{:S(2)}) collective-permute-start(f32[150,2,128]{2,1,0:T(2,128)S(1)} %get-tuple-element.77), channel_id=1, source_target_pairs={{0,112},{16,32},{32,16},{48,64},{64,48},{80,96},{96,80},{112,0},{1... | collective-permute-start | bytes 460808 | tf_op jit(solution)/shard_map/ppermute | solution.py:575
  32.8 5.7 %collective-permute-start.7 = (f32[2,16,384]{2,1,0:T(8,128)S(1)}, f32[2,16,384]{2,1,0:T(8,128)S(1)}, u32[]{:S(2)}, u32[]{:S(2)}) collective-permute-start(f32[2,16,384]{2,1,0:T(8,128)S(1)} %get-tuple-element.68), channel_id=1, source_target_pairs={{0,4},{1,5},{2,6},{3,7},{4,8},{5,9},{6,10},{7,11},{8,12},{9,13},{1... | collective-permute-start | bytes 147464 | tf_op jit(solution)/shard_map/ppermute | solution.py:600
  34.3 5.6 %collective-permute-start.8 = (f32[2,16,384]{2,1,0:T(8,128)S(1)}, f32[2,16,384]{2,1,0:T(8,128)S(1)}, u32[]{:S(2)}, u32[]{:S(2)}) collective-permute-start(f32[2,16,384]{2,1,0:T(8,128)S(1)} %get-tuple-element.69), channel_id=1, source_target_pairs={{0,8},{1,9},{2,10},{3,11},{4,12},{5,13},{6,14},{7,15},{8,0},{9,1},... | collective-permute-start | bytes 147464 | tf_op jit(solution)/shard_map/ppermute | solution.py:600
  37.1 4.1 %collective-permute-start.9 = (f32[2,16,384]{2,1,0:T(8,128)S(1)}, f32[2,16,384]{2,1,0:T(8,128)S(1)}, u32[]{:S(2)}, u32[]{:S(2)}) collective-permute-start(f32[2,16,384]{2,1,0:T(8,128)S(1)} %get-tuple-element.70), channel_id=1, source_target_pairs={{0,12},{1,13},{2,14},{3,15},{4,0},{5,1},{6,2},{7,3},{8,4},{9,5},{1... | collective-permute-start | bytes 147464 | tf_op jit(solution)/shard_map/ppermute | solution.py:600
  41.2 6.0 %collective-permute-start.10 = (f32[16,384]{1,0:T(8,128)S(1)}, f32[16,384]{1,0:T(8,128)S(1)}, u32[]{:S(2)}, u32[]{:S(2)}) collective-permute-start(f32[16,384]{1,0:T(8,128)S(1)} %get-tuple-element.72), channel_id=1, source_target_pairs={{0,2},{1,3},{2,0},{3,1},{4,6},{5,7},{6,4},{7,5},{8,10},{9,11},{10,... | collective-permute-start | bytes 73736 | tf_op jit(solution)/shard_map/ppermute | solution.py:600

commit v9 on v8

--- a/solution.py
+++ b/solution.py
@@ -280,17 +280,19 @@
             if plain is not None:
                 for a in range(5):
                     plain[h, i, a, b] = xs[a] + {0: -5.0, 4: 5.0}[a] * v[a] if a in (0, 4) else xs[a]
-            xs[0] = xs[0] - 5.0 * halo[0, h, 3 + i, b]
-            xs[4] = xs[4] + 5.0 * halo[1, h, 3 + i, b]
+            if halo is not None:
+                xs[0] = xs[0] - 5.0 * halo[0, h, 3 + i, b]
+                xs[4] = xs[4] + 5.0 * halo[1, h, 3 + i, b]
             for a in range(5):
                 grads[h, i, a, b] = xs[a]
 
     halves(3, one, True)
 
 
-def update_stress(stress_in, stress, grads, lam, mu):
+def update_stress(stress_in, stress, read, lam, mu):
     def one(a, h):
-        g = lambda j, i: grads[h, 3 * j + i, a]
+        at = read(h, a)
+        g = lambda j, i: at[3 * j + i]
         l, m = lam[h, a], mu[h, a]
         both = l * (g(0, 0) + g(1, 1) + g(2, 2))
         for i in range(3):
@@ -414,7 +416,7 @@
     finish_acceleration(acc, stress_in, rinv, halo, True)
     velocities(vel_in, vel, acc, rows)
     jump_gradients(vel, halo, grads, plain, perms, yj, zj)
-    update_stress(stress_in, stress, grads, lam, mu)
+    update_stress(stress_in, stress, lambda h, a: [grads[h, k, a] for k in range(9)], lam, mu)
 
 
 def middle_common(rows, vel_in, stress_in, acc_in, lam, mu, rinv, perms, near, far, r_near, r_far,
@@ -453,14 +455,59 @@
     plain_gradients(acc, f_early)
 
 
-def last_kernel(vel_in, stress_in, acc_in, lam, mu, rinv, perms, inject, near, far, r_near, r_far,
-                out, vel, stress, acc, halo, grads, yj, zj, rows_out, sems):
+def early_kernel(vel_in, acc, perms, inject, held, vel, grads, yj, zj):
+    zj[...] = jnp.zeros(zj.shape, f32)
+    velocities(vel_in, vel, acc, [inject[8 + i : 9 + i] for i in range(3)])
+    jump_gradients(vel, None, grads, None, perms, yj, zj)
+
+
+def plane_changes(change, turn, perms, zj):
+    along = Along(D_LIFT)
+    yj = []
+    for side, b in ((0, 4), (1, 0)):
+        face = jnp.concatenate(
+            [
+                jnp.concatenate([change[h, i, p, b] for h in range(2)], axis=1)
+                for i in range(3)
+                for p in range(2)
+            ],
+            axis=0,
+        )
+        yj.append(permuted(face, perms[side]))
+    rows, into = flat(change, 480), flat(zj, 480)
+    spare = jnp.zeros((2, N), f32)
+    for side, c in ((0, 4), (1, 0)):
+        face = jnp.concatenate([rows[pl.ds(240 * h + c, 30, 8), :] for h in range(2)], axis=1)
+        got = permuted(jnp.concatenate([face, spare], axis=0), perms[2 + side])
+        for h in range(2):
+            into[pl.ds(240 * h + (0, 4)[side], 30, 8), :] = got[:30, 128 * h : 128 * h + 128]
+    for h in range(2):
+        for i in range(3):
+            for p in range(2):
+                d = [change[h, i, p, b] for b in range(5)]
+                ys = derive_rows(d, D_LIFT)
+                at = 8 * (2 * i + p)
+                for b, got in ((0, yj[0]), (4, yj[1])):
+                    ys[b] = ys[b] + got[at : at + 8, 128 * h : 128 * h + 128]
+                for b in range(5):
+                    turn[h, i, p, b] = ys[b]
+                    turn[h, 3 + i, p, b] = along(d[b]) + zj[h, i, p, b]
+
+
+def last_kernel(early_vel, early, stress_in, lam, mu, rinv, perms, near, far, r_near, r_far,
+                out, vel, stress, halo, change, turn, zj, rows_out, sems):
     zj[...] = jnp.zeros(zj.shape, f32)
     load_halo(halo, *(flat(r, r.shape[0] * 2) for r in (near, far, r_near, r_far)), 6)
-    acc[...] = acc_in[...]
-    rows = [inject[8 + i : 9 + i] for i in range(3)]
-    finish_acceleration(acc, stress_in, rinv, halo, True)
-    velocities(vel_in, vel, acc, rows)
+    vel[...] = early_vel[...]
+    for h in range(2):
+        for i in range(3):
+            k = (0, 5, 4)[i]
+            for p, a in ((0, 0), (1, 4)):
+                d = (5.0 * time_step if p else -5.0 * time_step) * rinv[h, a] * halo[p, h, i]
+                change[h, i, p] = d
+                vel[h, i, a] = vel[h, i, a] + d
+            halo[0, h, 3 + i] = halo[0, h, 3 + i] + halo[0, h, 6] * stress_in[h, k, 0]
+            halo[1, h, 3 + i] = halo[1, h, 3 + i] - halo[1, h, 6] * stress_in[h, k, 4]
     dst = flat(rows_out, 2250)
 
     def leave(first, k, field):
@@ -478,8 +525,23 @@
         lax.fori_loop(0, count, one, 0)
 
     leave_all(0, 3, vel)
-    jump_gradients(vel, halo, grads, None, perms, yj, zj)
-    update_stress(stress_in, stress, grads, lam, mu)
+    plane_changes(change, turn, perms, zj)
+
+    def read(h, a):
+        at = [early[h, k, a] for k in range(9)]
+        low, high = float(D_LIFT[a, 0]), float(D_LIFT[a, 4])
+        for i in range(3):
+            if low:
+                at[i] = at[i] + low * change[h, i, 0]
+            if high:
+                at[i] = at[i] + high * change[h, i, 1]
+            if a in (0, 4):
+                at[i] = at[i] + (5.0 if a else -5.0) * halo[a // 4, h, 3 + i]
+                for k in (3, 6):
+                    at[k + i] = at[k + i] + turn[h, k - 3 + i, a // 4]
+        return at
+
+    update_stress(stress_in, stress, read, lam, mu)
     leave_all(3, 6, stress)
     for k in range(9):
         there = pl.ds(125 * k, 125)
@@ -583,7 +645,7 @@
             dst[high] = keep[2 * to + high] + got[2 * to + high]
 
 
-def line_sum_kernel(mine, one, two, three, keep, send):
+def line_sum_kernel(mine, one, two, three, held, keep, send):
     high = lax.rem(lax.div(lax.axis_index("shot"), 2), 2)
     for dst, k in ((keep, high), (send, 1 - high)):
         dst[...] = (mine[k] + one[k]) + (two[k] + three[k])
@@ -596,13 +658,17 @@
     out[...] = rows.reshape(125, 4, 128)[:, 0:3, 0:16]
 
 
-def reduce_over_shots(keep, send):
+def reduce_over_shots(keep, send, beside):
     hop = lambda v, to: lax.ppermute(v, "shot", [(i, to(i)) for i in range(16)])
-    pair, chunk = shape(2, 16, 384), shape(16, 384)
+    pair, chunk, hold = shape(2, 16, 384), shape(16, 384), pl.BlockSpec(memory_space=pl.ANY)
     mine, *others = call(core_sum_kernel, [V] * 2, (pair,) * 4, [], 1000, 1000)(keep, hop(send, lambda i: i ^ 1))
     got = [hop(x, lambda i: (i + 4 * d) % 16) for d, x in enumerate(others, 1)]
-    keep, send = call(line_sum_kernel, [V] * 4, (chunk,) * 2, [], 1000, 1000)(mine, *got)
-    return call(last_sum_kernel, [V] * 2, shape(125, 3, 16), [scr(shape(500, 128))], 1000, 1000)(keep, hop(send, lambda i: i ^ 2))
+    made = beside(mine)
+    keep, send = call(line_sum_kernel, [V] * 4 + [hold], (chunk,) * 2, [], 1000, 1000)(mine, *got, made[0])
+    result = call(last_sum_kernel, [V] * 2, shape(125, 3, 16), [scr(shape(500, 128))], 1000, 1000)(
+        keep, hop(send, lambda i: i ^ 2)
+    )
+    return result, made
 
 
 def body(fwd, adj, materials, nbr, source_element, pulse, receivers, residuals):
@@ -653,16 +719,26 @@
         [HALO, pltpu.VMEM((2, 2, 3, 5, 8, 128), f32), pltpu.VMEM((2, 2, 6, 5, 8, 128), f32), scr(shape(2, 384, 128))],
         1000, 1000,
     )(f_acc2, f_early, adj_vel_end, end_grads, first, rinv, f_near2, f_far2)
-    gradient = reduce_over_shots(keep, send)
+    early_step = call(
+        early_kernel,
+        [V] * 4 + [pl.BlockSpec(memory_space=pl.ANY)],
+        (field(3), field(9)),
+        JUMPS,
+        10**8, 8 * 10**6,
+    )
+    gradient, (early_vel, early) = reduce_over_shots(
+        keep, send, lambda held: early_step(a_vel1, a_acc2, perms, injected, held)
+    )
     adjoint_end = call(
         last_kernel,
-        [V] * 12,
+        [V] * 11,
         shape(1125, 2, 128),
-        [scr(field(3)), scr(field(6)), scr(field(3)), HALO, scr(field(9))] + JUMPS
+        [scr(field(3)), scr(field(6)), HALO]
+        + [pltpu.VMEM((2, k, 2, 5, 8, 128), f32) for k in (3, 6, 3)]
         + [scr(shape(1125, 2, 128)), pltpu.SemaphoreType.DMA((9,))],
         10**8, 8 * 10**6,
         pl.BlockSpec(memory_space=pltpu.HBM),
-    )(a_vel1, a_stress1, a_acc2, lam, mu, rinv, perms, injected, a_near2, a_far2, f_near, f_far)
+    )(early_vel, early, a_stress1, lam, mu, rinv, perms, a_near2, a_far2, f_near, f_far)
     return gradient.reshape(5, 5, 5, 3, 16).transpose(3, 0, 1, 2, 4), adjoint_end.reshape(1, 9, 5, 5, 5, N)
 
 

time: 48.1 us -> 47.7 us (level)
  waiting for transfers between devices: 7.12 us -> 6.35 us
    ppermute x5, waiting for transfers between devices: 2.67 us -> 1.9 us  [reduce_over_shots(): hop = lambda v, to: lax.ppermute(v, 'shot', [(i, to(i)) for i in range(16)])]
    pallas_call x2 -> x3, Pallas kernels: 2.31 us -> 2.63 us  [the longest x1 1.86 us: body(): call(last_kernel, [V] * 11, shape(1125, 2, 128), [scr(field(3)), scr(fiel...]
  transfers between devices with their start and end apart: 13 -> 13, of which waited for: 3 -> 3; matrix products, arithmetic and copies ran while one was open for 0% -> 0% of each run, Pallas kernels for 22% -> 23%
where the time goes in v9:
time: 47.7 us; the launch traced here: 47.6 us
  starting transfers between devices  24.6 us (52%)
  Pallas kernels  15.2 us (32%)
  waiting for transfers between devices  6.35 us (13%)
  between operations  1.44 us (3%)
    ppermute x5, starting transfers between devices, reduce_over_shots(): hop = lambda v, to: lax.ppermute(v, 'shot', [(i, to(i)) for i in range(16)])  9.47 us
    ppermute x4, starting transfers between devices, both_ways(): lax.ppermute(second, 'slab', far)  9.44 us
    ppermute x4, starting transfers between devices, both_ways(): lax.ppermute(first, 'slab', near)  5.69 us
    ppermute x4, waiting for transfers between devices, both_ways(): lax.ppermute(first, 'slab', near)  4.44 us
    pallas_call x1, Pallas kernels, body(): call(adjoint_middle_kernel, [V] * 16 + [S] * 2, (sends(6), sends(6), fiel...  4.17 us
    pallas_call x1, Pallas kernels, body(): call(forward_start_kernel, [pl.BlockSpec(memory_space=pltpu.HBM)] * 3, (s...  2.74 us
    pallas_call x1, Pallas kernels, body(): call(adjoint_start_kernel, [V] * 6, (sends(6), sends(6), field(3), field(...  2.08 us
    ppermute x5, waiting for transfers between devices, reduce_over_shots(): hop = lambda v, to: lax.ppermute(v, 'shot', [(i, to(i)) for i in range(16)])  1.9 us
  transfers between devices with their start and end apart: 13, of which 3 were waited for; matrix products, arithmetic and copies ran while one was open for 0% of the time, Pallas kernels for 23%

profile of v9, /device:TPU:0, one launch (start us, length us, event | category | flops | bytes accessed | tf_op | source)
XLA Modules:
  0.0 47.6 jit_solution(12619775294243416128)
XLA Ops:
  0.7 2.7 %shard_map.95 = (f32[175,2,128]{2,1,0:T(2,128)S(1)}, f32[175,2,128]{2,1,0:T(2,128)S(1)}, f32[2,3,5,5,8,128]{5,4,3,2,1,0:T(8,128)S(1)}, f32[2,3,5,5,8,128]{5,4,3,...) custom-call(f32[1125,2,128]{2,1,0:T(2,128)} %bitcast.19, ...), custom_call_target="tpu_custom_call" | custom-call | flops 100000000 | bytes 4000000 | tf_op jit(solution)/shard_map/pallas_call | solution.py:681
  3.4 0.0 copy-start.3
  3.4 2.1 %collective-permute-start.2 = (f32[175,2,128]{2,1,0:T(2,128)S(1)}, f32[175,2,128]{2,1,0:T(2,128)S(1)}, u32[]{:S(2)}, u32[]{:S(2)}) collective-permute-start(f32[175,2,128]{2,1,0:T(2,128)S(1)} %get-tuple-element.52), channel_id=1, source_target_pairs={{0,16},{16,0},{32,48},{48,32},{64,80},{80,64},{96,112},{112,96},{1... | collective-permute-start | bytes 537608 | tf_op jit(solution)/shard_map/ppermute | solution.py:637
  5.5 2.6 %collective-permute-start.3 = (f32[175,2,128]{2,1,0:T(2,128)S(1)}, f32[175,2,128]{2,1,0:T(2,128)S(1)}, u32[]{:S(2)}, u32[]{:S(2)}) collective-permute-start(f32[175,2,128]{2,1,0:T(2,128)S(1)} %get-tuple-element.53), channel_id=1, source_target_pairs={{0,112},{16,32},{32,16},{48,64},{64,48},{80,96},{96,80},{112,0},{1... | collective-permute-start | bytes 537608 | tf_op jit(solution)/shard_map/ppermute | solution.py:637
  8.1 2.1 %shard_map.96 = (f32[150,2,128]{2,1,0:T(2,128)S(1)}, f32[150,2,128]{2,1,0:T(2,128)S(1)}, f32[2,3,5,5,8,128]{5,4,3,2,1,0:T(8,128)S(1)}, f32[2,3,5,5,8,128]{5,4,3,...) custom-call(f32[1125,2,128]{2,1,0:T(2,128)S(1)} %bitcast.16, ...), custom_call_target="tpu_custom_call" | custom-call | flops 100000000 | bytes 4000000 | tf_op jit(solution)/shard_map/pallas_call | solution.py:689
  10.2 0.5 %collective-permute-start = (f32[150,2,128]{2,1,0:T(2,128)S(1)}, f32[150,2,128]{2,1,0:T(2,128)S(1)}, u32[]{:S(2)}, u32[]{:S(2)}) collective-permute-start(f32[150,2,128]{2,1,0:T(2,128)S(1)} %get-tuple-element.50), channel_id=1, source_target_pairs={{0,16},{16,0},{32,48},{48,32},{64,80},{80,64},{96,112},{112,96},{1... | collective-permute-start | bytes 460808 | tf_op jit(solution)/shard_map/ppermute | solution.py:637
  10.7 1.7 %collective-permute-start.1 = (f32[150,2,128]{2,1,0:T(2,128)S(1)}, f32[150,2,128]{2,1,0:T(2,128)S(1)}, u32[]{:S(2)}, u32[]{:S(2)}) collective-permute-start(f32[150,2,128]{2,1,0:T(2,128)S(1)} %get-tuple-element.51), channel_id=1, source_target_pairs={{0,112},{16,32},{32,16},{48,64},{64,48},{80,96},{96,80},{112,0},{1... | collective-permute-start | bytes 460808 | tf_op jit(solution)/shard_map/ppermute | solution.py:637
  13.1 4.4 %collective-permute-done.2.near.r_near = f32[175,2,128]{2,1,0:T(2,128)S(1)} collective-permute-done((f32[175,2,128]{2,1,0:T(2,128)S(1)}, f32[175,2,128]{2,1,0:T(2,128)S(1)}, u32[]{:S(2)}, u32[]{:S(2)}) %collective-permute-start.2) | collective-permute-done | bytes 179232 | tf_op jit(solution)/shard_map/ppermute | solution.py:637
  17.6 1.8 %shard_map.97 = (f32[75,2,128]{2,1,0:T(2,128)S(1)}, f32[75,2,128]{2,1,0:T(2,128)S(1)}, f32[2,3,5,5,8,128]{5,4,3,2,1,0:T(8,128)S(1)}, f32[2,3,5,5,8,128]{5,4,3,2,...) custom-call(f32[2,3,5,5,8,128]{5,4,3,2,1,0:T(8,128)S(1)} %get-tuple-element.54.vel_in, ...), custom_call_target="tpu_custom_call" | custom-call | flops 200000000 | bytes 8000000 | tf_op jit(solution)/shard_map/pallas_call | solution.py:699
  19.4 2.6 %collective-permute-start.4 = (f32[75,2,128]{2,1,0:T(2,128)S(1)}, f32[75,2,128]{2,1,0:T(2,128)S(1)}, u32[]{:S(2)}, u32[]{:S(2)}) collective-permute-start(f32[75,2,128]{2,1,0:T(2,128)S(1)} %get-tuple-element.65), channel_id=1, source_target_pairs={{0,16},{16,0},{32,48},{48,32},{64,80},{80,64},{96,112},{112,96},{1... | collective-permute-start | bytes 230408 | tf_op jit(solution)/shard_map/ppermute | solution.py:637
  21.9 2.6 %collective-permute-start.5 = (f32[75,2,128]{2,1,0:T(2,128)S(1)}, f32[75,2,128]{2,1,0:T(2,128)S(1)}, u32[]{:S(2)}, u32[]{:S(2)}) collective-permute-start(f32[75,2,128]{2,1,0:T(2,128)S(1)} %get-tuple-element.66), channel_id=1, source_target_pairs={{0,112},{16,32},{32,16},{48,64},{64,48},{80,96},{96,80},{112,0},{1... | collective-permute-start | bytes 230408 | tf_op jit(solution)/shard_map/ppermute | solution.py:637
  24.5 0.0 collective-permute-done.near
  24.5 0.0 collective-permute-done.1.far
  24.5 4.2 %shard_map.98 = (f32[150,2,128]{2,1,0:T(2,128)S(1)}, f32[150,2,128]{2,1,0:T(2,128)S(1)}, f32[2,3,5,5,8,128]{5,4,3,2,1,0:T(8,128)S(1)}, f32[2,6,5,5,8,128]{5,4,3,...) custom-call(f32[2,3,5,5,8,128]{5,4,3,2,1,0:T(8,128)S(1)} %get-tuple-, ...), custom_call_target="tpu_custom_call" | custom-call | flops 200000000 | bytes 8000000 | tf_op jit(solution)/shard_map/pallas_call | solution.py:707
  28.7 0.0 collective-permute-done.4.near
  28.7 0.8 %shard_map.99 = (f32[8,16,384]{2,1,0:T(8,128)S(1)}, f32[8,16,384]{2,1,0:T(8,128)S(1)}) custom-call(f32[2,3,5,5,8,128]{5,4,3,2,1,0:T(8,128)S(1)} %get-tuple-element.61.acc, f32[2,9,5,5,8,128]{5,4,3,2,1,0:T(8,128)S(1)} %get-tuple-element.62.early, f32[2,3,5,5,8,128]{5,4,3,2,1,0:T(8,128)S(1)} %get-tuple-element.44.vel_in.adj_vel, ...), custom_call_target="tpu_custom_call" | custom-call | flops 1000 | bytes 1000 | tf_op jit(solution)/shard_map/pallas_call | solution.py:715
  29.6 0.1 collective-permute-start.6
  29.7 0.5 %collective-permute-start.11 = (f32[150,2,128]{2,1,0:T(2,128)S(1)}, f32[150,2,128]{2,1,0:T(2,128)S(1)}, u32[]{:S(2)}, u32[]{:S(2)}) collective-permute-start(f32[150,2,128]{2,1,0:T(2,128)S(1)} %get-tuple-element.80), channel_id=1, source_target_pairs={{0,16},{16,0},{32,48},{48,32},{64,80},{80,64},{96,112},{112,96},{1... | collective-permute-start | bytes 460808 | tf_op jit(solution)/shard_map/ppermute | solution.py:637
  30.2 2.5 %collective-permute-start.12 = (f32[150,2,128]{2,1,0:T(2,128)S(1)}, f32[150,2,128]{2,1,0:T(2,128)S(1)}, u32[]{:S(2)}, u32[]{:S(2)}) collective-permute-start(f32[150,2,128]{2,1,0:T(2,128)S(1)} %get-tuple-element.81), channel_id=1, source_target_pairs={{0,112},{16,32},{32,16},{48,64},{64,48},{80,96},{96,80},{112,0},{1... | collective-permute-start | bytes 460808 | tf_op jit(solution)/shard_map/ppermute | solution.py:637
  32.7 0.0 collective-permute-done.6.got
  32.8 1.6 %collective-permute-start.7 = (f32[2,16,384]{2,1,0:T(8,128)S(1)}, f32[2,16,384]{2,1,0:T(8,128)S(1)}, u32[]{:S(2)}, u32[]{:S(2)}) collective-permute-start(f32[2,16,384]{2,1,0:T(8,128)S(1)} %get-tuple-element.70), channel_id=1, source_target_pairs={{0,4},{1,5},{2,6},{3,7},{4,8},{5,9},{6,10},{7,11},{8,12},{9,13},{1... | collective-permute-start | bytes 147464 | tf_op jit(solution)/shard_map/ppermute | solution.py:662
  34.3 2.7 %collective-permute-start.8 = (f32[2,16,384]{2,1,0:T(8,128)S(1)}, f32[2,16,384]{2,1,0:T(8,128)S(1)}, u32[]{:S(2)}, u32[]{:S(2)}) collective-permute-start(f32[2,16,384]{2,1,0:T(8,128)S(1)} %get-tuple-element.71), channel_id=1, source_target_pairs={{0,8},{1,9},{2,10},{3,11},{4,12},{5,13},{6,14},{7,15},{8,0},{9,1},... | collective-permute-start | bytes 147464 | tf_op jit(solution)/shard_map/ppermute | solution.py:662
  37.1 1.4 %collective-permute-start.9 = (f32[2,16,384]{2,1,0:T(8,128)S(1)}, f32[2,16,384]{2,1,0:T(8,128)S(1)}, u32[]{:S(2)}, u32[]{:S(2)}) collective-permute-start(f32[2,16,384]{2,1,0:T(8,128)S(1)} %get-tuple-element.72), channel_id=1, source_target_pairs={{0,12},{1,13},{2,14},{3,15},{4,0},{5,1},{6,2},{7,3},{8,4},{9,5},{1... | collective-permute-start | bytes 147464 | tf_op jit(solution)/shard_map/ppermute | solution.py:662
  38.5 0.8 %shard_map.101 = (f32[2,3,5,5,8,128]{5,4,3,2,1,0:T(8,128)S(1)}, f32[2,9,5,5,8,128]{5,4,3,2,1,0:T(8,128)S(1)}) custom-call(f32[2,3,5,5,8,128]{5,4,3,2,1,0:T(8,128)S(1)} %get-tuple-element.73.vel_in, f32[2,3,5,5,8,128]{5,4,3,2,1,0:T(8,128)S(1)} %get-tuple-element.74.acc, bf16[4,256,256]{2,1,0:T(8,128)(2,1)S(1)} %get-tuple-element.43.perms, ...), custom_call_target="tpu_custom_call" | custom-call | flops 100000000 | bytes 8000000 | tf_op jit(solution)/shard_map/pallas_call | solution.py:730
  39.3 0.0 collective-permute-done.7.one
  39.3 0.7 %collective-permute-done.8.two = f32[2,16,384]{2,1,0:T(8,128)S(1)} collective-permute-done((f32[2,16,384]{2,1,0:T(8,128)S(1)}, f32[2,16,384]{2,1,0:T(8,128)S(1)}, u32[]{:S(2)}, u32[]{:S(2)}) %collective-permute-start.8) | collective-permute-done | bytes 49184 | tf_op jit(solution)/shard_map/ppermute | solution.py:662
  39.9 1.2 %collective-permute-done.9.three = f32[2,16,384]{2,1,0:T(8,128)S(1)} collective-permute-done((f32[2,16,384]{2,1,0:T(8,128)S(1)}, f32[2,16,384]{2,1,0:T(8,128)S(1)}, u32[]{:S(2)}, u32[]{:S(2)}) %collective-permute-start.9) | collective-permute-done | bytes 49184 | tf_op jit(solution)/shard_map/ppermute | solution.py:662
  41.2 3.7 %collective-permute-start.10 = (f32[16,384]{1,0:T(8,128)S(1)}, f32[16,384]{1,0:T(8,128)S(1)}, u32[]{:S(2)}, u32[]{:S(2)}) collective-permute-start(f32[16,384]{1,0:T(8,128)S(1)} %get-tuple-element.77), channel_id=1, source_target_pairs={{0,2},{1,3},{2,0},{3,1},{4,6},{5,7},{6,4},{7,5},{8,10},{9,11},{10,... | collective-permute-start | bytes 73736 | tf_op jit(solution)/shard_map/ppermute | solution.py:662
  44.8 0.0 collective-permute-done.12.far
  44.8 1.9 %shard_map.104 = f32[1125,2,128]{2,1,0:T(2,128)} custom-call(f32[2,3,5,5,8,128]{5,4,3,2,1,0:T(8,128)S(1)} %get-tuple-element.75.held.early_vel, f32[2,9,5,5,8,128]{5,4,3,2,1,0:T(8,128)S(1)} %get-tuple-element.78.early, f32[2,6,5,5,8,128]{5,4,3,2,1,0:T(8,128)S(1)} %get-tuple-element.79.stress_in, f32[2,5,5,8,128]{4,3,2,1,0:T(8,128)S(1)} %get-tuple-element.47.lam, ...), custom_call_target="tpu_custom_call" | custom-call | flops 100000000 | bytes 8000000 | tf_op jit(solution)/shard_map/pallas_call | solution.py:732
  46.7 0.0 collective-permute-done.10.got
  46.7 0.9 %shard_map.103 = f32[125,3,16]{2,1,0:T(4,128)} custom-call(f32[16,384]{1,0:T(8,128)S(1)} %get-tuple-element.76.keep, f32[16,384]{1,0:T(8,128)S(1)} %collective-permute-done.10.got), custom_call_target="tpu_custom_call" | custom-call | flops 1000 | bytes 1000 | tf_op jit(solution)/shard_map/pallas_call | solution.py:668
  (14 shorter events, 0.1 us)
Async XLA Ops:
  0.6 7.4 %copy-start = (f32[3,5,5,5,256]{4,0,3,2,1:T(4,128)S(1)}, f32[3,5,5,5,256]{4,0,3,2,1:T(4,128)}, u32[]{:S(2)}) copy-start(f32[3,5,5,5,256]{4,0,3,2,1:T(4,128)} %param.10) | copy-start | bytes 1152004
  0.6 7.4 %copy-start.2 = (f32[1,2,3,256]{3,1,2,0:T(2,128)S(1)}, f32[1,2,3,256]{3,1,2,0:T(2,128)}, u32[]{:S(2)}) copy-start(f32[1,2,3,256]{3,1,2,0:T(2,128)} %param.15) | copy-start | bytes 18436
  0.7 7.4 %copy-start.4 = (s32[256]{0:T(256)S(1)}, s32[256]{0:T(256)}, u32[]{:S(2)}) copy-start(s32[256]{0:T(256)} %param.14) | copy-start | bytes 3076
  0.7 7.4 %copy-start.1 = (f32[1,9,5,5,5,256]{5,0,4,3,2,1:T(1,128)S(1)}, f32[1,9,5,5,5,256]{5,0,4,3,2,1:T(1,128)}, u32[]{:S(2)}) copy-start(f32[1,9,5,5,5,256]{5,0,4,3,2,1:T(1,128)} %param.9) | copy-start | bytes 3456004
  3.4 14.1 %copy-start.3 = (f32[1,2,3]{2,1,0:T(2,128)S(1)}, f32[1,2,3]{2,1,0:T(2,128)}, u32[]{:S(2)}) copy-start(f32[1,2,3]{2,1,0:T(2,128)} %pulse.1) | copy-start | bytes 76
  3.4 14.1 %collective-permute-start.2 = (f32[175,2,128]{2,1,0:T(2,128)S(1)}, f32[175,2,128]{2,1,0:T(2,128)S(1)}, u32[]{:S(2)}, u32[]{:S(2)}) collective-permute-start(f32[175,2,128]{2,1,0:T(2,128)S(1)} %get-tuple-element.52), channel_id=1, source_target_pairs={{0,16},{16,0},{32,48},{48,32},{64,80},{80,64},{96,112},{112,96},{1... | collective-permute-start | bytes 537608 | tf_op jit(solution)/shard_map/ppermute | solution.py:637
  5.5 12.1 %collective-permute-start.3 = (f32[175,2,128]{2,1,0:T(2,128)S(1)}, f32[175,2,128]{2,1,0:T(2,128)S(1)}, u32[]{:S(2)}, u32[]{:S(2)}) collective-permute-start(f32[175,2,128]{2,1,0:T(2,128)S(1)} %get-tuple-element.53), channel_id=1, source_target_pairs={{0,112},{16,32},{32,16},{48,64},{64,48},{80,96},{96,80},{112,0},{1... | collective-permute-start | bytes 537608 | tf_op jit(solution)/shard_map/ppermute | solution.py:637
  10.2 14.3 %collective-permute-start = (f32[150,2,128]{2,1,0:T(2,128)S(1)}, f32[150,2,128]{2,1,0:T(2,128)S(1)}, u32[]{:S(2)}, u32[]{:S(2)}) collective-permute-start(f32[150,2,128]{2,1,0:T(2,128)S(1)} %get-tuple-element.50), channel_id=1, source_target_pairs={{0,16},{16,0},{32,48},{48,32},{64,80},{80,64},{96,112},{112,96},{1... | collective-permute-start | bytes 460808 | tf_op jit(solution)/shard_map/ppermute | solution.py:637
  10.7 13.8 %collective-permute-start.1 = (f32[150,2,128]{2,1,0:T(2,128)S(1)}, f32[150,2,128]{2,1,0:T(2,128)S(1)}, u32[]{:S(2)}, u32[]{:S(2)}) collective-permute-start(f32[150,2,128]{2,1,0:T(2,128)S(1)} %get-tuple-element.51), channel_id=1, source_target_pairs={{0,112},{16,32},{32,16},{48,64},{64,48},{80,96},{96,80},{112,0},{1... | collective-permute-start | bytes 460808 | tf_op jit(solution)/shard_map/ppermute | solution.py:637
  19.4 9.3 %collective-permute-start.4 = (f32[75,2,128]{2,1,0:T(2,128)S(1)}, f32[75,2,128]{2,1,0:T(2,128)S(1)}, u32[]{:S(2)}, u32[]{:S(2)}) collective-permute-start(f32[75,2,128]{2,1,0:T(2,128)S(1)} %get-tuple-element.65), channel_id=1, source_target_pairs={{0,16},{16,0},{32,48},{48,32},{64,80},{80,64},{96,112},{112,96},{1... | collective-permute-start | bytes 230408 | tf_op jit(solution)/shard_map/ppermute | solution.py:637
  21.9 6.8 %collective-permute-start.5 = (f32[75,2,128]{2,1,0:T(2,128)S(1)}, f32[75,2,128]{2,1,0:T(2,128)S(1)}, u32[]{:S(2)}, u32[]{:S(2)}) collective-permute-start(f32[75,2,128]{2,1,0:T(2,128)S(1)} %get-tuple-element.66), channel_id=1, source_target_pairs={{0,112},{16,32},{32,16},{48,64},{64,48},{80,96},{96,80},{112,0},{1... | collective-permute-start | bytes 230408 | tf_op jit(solution)/shard_map/ppermute | solution.py:637
  29.6 3.2 %collective-permute-start.6 = (f32[8,16,384]{2,1,0:T(8,128)S(1)}, f32[8,16,384]{2,1,0:T(8,128)S(1)}, u32[]{:S(2)}, u32[]{:S(2)}) collective-permute-start(f32[8,16,384]{2,1,0:T(8,128)S(1)} %get-tuple-element.68), channel_id=1, source_target_pairs={{0,1},{1,0},{2,3},{3,2},{4,5},{5,4},{6,7},{7,6},{8,9},{9,8},{10,11... | collective-permute-start | bytes 589832 | tf_op jit(solution)/shard_map/ppermute | solution.py:662
  29.7 15.2 %collective-permute-start.11 = (f32[150,2,128]{2,1,0:T(2,128)S(1)}, f32[150,2,128]{2,1,0:T(2,128)S(1)}, u32[]{:S(2)}, u32[]{:S(2)}) collective-permute-start(f32[150,2,128]{2,1,0:T(2,128)S(1)} %get-tuple-element.80), channel_id=1, source_target_pairs={{0,16},{16,0},{32,48},{48,32},{64,80},{80,64},{96,112},{112,96},{1... | collective-permute-start | bytes 460808 | tf_op jit(solution)/shard_map/ppermute | solution.py:637
  30.2 14.6 %collective-permute-start.12 = (f32[150,2,128]{2,1,0:T(2,128)S(1)}, f32[150,2,128]{2,1,0:T(2,128)S(1)}, u32[]{:S(2)}, u32[]{:S(2)}) collective-permute-start(f32[150,2,128]{2,1,0:T(2,128)S(1)} %get-tuple-element.81), channel_id=1, source_target_pairs={{0,112},{16,32},{32,16},{48,64},{64,48},{80,96},{96,80},{112,0},{1... | collective-permute-start | bytes 460808 | tf_op jit(solution)/shard_map/ppermute | solution.py:637
  32.8 6.5 %collective-permute-start.7 = (f32[2,16,384]{2,1,0:T(8,128)S(1)}, f32[2,16,384]{2,1,0:T(8,128)S(1)}, u32[]{:S(2)}, u32[]{:S(2)}) collective-permute-start(f32[2,16,384]{2,1,0:T(8,128)S(1)} %get-tuple-element.70), channel_id=1, source_target_pairs={{0,4},{1,5},{2,6},{3,7},{4,8},{5,9},{6,10},{7,11},{8,12},{9,13},{1... | collective-permute-start | bytes 147464 | tf_op jit(solution)/shard_map/ppermute | solution.py:662
  34.3 5.6 %collective-permute-start.8 = (f32[2,16,384]{2,1,0:T(8,128)S(1)}, f32[2,16,384]{2,1,0:T(8,128)S(1)}, u32[]{:S(2)}, u32[]{:S(2)}) collective-permute-start(f32[2,16,384]{2,1,0:T(8,128)S(1)} %get-tuple-element.71), channel_id=1, source_target_pairs={{0,8},{1,9},{2,10},{3,11},{4,12},{5,13},{6,14},{7,15},{8,0},{9,1},... | collective-permute-start | bytes 147464 | tf_op jit(solution)/shard_map/ppermute | solution.py:662
  37.1 4.1 %collective-permute-start.9 = (f32[2,16,384]{2,1,0:T(8,128)S(1)}, f32[2,16,384]{2,1,0:T(8,128)S(1)}, u32[]{:S(2)}, u32[]{:S(2)}) collective-permute-start(f32[2,16,384]{2,1,0:T(8,128)S(1)} %get-tuple-element.72), channel_id=1, source_target_pairs={{0,12},{1,13},{2,14},{3,15},{4,0},{5,1},{6,2},{7,3},{8,4},{9,5},{1... | collective-permute-start | bytes 147464 | tf_op jit(solution)/shard_map/ppermute | solution.py:662
  41.2 5.5 %collective-permute-start.10 = (f32[16,384]{1,0:T(8,128)S(1)}, f32[16,384]{1,0:T(8,128)S(1)}, u32[]{:S(2)}, u32[]{:S(2)}) collective-permute-start(f32[16,384]{1,0:T(8,128)S(1)} %get-tuple-element.77), channel_id=1, source_target_pairs={{0,2},{1,3},{2,0},{3,1},{4,6},{5,7},{6,4},{7,5},{8,10},{9,11},{10,... | collective-permute-start | bytes 73736 | tf_op jit(solution)/shard_map/ppermute | solution.py:662

commit v10 on v9

--- a/solution.py
+++ b/solution.py
@@ -639,7 +639,7 @@
 
 def core_sum_kernel(keep, got, mine, *others):
     line = lax.div(lax.axis_index("shot"), 4)
-    for d, dst in enumerate((mine, *others)):
+    for d, dst in zip((0, 2, 1, 3), (mine, *others)):
         to = lax.rem(line + d, 4)
         for high in range(2):
             dst[high] = keep[2 * to + high] + got[2 * to + high]
@@ -662,7 +662,7 @@
     hop = lambda v, to: lax.ppermute(v, "shot", [(i, to(i)) for i in range(16)])
     pair, chunk, hold = shape(2, 16, 384), shape(16, 384), pl.BlockSpec(memory_space=pl.ANY)
     mine, *others = call(core_sum_kernel, [V] * 2, (pair,) * 4, [], 1000, 1000)(keep, hop(send, lambda i: i ^ 1))
-    got = [hop(x, lambda i: (i + 4 * d) % 16) for d, x in enumerate(others, 1)]
+    got = [hop(x, lambda i: (i + 4 * d) % 16) for d, x in zip((2, 1, 3), others)]
     made = beside(mine)
     keep, send = call(line_sum_kernel, [V] * 4 + [hold], (chunk,) * 2, [], 1000, 1000)(mine, *got, made[0])
     result = call(last_sum_kernel, [V] * 2, shape(125, 3, 16), [scr(shape(500, 128))], 1000, 1000)(

time: 47.7 us -> 48.1 us (level)
  waiting for transfers between devices: 6.35 us -> 5.75 us
  starting transfers between devices: 24.6 us -> 25.2 us
    ppermute x5, starting transfers between devices: 9.47 us -> 10.1 us  [reduce_over_shots(): hop = lambda v, to: lax.ppermute(v, 'shot', [(i, to(i)) for i in range(16)])]
    ppermute x5, waiting for transfers between devices: 1.9 us -> 1.3 us  [reduce_over_shots(): hop = lambda v, to: lax.ppermute(v, 'shot', [(i, to(i)) for i in range(16)])]
  transfers between devices with their start and end apart: 13 -> 13, of which waited for: 3 -> 2; matrix products, arithmetic and copies ran while one was open for 0% -> 0% of each run, Pallas kernels for 23% -> 23%
where the time goes in v10:
time: 48.1 us; the launch traced here: 47.6 us
  starting transfers between devices  25.2 us (52%)
  Pallas kernels  15.2 us (32%)
  waiting for transfers between devices  5.75 us (12%)
  between operations  1.44 us (3%)
    ppermute x5, starting transfers between devices, reduce_over_shots(): hop = lambda v, to: lax.ppermute(v, 'shot', [(i, to(i)) for i in range(16)])  10.1 us
    ppermute x4, starting transfers between devices, both_ways(): lax.ppermute(second, 'slab', far)  9.44 us
    ppermute x4, starting transfers between devices, both_ways(): lax.ppermute(first, 'slab', near)  5.69 us
    ppermute x4, waiting for transfers between devices, both_ways(): lax.ppermute(first, 'slab', near)  4.44 us
    pallas_call x1, Pallas kernels, body(): call(adjoint_middle_kernel, [V] * 16 + [S] * 2, (sends(6), sends(6), fiel...  4.17 us
    pallas_call x1, Pallas kernels, body(): call(forward_start_kernel, [pl.BlockSpec(memory_space=pltpu.HBM)] * 3, (s...  2.74 us
    pallas_call x1, Pallas kernels, body(): call(adjoint_start_kernel, [V] * 6, (sends(6), sends(6), field(3), field(...  2.08 us
    pallas_call x1, Pallas kernels, body(): call(last_kernel, [V] * 11, shape(1125, 2, 128), [scr(field(3)), scr(fiel...  1.87 us
  transfers between devices with their start and end apart: 13, of which 2 were waited for; matrix products, arithmetic and copies ran while one was open for 0% of the time, Pallas kernels for 23%

profile of v10, /device:TPU:0, one launch (start us, length us, event | category | flops | bytes accessed | tf_op | source)
XLA Modules:
  0.0 47.6 jit_solution(17743597997987592188)
XLA Ops:
  0.7 2.7 %shard_map.95 = (f32[175,2,128]{2,1,0:T(2,128)S(1)}, f32[175,2,128]{2,1,0:T(2,128)S(1)}, f32[2,3,5,5,8,128]{5,4,3,2,1,0:T(8,128)S(1)}, f32[2,3,5,5,8,128]{5,4,3,...) custom-call(f32[1125,2,128]{2,1,0:T(2,128)} %bitcast.19, ...), custom_call_target="tpu_custom_call" | custom-call | flops 100000000 | bytes 4000000 | tf_op jit(solution)/shard_map/pallas_call | solution.py:681
  3.4 0.0 copy-start.3
  3.4 2.1 %collective-permute-start.2 = (f32[175,2,128]{2,1,0:T(2,128)S(1)}, f32[175,2,128]{2,1,0:T(2,128)S(1)}, u32[]{:S(2)}, u32[]{:S(2)}) collective-permute-start(f32[175,2,128]{2,1,0:T(2,128)S(1)} %get-tuple-element.52), channel_id=1, source_target_pairs={{0,16},{16,0},{32,48},{48,32},{64,80},{80,64},{96,112},{112,96},{1... | collective-permute-start | bytes 537608 | tf_op jit(solution)/shard_map/ppermute | solution.py:637
  5.5 2.6 %collective-permute-start.3 = (f32[175,2,128]{2,1,0:T(2,128)S(1)}, f32[175,2,128]{2,1,0:T(2,128)S(1)}, u32[]{:S(2)}, u32[]{:S(2)}) collective-permute-start(f32[175,2,128]{2,1,0:T(2,128)S(1)} %get-tuple-element.53), channel_id=1, source_target_pairs={{0,112},{16,32},{32,16},{48,64},{64,48},{80,96},{96,80},{112,0},{1... | collective-permute-start | bytes 537608 | tf_op jit(solution)/shard_map/ppermute | solution.py:637
  8.1 2.1 %shard_map.96 = (f32[150,2,128]{2,1,0:T(2,128)S(1)}, f32[150,2,128]{2,1,0:T(2,128)S(1)}, f32[2,3,5,5,8,128]{5,4,3,2,1,0:T(8,128)S(1)}, f32[2,3,5,5,8,128]{5,4,3,...) custom-call(f32[1125,2,128]{2,1,0:T(2,128)S(1)} %bitcast.16, ...), custom_call_target="tpu_custom_call" | custom-call | flops 100000000 | bytes 4000000 | tf_op jit(solution)/shard_map/pallas_call | solution.py:689
  10.2 0.5 %collective-permute-start = (f32[150,2,128]{2,1,0:T(2,128)S(1)}, f32[150,2,128]{2,1,0:T(2,128)S(1)}, u32[]{:S(2)}, u32[]{:S(2)}) collective-permute-start(f32[150,2,128]{2,1,0:T(2,128)S(1)} %get-tuple-element.50), channel_id=1, source_target_pairs={{0,16},{16,0},{32,48},{48,32},{64,80},{80,64},{96,112},{112,96},{1... | collective-permute-start | bytes 460808 | tf_op jit(solution)/shard_map/ppermute | solution.py:637
  10.7 1.7 %collective-permute-start.1 = (f32[150,2,128]{2,1,0:T(2,128)S(1)}, f32[150,2,128]{2,1,0:T(2,128)S(1)}, u32[]{:S(2)}, u32[]{:S(2)}) collective-permute-start(f32[150,2,128]{2,1,0:T(2,128)S(1)} %get-tuple-element.51), channel_id=1, source_target_pairs={{0,112},{16,32},{32,16},{48,64},{64,48},{80,96},{96,80},{112,0},{1... | collective-permute-start | bytes 460808 | tf_op jit(solution)/shard_map/ppermute | solution.py:637
  13.1 4.4 %collective-permute-done.2.near.r_near = f32[175,2,128]{2,1,0:T(2,128)S(1)} collective-permute-done((f32[175,2,128]{2,1,0:T(2,128)S(1)}, f32[175,2,128]{2,1,0:T(2,128)S(1)}, u32[]{:S(2)}, u32[]{:S(2)}) %collective-permute-start.2) | collective-permute-done | bytes 179232 | tf_op jit(solution)/shard_map/ppermute | solution.py:637
  17.6 0.0 collective-permute-done.3.far.r_far
  17.6 1.8 %shard_map.97 = (f32[75,2,128]{2,1,0:T(2,128)S(1)}, f32[75,2,128]{2,1,0:T(2,128)S(1)}, f32[2,3,5,5,8,128]{5,4,3,2,1,0:T(8,128)S(1)}, f32[2,3,5,5,8,128]{5,4,3,2,...) custom-call(f32[2,3,5,5,8,128]{5,4,3,2,1,0:T(8,128)S(1)} %get-tuple-element.54.vel_in, ...), custom_call_target="tpu_custom_call" | custom-call | flops 200000000 | bytes 8000000 | tf_op jit(solution)/shard_map/pallas_call | solution.py:699
  19.4 2.6 %collective-permute-start.4 = (f32[75,2,128]{2,1,0:T(2,128)S(1)}, f32[75,2,128]{2,1,0:T(2,128)S(1)}, u32[]{:S(2)}, u32[]{:S(2)}) collective-permute-start(f32[75,2,128]{2,1,0:T(2,128)S(1)} %get-tuple-element.65), channel_id=1, source_target_pairs={{0,16},{16,0},{32,48},{48,32},{64,80},{80,64},{96,112},{112,96},{1... | collective-permute-start | bytes 230408 | tf_op jit(solution)/shard_map/ppermute | solution.py:637
  21.9 2.6 %collective-permute-start.5 = (f32[75,2,128]{2,1,0:T(2,128)S(1)}, f32[75,2,128]{2,1,0:T(2,128)S(1)}, u32[]{:S(2)}, u32[]{:S(2)}) collective-permute-start(f32[75,2,128]{2,1,0:T(2,128)S(1)} %get-tuple-element.66), channel_id=1, source_target_pairs={{0,112},{16,32},{32,16},{48,64},{64,48},{80,96},{96,80},{112,0},{1... | collective-permute-start | bytes 230408 | tf_op jit(solution)/shard_map/ppermute | solution.py:637
  24.5 0.0 collective-permute-done.near
  24.5 0.0 collective-permute-done.1.far
  24.5 4.2 %shard_map.98 = (f32[150,2,128]{2,1,0:T(2,128)S(1)}, f32[150,2,128]{2,1,0:T(2,128)S(1)}, f32[2,3,5,5,8,128]{5,4,3,2,1,0:T(8,128)S(1)}, f32[2,6,5,5,8,128]{5,4,3,...) custom-call(f32[2,3,5,5,8,128]{5,4,3,2,1,0:T(8,128)S(1)} %get-tuple-, ...), custom_call_target="tpu_custom_call" | custom-call | flops 200000000 | bytes 8000000 | tf_op jit(solution)/shard_map/pallas_call | solution.py:707
  28.7 0.0 collective-permute-done.4.near
  28.7 0.0 collective-permute-done.5.far
  28.7 0.8 %shard_map.99 = (f32[8,16,384]{2,1,0:T(8,128)S(1)}, f32[8,16,384]{2,1,0:T(8,128)S(1)}) custom-call(f32[2,3,5,5,8,128]{5,4,3,2,1,0:T(8,128)S(1)} %get-tuple-element.61.acc, f32[2,9,5,5,8,128]{5,4,3,2,1,0:T(8,128)S(1)} %get-tuple-element.62.early, f32[2,3,5,5,8,128]{5,4,3,2,1,0:T(8,128)S(1)} %get-tuple-element.44.vel_in.adj_vel, ...), custom_call_target="tpu_custom_call" | custom-call | flops 1000 | bytes 1000 | tf_op jit(solution)/shard_map/pallas_call | solution.py:715
  29.6 0.1 collective-permute-start.6
  29.7 0.5 %collective-permute-start.11 = (f32[150,2,128]{2,1,0:T(2,128)S(1)}, f32[150,2,128]{2,1,0:T(2,128)S(1)}, u32[]{:S(2)}, u32[]{:S(2)}) collective-permute-start(f32[150,2,128]{2,1,0:T(2,128)S(1)} %get-tuple-element.80), channel_id=1, source_target_pairs={{0,16},{16,0},{32,48},{48,32},{64,80},{80,64},{96,112},{112,96},{1... | collective-permute-start | bytes 460808 | tf_op jit(solution)/shard_map/ppermute | solution.py:637
  30.2 2.5 %collective-permute-start.12 = (f32[150,2,128]{2,1,0:T(2,128)S(1)}, f32[150,2,128]{2,1,0:T(2,128)S(1)}, u32[]{:S(2)}, u32[]{:S(2)}) collective-permute-start(f32[150,2,128]{2,1,0:T(2,128)S(1)} %get-tuple-element.81), channel_id=1, source_target_pairs={{0,112},{16,32},{32,16},{48,64},{64,48},{80,96},{96,80},{112,0},{1... | collective-permute-start | bytes 460808 | tf_op jit(solution)/shard_map/ppermute | solution.py:637
  32.7 0.0 collective-permute-done.6.got
  32.8 3.1 %collective-permute-start.7 = (f32[2,16,384]{2,1,0:T(8,128)S(1)}, f32[2,16,384]{2,1,0:T(8,128)S(1)}, u32[]{:S(2)}, u32[]{:S(2)}) collective-permute-start(f32[2,16,384]{2,1,0:T(8,128)S(1)} %get-tuple-element.70), channel_id=1, source_target_pairs={{0,8},{1,9},{2,10},{3,11},{4,12},{5,13},{6,14},{7,15},{8,0},{9,1},... | collective-permute-start | bytes 147464 | tf_op jit(solution)/shard_map/ppermute | solution.py:662
  35.9 0.6 %collective-permute-start.8 = (f32[2,16,384]{2,1,0:T(8,128)S(1)}, f32[2,16,384]{2,1,0:T(8,128)S(1)}, u32[]{:S(2)}, u32[]{:S(2)}) collective-permute-start(f32[2,16,384]{2,1,0:T(8,128)S(1)} %get-tuple-element.71), channel_id=1, source_target_pairs={{0,4},{1,5},{2,6},{3,7},{4,8},{5,9},{6,10},{7,11},{8,12},{9,13},{1... | collective-permute-start | bytes 147464 | tf_op jit(solution)/shard_map/ppermute | solution.py:662
  36.5 2.6 %collective-permute-start.9 = (f32[2,16,384]{2,1,0:T(8,128)S(1)}, f32[2,16,384]{2,1,0:T(8,128)S(1)}, u32[]{:S(2)}, u32[]{:S(2)}) collective-permute-start(f32[2,16,384]{2,1,0:T(8,128)S(1)} %get-tuple-element.72), channel_id=1, source_target_pairs={{0,12},{1,13},{2,14},{3,15},{4,0},{5,1},{6,2},{7,3},{8,4},{9,5},{1... | collective-permute-start | bytes 147464 | tf_op jit(solution)/shard_map/ppermute | solution.py:662
  39.1 0.8 %shard_map.101 = (f32[2,3,5,5,8,128]{5,4,3,2,1,0:T(8,128)S(1)}, f32[2,9,5,5,8,128]{5,4,3,2,1,0:T(8,128)S(1)}) custom-call(f32[2,3,5,5,8,128]{5,4,3,2,1,0:T(8,128)S(1)} %get-tuple-element.73.vel_in, f32[2,3,5,5,8,128]{5,4,3,2,1,0:T(8,128)S(1)} %get-tuple-element.74.acc, bf16[4,256,256]{2,1,0:T(8,128)(2,1)S(1)} %get-tuple-element.43.perms, ...), custom_call_target="tpu_custom_call" | custom-call | flops 100000000 | bytes 8000000 | tf_op jit(solution)/shard_map/pallas_call | solution.py:730
  39.9 1.3 %collective-permute-done.8.two = f32[2,16,384]{2,1,0:T(8,128)S(1)} collective-permute-done((f32[2,16,384]{2,1,0:T(8,128)S(1)}, f32[2,16,384]{2,1,0:T(8,128)S(1)}, u32[]{:S(2)}, u32[]{:S(2)}) %collective-permute-start.8) | collective-permute-done | bytes 49184 | tf_op jit(solution)/shard_map/ppermute | solution.py:662
  41.2 3.7 %collective-permute-start.10 = (f32[16,384]{1,0:T(8,128)S(1)}, f32[16,384]{1,0:T(8,128)S(1)}, u32[]{:S(2)}, u32[]{:S(2)}) collective-permute-start(f32[16,384]{1,0:T(8,128)S(1)} %get-tuple-element.77), channel_id=1, source_target_pairs={{0,2},{1,3},{2,0},{3,1},{4,6},{5,7},{6,4},{7,5},{8,10},{9,11},{10,... | collective-permute-start | bytes 73736 | tf_op jit(solution)/shard_map/ppermute | solution.py:662
  44.9 0.0 collective-permute-done.11.near
  44.9 0.0 collective-permute-done.12.far
  44.9 1.9 %shard_map.104 = f32[1125,2,128]{2,1,0:T(2,128)} custom-call(f32[2,3,5,5,8,128]{5,4,3,2,1,0:T(8,128)S(1)} %get-tuple-element.75.held.early_vel, f32[2,9,5,5,8,128]{5,4,3,2,1,0:T(8,128)S(1)} %get-tuple-element.78.early, f32[2,6,5,5,8,128]{5,4,3,2,1,0:T(8,128)S(1)} %get-tuple-element.79.stress_in, f32[2,5,5,8,128]{4,3,2,1,0:T(8,128)S(1)} %get-tuple-element.47.lam, ...), custom_call_target="tpu_custom_call" | custom-call | flops 100000000 | bytes 8000000 | tf_op jit(solution)/shard_map/pallas_call | solution.py:732
  46.7 0.9 %shard_map.103 = f32[125,3,16]{2,1,0:T(4,128)} custom-call(f32[16,384]{1,0:T(8,128)S(1)} %get-tuple-element.76.keep, f32[16,384]{1,0:T(8,128)S(1)} %collective-permute-done.10.got), custom_call_target="tpu_custom_call" | custom-call | flops 1000 | bytes 1000 | tf_op jit(solution)/shard_map/pallas_call | solution.py:668
  (14 shorter events, 0.1 us)
Async XLA Ops:
  0.6 7.4 %copy-start = (f32[3,5,5,5,256]{4,0,3,2,1:T(4,128)S(1)}, f32[3,5,5,5,256]{4,0,3,2,1:T(4,128)}, u32[]{:S(2)}) copy-start(f32[3,5,5,5,256]{4,0,3,2,1:T(4,128)} %param.10) | copy-start | bytes 1152004
  0.6 7.4 %copy-start.2 = (f32[1,2,3,256]{3,1,2,0:T(2,128)S(1)}, f32[1,2,3,256]{3,1,2,0:T(2,128)}, u32[]{:S(2)}) copy-start(f32[1,2,3,256]{3,1,2,0:T(2,128)} %param.15) | copy-start | bytes 18436
  0.7 7.4 %copy-start.4 = (s32[256]{0:T(256)S(1)}, s32[256]{0:T(256)}, u32[]{:S(2)}) copy-start(s32[256]{0:T(256)} %param.14) | copy-start | bytes 3076
  0.7 7.4 %copy-start.1 = (f32[1,9,5,5,5,256]{5,0,4,3,2,1:T(1,128)S(1)}, f32[1,9,5,5,5,256]{5,0,4,3,2,1:T(1,128)}, u32[]{:S(2)}) copy-start(f32[1,9,5,5,5,256]{5,0,4,3,2,1:T(1,128)} %param.9) | copy-start | bytes 3456004
  3.4 14.1 %copy-start.3 = (f32[1,2,3]{2,1,0:T(2,128)S(1)}, f32[1,2,3]{2,1,0:T(2,128)}, u32[]{:S(2)}) copy-start(f32[1,2,3]{2,1,0:T(2,128)} %pulse.1) | copy-start | bytes 76
  3.4 14.1 %collective-permute-start.2 = (f32[175,2,128]{2,1,0:T(2,128)S(1)}, f32[175,2,128]{2,1,0:T(2,128)S(1)}, u32[]{:S(2)}, u32[]{:S(2)}) collective-permute-start(f32[175,2,128]{2,1,0:T(2,128)S(1)} %get-tuple-element.52), channel_id=1, source_target_pairs={{0,16},{16,0},{32,48},{48,32},{64,80},{80,64},{96,112},{112,96},{1... | collective-permute-start | bytes 537608 | tf_op jit(solution)/shard_map/ppermute | solution.py:637
  5.5 12.1 %collective-permute-start.3 = (f32[175,2,128]{2,1,0:T(2,128)S(1)}, f32[175,2,128]{2,1,0:T(2,128)S(1)}, u32[]{:S(2)}, u32[]{:S(2)}) collective-permute-start(f32[175,2,128]{2,1,0:T(2,128)S(1)} %get-tuple-element.53), channel_id=1, source_target_pairs={{0,112},{16,32},{32,16},{48,64},{64,48},{80,96},{96,80},{112,0},{1... | collective-permute-start | bytes 537608 | tf_op jit(solution)/shard_map/ppermute | solution.py:637
  10.2 14.3 %collective-permute-start = (f32[150,2,128]{2,1,0:T(2,128)S(1)}, f32[150,2,128]{2,1,0:T(2,128)S(1)}, u32[]{:S(2)}, u32[]{:S(2)}) collective-permute-start(f32[150,2,128]{2,1,0:T(2,128)S(1)} %get-tuple-element.50), channel_id=1, source_target_pairs={{0,16},{16,0},{32,48},{48,32},{64,80},{80,64},{96,112},{112,96},{1... | collective-permute-start | bytes 460808 | tf_op jit(solution)/shard_map/ppermute | solution.py:637
  10.7 13.8 %collective-permute-start.1 = (f32[150,2,128]{2,1,0:T(2,128)S(1)}, f32[150,2,128]{2,1,0:T(2,128)S(1)}, u32[]{:S(2)}, u32[]{:S(2)}) collective-permute-start(f32[150,2,128]{2,1,0:T(2,128)S(1)} %get-tuple-element.51), channel_id=1, source_target_pairs={{0,112},{16,32},{32,16},{48,64},{64,48},{80,96},{96,80},{112,0},{1... | collective-permute-start | bytes 460808 | tf_op jit(solution)/shard_map/ppermute | solution.py:637
  19.4 9.3 %collective-permute-start.4 = (f32[75,2,128]{2,1,0:T(2,128)S(1)}, f32[75,2,128]{2,1,0:T(2,128)S(1)}, u32[]{:S(2)}, u32[]{:S(2)}) collective-permute-start(f32[75,2,128]{2,1,0:T(2,128)S(1)} %get-tuple-element.65), channel_id=1, source_target_pairs={{0,16},{16,0},{32,48},{48,32},{64,80},{80,64},{96,112},{112,96},{1... | collective-permute-start | bytes 230408 | tf_op jit(solution)/shard_map/ppermute | solution.py:637
  21.9 6.8 %collective-permute-start.5 = (f32[75,2,128]{2,1,0:T(2,128)S(1)}, f32[75,2,128]{2,1,0:T(2,128)S(1)}, u32[]{:S(2)}, u32[]{:S(2)}) collective-permute-start(f32[75,2,128]{2,1,0:T(2,128)S(1)} %get-tuple-element.66), channel_id=1, source_target_pairs={{0,112},{16,32},{32,16},{48,64},{64,48},{80,96},{96,80},{112,0},{1... | collective-permute-start | bytes 230408 | tf_op jit(solution)/shard_map/ppermute | solution.py:637
  29.6 3.2 %collective-permute-start.6 = (f32[8,16,384]{2,1,0:T(8,128)S(1)}, f32[8,16,384]{2,1,0:T(8,128)S(1)}, u32[]{:S(2)}, u32[]{:S(2)}) collective-permute-start(f32[8,16,384]{2,1,0:T(8,128)S(1)} %get-tuple-element.68), channel_id=1, source_target_pairs={{0,1},{1,0},{2,3},{3,2},{4,5},{5,4},{6,7},{7,6},{8,9},{9,8},{10,11... | collective-permute-start | bytes 589832 | tf_op jit(solution)/shard_map/ppermute | solution.py:662
  29.7 15.2 %collective-permute-start.11 = (f32[150,2,128]{2,1,0:T(2,128)S(1)}, f32[150,2,128]{2,1,0:T(2,128)S(1)}, u32[]{:S(2)}, u32[]{:S(2)}) collective-permute-start(f32[150,2,128]{2,1,0:T(2,128)S(1)} %get-tuple-element.80), channel_id=1, source_target_pairs={{0,16},{16,0},{32,48},{48,32},{64,80},{80,64},{96,112},{112,96},{1... | collective-permute-start | bytes 460808 | tf_op jit(solution)/shard_map/ppermute | solution.py:637
  30.2 14.7 %collective-permute-start.12 = (f32[150,2,128]{2,1,0:T(2,128)S(1)}, f32[150,2,128]{2,1,0:T(2,128)S(1)}, u32[]{:S(2)}, u32[]{:S(2)}) collective-permute-start(f32[150,2,128]{2,1,0:T(2,128)S(1)} %get-tuple-element.81), channel_id=1, source_target_pairs={{0,112},{16,32},{32,16},{48,64},{64,48},{80,96},{96,80},{112,0},{1... | collective-permute-start | bytes 460808 | tf_op jit(solution)/shard_map/ppermute | solution.py:637
  32.8 7.1 %collective-permute-start.7 = (f32[2,16,384]{2,1,0:T(8,128)S(1)}, f32[2,16,384]{2,1,0:T(8,128)S(1)}, u32[]{:S(2)}, u32[]{:S(2)}) collective-permute-start(f32[2,16,384]{2,1,0:T(8,128)S(1)} %get-tuple-element.70), channel_id=1, source_target_pairs={{0,8},{1,9},{2,10},{3,11},{4,12},{5,13},{6,14},{7,15},{8,0},{9,1},... | collective-permute-start | bytes 147464 | tf_op jit(solution)/shard_map/ppermute | solution.py:662
  35.9 5.3 %collective-permute-start.8 = (f32[2,16,384]{2,1,0:T(8,128)S(1)}, f32[2,16,384]{2,1,0:T(8,128)S(1)}, u32[]{:S(2)}, u32[]{:S(2)}) collective-permute-start(f32[2,16,384]{2,1,0:T(8,128)S(1)} %get-tuple-element.71), channel_id=1, source_target_pairs={{0,4},{1,5},{2,6},{3,7},{4,8},{5,9},{6,10},{7,11},{8,12},{9,13},{1... | collective-permute-start | bytes 147464 | tf_op jit(solution)/shard_map/ppermute | solution.py:662
  36.5 4.7 %collective-permute-start.9 = (f32[2,16,384]{2,1,0:T(8,128)S(1)}, f32[2,16,384]{2,1,0:T(8,128)S(1)}, u32[]{:S(2)}, u32[]{:S(2)}) collective-permute-start(f32[2,16,384]{2,1,0:T(8,128)S(1)} %get-tuple-element.72), channel_id=1, source_target_pairs={{0,12},{1,13},{2,14},{3,15},{4,0},{5,1},{6,2},{7,3},{8,4},{9,5},{1... | collective-permute-start | bytes 147464 | tf_op jit(solution)/shard_map/ppermute | solution.py:662
  41.2 5.5 %collective-permute-start.10 = (f32[16,384]{1,0:T(8,128)S(1)}, f32[16,384]{1,0:T(8,128)S(1)}, u32[]{:S(2)}, u32[]{:S(2)}) collective-permute-start(f32[16,384]{1,0:T(8,128)S(1)} %get-tuple-element.77), channel_id=1, source_target_pairs={{0,2},{1,3},{2,0},{3,1},{4,6},{5,7},{6,4},{7,5},{8,10},{9,11},{10,... | collective-permute-start | bytes 73736 | tf_op jit(solution)/shard_map/ppermute | solution.py:662
